TPU v7x, 32 devices: a whole 2x2x4 slice. The times are simulated.
32 devices in a mesh: expert: 16 (over z, y, x), tensor: 2 (over core).
Axes of the slice: x: 2, y: 2, z: 4, core: 2. Of those that a mesh axis runs over, the one named last changes fastest.
Arguments:
- tokens: bfloat16 [4096, 2048], P('expert', 'tensor'), may hold values from -6 to 6
- upstream: bfloat16 [4096, 2048], P('expert', 'tensor'), may hold values from -6 to 6
- expert_ids: int32 [4096, 1], P('expert'), may hold values from 0 to 15; in each aligned block of 256 rows (0 to 255, 256 to 511, ...) at most 32 rows name the same one
- w_gate: bfloat16 [16, 1408, 2048], P('expert', 'tensor'), may hold values from -0.125 to 0.125
- w_up: bfloat16 [16, 1408, 2048], P('expert', 'tensor'), may hold values from -0.125 to 0.125
- w_down: bfloat16 [16, 1408, 2048], P('expert', 'tensor'), may hold values from -0.15625 to 0.15625
Outputs:
- grad_tokens: bfloat16 [4096, 2048], P('expert', 'tensor')
- grad_gate: bfloat16 [16, 1408, 2048], P('expert', 'tensor')
- grad_up: bfloat16 [16, 1408, 2048], P('expert', 'tensor')
- grad_down: bfloat16 [16, 1408, 2048], P('expert', 'tensor')
Inputs may be any that keep to these rules, and one draw needn't show every extreme that they name: `expert_ids`: among the 256 tokens of one index of expert, at most 32 name the same expert, and in some such block one expert is named exactly 32 times; every expert is named somewhere.
All inputs are finite; a program needn't handle non-finite values.
Results may differ from a plain program's by a relative error of at most 0.014.
Values may be sent and summed in bfloat16 or wider, within the bound.
No kernel may reach another device: no remote copies, remote signals or barrier semaphores. Data moves between devices by JAX's collectives and lax.ppermute only.
A program may use at most 64 MiB of HBM per device.

v0:
```python
import jax
import jax.numpy as jnp
from jax import lax
from jax.sharding import PartitionSpec as P


def on_device(tokens, upstream, expert_ids, w_gate, w_up, w_down):
    experts = lax.axis_size("expert")
    tok_rows = tokens.shape[0]
    capacity = max(2, 2 * tok_rows // experts)
    slot_count = experts * capacity
    route = expert_ids[:, 0]
    onehot = (route[:, None] == jnp.arange(experts, dtype=jnp.int32)[None, :]).astype(jnp.int32)
    before = jnp.cumsum(onehot, axis=0) - onehot
    within = jnp.sum(before * onehot, axis=1)
    target = route * capacity + within
    placing = (target[None, :] == jnp.arange(slot_count, dtype=jnp.int32)[:, None]).astype(
        jnp.bfloat16
    )
    gate_rows = w_gate[0]
    up_rows = w_up[0]
    down_rows = w_down[0]
    full_width = gate_rows.shape[1]

    def spread(values):
        placed = jnp.dot(placing, values, preferred_element_type=jnp.float32).astype(jnp.bfloat16)
        return placed.reshape(experts, capacity, values.shape[1])

    got_x, got_dy = (
        lax.all_to_all(spread(tokens), "expert", split_axis=0, concat_axis=0, tiled=True),
        lax.all_to_all(spread(upstream), "expert", split_axis=0, concat_axis=0, tiled=True),
    )
    x_all = lax.all_gather(got_x.reshape(slot_count, tokens.shape[1]), "tensor", axis=1, tiled=True)
    dy_all = got_dy.reshape(slot_count, tokens.shape[1])
    gate_pre = lax.dot_general(
        x_all, gate_rows, (((1,), (1,)), ((), ())), preferred_element_type=jnp.float32
    )
    up_pre = lax.dot_general(
        x_all, up_rows, (((1,), (1,)), ((), ())), preferred_element_type=jnp.float32
    )
    gate_pre, up_pre = (gate_pre, up_pre)
    sig_gate = jax.nn.sigmoid(gate_pre)
    silu_gate = gate_pre * sig_gate
    hidden = (silu_gate * up_pre).astype(jnp.bfloat16)
    piece = lax.all_gather(dy_all, "tensor", axis=1, tiled=True)
    d_hidden = lax.dot_general(
        piece, down_rows, (((1,), (1,)), ((), ())), preferred_element_type=jnp.float32
    )
    block_grad = lax.dot_general(
        hidden, piece, (((0,), (0,)), ((), ())), preferred_element_type=jnp.float32
    )
    down_grad = block_grad
    d_hidden, down_grad = (d_hidden, down_grad)
    d_up = (d_hidden * silu_gate).astype(jnp.bfloat16)
    d_gate = (d_hidden * up_pre * sig_gate * (1.0 + gate_pre * (1.0 - sig_gate))).astype(
        jnp.bfloat16
    )
    grad_gate = lax.dot_general(
        d_gate, x_all, (((0,), (0,)), ((), ())), preferred_element_type=jnp.float32
    ).astype(jnp.bfloat16)
    grad_up = lax.dot_general(
        d_up, x_all, (((0,), (0,)), ((), ())), preferred_element_type=jnp.float32
    ).astype(jnp.bfloat16)
    grad_down = down_grad.astype(jnp.bfloat16)
    partial_rows = jnp.dot(d_gate, gate_rows, preferred_element_type=jnp.float32) + jnp.dot(
        d_up, up_rows, preferred_element_type=jnp.float32
    )
    feat_width = tokens.shape[1]
    totals = lax.psum(partial_rows.astype(jnp.bfloat16), "tensor")
    arrived = lax.all_to_all(
        totals.reshape(experts, capacity, full_width),
        "expert",
        split_axis=0,
        concat_axis=0,
        tiled=True,
    )
    returned = lax.dynamic_slice_in_dim(
        arrived.reshape(slot_count, full_width),
        lax.axis_index("tensor") * feat_width,
        feat_width,
        1,
    )
    grad_tokens = lax.dot_general(
        placing, returned, (((0,), (0,)), ((), ())), preferred_element_type=jnp.float32
    ).astype(jnp.bfloat16)
    return (grad_tokens, grad_gate[None], grad_up[None], grad_down[None])


def solution(mesh):
    in_specs = (
        P("expert", "tensor"),
        P("expert", "tensor"),
        P("expert", None),
        P("expert", "tensor", None),
        P("expert", "tensor", None),
        P("expert", "tensor", None),
    )
    out_specs = (
        P("expert", "tensor"),
        P("expert", "tensor", None),
        P("expert", "tensor", None),
        P("expert", "tensor", None),
    )
    return jax.shard_map(
        on_device, mesh=mesh, in_specs=in_specs, out_specs=out_specs, check_vma=False
    )
```

profile of v0, /device:TPU:8, one launch (start us, length us, event | category | flops | bytes accessed | tf_op | source)
XLA Modules:
  0.0 181.3 jit_solution(10140718664664908539)
XLA Ops:
  7.2 0.0 copy-start
  7.2 0.0 all-gather.5.cloned.1.call-start
  7.2 0.8 fusion.21
  8.1 0.6 reduce-window.6
  8.6 0.2 slice_reduce_fusion
  8.9 0.8 fusion.20
  9.6 0.7 multiply_add_fusion
  10.3 1.5 convolution_convert_fusion.3
  11.9 32.8 %all_to_all.15 = bf16[16,32,1024]{2,1,0:T(8,128)(2,1)} all-to-all(bf16[16,32,1024]{2,1,0:T(8,128)(2,1)S(1)} %bitcast.62), channel_id=1, replica_groups=mesh['expert'=16,'tensor'=2] {'expert'}, dimensions={0} | all-to-all | bytes 2097152 | tf_op jit(solution)/shard_map/all_to_all | solution.py:30
  44.7 0.0 all-gather.5.cloned.1.call-update
  44.7 0.0 all-gather.3.cloned.1.call-start
  44.8 0.0 copy-done.2
  44.8 0.4 convolution_convert_fusion.4
  45.2 29.5 %all_to_all.16 = bf16[16,32,1024]{2,1,0:T(8,128)(2,1)} all-to-all(bf16[16,32,1024]{2,1,0:T(8,128)(2,1)S(1)} %bitcast.63), channel_id=1, replica_groups=mesh['expert'=16,'tensor'=2] {'expert'}, dimensions={0} | all-to-all | bytes 2097152 | tf_op jit(solution)/shard_map/all_to_all | solution.py:31
  74.7 0.0 all-gather.3.cloned.1.call-update
  74.7 0.0 all-reduce.2.cloned.1.call-start
  74.8 0.0 all-gather.5.cloned.1.call-done
  74.8 0.0 copy-done
  74.8 0.0 copy-start.3
  74.8 0.0 copy-start.5
  74.8 4.6 %fusion.5 = f32[512,704]{0,1:T(8,128)} fusion(bf16[512,2048]{1,0:T(8,128)(2,1)} %all-gather.5.cloned.1.call-done, bf16[1,704,2048]{2,1,0:T(8,128)(2,1)S(1)} %copy-done), kind=kOutput, calls=%fused_computation.9 | convolution fusion | flops 1476395008 | bytes 6422528 | tf_op jit(solution)/shard_map/dot_general | solution.py:35
  79.4 0.0 copy-done.3
  79.4 0.0 copy-done.5
  79.4 2.8 %fusion.8 = f32[512,704]{0,1:T(8,128)} fusion(bf16[512,2048]{1,0:T(8,128)(2,1)S(1)} %copy-done.5, bf16[1,704,2048]{2,1,0:T(8,128)(2,1)S(1)} %copy-done.3), kind=kOutput, calls=%fused_computation.12 | convolution fusion | flops 1476395008 | bytes 6422528 | tf_op jit(solution)/shard_map/dot_general | solution.py:38
  82.2 1.9 %all-gather.3.cloned.1.call-done = bf16[512,2048]{1,0:T(8,128)(2,1)} async-done(((bf16[512,1024]{1,0:T(8,128)(2,1)}), bf16[512,2048]{1,0:T(8,128)(2,1)}) %all-gather.3.cloned.1.call-update) | async-done | bytes 2097168 | tf_op jit(solution)/shard_map/all_gather | solution.py:45
  84.2 5.4 %multiply_convert_fusion.1 = (bf16[512,704]{0,1:T(8,128)(2,1)S(1)}, bf16[512,704]{0,1:T(8,128)(2,1)S(1)}) fusion(f32[512,704]{0,1:T(8,128)} %fusion.5, f32[512,704]{0,1:T(8,128)} %fusion.8, bf16[512,2048]{1,0:T(8,128)(2,1)} %all-gather.3.cloned.1.call-done, bf16[1,704,2048]{2,1,0:T(8,128)(2,1)} %param.11), kind=kOutput, calls=%fused_computation.19 | convolution fusion | flops 1481080832 | bytes 9306112 | tf_op jit(solution)/shard_map/dot_general | solution.py:46
  89.5 0.0 copy-start.1
  89.6 0.0 copy-start.8
  89.6 0.0 copy-start.4
  89.6 1.8 %fusion.3 = f32[512,2048]{1,0:T(8,128)S(1)} fusion(bf16[512,704]{0,1:T(8,128)(2,1)S(1)} %get-tuple-element.5, bf16[1,704,2048]{2,1,0:T(8,128)(2,1)S(1)} %copy-done), kind=kOutput, calls=%fused_computation.7 | convolution fusion | flops 1476395008 | bytes 7798784 | tf_op jit(solution)/shard_map/dot_general | solution.py:65
  91.4 0.0 copy-done.1
  91.5 0.0 copy-done.8
  91.5 0.4 copy-done.4
  91.9 3.3 %add_convert_fusion = bf16[512,2048]{1,0:T(8,128)(2,1)} fusion(f32[512,2048]{1,0:T(8,128)S(1)} %fusion.3, bf16[512,704]{0,1:T(8,128)(2,1)S(1)} %get-tuple-element.4, bf16[1,704,2048]{2,1,0:T(8,128)(2,1)S(1)} %copy-done.4), kind=kOutput, calls=%fused_computation | convolution fusion | flops 1478492160 | bytes 9895936 | tf_op jit(solution)/shard_map/dot_general | solution.py:65
  95.2 0.0 all-reduce.2.cloned.1.call-update
  95.2 22.6 %all-reduce.2.cloned.1.call-done = bf16[16,32,2048]{2,1,0:T(8,128)(2,1)} async-done(((bf16[16,32,2048]{2,1,0:T(8,128)(2,1)}), bf16[16,32,2048]{2,1,0:T(8,128)(2,1)}) %all-reduce.2.cloned.1.call-update) | async-done | bytes 2097168 | tf_op jit(solution)/shard_map/psum | solution.py:69
  117.8 7.0 %all-to-all-start.2 = ((bf16[16,32,2048]{2,1,0:T(8,128)(2,1)}), bf16[16,32,2048]{2,1,0:T(8,128)(2,1)}, u32[]{:S(2)}, u32[]{:S(2)}) async-start(bf16[16,32,2048]{2,1,0:T(8,128)(2,1)} %all-reduce.2.cloned.1.call-done), calls=%async_computation.2 | async-start | bytes 4194304 | tf_op jit(solution)/shard_map/all_to_all | solution.py:70
  124.8 0.0 copy-start.9
  124.8 5.2 %fusion = bf16[1,704,2048]{2,1,0:T(8,128)(2,1)} fusion(bf16[512,704]{0,1:T(8,128)(2,1)} %copy-done.1, bf16[512,2048]{1,0:T(8,128)(2,1)} %all-gather.5.cloned.1.call-done), kind=kOutput, calls=%fused_computation.4 | convolution fusion | flops 1477836800 | bytes 5701632 | tf_op jit(solution)/shard_map/dot_general | solution.py:58
  130.0 0.0 copy-done.6
  130.0 0.0 copy-done.9
  130.0 0.0 copy-start.10
  130.0 0.0 copy-start.11
  130.0 3.2 %fusion.1 = bf16[1,704,2048]{2,1,0:T(8,128)(2,1)} fusion(bf16[512,704]{0,1:T(8,128)(2,1)S(1)} %copy-done.9, bf16[512,2048]{1,0:T(8,128)(2,1)S(1)} %copy-done.6), kind=kOutput, calls=%fused_computation.5 | convolution fusion | flops 1477836800 | bytes 5701632 | tf_op jit(solution)/shard_map/dot_general | solution.py:61
  133.3 0.0 copy-done.11
  133.3 3.3 %fusion.2 = bf16[1,704,2048]{2,1,0:T(8,128)(2,1)} fusion(bf16[512,2048]{1,0:T(8,128)(2,1)S(1)} %copy-done.7, f32[512,704]{0,1:T(8,128)S(1)} %copy-done.11, f32[512,704]{0,1:T(8,128)S(1)} %copy-done.10), kind=kOutput, calls=%fused_computation.6 | convolution fusion | flops 1479999488 | bytes 7864320 | tf_op jit(solution)/shard_map/dot_general | solution.py:49
  136.6 35.7 %all-to-all-done.2 = bf16[16,32,2048]{2,1,0:T(8,128)(2,1)} async-done(((bf16[16,32,2048]{2,1,0:T(8,128)(2,1)}), bf16[16,32,2048]{2,1,0:T(8,128)(2,1)}, u32[]{:S(2)}, u32[]{:S(2)}) %all-to-all-start.2) | async-done | bytes 2097184 | tf_op jit(solution)/shard_map/all_to_all | solution.py:70
  172.3 2.5 %convolution_convert_fusion.5 = bf16[256,1024]{1,0:T(8,128)(2,1)} fusion(bf16[512,2048]{1,0:T(8,128)(2,1)} %bitcast.11, s32[]{:T(128)S(6)} %select_n.3, s32[256]{0:T(256)S(1)} %multiply_add_fusion), kind=kOutput, calls=%fused_computation.23 | convolution fusion | flops 268828672 | bytes 1573892 | tf_op jit(solution)/shard_map/dot_general | solution.py:83
  (7 shorter events, 0.1 us)
Async XLA Ops:
  7.2 67.6 %copy-start = (bf16[1,704,2048]{2,1,0:T(8,128)(2,1)S(1)}, bf16[1,704,2048]{2,1,0:T(8,128)(2,1)}, u32[]{:S(2)}) copy-start(bf16[1,704,2048]{2,1,0:T(8,128)(2,1)} %param.9) | copy-start | bytes 8650756
  7.2 67.6 %all-gather.5.cloned.1.call-start = ((), (), s32[]{:S(2)}) async-start(), calls=%async_computation.4 | async-start | bytes 3145728 | tf_op jit(solution)/shard_map/all_gather | solution.py:33
  10.3 34.5 %copy-start.2 = (bf16[256,1024]{1,0:T(8,128)(2,1)S(1)}, bf16[256,1024]{1,0:T(8,128)(2,1)}, u32[]{:S(2)}) copy-start(bf16[256,1024]{1,0:T(8,128)(2,1)} %param.7) | copy-start | bytes 1572868
  44.7 39.5 %all-gather.3.cloned.1.call-start = ((), (), s32[]{:S(2)}) async-start(), calls=%async_computation.3 | async-start | bytes 3145728 | tf_op jit(solution)/shard_map/all_gather | solution.py:45
  74.7 43.1 %all-reduce.2.cloned.1.call-start = ((), (), s32[]{:S(2)}) async-start(), calls=%async_computation.5 | async-start | bytes 4194304 | tf_op jit(solution)/shard_map/psum | solution.py:69
  74.8 4.6 %copy-start.3 = (bf16[1,704,2048]{2,1,0:T(8,128)(2,1)S(1)}, bf16[1,704,2048]{2,1,0:T(8,128)(2,1)}, u32[]{:S(2)}) copy-start(bf16[1,704,2048]{2,1,0:T(8,128)(2,1)} %param.10) | copy-start | bytes 8650756
  74.8 4.6 %copy-start.5 = (bf16[512,2048]{1,0:T(8,128)(2,1)S(1)}, bf16[512,2048]{1,0:T(8,128)(2,1)}, u32[]{:S(2)}) copy-start(bf16[512,2048]{1,0:T(8,128)(2,1)} %all-gather.5.cloned.1.call-done) | copy-start | bytes 6291460
  89.5 1.9 %copy-start.1 = (bf16[512,704]{0,1:T(8,128)(2,1)}, bf16[512,704]{0,1:T(8,128)(2,1)S(1)}, u32[]{:S(2)}) copy-start(bf16[512,704]{0,1:T(8,128)(2,1)S(1)} %get-tuple-element.5) | copy-start | bytes 2162692
  89.6 1.9 %copy-start.8 = (bf16[512,704]{0,1:T(8,128)(2,1)}, bf16[512,704]{0,1:T(8,128)(2,1)S(1)}, u32[]{:S(2)}) copy-start(bf16[512,704]{0,1:T(8,128)(2,1)S(1)} %get-tuple-element.4) | copy-start | bytes 2162692
  89.6 2.3 %copy-start.4 = (bf16[1,704,2048]{2,1,0:T(8,128)(2,1)S(1)}, bf16[1,704,2048]{2,1,0:T(8,128)(2,1)}, u32[]{:S(2)}) copy-start(bf16[1,704,2048]{2,1,0:T(8,128)(2,1)} %param.10) | copy-start | bytes 8650756
  117.8 54.5 %all-to-all-start.2 = ((bf16[16,32,2048]{2,1,0:T(8,128)(2,1)}), bf16[16,32,2048]{2,1,0:T(8,128)(2,1)}, u32[]{:S(2)}, u32[]{:S(2)}) async-start(bf16[16,32,2048]{2,1,0:T(8,128)(2,1)} %all-reduce.2.cloned.1.call-done), calls=%async_computation.2 | async-start | bytes 4194304 | tf_op jit(solution)/shard_map/all_to_all | solution.py:70
  124.8 5.2 %copy-start.6 = (bf16[512,2048]{1,0:T(8,128)(2,1)S(1)}, bf16[512,2048]{1,0:T(8,128)(2,1)}, u32[]{:S(2)}) copy-start(bf16[512,2048]{1,0:T(8,128)(2,1)} %all-gather.5.cloned.1.call-done) | copy-start | bytes 6291460
  124.8 5.2 %copy-start.9 = (bf16[512,704]{0,1:T(8,128)(2,1)S(1)}, bf16[512,704]{0,1:T(8,128)(2,1)}, u32[]{:S(2)}) copy-start(bf16[512,704]{0,1:T(8,128)(2,1)} %copy-done.8) | copy-start | bytes 2162692
  130.0 3.3 %copy-start.7 = (bf16[512,2048]{1,0:T(8,128)(2,1)S(1)}, bf16[512,2048]{1,0:T(8,128)(2,1)}, u32[]{:S(2)}) copy-start(bf16[512,2048]{1,0:T(8,128)(2,1)} %all-gather.3.cloned.1.call-done) | copy-start | bytes 6291460
  130.0 3.3 %copy-start.10 = (f32[512,704]{0,1:T(8,128)S(1)}, f32[512,704]{0,1:T(8,128)}, u32[]{:S(2)}) copy-start(f32[512,704]{0,1:T(8,128)} %fusion.5) | copy-start | bytes 4325380
  130.0 3.3 %copy-start.11 = (f32[512,704]{0,1:T(8,128)S(1)}, f32[512,704]{0,1:T(8,128)}, u32[]{:S(2)}) copy-start(f32[512,704]{0,1:T(8,128)} %fusion.8) | copy-start | bytes 4325380
Sparse Core Ops, SparseCore 0:
  44.8 9.3 all-gather.4
  74.8 9.2 all-gather.2
  95.4 22.3 all-reduce.1
where the time goes:
time: 183 us; the launch traced here: 181 us
  blocking collectives  62.3 us (34%)
  waiting for transfers between devices  60.3 us (33%)
  matrix products  34.1 us (19%)
  between operations  13.9 us (8%)
  starting transfers between devices  7.1 us (4%)
  other arithmetic  2.9 us (2%)
    all_to_all x1, waiting for transfers between devices, on_device(): lax.all_to_all(totals.reshape(experts, capacity, full_width), 'expert', s...  35.7 us
    all_to_all x1, blocking collectives, on_device(): lax.all_to_all(spread(tokens), 'expert', split_axis=0, concat_axis=0, til...  32.8 us
    all_to_all x1, blocking collectives, on_device(): lax.all_to_all(spread(upstream), 'expert', split_axis=0, concat_axis=0, t...  29.5 us
    psum x1, waiting for transfers between devices, on_device(): totals = lax.psum(partial_rows.astype(jnp.bfloat16), 'tensor')  22.6 us
    all_to_all x1, starting transfers between devices, on_device(): lax.all_to_all(totals.reshape(experts, capacity, full_width), 'expert', s...  6.97 us
    dot_general x1, matrix products, on_device(): lax.dot_general(piece, down_rows, (((1,), (1,)), ((), ())), preferred_ele...  5.37 us
    dot_general x1, matrix products, on_device(): lax.dot_general(d_gate, x_all, (((0,), (0,)), ((), ())), preferred_elemen...  5.2 us
    dot_general x1, matrix products, on_device(): lax.dot_general(x_all, gate_rows, (((1,), (1,)), ((), ())), preferred_ele...  4.61 us
  transfers between devices with their start and end apart: 4, of which 3 were waited for; matrix products, arithmetic and copies ran while one was open for 11% of the time, Pallas kernels for 0%

commit v1 on v0

v1 whole, which is shorter than its diff:
```python
import jax
import jax.numpy as jnp
from jax import lax
from jax.sharding import PartitionSpec as P

F32 = jnp.float32
BF16 = jnp.bfloat16


def gather_features(own):
    if lax.axis_size("tensor") != 2:
        return lax.all_gather(own, "tensor", axis=1, tiled=True)
    other = lax.ppermute(own, "tensor", [(0, 1), (1, 0)])
    first = lax.axis_index("tensor") == 0
    return jnp.concatenate(
        [jnp.where(first, own, other), jnp.where(first, other, own)], axis=1
    )


def scatter_sum(partial):
    parts = lax.axis_size("tensor")
    width = partial.shape[1] // parts
    if parts != 2:
        return lax.psum_scatter(
            partial.astype(BF16), "tensor", scatter_dimension=1, tiled=True
        )
    first = lax.axis_index("tensor") == 0
    lower, upper = partial[:, :width], partial[:, width:]
    sent = jnp.where(first, upper, lower).astype(BF16)
    kept = jnp.where(first, lower, upper)
    got = lax.ppermute(sent, "tensor", [(0, 1), (1, 0)])
    return (kept + got.astype(F32)).astype(BF16)


def on_device(tokens, upstream, expert_ids, w_gate, w_up, w_down):
    experts = lax.axis_size("expert")
    tok_rows, feat_width = tokens.shape
    capacity = max(2, 2 * tok_rows // experts)
    slot_count = experts * capacity
    route = expert_ids[:, 0]
    onehot = (route[:, None] == jnp.arange(experts, dtype=jnp.int32)[None, :]).astype(jnp.int32)
    before = jnp.cumsum(onehot, axis=0) - onehot
    within = jnp.sum(before * onehot, axis=1)
    target = route * capacity + within
    placing = (target[None, :] == jnp.arange(slot_count, dtype=jnp.int32)[:, None]).astype(BF16)
    gate_rows, up_rows, down_rows = w_gate[0], w_up[0], w_down[0]

    def spread(values):
        placed = jnp.dot(placing, values, preferred_element_type=F32).astype(BF16)
        placed = placed.reshape(experts, capacity, feat_width)
        got = lax.all_to_all(placed, "expert", split_axis=0, concat_axis=0, tiled=True)
        return got.reshape(slot_count, feat_width)

    def rows_by_weights(rows, weights):
        return lax.dot_general(
            rows, weights, (((1,), (1,)), ((), ())), preferred_element_type=F32
        )

    def weight_grad(left, right):
        return lax.dot_general(
            left, right, (((0,), (0,)), ((), ())), preferred_element_type=F32
        ).astype(BF16)

    got_x, got_dy = spread(tokens), spread(upstream)
    x_all = gather_features(got_x)
    gate_pre = rows_by_weights(x_all, gate_rows)
    up_pre = rows_by_weights(x_all, up_rows)
    sig_gate = jax.nn.sigmoid(gate_pre)
    silu_gate = gate_pre * sig_gate
    hidden = (silu_gate * up_pre).astype(BF16)
    dy_all = gather_features(got_dy)
    d_hidden = rows_by_weights(dy_all, down_rows)
    d_up = (d_hidden * silu_gate).astype(BF16)
    d_gate = (d_hidden * up_pre * sig_gate * (1.0 + gate_pre * (1.0 - sig_gate))).astype(BF16)
    partial_rows = jnp.dot(d_gate, gate_rows, preferred_element_type=F32) + jnp.dot(
        d_up, up_rows, preferred_element_type=F32
    )
    totals = scatter_sum(partial_rows)
    returned = lax.all_to_all(
        totals.reshape(experts, capacity, feat_width),
        "expert",
        split_axis=0,
        concat_axis=0,
        tiled=True,
    ).reshape(slot_count, feat_width)
    grad_gate = weight_grad(d_gate, x_all)
    grad_up = weight_grad(d_up, x_all)
    grad_down = weight_grad(hidden, dy_all)
    grad_tokens = weight_grad(placing, returned)
    return (grad_tokens, grad_gate[None], grad_up[None], grad_down[None])


def solution(mesh):
    rows = P("expert", "tensor")
    weights = P("expert", "tensor", None)
    return jax.shard_map(
        on_device,
        mesh=mesh,
        in_specs=(rows, rows, P("expert", None), weights, weights, weights),
        out_specs=(rows, weights, weights, weights),
        check_vma=False,
    )
```

time: 183 us -> 121 us (0.66)
  blocking collectives: 62.3 us -> 0 us
  between operations: 13.9 us -> 0.95 us
  starting transfers between devices: 7.1 us -> 17 us
  matrix products: 34.1 us -> 27.3 us
  other arithmetic: 2.9 us -> 8.48 us
  waiting for transfers between devices: 60.3 us -> 65.1 us
    all_to_all x2 -> x0, blocking collectives: 62.3 us -> none  [the longest x1 32.8 us: on_device(): lax.all_to_all(spread(tokens), 'expert', split_axis=0, concat_axis=0, til...]
    all_to_all x1 -> x3, waiting for transfers between devices: 35.7 us -> 62.4 us  [the longest x2 48.3 us: spread(): lax.all_to_all(placed, 'expert', split_axis=0, concat_axis=0, tiled=True)]
    psum x1 -> x0, waiting for transfers between devices: 22.6 us -> none  [on_device(): totals = lax.psum(partial_rows.astype(jnp.bfloat16), 'tensor')]
    all_to_all x1 -> x3, starting transfers between devices: 6.97 us -> 16.9 us  [the longest x2 12 us: spread(): lax.all_to_all(placed, 'expert', split_axis=0, concat_axis=0, tiled=True)]
    dot_general x11, matrix products: 34.1 us -> 27.3 us  [the longest x4 14.2 us: weight_grad(): lax.dot_general(left, right, (((0,), (0,)), ((), ())), preferred_element_...]
    select_n x0 -> x2, other arithmetic: none -> 3.75 us  [gather_features(): jnp.where(first, own, other)]
    ppermute x0 -> x3, waiting for transfers between devices: none -> 2.65 us  [the longest x1 2.65 us: scatter_sum(): got = lax.ppermute(sent, 'tensor', [(0, 1), (1, 0)])]
    all_gather x2 -> x0, waiting for transfers between devices: 1.97 us -> none  [the longest x1 1.95 us: on_device(): piece = lax.all_gather(dy_all, 'tensor', axis=1, tiled=True)]
  transfers between devices with their start and end apart: 4 -> 6, of which waited for: 3 -> 4; matrix products, arithmetic and copies ran while one was open for 11% -> 15% of each run, Pallas kernels for 0% -> 0%
where the time goes in v1:
time: 121 us; the launch traced here: 120 us
  waiting for transfers between devices  65.1 us (54%)
  matrix products  27.3 us (23%)
  starting transfers between devices  17 us (14%)
  other arithmetic  8.48 us (7%)
  local copies, waits for them, and re-layouts  1.52 us (1%)
    all_to_all x2, waiting for transfers between devices, spread(): lax.all_to_all(placed, 'expert', split_axis=0, concat_axis=0, tiled=True)  48.3 us
    dot_general x4, matrix products, weight_grad(): lax.dot_general(left, right, (((0,), (0,)), ((), ())), preferred_element_...  14.2 us
    all_to_all x1, waiting for transfers between devices, on_device(): lax.all_to_all(totals.reshape(experts, capacity, feat_width), 'expert', s...  14.1 us
    all_to_all x2, starting transfers between devices, spread(): lax.all_to_all(placed, 'expert', split_axis=0, concat_axis=0, tiled=True)  12 us
    dot_general x3, matrix products, rows_by_weights(): lax.dot_general(rows, weights, (((1,), (1,)), ((), ())), preferred_elemen...  5.5 us
    all_to_all x1, starting transfers between devices, on_device(): lax.all_to_all(totals.reshape(experts, capacity, feat_width), 'expert', s...  4.93 us
    dot_general x2, matrix products, spread(): placed = jnp.dot(placing, values, preferred_element_type=F32).astype(BF16)  3.88 us
    select_n x2, other arithmetic, gather_features(): jnp.where(first, own, other)  3.75 us
  transfers between devices with their start and end apart: 6, of which 4 were waited for; matrix products, arithmetic and copies ran while one was open for 15% of the time, Pallas kernels for 0%

profile of v1, /device:TPU:8, one launch (start us, length us, event | category | flops | bytes accessed | tf_op | source)
XLA Modules:
  0.0 120.3 jit_solution(11981672798778654512)
XLA Ops:
  0.6 0.0 copy-start
  0.6 0.0 copy-start.13
  0.7 0.8 fusion.20
  1.5 0.6 reduce-window.6
  2.1 0.2 slice_reduce_fusion
  2.3 0.8 fusion.19
  3.1 0.7 multiply_add_fusion
  3.8 2.5 %convolution_convert_fusion.3 = bf16[512,1024]{1,0:T(8,128)(2,1)} fusion(bf16[256,1024]{1,0:T(8,128)(2,1)} %param.6, s32[256]{0:T(256)S(1)} %multiply_add_fusion), kind=kOutput, calls=%fused_computation.20 | convolution fusion | flops 269090816 | bytes 1573888 | tf_op jit(solution)/shard_map/dot_general | solution.py:49
  6.2 7.2 %all-to-all-start.1 = ((bf16[16,32,1024]{2,1,0:T(8,128)(2,1)}), bf16[16,32,1024]{2,1,0:T(8,128)(2,1)}, u32[]{:S(2)}, u32[]{:S(2)}) async-start(bf16[16,32,1024]{2,1,0:T(8,128)(2,1)} %bitcast.61), calls=%async_computation.1 | async-start | bytes 2097152 | tf_op jit(solution)/shard_map/all_to_all | solution.py:51
  13.4 0.0 copy-done.13
  13.4 1.4 %convolution_convert_fusion.4 = bf16[512,1024]{1,0:T(8,128)(2,1)} fusion(bf16[256,1024]{1,0:T(8,128)(2,1)S(1)} %copy-done.13, s32[256]{0:T(256)S(1)} %multiply_add_fusion), kind=kOutput, calls=%fused_computation.21 | convolution fusion | flops 269090816 | bytes 1573888 | tf_op jit(solution)/shard_map/dot_general | solution.py:49
  14.9 24.2 %all-to-all-done.1 = bf16[16,32,1024]{2,1,0:T(8,128)(2,1)} async-done(((bf16[16,32,1024]{2,1,0:T(8,128)(2,1)}), bf16[16,32,1024]{2,1,0:T(8,128)(2,1)}, u32[]{:S(2)}, u32[]{:S(2)}) %all-to-all-start.1) | async-done | bytes 1048608 | tf_op jit(solution)/shard_map/all_to_all | solution.py:51
  39.1 4.7 %all-to-all-start = ((bf16[16,32,1024]{2,1,0:T(8,128)(2,1)}), bf16[16,32,1024]{2,1,0:T(8,128)(2,1)}, u32[]{:S(2)}, u32[]{:S(2)}) async-start(bf16[16,32,1024]{2,1,0:T(8,128)(2,1)} %bitcast.60), calls=%async_computation | async-start | bytes 2097152 | tf_op jit(solution)/shard_map/all_to_all | solution.py:51
  43.8 0.0 collective-permute-start.1
  43.8 24.1 %all-to-all-done = bf16[16,32,1024]{2,1,0:T(8,128)(2,1)} async-done(((bf16[16,32,1024]{2,1,0:T(8,128)(2,1)}), bf16[16,32,1024]{2,1,0:T(8,128)(2,1)}, u32[]{:S(2)}, u32[]{:S(2)}) %all-to-all-start) | async-done | bytes 1048608 | tf_op jit(solution)/shard_map/all_to_all | solution.py:51
  68.0 0.0 collective-permute-start
  68.0 0.0 collective-permute-done.1
  68.0 1.8 %broadcast_select_fusion.1 = (bf16[512,1024]{1,0:T(8,128)(2,1)S(1)}, bf16[512,1024]{1,0:T(8,128)(2,1)S(1)}) fusion(bf16[512,1024]{1,0:T(8,128)(2,1)} %collective-permute-done.1, pred[]{:T(512)S(6)} %eq.51, bf16[16,32,1024]{2,1,0:T(8,128)(2,1)} %all-to-all-done.1), kind=kLoop, calls=%fused_computation.29 | loop fusion | flops 1048576 | bytes 4194305 | tf_op jit(solution)/shard_map/jit(_where)/select_n | solution.py:16
  69.8 0.0 copy-start.2
  69.8 0.0 copy-start.4
  69.8 0.6 copy-done.1
  70.4 1.7 %fusion.8 = f32[512,704]{0,1:T(8,128)S(1)} fusion(bf16[1,704,2048]{2,1,0:T(8,128)(2,1)S(1)} %copy-done.1, bf16[512,1024]{1,0:T(8,128)(2,1)S(1)} %get-tuple-element.9, bf16[512,1024]{1,0:T(8,128)(2,1)S(1)} %get-tuple-element.8), kind=kOutput, calls=%fused_computation.12 | convolution fusion | flops 1480589312 | bytes 6422528 | tf_op jit(solution)/shard_map/dot_general | solution.py:55
  72.1 0.0 copy-done.2
  72.1 0.0 copy-done.4
  72.1 0.0 copy-start.15
  72.1 1.7 %fusion.5 = f32[512,704]{0,1:T(8,128)S(1)} fusion(bf16[1,704,2048]{2,1,0:T(8,128)(2,1)S(1)} %copy-done, bf16[512,1024]{1,0:T(8,128)(2,1)S(1)} %get-tuple-element.9, bf16[512,1024]{1,0:T(8,128)(2,1)S(1)} %get-tuple-element.8), kind=kOutput, calls=%fused_computation.9 | convolution fusion | flops 1480589312 | bytes 6422528 | tf_op jit(solution)/shard_map/dot_general | solution.py:55
  73.8 0.0 copy-start.14
  73.9 0.0 collective-permute-done
  73.9 1.9 %broadcast_select_fusion.3 = (bf16[512,1024]{1,0:T(8,128)(2,1)S(1)}, bf16[512,1024]{1,0:T(8,128)(2,1)S(1)}) fusion(bf16[512,1024]{1,0:T(8,128)(2,1)S(1)} %collective-permute-done, pred[]{:T(512)S(6)} %eq.51, bf16[16,32,1024]{2,1,0:T(8,128)(2,1)} %all-to-all-done), kind=kLoop, calls=%fused_computation.31 | loop fusion | flops 1048576 | bytes 4194305 | tf_op jit(solution)/shard_map/jit(_where)/select_n | solution.py:16
  75.8 0.7 copy-done.14
  76.5 2.1 %multiply_convert_fusion.1 = (bf16[512,704]{0,1:T(8,128)(2,1)S(1)}, bf16[512,704]{0,1:T(8,128)(2,1)S(1)}) fusion(f32[512,704]{0,1:T(8,128)S(1)} %fusion.5, f32[512,704]{0,1:T(8,128)S(1)} %fusion.8, bf16[1,704,2048]{2,1,0:T(8,128)(2,1)S(1)} %copy-done.14, bf16[512,1024]{1,0:T(8,128)(2,1)S(1)} %get-tuple-element.7, bf16[512,1024]{1,0:T(8,128)(2,1)S(1)} %get-tuple-element.6), kind=kOutput, calls=%fused_computation.23 | convolution fusion | flops 1485275136 | bytes 9306112 | tf_op jit(solution)/shard_map/dot_general | solution.py:55
  78.7 1.9 %fusion.3 = f32[512,2048]{1,0:T(8,128)S(1)} fusion(bf16[512,704]{0,1:T(8,128)(2,1)S(1)} %get-tuple-element.5, bf16[1,704,2048]{2,1,0:T(8,128)(2,1)S(1)} %copy-done), kind=kOutput, calls=%fused_computation.7 | convolution fusion | flops 1476395008 | bytes 7798784 | tf_op jit(solution)/shard_map/dot_general | solution.py:75
  80.6 1.8 %convolution_add_fusion = f32[512,2048]{1,0:T(8,128)S(1)} fusion(f32[512,2048]{1,0:T(8,128)S(1)} %fusion.3, bf16[512,704]{0,1:T(8,128)(2,1)S(1)} %get-tuple-element.4, bf16[1,704,2048]{2,1,0:T(8,128)(2,1)S(1)} %copy-done.1), kind=kOutput, calls=%fused_computation.3 | convolution fusion | flops 1477443584 | bytes 11993088 | tf_op jit(solution)/shard_map/dot_general | solution.py:75
  82.4 0.2 select_convert_fusion
  82.6 0.1 collective-permute-start.2
  82.7 2.6 %collective-permute-done.2 = bf16[512,1024]{1,0:T(8,128)(2,1)S(1)} collective-permute-done((bf16[512,1024]{1,0:T(8,128)(2,1)S(1)}, bf16[512,1024]{1,0:T(8,128)(2,1)S(1)}, u32[]{:S(2)}, u32[]{:S(2)}) %collective-permute-start.2) | collective-permute-done | bytes 1048608 | tf_op jit(solution)/shard_map/ppermute | solution.py:31
  85.3 1.6 %add_convert_fusion = bf16[512,1024]{1,0:T(8,128)(2,1)} fusion(bf16[512,1024]{1,0:T(8,128)(2,1)S(1)} %collective-permute-done.2, f32[512,2048]{1,0:T(8,128)S(1)} %convolution_add_fusion, pred[]{:T(512)S(6)} %eq.51), kind=kLoop, calls=%fused_computation.18 | loop fusion | flops 2097152 | bytes 6291457 | tf_op jit(solution)/shard_map/convert_element_type | solution.py:32
  87.0 4.9 %all-to-all-start.2 = ((bf16[16,32,1024]{2,1,0:T(8,128)(2,1)}), bf16[16,32,1024]{2,1,0:T(8,128)(2,1)}, u32[]{:S(2)}, u32[]{:S(2)}) async-start(bf16[16,32,1024]{2,1,0:T(8,128)(2,1)} %bitcast.59), calls=%async_computation.2 | async-start | bytes 2097152 | tf_op jit(solution)/shard_map/all_to_all | solution.py:79
  91.9 0.0 copy-start.5
  91.9 5.1 %fusion = bf16[1,704,2048]{2,1,0:T(8,128)(2,1)} fusion(bf16[512,704]{0,1:T(8,128)(2,1)} %copy-done.12, bf16[512,1024]{1,0:T(8,128)(2,1)} %copy-done.4, bf16[512,1024]{1,0:T(8,128)(2,1)} %copy-done.2), kind=kOutput, calls=%fused_computation.4 | convolution fusion | flops 1482031104 | bytes 5701632 | tf_op jit(solution)/shard_map/dot_general | solution.py:60
  97.1 0.0 copy-done.11
  97.1 0.0 copy-start.7
  97.1 0.0 copy-start.9
  97.1 0.0 copy-start.16
  97.1 3.2 %fusion.1 = bf16[1,704,2048]{2,1,0:T(8,128)(2,1)} fusion(bf16[512,704]{0,1:T(8,128)(2,1)S(1)} %copy-done.11, bf16[512,1024]{1,0:T(8,128)(2,1)S(1)} %copy-done.5, bf16[512,1024]{1,0:T(8,128)(2,1)S(1)} %copy-done.3), kind=kOutput, calls=%fused_computation.5 | convolution fusion | flops 1482031104 | bytes 5701632 | tf_op jit(solution)/shard_map/dot_general | solution.py:60
  100.4 3.3 %fusion.2 = bf16[1,704,2048]{2,1,0:T(8,128)(2,1)} fusion(bf16[512,1024]{1,0:T(8,128)(2,1)S(1)} %copy-done.9, bf16[512,1024]{1,0:T(8,128)(2,1)S(1)} %copy-done.7, f32[512,704]{0,1:T(8,128)S(1)} %copy-done.16, f32[512,704]{0,1:T(8,128)S(1)} %copy-done.18), kind=kOutput, calls=%fused_computation.6 | convolution fusion | flops 1484193792 | bytes 7864320 | tf_op jit(solution)/shard_map/dot_general | solution.py:60
  103.7 14.1 %all-to-all-done.2 = bf16[16,32,1024]{2,1,0:T(8,128)(2,1)} async-done(((bf16[16,32,1024]{2,1,0:T(8,128)(2,1)}), bf16[16,32,1024]{2,1,0:T(8,128)(2,1)}, u32[]{:S(2)}, u32[]{:S(2)}) %all-to-all-start.2) | async-done | bytes 1048608 | tf_op jit(solution)/shard_map/all_to_all | solution.py:79
  117.8 2.5 %convolution_convert_fusion.5 = bf16[256,1024]{1,0:T(8,128)(2,1)} fusion(bf16[512,1024]{1,0:T(8,128)(2,1)} %bitcast.11, s32[256]{0:T(256)S(1)} %multiply_add_fusion), kind=kOutput, calls=%fused_computation.27 | convolution fusion | flops 268828672 | bytes 1573888 | tf_op jit(solution)/shard_map/dot_general | solution.py:60
  (24 shorter events, 0.1 us)
Async XLA Ops:
  0.6 71.5 %copy-start = (bf16[1,704,2048]{2,1,0:T(8,128)(2,1)S(1)}, bf16[1,704,2048]{2,1,0:T(8,128)(2,1)}, u32[]{:S(2)}) copy-start(bf16[1,704,2048]{2,1,0:T(8,128)(2,1)} %param.9) | copy-start | bytes 8650756
  0.6 12.8 %copy-start.13 = (bf16[256,1024]{1,0:T(8,128)(2,1)S(1)}, bf16[256,1024]{1,0:T(8,128)(2,1)}, u32[]{:S(2)}) copy-start(bf16[256,1024]{1,0:T(8,128)(2,1)} %param.7) | copy-start | bytes 1572868
  6.2 32.9 %all-to-all-start.1 = ((bf16[16,32,1024]{2,1,0:T(8,128)(2,1)}), bf16[16,32,1024]{2,1,0:T(8,128)(2,1)}, u32[]{:S(2)}, u32[]{:S(2)}) async-start(bf16[16,32,1024]{2,1,0:T(8,128)(2,1)} %bitcast.61), calls=%async_computation.1 | async-start | bytes 2097152 | tf_op jit(solution)/shard_map/all_to_all | solution.py:51
  39.1 28.9 %all-to-all-start = ((bf16[16,32,1024]{2,1,0:T(8,128)(2,1)}), bf16[16,32,1024]{2,1,0:T(8,128)(2,1)}, u32[]{:S(2)}, u32[]{:S(2)}) async-start(bf16[16,32,1024]{2,1,0:T(8,128)(2,1)} %bitcast.60), calls=%async_computation | async-start | bytes 2097152 | tf_op jit(solution)/shard_map/all_to_all | solution.py:51
  43.8 24.2 %collective-permute-start.1 = (bf16[512,1024]{1,0:T(8,128)(2,1)}, bf16[512,1024]{1,0:T(8,128)(2,1)}, u32[]{:S(2)}, u32[]{:S(2)}) collective-permute-start(bf16[512,1024]{1,0:T(8,128)(2,1)} %bitcast.7), channel_id=1, source_target_pairs={{0,1},{1,0},{2,3},{3,2},{4,5},{5,4},{6,7},{7,6},{8,9},{9,8},{10,11... | collective-permute-start | bytes 3145736 | tf_op jit(solution)/shard_map/ppermute | solution.py:13
  68.0 2.4 %copy-start.1 = (bf16[1,704,2048]{2,1,0:T(8,128)(2,1)S(1)}, bf16[1,704,2048]{2,1,0:T(8,128)(2,1)}, u32[]{:S(2)}) copy-start(bf16[1,704,2048]{2,1,0:T(8,128)(2,1)} %param.10) | copy-start | bytes 8650756
  68.0 5.9 %collective-permute-start = (bf16[512,1024]{1,0:T(8,128)(2,1)}, bf16[512,1024]{1,0:T(8,128)(2,1)S(1)}, u32[]{:S(2)}, u32[]{:S(2)}) collective-permute-start(bf16[512,1024]{1,0:T(8,128)(2,1)} %bitcast.4), channel_id=1, source_target_pairs={{0,1},{1,0},{2,3},{3,2},{4,5},{5,4},{6,7},{7,6},{8,9},{9,8},{10,11... | collective-permute-start | bytes 3145736 | tf_op jit(solution)/shard_map/ppermute | solution.py:13
  69.8 2.3 %copy-start.2 = (bf16[512,1024]{1,0:T(8,128)(2,1)}, bf16[512,1024]{1,0:T(8,128)(2,1)S(1)}, u32[]{:S(2)}) copy-start(bf16[512,1024]{1,0:T(8,128)(2,1)S(1)} %get-tuple-element.8) | copy-start | bytes 3145732
  69.8 2.3 %copy-start.4 = (bf16[512,1024]{1,0:T(8,128)(2,1)}, bf16[512,1024]{1,0:T(8,128)(2,1)S(1)}, u32[]{:S(2)}) copy-start(bf16[512,1024]{1,0:T(8,128)(2,1)S(1)} %get-tuple-element.9) | copy-start | bytes 3145732
  72.1 3.7 %copy-start.15 = (f32[512,704]{0,1:T(8,128)}, f32[512,704]{0,1:T(8,128)S(1)}, u32[]{:S(2)}) copy-start(f32[512,704]{0,1:T(8,128)S(1)} %fusion.8) | copy-start | bytes 4325380
  73.8 2.0 %copy-start.17 = (f32[512,704]{0,1:T(8,128)}, f32[512,704]{0,1:T(8,128)S(1)}, u32[]{:S(2)}) copy-start(f32[512,704]{0,1:T(8,128)S(1)} %fusion.5) | copy-start | bytes 4325380
  73.8 2.7 %copy-start.14 = (bf16[1,704,2048]{2,1,0:T(8,128)(2,1)S(1)}, bf16[1,704,2048]{2,1,0:T(8,128)(2,1)}, u32[]{:S(2)}) copy-start(bf16[1,704,2048]{2,1,0:T(8,128)(2,1)} %param.11) | copy-start | bytes 8650756
  75.8 2.8 %copy-start.6 = (bf16[512,1024]{1,0:T(8,128)(2,1)}, bf16[512,1024]{1,0:T(8,128)(2,1)S(1)}, u32[]{:S(2)}) copy-start(bf16[512,1024]{1,0:T(8,128)(2,1)S(1)} %get-tuple-element.6) | copy-start | bytes 3145732
  75.8 2.8 %copy-start.8 = (bf16[512,1024]{1,0:T(8,128)(2,1)}, bf16[512,1024]{1,0:T(8,128)(2,1)S(1)}, u32[]{:S(2)}) copy-start(bf16[512,1024]{1,0:T(8,128)(2,1)S(1)} %get-tuple-element.7) | copy-start | bytes 3145732
  78.7 1.9 %copy-start.12 = (bf16[512,704]{0,1:T(8,128)(2,1)}, bf16[512,704]{0,1:T(8,128)(2,1)S(1)}, u32[]{:S(2)}) copy-start(bf16[512,704]{0,1:T(8,128)(2,1)S(1)} %get-tuple-element.5) | copy-start | bytes 2162692
  78.7 1.9 %copy-start.10 = (bf16[512,704]{0,1:T(8,128)(2,1)}, bf16[512,704]{0,1:T(8,128)(2,1)S(1)}, u32[]{:S(2)}) copy-start(bf16[512,704]{0,1:T(8,128)(2,1)S(1)} %get-tuple-element.4) | copy-start | bytes 2162692
  82.6 2.7 %collective-permute-start.2 = (bf16[512,1024]{1,0:T(8,128)(2,1)S(1)}, bf16[512,1024]{1,0:T(8,128)(2,1)S(1)}, u32[]{:S(2)}, u32[]{:S(2)}) collective-permute-start(bf16[512,1024]{1,0:T(8,128)(2,1)S(1)} %select_convert_fusion), channel_id=1, source_target_pairs={{0,1},{1,0},{2,3},{3,2},{4,5},{5,4},{6,7},{7,6},{8,9},{9,8},{10,11... | collective-permute-start | bytes 3145736 | tf_op jit(solution)/shard_map/ppermute | solution.py:31
  87.0 30.8 %all-to-all-start.2 = ((bf16[16,32,1024]{2,1,0:T(8,128)(2,1)}), bf16[16,32,1024]{2,1,0:T(8,128)(2,1)}, u32[]{:S(2)}, u32[]{:S(2)}) async-start(bf16[16,32,1024]{2,1,0:T(8,128)(2,1)} %bitcast.59), calls=%async_computation.2 | async-start | bytes 2097152 | tf_op jit(solution)/shard_map/all_to_all | solution.py:79
  91.9 5.2 %copy-start.3 = (bf16[512,1024]{1,0:T(8,128)(2,1)S(1)}, bf16[512,1024]{1,0:T(8,128)(2,1)}, u32[]{:S(2)}) copy-start(bf16[512,1024]{1,0:T(8,128)(2,1)} %copy-done.2) | copy-start | bytes 3145732
  91.9 5.2 %copy-start.5 = (bf16[512,1024]{1,0:T(8,128)(2,1)S(1)}, bf16[512,1024]{1,0:T(8,128)(2,1)}, u32[]{:S(2)}) copy-start(bf16[512,1024]{1,0:T(8,128)(2,1)} %copy-done.4) | copy-start | bytes 3145732
  91.9 5.2 %copy-start.11 = (bf16[512,704]{0,1:T(8,128)(2,1)S(1)}, bf16[512,704]{0,1:T(8,128)(2,1)}, u32[]{:S(2)}) copy-start(bf16[512,704]{0,1:T(8,128)(2,1)} %copy-done.10) | copy-start | bytes 2162692
  97.1 3.3 %copy-start.7 = (bf16[512,1024]{1,0:T(8,128)(2,1)S(1)}, bf16[512,1024]{1,0:T(8,128)(2,1)}, u32[]{:S(2)}) copy-start(bf16[512,1024]{1,0:T(8,128)(2,1)} %copy-done.6) | copy-start | bytes 3145732
  97.1 3.3 %copy-start.9 = (bf16[512,1024]{1,0:T(8,128)(2,1)S(1)}, bf16[512,1024]{1,0:T(8,128)(2,1)}, u32[]{:S(2)}) copy-start(bf16[512,1024]{1,0:T(8,128)(2,1)} %copy-done.8) | copy-start | bytes 3145732
  97.1 3.3 %copy-start.16 = (f32[512,704]{0,1:T(8,128)S(1)}, f32[512,704]{0,1:T(8,128)}, u32[]{:S(2)}) copy-start(f32[512,704]{0,1:T(8,128)} %copy-done.15) | copy-start | bytes 4325380
  97.1 3.3 %copy-start.18 = (f32[512,704]{0,1:T(8,128)S(1)}, f32[512,704]{0,1:T(8,128)}, u32[]{:S(2)}) copy-start(f32[512,704]{0,1:T(8,128)} %copy-done.17) | copy-start | bytes 4325380

commit v2 on v1

--- a/solution.py
+++ b/solution.py
@@ -1,10 +1,58 @@
+import functools
+
 import jax
 import jax.numpy as jnp
 from jax import lax
+from jax.experimental import pallas as pl
+from jax.experimental.pallas import tpu as pltpu
 from jax.sharding import PartitionSpec as P
 
 F32 = jnp.float32
 BF16 = jnp.bfloat16
+VMEM = pltpu.VMEM
+LIMIT = 48 * 2**20
+
+
+def whole(count):
+    return [pl.BlockSpec(memory_space=VMEM)] * count
+
+
+def place_kernel(capacity, col_ref, row_ref, x_ref, dy_ref, *slabs):
+    me = lax.axis_index("expert")
+    rows = x_ref.shape[0]
+    col, row = col_ref[...], row_ref[...]
+    earlier = lax.broadcasted_iota(jnp.int32, (rows, rows), 0) < lax.broadcasted_iota(
+        jnp.int32, (rows, rows), 1
+    )
+    same = jnp.where((col == row) & earlier, 1.0, 0.0)
+    within = jnp.sum(same, axis=0, keepdims=True).astype(jnp.int32)
+    target = (row ^ me) * capacity + within
+    slots = len(slabs) * capacity
+    slot = lax.broadcasted_iota(jnp.int32, (slots, rows), 0)
+    placing = jnp.where(slot == target, 1.0, 0.0).astype(BF16)
+    x = jnp.dot(placing, x_ref[...], preferred_element_type=F32).astype(BF16)
+    dy = jnp.dot(placing, dy_ref[...], preferred_element_type=F32).astype(BF16)
+    for k, slab in enumerate(slabs):
+        slab[:capacity, :] = x[k * capacity : (k + 1) * capacity]
+        slab[capacity:, :] = dy[k * capacity : (k + 1) * capacity]
+
+
+def combine_kernel(capacity, col_ref, row_ref, *refs):
+    *slabs, out_ref = refs
+    me = lax.axis_index("expert")
+    rows = out_ref.shape[0]
+    col, row = col_ref[...], row_ref[...]
+    earlier = lax.broadcasted_iota(jnp.int32, (rows, rows), 1) < lax.broadcasted_iota(
+        jnp.int32, (rows, rows), 0
+    )
+    same = jnp.where((col == row) & earlier, 1.0, 0.0)
+    within = jnp.sum(same, axis=1, keepdims=True).astype(jnp.int32)
+    target = (col ^ me) * capacity + within
+    slots = len(slabs) * capacity
+    slot = lax.broadcasted_iota(jnp.int32, (rows, slots), 1)
+    placing = jnp.where(slot == target, 1.0, 0.0).astype(BF16)
+    returned = jnp.concatenate([slab[...] for slab in slabs], axis=0)
+    out_ref[...] = jnp.dot(placing, returned, preferred_element_type=F32).astype(BF16)
 
 
 def gather_features(own):
@@ -36,20 +84,17 @@
     experts = lax.axis_size("expert")
     tok_rows, feat_width = tokens.shape
     capacity = max(2, 2 * tok_rows // experts)
-    slot_count = experts * capacity
-    route = expert_ids[:, 0]
-    onehot = (route[:, None] == jnp.arange(experts, dtype=jnp.int32)[None, :]).astype(jnp.int32)
-    before = jnp.cumsum(onehot, axis=0) - onehot
-    within = jnp.sum(before * onehot, axis=1)
-    target = route * capacity + within
-    placing = (target[None, :] == jnp.arange(slot_count, dtype=jnp.int32)[:, None]).astype(BF16)
     gate_rows, up_rows, down_rows = w_gate[0], w_up[0], w_down[0]
+    ids_row = expert_ids.reshape(1, tok_rows)
 
-    def spread(values):
-        placed = jnp.dot(placing, values, preferred_element_type=F32).astype(BF16)
-        placed = placed.reshape(experts, capacity, feat_width)
-        got = lax.all_to_all(placed, "expert", split_axis=0, concat_axis=0, tiled=True)
-        return got.reshape(slot_count, feat_width)
+    def swap(slab, k):
+        if k == 0:
+            return slab
+        return lax.ppermute(slab, "expert", [(e, e ^ k) for e in range(experts)])
+
+    def swap_all(slabs):
+        got = {k: swap(slabs[k], k) for k in reversed(range(experts))}
+        return [got[k] for k in range(experts)]
 
     def rows_by_weights(rows, weights):
         return lax.dot_general(
@@ -61,7 +106,17 @@
             left, right, (((0,), (0,)), ((), ())), preferred_element_type=F32
         ).astype(BF16)
 
-    got_x, got_dy = spread(tokens), spread(upstream)
+    slabs = pl.pallas_call(
+        functools.partial(place_kernel, capacity),
+        out_shape=[jax.ShapeDtypeStruct((2 * capacity, feat_width), BF16)] * experts,
+        in_specs=whole(4),
+        out_specs=whole(experts),
+        compiler_params=pltpu.CompilerParams(vmem_limit_bytes=LIMIT),
+        name="place",
+    )(expert_ids, ids_row, tokens, upstream)
+    arrived = swap_all(slabs)
+    got_x = jnp.concatenate([slab[:capacity] for slab in arrived], axis=0)
+    got_dy = jnp.concatenate([slab[capacity:] for slab in arrived], axis=0)
     x_all = gather_features(got_x)
     gate_pre = rows_by_weights(x_all, gate_rows)
     up_pre = rows_by_weights(x_all, up_rows)
@@ -76,17 +131,18 @@
         d_up, up_rows, preferred_element_type=F32
     )
     totals = scatter_sum(partial_rows)
-    returned = lax.all_to_all(
-        totals.reshape(experts, capacity, feat_width),
-        "expert",
-        split_axis=0,
-        concat_axis=0,
-        tiled=True,
-    ).reshape(slot_count, feat_width)
+    returned = swap_all([totals[k * capacity : (k + 1) * capacity] for k in range(experts)])
     grad_gate = weight_grad(d_gate, x_all)
     grad_up = weight_grad(d_up, x_all)
     grad_down = weight_grad(hidden, dy_all)
-    grad_tokens = weight_grad(placing, returned)
+    grad_tokens = pl.pallas_call(
+        functools.partial(combine_kernel, capacity),
+        out_shape=jax.ShapeDtypeStruct((tok_rows, feat_width), BF16),
+        in_specs=whole(2 + experts),
+        out_specs=pl.BlockSpec(memory_space=VMEM),
+        compiler_params=pltpu.CompilerParams(vmem_limit_bytes=LIMIT),
+        name="combine",
+    )(expert_ids, ids_row, *returned)
     return (grad_tokens, grad_gate[None], grad_up[None], grad_down[None])
 
 

time: 121 us -> 127 us (1.050)
  starting transfers between devices: 17 us -> 48.8 us
  waiting for transfers between devices: 65.1 us -> 35.7 us
  local copies, waits for them, and re-layouts: 1.52 us -> 15 us
  matrix products: 27.3 us -> 19 us
  other arithmetic: 8.48 us -> 4.15 us
  Pallas kernels: 0 us -> 2.33 us
    all_to_all x3 -> x0, waiting for transfers between devices: 62.4 us -> none  [the longest x2 48.3 us: spread(): lax.all_to_all(placed, 'expert', split_axis=0, concat_axis=0, tiled=True)]
    ppermute x0 -> x30, starting transfers between devices: none -> 48.1 us  [swap(): return lax.ppermute(slab, 'expert', [(e, e ^ k) for e in range(experts)])]
    ppermute x0 -> x30, waiting for transfers between devices: none -> 29.6 us  [swap(): return lax.ppermute(slab, 'expert', [(e, e ^ k) for e in range(experts)])]
    all_to_all x3 -> x0, starting transfers between devices: 16.9 us -> none  [the longest x2 12 us: spread(): lax.all_to_all(placed, 'expert', split_axis=0, concat_axis=0, tiled=True)]
    unnamed x38 -> x30, local copies, waits for them, and re-layouts: 1.33 us -> 14.2 us
    dot_general x4 -> x3, matrix products: 14.2 us -> 9.77 us  [weight_grad(): lax.dot_general(left, right, (((0,), (0,)), ((), ())), preferred_element_...]
    dot_general x2 -> x0, matrix products: 3.88 us -> none  [spread(): placed = jnp.dot(placing, values, preferred_element_type=F32).astype(BF16)]
    ppermute x2, waiting for transfers between devices: 0.01 us -> 3.62 us  [gather_features(): other = lax.ppermute(own, 'tensor', [(0, 1), (1, 0)])]
  transfers between devices with their start and end apart: 6 -> 33, of which waited for: 4 -> 14; matrix products, arithmetic and copies ran while one was open for 15% -> 20% of each run, Pallas kernels for 0% -> 0%
where the time goes in v2:
time: 127 us; the launch traced here: 126 us
  starting transfers between devices  48.8 us (38%)
  waiting for transfers between devices  35.7 us (28%)
  matrix products  19 us (15%)
  local copies, waits for them, and re-layouts  15 us (12%)
  other arithmetic  4.15 us (3%)
  Pallas kernels  2.33 us (2%)
    ppermute x30, starting transfers between devices, swap(): return lax.ppermute(slab, 'expert', [(e, e ^ k) for e in range(experts)])  48.1 us
    ppermute x30, waiting for transfers between devices, swap(): return lax.ppermute(slab, 'expert', [(e, e ^ k) for e in range(experts)])  29.6 us
    unnamed x30, local copies, waits for them, and re-layouts  14.2 us
    dot_general x3, matrix products, weight_grad(): lax.dot_general(left, right, (((0,), (0,)), ((), ())), preferred_element_...  9.77 us
    dot_general x3, matrix products, rows_by_weights(): lax.dot_general(rows, weights, (((1,), (1,)), ((), ())), preferred_elemen...  5.49 us
    ppermute x2, waiting for transfers between devices, gather_features(): other = lax.ppermute(own, 'tensor', [(0, 1), (1, 0)])  3.62 us
    select_n x2, other arithmetic, gather_features(): jnp.where(first, own, other)  3.33 us
  transfers between devices with their start and end apart: 33, of which 14 were waited for; matrix products, arithmetic and copies ran while one was open for 20% of the time, Pallas kernels for 0%

profile of v2, /device:TPU:8, one launch (start us, length us, event | category | flops | bytes accessed | tf_op | source)
XLA Modules:
  0.0 125.8 jit_solution(6682374477557836381)
XLA Ops:
  0.6 1.0 copy.11.col_ref
  1.6 1.0 copy-done.1
  2.7 1.0 copy-done.2
  4.4 0.8 place.1
  5.2 1.6 %collective-permute-start = (bf16[64,1024]{1,0:T(8,128)(2,1)S(1)}, bf16[64,1024]{1,0:T(8,128)(2,1)S(1)}, u32[]{:S(2)}, u32[]{:S(2)}) collective-permute-start(bf16[64,1024]{1,0:T(8,128)(2,1)S(1)} %get-tuple-element.21), channel_id=1, source_target_pairs={{0,2},{2,0},{4,6},{6,4},{8,10},{10,8},{12,14},{14,12},{16,18},{18,... | collective-permute-start | bytes 393224 | tf_op jit(solution)/shard_map/ppermute | solution.py:93
  6.7 1.5 %collective-permute-start.1 = (bf16[64,1024]{1,0:T(8,128)(2,1)S(1)}, bf16[64,1024]{1,0:T(8,128)(2,1)S(1)}, u32[]{:S(2)}, u32[]{:S(2)}) collective-permute-start(bf16[64,1024]{1,0:T(8,128)(2,1)S(1)} %get-tuple-element.22), channel_id=1, source_target_pairs={{0,4},{2,6},{4,0},{6,2},{8,12},{10,14},{12,8},{14,10},{16,20},{18,... | collective-permute-start | bytes 393224 | tf_op jit(solution)/shard_map/ppermute | solution.py:93
  8.7 3.0 %collective-permute-start.4 = (bf16[64,1024]{1,0:T(8,128)(2,1)S(1)}, bf16[64,1024]{1,0:T(8,128)(2,1)S(1)}, u32[]{:S(2)}, u32[]{:S(2)}) collective-permute-start(bf16[64,1024]{1,0:T(8,128)(2,1)S(1)} %get-tuple-element.25), channel_id=1, source_target_pairs={{0,10},{2,8},{4,14},{6,12},{8,2},{10,0},{12,6},{14,4},{16,26},{18,... | collective-permute-start | bytes 393224 | tf_op jit(solution)/shard_map/ppermute | solution.py:93
  12.4 1.4 %collective-permute-start.5 = (bf16[64,1024]{1,0:T(8,128)(2,1)S(1)}, bf16[64,1024]{1,0:T(8,128)(2,1)S(1)}, u32[]{:S(2)}, u32[]{:S(2)}) collective-permute-start(bf16[64,1024]{1,0:T(8,128)(2,1)S(1)} %get-tuple-element.26), channel_id=1, source_target_pairs={{0,12},{2,14},{4,8},{6,10},{8,4},{10,6},{12,0},{14,2},{16,28},{18,... | collective-permute-start | bytes 393224 | tf_op jit(solution)/shard_map/ppermute | solution.py:93
  14.4 1.7 %collective-permute-start.6 = (bf16[64,1024]{1,0:T(8,128)(2,1)S(1)}, bf16[64,1024]{1,0:T(8,128)(2,1)S(1)}, u32[]{:S(2)}, u32[]{:S(2)}) collective-permute-start(bf16[64,1024]{1,0:T(8,128)(2,1)S(1)} %get-tuple-element.27), channel_id=1, source_target_pairs={{0,14},{2,12},{4,10},{6,8},{8,6},{10,4},{12,2},{14,0},{16,30},{18,... | collective-permute-start | bytes 393224 | tf_op jit(solution)/shard_map/ppermute | solution.py:93
  16.8 2.6 %collective-permute-start.7 = (bf16[64,1024]{1,0:T(8,128)(2,1)S(1)}, bf16[64,1024]{1,0:T(8,128)(2,1)S(1)}, u32[]{:S(2)}, u32[]{:S(2)}) collective-permute-start(bf16[64,1024]{1,0:T(8,128)(2,1)S(1)} %get-tuple-element.28), channel_id=1, source_target_pairs={{0,16},{2,18},{4,20},{6,22},{8,24},{10,26},{12,28},{14,30},{16,0},... | collective-permute-start | bytes 393224 | tf_op jit(solution)/shard_map/ppermute | solution.py:93
  20.1 1.0 collective-permute-start.8
  21.8 3.5 %collective-permute-start.9 = (bf16[64,1024]{1,0:T(8,128)(2,1)S(1)}, bf16[64,1024]{1,0:T(8,128)(2,1)S(1)}, u32[]{:S(2)}, u32[]{:S(2)}) collective-permute-start(bf16[64,1024]{1,0:T(8,128)(2,1)S(1)} %get-tuple-element.30), channel_id=1, source_target_pairs={{0,20},{2,22},{4,16},{6,18},{8,28},{10,30},{12,24},{14,26},{16,4},... | collective-permute-start | bytes 393224 | tf_op jit(solution)/shard_map/ppermute | solution.py:93
  26.0 2.2 %collective-permute-start.10 = (bf16[64,1024]{1,0:T(8,128)(2,1)S(1)}, bf16[64,1024]{1,0:T(8,128)(2,1)S(1)}, u32[]{:S(2)}, u32[]{:S(2)}) collective-permute-start(bf16[64,1024]{1,0:T(8,128)(2,1)S(1)} %get-tuple-element.31), channel_id=1, source_target_pairs={{0,22},{2,20},{4,18},{6,16},{8,30},{10,28},{12,26},{14,24},{16,6},... | collective-permute-start | bytes 393224 | tf_op jit(solution)/shard_map/ppermute | solution.py:93
  29.5 9.9 %collective-permute-done.7 = bf16[64,1024]{1,0:T(8,128)(2,1)S(1)} collective-permute-done((bf16[64,1024]{1,0:T(8,128)(2,1)S(1)}, bf16[64,1024]{1,0:T(8,128)(2,1)S(1)}, u32[]{:S(2)}, u32[]{:S(2)}) %collective-permute-start.7) | collective-permute-done | bytes 131104 | tf_op jit(solution)/shard_map/ppermute | solution.py:93
  39.4 1.6 %collective-permute-start.12 = (bf16[64,1024]{1,0:T(8,128)(2,1)S(1)}, bf16[64,1024]{1,0:T(8,128)(2,1)S(1)}, u32[]{:S(2)}, u32[]{:S(2)}) collective-permute-start(bf16[64,1024]{1,0:T(8,128)(2,1)S(1)} %get-tuple-element.33), channel_id=1, source_target_pairs={{0,26},{2,24},{4,30},{6,28},{8,18},{10,16},{12,22},{14,20},{16,10}... | collective-permute-start | bytes 393224 | tf_op jit(solution)/shard_map/ppermute | solution.py:93
  42.2 1.5 %collective-permute-start.13 = (bf16[64,1024]{1,0:T(8,128)(2,1)S(1)}, bf16[64,1024]{1,0:T(8,128)(2,1)S(1)}, u32[]{:S(2)}, u32[]{:S(2)}) collective-permute-start(bf16[64,1024]{1,0:T(8,128)(2,1)S(1)} %get-tuple-element.34), channel_id=1, source_target_pairs={{0,28},{2,30},{4,24},{6,26},{8,20},{10,22},{12,16},{14,18},{16,12}... | collective-permute-start | bytes 393224 | tf_op jit(solution)/shard_map/ppermute | solution.py:93
  45.0 3.2 %collective-permute-start.14 = (bf16[64,1024]{1,0:T(8,128)(2,1)S(1)}, bf16[64,1024]{1,0:T(8,128)(2,1)S(1)}, u32[]{:S(2)}, u32[]{:S(2)}) collective-permute-start(bf16[64,1024]{1,0:T(8,128)(2,1)S(1)} %get-tuple-element.35), channel_id=1, source_target_pairs={{0,30},{2,28},{4,26},{6,24},{8,22},{10,20},{12,18},{14,16},{16,14}... | collective-permute-start | bytes 393224 | tf_op jit(solution)/shard_map/ppermute | solution.py:93
  48.8 3.3 %collective-permute-done.10 = bf16[64,1024]{1,0:T(8,128)(2,1)S(1)} collective-permute-done((bf16[64,1024]{1,0:T(8,128)(2,1)S(1)}, bf16[64,1024]{1,0:T(8,128)(2,1)S(1)}, u32[]{:S(2)}, u32[]{:S(2)}) %collective-permute-start.10) | collective-permute-done | bytes 131104 | tf_op jit(solution)/shard_map/ppermute | solution.py:93
  52.8 4.2 %collective-permute-done.11 = bf16[64,1024]{1,0:T(8,128)(2,1)S(1)} collective-permute-done((bf16[64,1024]{1,0:T(8,128)(2,1)S(1)}, bf16[64,1024]{1,0:T(8,128)(2,1)S(1)}, u32[]{:S(2)}, u32[]{:S(2)}) %collective-permute-start.11) | collective-permute-done | bytes 131104 | tf_op jit(solution)/shard_map/ppermute | solution.py:93
  57.7 3.4 %collective-permute-done.12 = bf16[64,1024]{1,0:T(8,128)(2,1)S(1)} collective-permute-done((bf16[64,1024]{1,0:T(8,128)(2,1)S(1)}, bf16[64,1024]{1,0:T(8,128)(2,1)S(1)}, u32[]{:S(2)}, u32[]{:S(2)}) %collective-permute-start.12) | collective-permute-done | bytes 131104 | tf_op jit(solution)/shard_map/ppermute | solution.py:93
  61.7 1.7 %collective-permute-done.13 = bf16[64,1024]{1,0:T(8,128)(2,1)S(1)} collective-permute-done((bf16[64,1024]{1,0:T(8,128)(2,1)S(1)}, bf16[64,1024]{1,0:T(8,128)(2,1)S(1)}, u32[]{:S(2)}, u32[]{:S(2)}) %collective-permute-start.13) | collective-permute-done | bytes 131104 | tf_op jit(solution)/shard_map/ppermute | solution.py:93
  64.1 1.2 collective-permute-done.14
  66.5 3.6 %collective-permute-done.16 = bf16[512,1024]{1,0:T(8,128)(2,1)} collective-permute-done((bf16[512,1024]{1,0:T(8,128)(2,1)}, bf16[512,1024]{1,0:T(8,128)(2,1)}, u32[]{:S(2)}, u32[]{:S(2)}) %collective-permute-start.16) | collective-permute-done | bytes 1048608 | tf_op jit(solution)/shard_map/ppermute | solution.py:61
  70.1 1.7 %broadcast_select_fusion.1 = (bf16[512,1024]{1,0:T(8,128)(2,1)S(1)}, bf16[512,1024]{1,0:T(8,128)(2,1)S(1)}) fusion(bf16[512,1024]{1,0:T(8,128)(2,1)} %get-tuple-element.59, bf16[512,1024]{1,0:T(8,128)(2,1)} %collective-permute-done.16, pred[]{:T(512)S(6)} %eq.2), kind=kLoop, calls=%fused_computation.26 | loop fusion | flops 1048576 | bytes 4194305 | tf_op jit(solution)/shard_map/jit(_where)/select_n | solution.py:64
  71.8 1.7 %fusion.5 = f32[512,704]{0,1:T(8,128)S(1)} fusion(bf16[1,704,2048]{2,1,0:T(8,128)(2,1)S(1)} %copy-done, bf16[512,1024]{1,0:T(8,128)(2,1)S(1)} %get-tuple-element.41, bf16[512,1024]{1,0:T(8,128)(2,1)S(1)} %get-tuple-element.40), kind=kOutput, calls=%fused_computation.9 | convolution fusion | flops 1480589312 | bytes 6422528 | tf_op jit(solution)/shard_map/dot_general | solution.py:100
  73.6 1.7 %fusion.8 = f32[512,704]{0,1:T(8,128)S(1)} fusion(bf16[1,704,2048]{2,1,0:T(8,128)(2,1)S(1)} %copy-done.5, bf16[512,1024]{1,0:T(8,128)(2,1)S(1)} %get-tuple-element.41, bf16[512,1024]{1,0:T(8,128)(2,1)S(1)} %get-tuple-element.40), kind=kOutput, calls=%fused_computation.12 | convolution fusion | flops 1480589312 | bytes 6422528 | tf_op jit(solution)/shard_map/dot_general | solution.py:100
  75.3 1.6 %broadcast_select_fusion.3 = (bf16[512,1024]{1,0:T(8,128)(2,1)S(1)}, bf16[512,1024]{1,0:T(8,128)(2,1)S(1)}) fusion(bf16[512,1024]{1,0:T(8,128)(2,1)} %get-tuple-element.58, bf16[512,1024]{1,0:T(8,128)(2,1)S(1)} %collective-permute-done.15, pred[]{:T(512)S(6)} %eq.2), kind=kLoop, calls=%fused_computation.28 | loop fusion | flops 1048576 | bytes 4194305 | tf_op jit(solution)/shard_map/jit(_where)/select_n | solution.py:64
  77.4 2.1 %multiply_convert_fusion.1 = (bf16[512,704]{0,1:T(8,128)(2,1)S(1)}, bf16[512,704]{0,1:T(8,128)(2,1)S(1)}) fusion(f32[512,704]{0,1:T(8,128)S(1)} %fusion.5, f32[512,704]{0,1:T(8,128)S(1)} %fusion.8, bf16[1,704,2048]{2,1,0:T(8,128)(2,1)S(1)} %copy-done.6, bf16[512,1024]{1,0:T(8,128)(2,1)S(1)} %get-tuple-element.39, bf16[512,1024]{1,0:T(8,128)(2,1)S(1)} %get-tuple-element.38), kind=kOutput, calls=%fused_computation.21 | convolution fusion | flops 1485275136 | bytes 9306112 | tf_op jit(solution)/shard_map/dot_general | solution.py:100
  79.6 1.9 %fusion.3 = f32[512,2048]{1,0:T(8,128)S(1)} fusion(bf16[512,704]{0,1:T(8,128)(2,1)S(1)} %get-tuple-element.37, bf16[1,704,2048]{2,1,0:T(8,128)(2,1)S(1)} %copy-done), kind=kOutput, calls=%fused_computation.7 | convolution fusion | flops 1476395008 | bytes 7798784 | tf_op jit(solution)/shard_map/dot_general | solution.py:130
  81.4 1.8 %convolution_add_fusion = f32[512,2048]{1,0:T(8,128)S(1)} fusion(f32[512,2048]{1,0:T(8,128)S(1)} %fusion.3, bf16[512,704]{0,1:T(8,128)(2,1)S(1)} %get-tuple-element.36, bf16[1,704,2048]{2,1,0:T(8,128)(2,1)S(1)} %copy-done.5), kind=kOutput, calls=%fused_computation.3 | convolution fusion | flops 1477443584 | bytes 11993088 | tf_op jit(solution)/shard_map/dot_general | solution.py:130
  83.7 2.5 %collective-permute-done.17 = bf16[512,1024]{1,0:T(8,128)(2,1)S(1)} collective-permute-done((bf16[512,1024]{1,0:T(8,128)(2,1)S(1)}, bf16[512,1024]{1,0:T(8,128)(2,1)S(1)}, u32[]{:S(2)}, u32[]{:S(2)}) %collective-permute-start.17) | collective-permute-done | bytes 1048608 | tf_op jit(solution)/shard_map/ppermute | solution.py:79
  87.0 1.0 collective-permute-start.18
  88.7 1.9 %collective-permute-start.20 = (bf16[32,1024]{1,0:T(8,128)(2,1)S(1)}, bf16[32,1024]{1,0:T(8,128)(2,1)S(1)}, u32[]{:S(2)}, u32[]{:S(2)}) collective-permute-start(bf16[32,1024]{1,0:T(8,128)(2,1)S(1)} %get-tuple-element.54), channel_id=1, source_target_pairs={{0,6},{2,4},{4,2},{6,0},{8,14},{10,12},{12,10},{14,8},{16,22},{18,... | collective-permute-start | bytes 196616 | tf_op jit(solution)/shard_map/ppermute | solution.py:93
  90.5 2.4 %collective-permute-start.22 = (bf16[32,1024]{1,0:T(8,128)(2,1)S(1)}, bf16[32,1024]{1,0:T(8,128)(2,1)S(1)}, u32[]{:S(2)}, u32[]{:S(2)}) collective-permute-start(bf16[32,1024]{1,0:T(8,128)(2,1)S(1)} %get-tuple-element.52), channel_id=1, source_target_pairs={{0,10},{2,8},{4,14},{6,12},{8,2},{10,0},{12,6},{14,4},{16,26},{18,... | collective-permute-start | bytes 196616 | tf_op jit(solution)/shard_map/ppermute | solution.py:93
  92.9 3.3 %fusion.2 = bf16[1,704,2048]{2,1,0:T(8,128)(2,1)} fusion(bf16[512,1024]{1,0:T(8,128)(2,1)S(1)} %get-tuple-element.39, bf16[512,1024]{1,0:T(8,128)(2,1)S(1)} %get-tuple-element.38, f32[512,704]{0,1:T(8,128)S(1)} %fusion.8, f32[512,704]{0,1:T(8,128)S(1)} %fusion.5), kind=kOutput, calls=%fused_computation.6 | convolution fusion | flops 1484193792 | bytes 7864320 | tf_op jit(solution)/shard_map/dot_general | solution.py:105
  96.3 3.3 %collective-permute-start.24 = (bf16[32,1024]{1,0:T(8,128)(2,1)S(1)}, bf16[32,1024]{1,0:T(8,128)(2,1)S(1)}, u32[]{:S(2)}, u32[]{:S(2)}) collective-permute-start(bf16[32,1024]{1,0:T(8,128)(2,1)S(1)} %get-tuple-element.50), channel_id=1, source_target_pairs={{0,14},{2,12},{4,10},{6,8},{8,6},{10,4},{12,2},{14,0},{16,30},{18,... | collective-permute-start | bytes 196616 | tf_op jit(solution)/shard_map/ppermute | solution.py:93
  100.3 2.7 %collective-permute-start.26 = (bf16[32,1024]{1,0:T(8,128)(2,1)S(1)}, bf16[32,1024]{1,0:T(8,128)(2,1)S(1)}, u32[]{:S(2)}, u32[]{:S(2)}) collective-permute-start(bf16[32,1024]{1,0:T(8,128)(2,1)S(1)} %get-tuple-element.48), channel_id=1, source_target_pairs={{0,18},{2,16},{4,22},{6,20},{8,26},{10,24},{12,30},{14,28},{16,2},... | collective-permute-start | bytes 196616 | tf_op jit(solution)/shard_map/ppermute | solution.py:93
  103.4 3.2 %fusion = bf16[1,704,2048]{2,1,0:T(8,128)(2,1)} fusion(bf16[512,704]{0,1:T(8,128)(2,1)S(1)} %get-tuple-element.37, bf16[512,1024]{1,0:T(8,128)(2,1)S(1)} %get-tuple-element.41, bf16[512,1024]{1,0:T(8,128)(2,1)S(1)} %get-tuple-element.40), kind=kOutput, calls=%fused_computation.4 | convolution fusion | flops 1482031104 | bytes 5701632 | tf_op jit(solution)/shard_map/dot_general | solution.py:105
  106.6 4.0 %collective-permute-start.28 = (bf16[32,1024]{1,0:T(8,128)(2,1)S(1)}, bf16[32,1024]{1,0:T(8,128)(2,1)S(1)}, u32[]{:S(2)}, u32[]{:S(2)}) collective-permute-start(bf16[32,1024]{1,0:T(8,128)(2,1)S(1)} %get-tuple-element.46), channel_id=1, source_target_pairs={{0,22},{2,20},{4,18},{6,16},{8,30},{10,28},{12,26},{14,24},{16,6},... | collective-permute-start | bytes 196616 | tf_op jit(solution)/shard_map/ppermute | solution.py:93
  110.6 1.2 collective-permute-start.29
  111.8 1.2 collective-permute-start.30
  113.0 0.9 collective-permute-start.31
  113.9 2.5 %collective-permute-start.32 = (bf16[32,1024]{1,0:T(8,128)(2,1)S(1)}, bf16[32,1024]{1,0:T(8,128)(2,1)S(1)}, u32[]{:S(2)}, u32[]{:S(2)}) collective-permute-start(bf16[32,1024]{1,0:T(8,128)(2,1)S(1)} %get-tuple-element.42), channel_id=1, source_target_pairs={{0,30},{2,28},{4,26},{6,24},{8,22},{10,20},{12,18},{14,16},{16,14}... | collective-permute-start | bytes 196616 | tf_op jit(solution)/shard_map/ppermute | solution.py:93
  116.4 3.2 %fusion.1 = bf16[1,704,2048]{2,1,0:T(8,128)(2,1)} fusion(bf16[512,704]{0,1:T(8,128)(2,1)S(1)} %get-tuple-element.36, bf16[512,1024]{1,0:T(8,128)(2,1)S(1)} %get-tuple-element.41, bf16[512,1024]{1,0:T(8,128)(2,1)S(1)} %get-tuple-element.40), kind=kOutput, calls=%fused_computation.5 | convolution fusion | flops 1482031104 | bytes 5701632 | tf_op jit(solution)/shard_map/dot_general | solution.py:105
  119.7 0.9 collective-permute-done.29.refs_12_
  120.6 1.4 %collective-permute-done.30.refs_13_ = bf16[32,1024]{1,0:T(8,128)(2,1)S(1)} collective-permute-done((bf16[32,1024]{1,0:T(8,128)(2,1)S(1)}, bf16[32,1024]{1,0:T(8,128)(2,1)S(1)}, u32[]{:S(2)}, u32[]{:S(2)}) %collective-permute-start.30) | collective-permute-done | bytes 65568 | tf_op jit(solution)/shard_map/ppermute | solution.py:93
  122.5 1.7 %collective-permute-done.32.refs_15_ = bf16[32,1024]{1,0:T(8,128)(2,1)S(1)} collective-permute-done((bf16[32,1024]{1,0:T(8,128)(2,1)S(1)}, bf16[32,1024]{1,0:T(8,128)(2,1)S(1)}, u32[]{:S(2)}, u32[]{:S(2)}) %collective-permute-start.32) | collective-permute-done | bytes 65568 | tf_op jit(solution)/shard_map/ppermute | solution.py:93
  124.2 1.5 %combine.1 = bf16[256,1024]{1,0:T(8,128)(2,1)} custom-call(s32[256,1]{1,0:T(8,128)S(1)} %copy.11.col_ref, s32[1,256]{1,0:T(1,128)S(1)} %bitcast.27, bf16[32,1024]{1,0:T(8,128)(2,1)S(1)} %get-tuple-element.57.refs_0_, bf16[32,1024]{1,0:T(8,128)(2,1)S(1)} %collective-permute-done.18.refs_1_, bf16[32,1024]{1,0:T(8,128)(2,1)S(1)} %collective-permute-done.19.refs_2_, ...), custom_call_target="tpu_custom_call" | custom-call | tf_op jit(solution)/shard_map/combine/pallas_call | solution.py:138
  (64 shorter events, 17.5 us)
Async XLA Ops:
  0.6 71.1 %copy-start = (bf16[1,704,2048]{2,1,0:T(8,128)(2,1)S(1)}, bf16[1,704,2048]{2,1,0:T(8,128)(2,1)}, u32[]{:S(2)}) copy-start(bf16[1,704,2048]{2,1,0:T(8,128)(2,1)} %param.9) | copy-start | bytes 8650756
  1.6 1.0 copy-start.1
  2.7 1.0 copy-start.2
  3.7 0.7 copy-start.3
  5.2 7.2 %collective-permute-start = (bf16[64,1024]{1,0:T(8,128)(2,1)S(1)}, bf16[64,1024]{1,0:T(8,128)(2,1)S(1)}, u32[]{:S(2)}, u32[]{:S(2)}) collective-permute-start(bf16[64,1024]{1,0:T(8,128)(2,1)S(1)} %get-tuple-element.21), channel_id=1, source_target_pairs={{0,2},{2,0},{4,6},{6,4},{8,10},{10,8},{12,14},{14,12},{16,18},{18,... | collective-permute-start | bytes 393224 | tf_op jit(solution)/shard_map/ppermute | solution.py:93
  6.7 7.7 %collective-permute-start.1 = (bf16[64,1024]{1,0:T(8,128)(2,1)S(1)}, bf16[64,1024]{1,0:T(8,128)(2,1)S(1)}, u32[]{:S(2)}, u32[]{:S(2)}) collective-permute-start(bf16[64,1024]{1,0:T(8,128)(2,1)S(1)} %get-tuple-element.22), channel_id=1, source_target_pairs={{0,4},{2,6},{4,0},{6,2},{8,12},{10,14},{12,8},{14,10},{16,20},{18,... | collective-permute-start | bytes 393224 | tf_op jit(solution)/shard_map/ppermute | solution.py:93
  8.3 8.6 %collective-permute-start.2 = (bf16[64,1024]{1,0:T(8,128)(2,1)S(1)}, bf16[64,1024]{1,0:T(8,128)(2,1)S(1)}, u32[]{:S(2)}, u32[]{:S(2)}) collective-permute-start(bf16[64,1024]{1,0:T(8,128)(2,1)S(1)} %get-tuple-element.23), channel_id=1, source_target_pairs={{0,6},{2,4},{4,2},{6,0},{8,14},{10,12},{12,10},{14,8},{16,22},{18,... | collective-permute-start | bytes 393224 | tf_op jit(solution)/shard_map/ppermute | solution.py:93
  8.7 11.3 %collective-permute-start.3 = (bf16[64,1024]{1,0:T(8,128)(2,1)S(1)}, bf16[64,1024]{1,0:T(8,128)(2,1)S(1)}, u32[]{:S(2)}, u32[]{:S(2)}) collective-permute-start(bf16[64,1024]{1,0:T(8,128)(2,1)S(1)} %get-tuple-element.24), channel_id=1, source_target_pairs={{0,8},{2,10},{4,12},{6,14},{8,0},{10,2},{12,4},{14,6},{16,24},{18,... | collective-permute-start | bytes 393224 | tf_op jit(solution)/shard_map/ppermute | solution.py:93
  8.7 13.0 %collective-permute-start.4 = (bf16[64,1024]{1,0:T(8,128)(2,1)S(1)}, bf16[64,1024]{1,0:T(8,128)(2,1)S(1)}, u32[]{:S(2)}, u32[]{:S(2)}) collective-permute-start(bf16[64,1024]{1,0:T(8,128)(2,1)S(1)} %get-tuple-element.25), channel_id=1, source_target_pairs={{0,10},{2,8},{4,14},{6,12},{8,2},{10,0},{12,6},{14,4},{16,26},{18,... | collective-permute-start | bytes 393224 | tf_op jit(solution)/shard_map/ppermute | solution.py:93
  12.4 13.6 %collective-permute-start.5 = (bf16[64,1024]{1,0:T(8,128)(2,1)S(1)}, bf16[64,1024]{1,0:T(8,128)(2,1)S(1)}, u32[]{:S(2)}, u32[]{:S(2)}) collective-permute-start(bf16[64,1024]{1,0:T(8,128)(2,1)S(1)} %get-tuple-element.26), channel_id=1, source_target_pairs={{0,12},{2,14},{4,8},{6,10},{8,4},{10,6},{12,0},{14,2},{16,28},{18,... | collective-permute-start | bytes 393224 | tf_op jit(solution)/shard_map/ppermute | solution.py:93
  14.4 14.4 %collective-permute-start.6 = (bf16[64,1024]{1,0:T(8,128)(2,1)S(1)}, bf16[64,1024]{1,0:T(8,128)(2,1)S(1)}, u32[]{:S(2)}, u32[]{:S(2)}) collective-permute-start(bf16[64,1024]{1,0:T(8,128)(2,1)S(1)} %get-tuple-element.27), channel_id=1, source_target_pairs={{0,14},{2,12},{4,10},{6,8},{8,6},{10,4},{12,2},{14,0},{16,30},{18,... | collective-permute-start | bytes 393224 | tf_op jit(solution)/shard_map/ppermute | solution.py:93
  16.8 22.5 %collective-permute-start.7 = (bf16[64,1024]{1,0:T(8,128)(2,1)S(1)}, bf16[64,1024]{1,0:T(8,128)(2,1)S(1)}, u32[]{:S(2)}, u32[]{:S(2)}) collective-permute-start(bf16[64,1024]{1,0:T(8,128)(2,1)S(1)} %get-tuple-element.28), channel_id=1, source_target_pairs={{0,16},{2,18},{4,20},{6,22},{8,24},{10,26},{12,28},{14,30},{16,0},... | collective-permute-start | bytes 393224 | tf_op jit(solution)/shard_map/ppermute | solution.py:93
  20.1 22.1 %collective-permute-start.8 = (bf16[64,1024]{1,0:T(8,128)(2,1)S(1)}, bf16[64,1024]{1,0:T(8,128)(2,1)S(1)}, u32[]{:S(2)}, u32[]{:S(2)}) collective-permute-start(bf16[64,1024]{1,0:T(8,128)(2,1)S(1)} %get-tuple-element.29), channel_id=1, source_target_pairs={{0,18},{2,16},{4,22},{6,20},{8,26},{10,24},{12,30},{14,28},{16,2},... | collective-permute-start | bytes 393224 | tf_op jit(solution)/shard_map/ppermute | solution.py:93
  21.8 23.2 %collective-permute-start.9 = (bf16[64,1024]{1,0:T(8,128)(2,1)S(1)}, bf16[64,1024]{1,0:T(8,128)(2,1)S(1)}, u32[]{:S(2)}, u32[]{:S(2)}) collective-permute-start(bf16[64,1024]{1,0:T(8,128)(2,1)S(1)} %get-tuple-element.30), channel_id=1, source_target_pairs={{0,20},{2,22},{4,16},{6,18},{8,28},{10,30},{12,24},{14,26},{16,4},... | collective-permute-start | bytes 393224 | tf_op jit(solution)/shard_map/ppermute | solution.py:93
  26.0 26.2 %collective-permute-start.10 = (bf16[64,1024]{1,0:T(8,128)(2,1)S(1)}, bf16[64,1024]{1,0:T(8,128)(2,1)S(1)}, u32[]{:S(2)}, u32[]{:S(2)}) collective-permute-start(bf16[64,1024]{1,0:T(8,128)(2,1)S(1)} %get-tuple-element.31), channel_id=1, source_target_pairs={{0,22},{2,20},{4,18},{6,16},{8,30},{10,28},{12,26},{14,24},{16,6},... | collective-permute-start | bytes 393224 | tf_op jit(solution)/shard_map/ppermute | solution.py:93
  28.8 28.2 %collective-permute-start.11 = (bf16[64,1024]{1,0:T(8,128)(2,1)S(1)}, bf16[64,1024]{1,0:T(8,128)(2,1)S(1)}, u32[]{:S(2)}, u32[]{:S(2)}) collective-permute-start(bf16[64,1024]{1,0:T(8,128)(2,1)S(1)} %get-tuple-element.32), channel_id=1, source_target_pairs={{0,24},{2,26},{4,28},{6,30},{8,16},{10,18},{12,20},{14,22},{16,8},... | collective-permute-start | bytes 393224 | tf_op jit(solution)/shard_map/ppermute | solution.py:93
  39.4 21.7 %collective-permute-start.12 = (bf16[64,1024]{1,0:T(8,128)(2,1)S(1)}, bf16[64,1024]{1,0:T(8,128)(2,1)S(1)}, u32[]{:S(2)}, u32[]{:S(2)}) collective-permute-start(bf16[64,1024]{1,0:T(8,128)(2,1)S(1)} %get-tuple-element.33), channel_id=1, source_target_pairs={{0,26},{2,24},{4,30},{6,28},{8,18},{10,16},{12,22},{14,20},{16,10}... | collective-permute-start | bytes 393224 | tf_op jit(solution)/shard_map/ppermute | solution.py:93
  42.2 21.2 %collective-permute-start.13 = (bf16[64,1024]{1,0:T(8,128)(2,1)S(1)}, bf16[64,1024]{1,0:T(8,128)(2,1)S(1)}, u32[]{:S(2)}, u32[]{:S(2)}) collective-permute-start(bf16[64,1024]{1,0:T(8,128)(2,1)S(1)} %get-tuple-element.34), channel_id=1, source_target_pairs={{0,28},{2,30},{4,24},{6,26},{8,20},{10,22},{12,16},{14,18},{16,12}... | collective-permute-start | bytes 393224 | tf_op jit(solution)/shard_map/ppermute | solution.py:93
  45.0 20.3 %collective-permute-start.14 = (bf16[64,1024]{1,0:T(8,128)(2,1)S(1)}, bf16[64,1024]{1,0:T(8,128)(2,1)S(1)}, u32[]{:S(2)}, u32[]{:S(2)}) collective-permute-start(bf16[64,1024]{1,0:T(8,128)(2,1)S(1)} %get-tuple-element.35), channel_id=1, source_target_pairs={{0,30},{2,28},{4,26},{6,24},{8,22},{10,20},{12,18},{14,16},{16,14}... | collective-permute-start | bytes 393224 | tf_op jit(solution)/shard_map/ppermute | solution.py:93
  66.0 4.1 %collective-permute-start.16 = (bf16[512,1024]{1,0:T(8,128)(2,1)}, bf16[512,1024]{1,0:T(8,128)(2,1)}, u32[]{:S(2)}, u32[]{:S(2)}) collective-permute-start(bf16[512,1024]{1,0:T(8,128)(2,1)} %get-tuple-element.59), channel_id=1, source_target_pairs={{0,1},{1,0},{2,3},{3,2},{4,5},{5,4},{6,7},{7,6},{8,9},{9,8},{10,11... | collective-permute-start | bytes 3145736 | tf_op jit(solution)/shard_map/ppermute | solution.py:61
  66.0 9.3 %collective-permute-start.15 = (bf16[512,1024]{1,0:T(8,128)(2,1)}, bf16[512,1024]{1,0:T(8,128)(2,1)S(1)}, u32[]{:S(2)}, u32[]{:S(2)}) collective-permute-start(bf16[512,1024]{1,0:T(8,128)(2,1)} %get-tuple-element.58), channel_id=1, source_target_pairs={{0,1},{1,0},{2,3},{3,2},{4,5},{5,4},{6,7},{7,6},{8,9},{9,8},{10,11... | collective-permute-start | bytes 3145736 | tf_op jit(solution)/shard_map/ppermute | solution.py:61
  71.8 1.8 %copy-start.5 = (bf16[1,704,2048]{2,1,0:T(8,128)(2,1)S(1)}, bf16[1,704,2048]{2,1,0:T(8,128)(2,1)}, u32[]{:S(2)}) copy-start(bf16[1,704,2048]{2,1,0:T(8,128)(2,1)} %param.10) | copy-start | bytes 8650756
  75.3 2.1 %copy-start.6 = (bf16[1,704,2048]{2,1,0:T(8,128)(2,1)S(1)}, bf16[1,704,2048]{2,1,0:T(8,128)(2,1)}, u32[]{:S(2)}) copy-start(bf16[1,704,2048]{2,1,0:T(8,128)(2,1)} %param.11) | copy-start | bytes 8650756
  83.5 2.7 %collective-permute-start.17 = (bf16[512,1024]{1,0:T(8,128)(2,1)S(1)}, bf16[512,1024]{1,0:T(8,128)(2,1)S(1)}, u32[]{:S(2)}, u32[]{:S(2)}) collective-permute-start(bf16[512,1024]{1,0:T(8,128)(2,1)S(1)} %select_convert_fusion), channel_id=1, source_target_pairs={{0,1},{1,0},{2,3},{3,2},{4,5},{5,4},{6,7},{7,6},{8,9},{9,8},{10,11... | collective-permute-start | bytes 3145736 | tf_op jit(solution)/shard_map/ppermute | solution.py:79
  87.0 9.3 %collective-permute-start.18 = (bf16[32,1024]{1,0:T(8,128)(2,1)S(1)}, bf16[32,1024]{1,0:T(8,128)(2,1)S(1)}, u32[]{:S(2)}, u32[]{:S(2)}) collective-permute-start(bf16[32,1024]{1,0:T(8,128)(2,1)S(1)} %get-tuple-element.56), channel_id=1, source_target_pairs={{0,2},{2,0},{4,6},{6,4},{8,10},{10,8},{12,14},{14,12},{16,18},{18,... | collective-permute-start | bytes 196616 | tf_op jit(solution)/shard_map/ppermute | solution.py:93
  88.0 8.4 %collective-permute-start.19 = (bf16[32,1024]{1,0:T(8,128)(2,1)S(1)}, bf16[32,1024]{1,0:T(8,128)(2,1)S(1)}, u32[]{:S(2)}, u32[]{:S(2)}) collective-permute-start(bf16[32,1024]{1,0:T(8,128)(2,1)S(1)} %get-tuple-element.55), channel_id=1, source_target_pairs={{0,4},{2,6},{4,0},{6,2},{8,12},{10,14},{12,8},{14,10},{16,20},{18,... | collective-permute-start | bytes 196616 | tf_op jit(solution)/shard_map/ppermute | solution.py:93
  88.7 11.0 %collective-permute-start.20 = (bf16[32,1024]{1,0:T(8,128)(2,1)S(1)}, bf16[32,1024]{1,0:T(8,128)(2,1)S(1)}, u32[]{:S(2)}, u32[]{:S(2)}) collective-permute-start(bf16[32,1024]{1,0:T(8,128)(2,1)S(1)} %get-tuple-element.54), channel_id=1, source_target_pairs={{0,6},{2,4},{4,2},{6,0},{8,14},{10,12},{12,10},{14,8},{16,22},{18,... | collective-permute-start | bytes 196616 | tf_op jit(solution)/shard_map/ppermute | solution.py:93
  90.5 9.8 %collective-permute-start.21 = (bf16[32,1024]{1,0:T(8,128)(2,1)S(1)}, bf16[32,1024]{1,0:T(8,128)(2,1)S(1)}, u32[]{:S(2)}, u32[]{:S(2)}) collective-permute-start(bf16[32,1024]{1,0:T(8,128)(2,1)S(1)} %get-tuple-element.53), channel_id=1, source_target_pairs={{0,8},{2,10},{4,12},{6,14},{8,0},{10,2},{12,4},{14,6},{16,24},{18,... | collective-permute-start | bytes 196616 | tf_op jit(solution)/shard_map/ppermute | solution.py:93
  90.5 12.5 %collective-permute-start.22 = (bf16[32,1024]{1,0:T(8,128)(2,1)S(1)}, bf16[32,1024]{1,0:T(8,128)(2,1)S(1)}, u32[]{:S(2)}, u32[]{:S(2)}) collective-permute-start(bf16[32,1024]{1,0:T(8,128)(2,1)S(1)} %get-tuple-element.52), channel_id=1, source_target_pairs={{0,10},{2,8},{4,14},{6,12},{8,2},{10,0},{12,6},{14,4},{16,26},{18,... | collective-permute-start | bytes 196616 | tf_op jit(solution)/shard_map/ppermute | solution.py:93
  96.2 10.4 %collective-permute-start.23 = (bf16[32,1024]{1,0:T(8,128)(2,1)S(1)}, bf16[32,1024]{1,0:T(8,128)(2,1)S(1)}, u32[]{:S(2)}, u32[]{:S(2)}) collective-permute-start(bf16[32,1024]{1,0:T(8,128)(2,1)S(1)} %get-tuple-element.51), channel_id=1, source_target_pairs={{0,12},{2,14},{4,8},{6,10},{8,4},{10,6},{12,0},{14,2},{16,28},{18,... | collective-permute-start | bytes 196616 | tf_op jit(solution)/shard_map/ppermute | solution.py:93
  96.3 14.2 %collective-permute-start.24 = (bf16[32,1024]{1,0:T(8,128)(2,1)S(1)}, bf16[32,1024]{1,0:T(8,128)(2,1)S(1)}, u32[]{:S(2)}, u32[]{:S(2)}) collective-permute-start(bf16[32,1024]{1,0:T(8,128)(2,1)S(1)} %get-tuple-element.50), channel_id=1, source_target_pairs={{0,14},{2,12},{4,10},{6,8},{8,6},{10,4},{12,2},{14,0},{16,30},{18,... | collective-permute-start | bytes 196616 | tf_op jit(solution)/shard_map/ppermute | solution.py:93
  99.7 12.1 %collective-permute-start.25 = (bf16[32,1024]{1,0:T(8,128)(2,1)S(1)}, bf16[32,1024]{1,0:T(8,128)(2,1)S(1)}, u32[]{:S(2)}, u32[]{:S(2)}) collective-permute-start(bf16[32,1024]{1,0:T(8,128)(2,1)S(1)} %get-tuple-element.49), channel_id=1, source_target_pairs={{0,16},{2,18},{4,20},{6,22},{8,24},{10,26},{12,28},{14,30},{16,0},... | collective-permute-start | bytes 196616 | tf_op jit(solution)/shard_map/ppermute | solution.py:93
  100.3 12.7 %collective-permute-start.26 = (bf16[32,1024]{1,0:T(8,128)(2,1)S(1)}, bf16[32,1024]{1,0:T(8,128)(2,1)S(1)}, u32[]{:S(2)}, u32[]{:S(2)}) collective-permute-start(bf16[32,1024]{1,0:T(8,128)(2,1)S(1)} %get-tuple-element.48), channel_id=1, source_target_pairs={{0,18},{2,16},{4,22},{6,20},{8,26},{10,24},{12,30},{14,28},{16,2},... | collective-permute-start | bytes 196616 | tf_op jit(solution)/shard_map/ppermute | solution.py:93
  103.0 10.9 %collective-permute-start.27 = (bf16[32,1024]{1,0:T(8,128)(2,1)S(1)}, bf16[32,1024]{1,0:T(8,128)(2,1)S(1)}, u32[]{:S(2)}, u32[]{:S(2)}) collective-permute-start(bf16[32,1024]{1,0:T(8,128)(2,1)S(1)} %get-tuple-element.47), channel_id=1, source_target_pairs={{0,20},{2,22},{4,16},{6,18},{8,28},{10,30},{12,24},{14,26},{16,4},... | collective-permute-start | bytes 196616 | tf_op jit(solution)/shard_map/ppermute | solution.py:93
  106.6 13.1 %collective-permute-start.28 = (bf16[32,1024]{1,0:T(8,128)(2,1)S(1)}, bf16[32,1024]{1,0:T(8,128)(2,1)S(1)}, u32[]{:S(2)}, u32[]{:S(2)}) collective-permute-start(bf16[32,1024]{1,0:T(8,128)(2,1)S(1)} %get-tuple-element.46), channel_id=1, source_target_pairs={{0,22},{2,20},{4,18},{6,16},{8,30},{10,28},{12,26},{14,24},{16,6},... | collective-permute-start | bytes 196616 | tf_op jit(solution)/shard_map/ppermute | solution.py:93
  110.6 10.0 %collective-permute-start.29 = (bf16[32,1024]{1,0:T(8,128)(2,1)S(1)}, bf16[32,1024]{1,0:T(8,128)(2,1)S(1)}, u32[]{:S(2)}, u32[]{:S(2)}) collective-permute-start(bf16[32,1024]{1,0:T(8,128)(2,1)S(1)} %get-tuple-element.45), channel_id=1, source_target_pairs={{0,24},{2,26},{4,28},{6,30},{8,16},{10,18},{12,20},{14,22},{16,8},... | collective-permute-start | bytes 196616 | tf_op jit(solution)/shard_map/ppermute | solution.py:93
  111.8 10.2 %collective-permute-start.30 = (bf16[32,1024]{1,0:T(8,128)(2,1)S(1)}, bf16[32,1024]{1,0:T(8,128)(2,1)S(1)}, u32[]{:S(2)}, u32[]{:S(2)}) collective-permute-start(bf16[32,1024]{1,0:T(8,128)(2,1)S(1)} %get-tuple-element.44), channel_id=1, source_target_pairs={{0,26},{2,24},{4,30},{6,28},{8,18},{10,16},{12,22},{14,20},{16,10}... | collective-permute-start | bytes 196616 | tf_op jit(solution)/shard_map/ppermute | solution.py:93
  113.0 9.5 %collective-permute-start.31 = (bf16[32,1024]{1,0:T(8,128)(2,1)S(1)}, bf16[32,1024]{1,0:T(8,128)(2,1)S(1)}, u32[]{:S(2)}, u32[]{:S(2)}) collective-permute-start(bf16[32,1024]{1,0:T(8,128)(2,1)S(1)} %get-tuple-element.43), channel_id=1, source_target_pairs={{0,28},{2,30},{4,24},{6,26},{8,20},{10,22},{12,16},{14,18},{16,12}... | collective-permute-start | bytes 196616 | tf_op jit(solution)/shard_map/ppermute | solution.py:93
  113.9 10.3 %copy-start.4 = (s32[256,1]{0,1:T(1,128)S(1)}, s32[256,1]{0,1:T(1,128)}, u32[]{:S(2)}) copy-start(s32[256,1]{0,1:T(1,128)} %param.8) | copy-start | bytes 3076
  113.9 10.3 %collective-permute-start.32 = (bf16[32,1024]{1,0:T(8,128)(2,1)S(1)}, bf16[32,1024]{1,0:T(8,128)(2,1)S(1)}, u32[]{:S(2)}, u32[]{:S(2)}) collective-permute-start(bf16[32,1024]{1,0:T(8,128)(2,1)S(1)} %get-tuple-element.42), channel_id=1, source_target_pairs={{0,30},{2,28},{4,26},{6,24},{8,22},{10,20},{12,18},{14,16},{16,14}... | collective-permute-start | bytes 196616 | tf_op jit(solution)/shard_map/ppermute | solution.py:93

commit v3 on v1

v3 whole, which is shorter than its diff:
```python
import functools

import jax
import jax.numpy as jnp
from jax import lax
from jax.experimental import pallas as pl
from jax.experimental.pallas import tpu as pltpu
from jax.sharding import PartitionSpec as P

F32 = jnp.float32
BF16 = jnp.bfloat16
LIMIT = 24 * 2**20
PIECES = 4


def rank_among_same(row, axis):
    rows = row.shape[1]
    down = lax.broadcasted_iota(jnp.int32, (rows, rows), 0)
    right = lax.broadcasted_iota(jnp.int32, (rows, rows), 1)
    col = jnp.sum(jnp.where(down == right, row, 0), axis=1, keepdims=True)
    earlier = down > right if axis else down < right
    same = jnp.where((col == row) & earlier, 1, 0)
    return (col if axis else row), jnp.sum(same, axis=axis, keepdims=True)


def place_kernel(capacity, row_ref, x_hbm, dy_hbm, out_ref, x_ref, dy_ref, sems):
    copies = [
        pltpu.make_async_copy(x_hbm, x_ref, sems.at[0]),
        pltpu.make_async_copy(dy_hbm, dy_ref, sems.at[1]),
    ]
    for copy in copies:
        copy.start()
    width = x_ref.shape[1]
    route, within = rank_among_same(row_ref[...], 0)
    slot = lax.broadcasted_iota(jnp.int32, (out_ref.shape[0], x_ref.shape[0]), 0)
    placing = jnp.where(slot == route * capacity + within, 1.0, 0.0).astype(BF16)
    for i, ref in enumerate((x_ref, dy_ref)):
        copies[i].wait()
        out_ref[:, i * width : (i + 1) * width] = jnp.dot(
            placing, ref[...], preferred_element_type=F32
        ).astype(BF16)


def combine_kernel(capacity, row_ref, back_hbm, out_ref, back_ref, sems):
    slots = back_ref.shape[0]
    step = slots // PIECES
    copies = [
        pltpu.make_async_copy(
            back_hbm.at[i * step : (i + 1) * step],
            back_ref.at[i * step : (i + 1) * step],
            sems.at[i],
        )
        for i in range(PIECES)
    ]
    for copy in copies:
        copy.start()
    route, within = rank_among_same(row_ref[...], 1)
    slot = lax.broadcasted_iota(jnp.int32, (out_ref.shape[0], slots), 1)
    placing = jnp.where(slot == route * capacity + within, 1.0, 0.0).astype(BF16)
    total = jnp.zeros(out_ref.shape, F32)
    for i, copy in enumerate(copies):
        copy.wait()
        total += jnp.dot(
            placing[:, i * step : (i + 1) * step],
            back_ref[i * step : (i + 1) * step],
            preferred_element_type=F32,
        )
    out_ref[...] = total.astype(BF16)


def rows_by_weights(rows, weights):
    return lax.dot_general(rows, weights, (((1,), (1,)), ((), ())), preferred_element_type=F32)


def weight_grad(left, right):
    return lax.dot_general(
        left, right, (((0,), (0,)), ((), ())), preferred_element_type=F32
    ).astype(BF16)


def on_device(tokens, upstream, expert_ids, w_gate, w_up, w_down):
    experts, parts = lax.axis_size("expert"), lax.axis_size("tensor")
    tok_rows, width = tokens.shape
    capacity = max(2, 2 * tok_rows // experts)
    slot_count = experts * capacity
    gate_rows, up_rows, down_rows = w_gate[0], w_up[0], w_down[0]
    ids_row = expert_ids.reshape(1, tok_rows)
    vmem = pl.BlockSpec(memory_space=pltpu.VMEM)
    hbm = pl.BlockSpec(memory_space=pl.ANY)
    params = pltpu.CompilerParams(vmem_limit_bytes=LIMIT)

    def to_experts(rows):
        return lax.all_to_all(
            rows.reshape(experts, capacity, rows.shape[1]),
            "expert",
            split_axis=0,
            concat_axis=0,
            tiled=True,
        ).reshape(slot_count, rows.shape[1])

    placed = pl.pallas_call(
        functools.partial(place_kernel, capacity),
        out_shape=jax.ShapeDtypeStruct((slot_count, 2 * width), BF16),
        in_specs=[vmem, hbm, hbm],
        out_specs=vmem,
        scratch_shapes=[
            pltpu.VMEM((tok_rows, width), BF16),
            pltpu.VMEM((tok_rows, width), BF16),
            pltpu.SemaphoreType.DMA((2,)),
        ],
        compiler_params=params,
        name="place",
    )(ids_row, tokens, upstream)
    own = to_experts(placed)
    own_x, own_dy = own[:, :width], own[:, width:]

    if parts == 2:
        other = lax.ppermute(own, "tensor", [(0, 1), (1, 0)])
        other_x, other_dy = other[:, :width], other[:, width:]
        mine = lax.axis_index("tensor")

        def halves(weights):
            return [
                lax.dynamic_slice_in_dim(weights, which * width, width, 1)
                for which in (mine, 1 - mine)
            ]

        gate_own, gate_other = halves(gate_rows)
        up_own, up_other = halves(up_rows)
        down_own, down_other = halves(down_rows)
        gate_pre = rows_by_weights(own_x, gate_own) + rows_by_weights(other_x, gate_other)
        up_pre = rows_by_weights(own_x, up_own) + rows_by_weights(other_x, up_other)
        d_hidden = rows_by_weights(own_dy, down_own) + rows_by_weights(other_dy, down_other)

        def in_order(left, right):
            first = mine == 0
            return jnp.concatenate(
                [jnp.where(first, left, right), jnp.where(first, right, left)], axis=1
            )

        x_all, dy_all = in_order(own_x, other_x), in_order(own_dy, other_dy)
    else:
        x_all = lax.all_gather(own_x, "tensor", axis=1, tiled=True)
        dy_all = lax.all_gather(own_dy, "tensor", axis=1, tiled=True)
        gate_pre = rows_by_weights(x_all, gate_rows)
        up_pre = rows_by_weights(x_all, up_rows)
        d_hidden = rows_by_weights(dy_all, down_rows)

    sig_gate = jax.nn.sigmoid(gate_pre)
    silu_gate = gate_pre * sig_gate
    hidden = (silu_gate * up_pre).astype(BF16)
    d_up = (d_hidden * silu_gate).astype(BF16)
    d_gate = (d_hidden * up_pre * sig_gate * (1.0 + gate_pre * (1.0 - sig_gate))).astype(BF16)

    def input_rows(gate_part, up_part):
        return jnp.dot(d_gate, gate_part, preferred_element_type=F32) + jnp.dot(
            d_up, up_part, preferred_element_type=F32
        )

    if parts == 2:
        sent = input_rows(gate_other, up_other).astype(BF16)
        got = lax.ppermute(sent, "tensor", [(0, 1), (1, 0)])
        totals = (input_rows(gate_own, up_own) + got.astype(F32)).astype(BF16)
    else:
        totals = lax.psum_scatter(
            input_rows(gate_rows, up_rows).astype(BF16),
            "tensor",
            scatter_dimension=1,
            tiled=True,
        )
    returned = to_experts(totals)
    grad_gate = weight_grad(d_gate, x_all)
    grad_up = weight_grad(d_up, x_all)
    grad_down = weight_grad(hidden, dy_all)
    grad_tokens = pl.pallas_call(
        functools.partial(combine_kernel, capacity),
        out_shape=jax.ShapeDtypeStruct((tok_rows, width), BF16),
        in_specs=[vmem, hbm],
        out_specs=vmem,
        scratch_shapes=[
            pltpu.VMEM((slot_count, width), BF16),
            pltpu.SemaphoreType.DMA((PIECES,)),
        ],
        compiler_params=params,
        name="combine",
    )(ids_row, returned)
    return (grad_tokens, grad_gate[None], grad_up[None], grad_down[None])


def solution(mesh):
    rows = P("expert", "tensor")
    weights = P("expert", "tensor", None)
    return jax.shard_map(
        on_device,
        mesh=mesh,
        in_specs=(rows, rows, P("expert", None), weights, weights, weights),
        out_specs=(rows, weights, weights, weights),
        check_vma=False,
    )
```

time: 121 us -> 117 us (0.967)
  blocking collectives: 0 us -> 55.3 us
  waiting for transfers between devices: 65.1 us -> 15.5 us
  starting transfers between devices: 17 us -> 5.42 us
  other arithmetic: 8.48 us -> 2.52 us
  Pallas kernels: 0 us -> 3.79 us
  matrix products: 27.3 us -> 29.9 us
  local copies, waits for them, and re-layouts: 1.52 us -> 2.97 us
    all_to_all x0 -> x1, blocking collectives: none -> 55.3 us  [to_experts(): lax.all_to_all(rows.reshape(experts, capacity, rows.shape[1]), 'expert',...]
    all_to_all x3 -> x1, waiting for transfers between devices: 62.4 us -> 14.2 us  [to_experts(): lax.all_to_all(rows.reshape(experts, capacity, rows.shape[1]), 'expert',...]
    all_to_all x3 -> x1, starting transfers between devices: 16.9 us -> 4.86 us  [to_experts(): lax.all_to_all(rows.reshape(experts, capacity, rows.shape[1]), 'expert',...]
    dot_general x3 -> x6, matrix products: 5.5 us -> 15 us  [rows_by_weights(): lax.dot_general(rows, weights, (((1,), (1,)), ((), ())), preferred_elemen...]
    dot_general x4 -> x3, matrix products: 14.2 us -> 9.81 us  [weight_grad(): lax.dot_general(left, right, (((0,), (0,)), ((), ())), preferred_element_...]
    pallas_call x0 -> x2, Pallas kernels: none -> 3.79 us  [the longest x1 2.59 us: on_device(): pl.pallas_call(functools.partial(combine_kernel, capacity), out_shape=jax...]
    convert_element_type x3 -> x0, other arithmetic: 2.67 us -> none  [the longest x1 1.64 us: scatter_sum(): return (kept + got.astype(F32)).astype(BF16)]
    dot_general x4, matrix products: 7.6 us -> 5.09 us  [the longest x2 3.05 us: input_rows(): jnp.dot(d_up, up_part, preferred_element_type=F32)]
  transfers between devices with their start and end apart: 6 -> 3, of which waited for: 4 -> 2; matrix products, arithmetic and copies ran while one was open for 15% -> 17% of each run, Pallas kernels for 0% -> 0%
where the time goes in v3:
time: 117 us; the launch traced here: 116 us
  blocking collectives  55.3 us (47%)
  matrix products  29.9 us (26%)
  waiting for transfers between devices  15.5 us (13%)
  starting transfers between devices  5.42 us (5%)
  Pallas kernels  3.79 us (3%)
  local copies, waits for them, and re-layouts  2.97 us (3%)
  other arithmetic  2.52 us (2%)
    all_to_all x1, blocking collectives, to_experts(): lax.all_to_all(rows.reshape(experts, capacity, rows.shape[1]), 'expert',...  55.3 us
    dot_general x6, matrix products, rows_by_weights(): lax.dot_general(rows, weights, (((1,), (1,)), ((), ())), preferred_elemen...  15 us
    all_to_all x1, waiting for transfers between devices, to_experts(): lax.all_to_all(rows.reshape(experts, capacity, rows.shape[1]), 'expert',...  14.2 us
    dot_general x3, matrix products, weight_grad(): lax.dot_general(left, right, (((0,), (0,)), ((), ())), preferred_element_...  9.81 us
    all_to_all x1, starting transfers between devices, to_experts(): lax.all_to_all(rows.reshape(experts, capacity, rows.shape[1]), 'expert',...  4.86 us
    dot_general x2, matrix products, input_rows(): jnp.dot(d_up, up_part, preferred_element_type=F32)  3.05 us
    unnamed x30, local copies, waits for them, and re-layouts  2.97 us
    pallas_call x1, Pallas kernels, on_device(): pl.pallas_call(functools.partial(combine_kernel, capacity), out_shape=jax...  2.59 us
  transfers between devices with their start and end apart: 3, of which 2 were waited for; matrix products, arithmetic and copies ran while one was open for 17% of the time, Pallas kernels for 0%

profile of v3, /device:TPU:8, one launch (start us, length us, event | category | flops | bytes accessed | tf_op | source)
XLA Modules:
  0.0 116.4 jit_solution(17371631241654885362)
XLA Ops:
  0.6 0.0 copy-start
  0.6 0.0 copy-start.1
  0.7 1.2 %copy-done.1 = bf16[256,1024]{1,0:T(8,128)(2,1)S(1)} copy-done((bf16[256,1024]{1,0:T(8,128)(2,1)S(1)}, bf16[256,1024]{1,0:T(8,128)(2,1)}, u32[]{:S(2)}) %copy-start.1) | copy-done | bytes 524312
  1.8 1.0 copy-done.2
  2.9 0.0 copy-start.3
  2.9 0.7 copy-done.3
  3.6 1.2 %place.1 = bf16[512,2048]{1,0:T(8,128)(2,1)S(1)} custom-call(s32[1,256]{1,0:T(1,128)S(1)} %bitcast.46, bf16[256,1024]{1,0:T(8,128)(2,1)S(1)} %copy-done.1, bf16[256,1024]{1,0:T(8,128)(2,1)S(1)} %copy-done.2), custom_call_target="tpu_custom_call" | custom-call | tf_op jit(solution)/shard_map/place/pallas_call | solution.py:101
  4.8 55.3 %all_to_all.10 = bf16[16,32,2048]{2,1,0:T(8,128)(2,1)} all-to-all(bf16[16,32,2048]{2,1,0:T(8,128)(2,1)S(1)} %bitcast.45), channel_id=1, replica_groups=mesh['expert'=16,'tensor'=2] {'expert'}, dimensions={0} | all-to-all | bytes 4194304 | tf_op jit(solution)/shard_map/all_to_all | solution.py:93
  60.1 0.0 collective-permute-start
  60.1 0.0 copy-done
  60.1 0.0 copy-start.8
  60.1 2.3 %fusion.11 = f32[512,704]{0,1:T(8,128)S(1)} fusion(bf16[1,704,2048]{2,1,0:T(8,128)(2,1)S(1)} %copy-done, s32[]{:T(128)S(6)} %select_n.30, bf16[512,2048]{1,0:T(8,128)(2,1)} %bitcast.2), kind=kOutput, calls=%fused_computation.20 | convolution fusion | flops 738197504 | bytes 3932164 | tf_op jit(solution)/shard_map/dot_general | solution.py:72
  62.4 0.0 copy-done.8
  62.4 0.0 copy-start.7
  62.4 2.4 %fusion.16 = f32[512,704]{0,1:T(8,128)S(1)} fusion(bf16[1,704,2048]{2,1,0:T(8,128)(2,1)S(1)} %copy-done.8, s32[]{:T(128)S(6)} %select_n.30, bf16[512,2048]{1,0:T(8,128)(2,1)} %bitcast.2), kind=kOutput, calls=%fused_computation.25 | convolution fusion | flops 738197504 | bytes 3932164 | tf_op jit(solution)/shard_map/dot_general | solution.py:72
  64.8 0.0 copy-done.7
  64.8 2.2 %fusion.19 = f32[512,704]{0,1:T(8,128)S(1)} fusion(bf16[1,704,2048]{2,1,0:T(8,128)(2,1)S(1)} %copy-done.7, s32[]{:T(128)S(6)} %select_n.30, bf16[512,2048]{1,0:T(8,128)(2,1)} %bitcast.2), kind=kOutput, calls=%fused_computation.28 | convolution fusion | flops 738197504 | bytes 3932164 | tf_op jit(solution)/shard_map/dot_general | solution.py:72
  67.0 0.0 collective-permute-done
  67.0 2.2 %convolution_add_fusion = f32[512,704]{0,1:T(8,128)S(1)} fusion(f32[512,704]{0,1:T(8,128)S(1)} %fusion.11, bf16[1,704,2048]{2,1,0:T(8,128)(2,1)S(1)} %copy-done, s32[]{:T(128)S(6)} %select_n.31, bf16[512,2048]{1,0:T(8,128)(2,1)} %collective-permute-done), kind=kOutput, calls=%fused_computation.12 | convolution fusion | flops 738557952 | bytes 5373956 | tf_op jit(solution)/shard_map/dot_general | solution.py:72
  69.2 0.0 copy-start.9
  69.2 2.7 %convolution_add_fusion.1 = f32[512,704]{0,1:T(8,128)S(1)} fusion(f32[512,704]{0,1:T(8,128)S(1)} %fusion.16, bf16[1,704,2048]{2,1,0:T(8,128)(2,1)S(1)} %copy-done.8, s32[]{:T(128)S(6)} %select_n.31, bf16[512,2048]{1,0:T(8,128)(2,1)} %collective-permute-done), kind=kOutput, calls=%fused_computation.13 | convolution fusion | flops 738557952 | bytes 5373956 | tf_op jit(solution)/shard_map/dot_general | solution.py:72
  72.0 0.0 copy-done.9
  72.0 0.0 copy-start.11
  72.0 3.2 %multiply_convert_fusion.1 = (bf16[512,704]{0,1:T(8,128)(2,1)S(1)}, bf16[512,704]{0,1:T(8,128)(2,1)S(1)}) fusion(f32[512,704]{0,1:T(8,128)S(1)} %convolution_add_fusion, f32[512,704]{0,1:T(8,128)S(1)} %convolution_add_fusion.1, f32[512,704]{0,1:T(8,128)S(1)} %fusion.19, bf16[1,704,2048]{2,1,0:T(8,128)(2,1)S(1)} %copy-done.7, s32[]{:T(128)S(6)} %select_n.31, ...), kind=kOutput, calls=%fused_computation.31 | convolution fusion | flops 743243776 | bytes 8257540 | tf_op jit(solution)/shard_map/dot_general | solution.py:72
  75.2 0.0 copy-done.11
  75.2 0.0 copy-start.5
  75.2 0.0 copy-start.13
  75.3 1.0 fusion.6
  76.3 1.0 add_convert_fusion.1
  77.3 0.6 collective-permute-start.1
  77.8 0.0 copy-done.5
  77.8 1.0 fusion.9
  78.9 1.3 %collective-permute-done.1 = bf16[512,1024]{1,0:T(8,128)(2,1)S(1)} collective-permute-done((bf16[512,1024]{1,0:T(8,128)(2,1)S(1)}, bf16[512,1024]{1,0:T(8,128)(2,1)S(1)}, u32[]{:S(2)}, u32[]{:S(2)}) %collective-permute-start.1) | collective-permute-done | bytes 1048608 | tf_op jit(solution)/shard_map/ppermute | solution.py:162
  80.1 0.0 copy-done.13
  80.1 2.0 %add_convert_fusion = bf16[512,1024]{1,0:T(8,128)(2,1)} fusion(bf16[512,1024]{1,0:T(8,128)(2,1)S(1)} %collective-permute-done.1, f32[512,1024]{1,0:T(8,128)S(1)} %fusion.9, bf16[512,704]{0,1:T(8,128)(2,1)S(1)} %get-tuple-element.8, bf16[1,704,2048]{2,1,0:T(8,128)(2,1)S(1)} %copy-done.8, s32[]{:T(128)S(6)} %select_n.30), kind=kOutput, calls=%fused_computation.10 | convolution fusion | flops 740294656 | bytes 6356996 | tf_op jit(solution)/shard_map/dot_general | solution.py:156
  82.2 4.9 %all-to-all-start.1 = ((bf16[16,32,1024]{2,1,0:T(8,128)(2,1)}), bf16[16,32,1024]{2,1,0:T(8,128)(2,1)}, u32[]{:S(2)}, u32[]{:S(2)}) async-start(bf16[16,32,1024]{2,1,0:T(8,128)(2,1)} %bitcast.48), calls=%async_computation.1 | async-start | bytes 2097152 | tf_op jit(solution)/shard_map/all_to_all | solution.py:93
  87.0 2.5 %broadcast_select_fusion.1 = (bf16[512,1024]{1,0:T(8,128)(2,1)S(1)}, bf16[512,1024]{1,0:T(8,128)(2,1)S(1)}, bf16[512,1024]{1,0:T(8,128)(2,1)S(1)}, bf16[512,1024]{1,0:T(8,128)(2,1)S(1)}) fusion(pred[]{:T(512)S(6)} %eq.4, bf16[512,2048]{1,0:T(8,128)(2,1)} %collective-permute-done, bf16[512,2048]{1,0:T(8,128)(2,1)} %bitcast.2), kind=kLoop, calls=%fused_computation.46 | loop fusion | flops 2097152 | bytes 8388609 | tf_op jit(solution)/shard_map/jit(_where)/select_n | solution.py:138
  89.6 0.0 copy-done.14
  89.6 0.0 copy-start.6
  89.6 3.2 %fusion.1 = bf16[1,704,2048]{2,1,0:T(8,128)(2,1)} fusion(bf16[512,704]{0,1:T(8,128)(2,1)S(1)} %copy-done.14, bf16[512,1024]{1,0:T(8,128)(2,1)S(1)} %get-tuple-element.5, bf16[512,1024]{1,0:T(8,128)(2,1)S(1)} %get-tuple-element.7), kind=kOutput, calls=%fused_computation.4 | convolution fusion | flops 1482031104 | bytes 5701632 | tf_op jit(solution)/shard_map/dot_general | solution.py:76
  92.8 0.0 copy-done.6
  92.8 3.3 %fusion = bf16[1,704,2048]{2,1,0:T(8,128)(2,1)} fusion(bf16[512,704]{0,1:T(8,128)(2,1)S(1)} %copy-done.6, bf16[512,1024]{1,0:T(8,128)(2,1)S(1)} %get-tuple-element.5, bf16[512,1024]{1,0:T(8,128)(2,1)S(1)} %get-tuple-element.7), kind=kOutput, calls=%fused_computation.3 | convolution fusion | flops 1482031104 | bytes 5701632 | tf_op jit(solution)/shard_map/dot_general | solution.py:76
  96.1 0.0 copy-done.10
  96.1 0.0 copy-done.12
  96.1 3.3 %fusion.2 = bf16[1,704,2048]{2,1,0:T(8,128)(2,1)} fusion(bf16[512,1024]{1,0:T(8,128)(2,1)S(1)} %get-tuple-element.6, bf16[512,1024]{1,0:T(8,128)(2,1)S(1)} %get-tuple-element.4, f32[512,704]{0,1:T(8,128)S(1)} %copy-done.12, f32[512,704]{0,1:T(8,128)S(1)} %copy-done.10), kind=kOutput, calls=%fused_computation.5 | convolution fusion | flops 1484193792 | bytes 7864320 | tf_op jit(solution)/shard_map/dot_general | solution.py:76
  99.4 14.2 %all-to-all-done.1 = bf16[16,32,1024]{2,1,0:T(8,128)(2,1)} async-done(((bf16[16,32,1024]{2,1,0:T(8,128)(2,1)}), bf16[16,32,1024]{2,1,0:T(8,128)(2,1)}, u32[]{:S(2)}, u32[]{:S(2)}) %all-to-all-start.1) | async-done | bytes 1048608 | tf_op jit(solution)/shard_map/all_to_all | solution.py:93
  113.6 0.0 copy-done.4
  113.6 2.6 %combine.1 = bf16[256,1024]{1,0:T(8,128)(2,1)} custom-call(s32[1,256]{1,0:T(1,128)S(1)} %bitcast.47, bf16[512,1024]{1,0:T(8,128)(2,1)} %bitcast.10.back_hbm), custom_call_target="tpu_custom_call" | custom-call | tf_op jit(solution)/shard_map/combine/pallas_call | solution.py:175
  (5 shorter events, 0.0 us)
Async XLA Ops:
  0.6 59.4 %copy-start = (bf16[1,704,2048]{2,1,0:T(8,128)(2,1)S(1)}, bf16[1,704,2048]{2,1,0:T(8,128)(2,1)}, u32[]{:S(2)}) copy-start(bf16[1,704,2048]{2,1,0:T(8,128)(2,1)} %param.9) | copy-start | bytes 8650756
  0.6 1.2 %copy-start.1 = (bf16[256,1024]{1,0:T(8,128)(2,1)S(1)}, bf16[256,1024]{1,0:T(8,128)(2,1)}, u32[]{:S(2)}) copy-start(bf16[256,1024]{1,0:T(8,128)(2,1)} %x_hbm.1) | copy-start | bytes 1572868
  1.8 1.0 copy-start.2
  2.9 0.7 copy-start.3
  60.1 7.0 %collective-permute-start = (bf16[512,2048]{1,0:T(8,128)(2,1)}, bf16[512,2048]{1,0:T(8,128)(2,1)}, u32[]{:S(2)}, u32[]{:S(2)}) collective-permute-start(bf16[512,2048]{1,0:T(8,128)(2,1)} %bitcast.2), channel_id=1, source_target_pairs={{0,1},{1,0},{2,3},{3,2},{4,5},{5,4},{6,7},{7,6},{8,9},{9,8},{10,11... | collective-permute-start | bytes 6291464 | tf_op jit(solution)/shard_map/ppermute | solution.py:118
  60.1 2.3 %copy-start.8 = (bf16[1,704,2048]{2,1,0:T(8,128)(2,1)S(1)}, bf16[1,704,2048]{2,1,0:T(8,128)(2,1)}, u32[]{:S(2)}) copy-start(bf16[1,704,2048]{2,1,0:T(8,128)(2,1)} %param.10) | copy-start | bytes 8650756
  62.4 2.4 %copy-start.7 = (bf16[1,704,2048]{2,1,0:T(8,128)(2,1)S(1)}, bf16[1,704,2048]{2,1,0:T(8,128)(2,1)}, u32[]{:S(2)}) copy-start(bf16[1,704,2048]{2,1,0:T(8,128)(2,1)} %param.11) | copy-start | bytes 8650756
  69.2 2.8 %copy-start.9 = (f32[512,704]{0,1:T(8,128)}, f32[512,704]{0,1:T(8,128)S(1)}, u32[]{:S(2)}) copy-start(f32[512,704]{0,1:T(8,128)S(1)} %convolution_add_fusion) | copy-start | bytes 4325380
  72.0 3.2 %copy-start.11 = (f32[512,704]{0,1:T(8,128)}, f32[512,704]{0,1:T(8,128)S(1)}, u32[]{:S(2)}) copy-start(f32[512,704]{0,1:T(8,128)S(1)} %convolution_add_fusion.1) | copy-start | bytes 4325380
  75.2 2.6 %copy-start.5 = (bf16[512,704]{0,1:T(8,128)(2,1)}, bf16[512,704]{0,1:T(8,128)(2,1)S(1)}, u32[]{:S(2)}) copy-start(bf16[512,704]{0,1:T(8,128)(2,1)S(1)} %get-tuple-element.9) | copy-start | bytes 2162692
  75.2 4.9 %copy-start.13 = (bf16[512,704]{0,1:T(8,128)(2,1)}, bf16[512,704]{0,1:T(8,128)(2,1)S(1)}, u32[]{:S(2)}) copy-start(bf16[512,704]{0,1:T(8,128)(2,1)S(1)} %get-tuple-element.8) | copy-start | bytes 2162692
  77.3 2.8 %collective-permute-start.1 = (bf16[512,1024]{1,0:T(8,128)(2,1)S(1)}, bf16[512,1024]{1,0:T(8,128)(2,1)S(1)}, u32[]{:S(2)}, u32[]{:S(2)}) collective-permute-start(bf16[512,1024]{1,0:T(8,128)(2,1)S(1)} %add_convert_fusion.1), channel_id=1, source_target_pairs={{0,1},{1,0},{2,3},{3,2},{4,5},{5,4},{6,7},{7,6},{8,9},{9,8},{10,11... | collective-permute-start | bytes 3145736 | tf_op jit(solution)/shard_map/ppermute | solution.py:162
  82.2 31.4 %all-to-all-start.1 = ((bf16[16,32,1024]{2,1,0:T(8,128)(2,1)}), bf16[16,32,1024]{2,1,0:T(8,128)(2,1)}, u32[]{:S(2)}, u32[]{:S(2)}) async-start(bf16[16,32,1024]{2,1,0:T(8,128)(2,1)} %bitcast.48), calls=%async_computation.1 | async-start | bytes 2097152 | tf_op jit(solution)/shard_map/all_to_all | solution.py:93
  87.0 2.5 %copy-start.14 = (bf16[512,704]{0,1:T(8,128)(2,1)S(1)}, bf16[512,704]{0,1:T(8,128)(2,1)}, u32[]{:S(2)}) copy-start(bf16[512,704]{0,1:T(8,128)(2,1)} %copy-done.13) | copy-start | bytes 2162692
  89.6 3.3 %copy-start.6 = (bf16[512,704]{0,1:T(8,128)(2,1)S(1)}, bf16[512,704]{0,1:T(8,128)(2,1)}, u32[]{:S(2)}) copy-start(bf16[512,704]{0,1:T(8,128)(2,1)} %copy-done.5) | copy-start | bytes 2162692
  92.8 3.3 %copy-start.10 = (f32[512,704]{0,1:T(8,128)S(1)}, f32[512,704]{0,1:T(8,128)}, u32[]{:S(2)}) copy-start(f32[512,704]{0,1:T(8,128)} %copy-done.9) | copy-start | bytes 4325380
  92.8 3.3 %copy-start.12 = (f32[512,704]{0,1:T(8,128)S(1)}, f32[512,704]{0,1:T(8,128)}, u32[]{:S(2)}) copy-start(f32[512,704]{0,1:T(8,128)} %copy-done.11) | copy-start | bytes 4325380
  96.1 17.5 %copy-start.4 = (s32[256,1]{0,1:T(1,128)S(1)}, s32[256,1]{0,1:T(1,128)}, u32[]{:S(2)}) copy-start(s32[256,1]{0,1:T(1,128)} %param.8) | copy-start | bytes 3076

commit v4 on v3

v4 whole, which is shorter than its diff:
```python
import functools

import jax
import jax.numpy as jnp
from jax import lax
from jax.experimental import pallas as pl
from jax.experimental.pallas import tpu as pltpu
from jax.sharding import PartitionSpec as P

F32 = jnp.float32
BF16 = jnp.bfloat16
SMALL = 20 * 2**20
LARGE = 56 * 2**20
PIECES = 4
IN_VMEM = pl.BlockSpec(memory_space=pltpu.VMEM)
ANYWHERE = pl.BlockSpec(memory_space=pl.ANY)


def rank_among_same(row, axis):
    rows = row.shape[1]
    down = lax.broadcasted_iota(jnp.int32, (rows, rows), 0)
    right = lax.broadcasted_iota(jnp.int32, (rows, rows), 1)
    col = jnp.sum(jnp.where(down == right, row, 0), axis=1, keepdims=True)
    earlier = down > right if axis else down < right
    same = jnp.where((col == row) & earlier, 1, 0)
    return (col if axis else row), jnp.sum(same, axis=axis, keepdims=True)


def place_kernel(capacity, row_ref, x_hbm, dy_hbm, *refs):
    *slabs, x_ref, dy_ref, sems = refs
    copies = [
        pltpu.make_async_copy(x_hbm, x_ref, sems.at[0]),
        pltpu.make_async_copy(dy_hbm, dy_ref, sems.at[1]),
    ]
    for copy in copies:
        copy.start()
    me = lax.axis_index("expert")
    route, within = rank_among_same(row_ref[...], 0)
    slots = len(slabs) * capacity
    slot = lax.broadcasted_iota(jnp.int32, (slots, x_ref.shape[0]), 0)
    placing = jnp.where(slot == (route ^ me) * capacity + within, 1.0, 0.0).astype(BF16)
    for i, ref in enumerate((x_ref, dy_ref)):
        copies[i].wait()
        placed = jnp.dot(placing, ref[...], preferred_element_type=F32).astype(BF16)
        for k, slab in enumerate(slabs):
            slab[i * capacity : (i + 1) * capacity, :] = placed[k * capacity : (k + 1) * capacity]


def collect_kernel(capacity, *refs):
    *slabs, out_ref = refs
    half = len(slabs) * capacity
    for i, slab in enumerate(slabs):
        out_ref[i * capacity : (i + 1) * capacity, :] = slab[:capacity, :]
        out_ref[half + i * capacity : half + (i + 1) * capacity, :] = slab[capacity:, :]


def side(which, width):
    return pl.ds(pl.multiple_of(which * width, width), width)


def input_rows(d_gate_ref, d_up_ref, gate_ref, up_ref, columns):
    over_hidden = (((0,), (0,)), ((), ()))
    return lax.dot_general(
        d_gate_ref[...], gate_ref[:, columns], over_hidden, preferred_element_type=F32
    ) + lax.dot_general(
        d_up_ref[...], up_ref[:, columns], over_hidden, preferred_element_type=F32
    )


def front_kernel(tile, own_ref, other_ref, gate_ref, up_ref, down_ref, *refs):
    x_ref, dy_ref, hidden_ref, d_gate_ref, d_up_ref, sent_ref = refs[-6:]
    rows, width = x_ref.shape[0], own_ref.shape[1]
    mine = lax.axis_index("tensor")
    for half, whole_ref in enumerate((x_ref, dy_ref)):
        whole_ref[:, side(mine, width)] = own_ref[half * rows : (half + 1) * rows, :]
        whole_ref[:, side(1 - mine, width)] = other_ref[half * rows : (half + 1) * rows, :]
    over_features = (((1,), (1,)), ((), ()))

    @pl.loop(0, hidden_ref.shape[0] // tile)
    def _(step):
        units = pl.ds(pl.multiple_of(step * tile, tile), tile)

        def product(weight_ref, whole_ref):
            return lax.dot_general(
                weight_ref[units, :], whole_ref[...], over_features, preferred_element_type=F32
            )

        gate_pre = product(gate_ref, x_ref)
        up_pre = product(up_ref, x_ref)
        d_hidden = product(down_ref, dy_ref)
        sig = jax.nn.sigmoid(gate_pre)
        silu = gate_pre * sig
        hidden_ref[units, :] = (silu * up_pre).astype(BF16)
        d_up_ref[units, :] = (d_hidden * silu).astype(BF16)
        d_gate_ref[units, :] = (
            d_hidden * up_pre * sig * (1.0 + gate_pre * (1.0 - sig))
        ).astype(BF16)

    sent_ref[...] = input_rows(
        d_gate_ref, d_up_ref, gate_ref, up_ref, side(1 - mine, width)
    ).astype(BF16)


def kept_kernel(d_gate_ref, d_up_ref, gate_ref, up_ref, out_ref):
    columns = side(lax.axis_index("tensor"), out_ref.shape[1])
    out_ref[...] = input_rows(d_gate_ref, d_up_ref, gate_ref, up_ref, columns)


def total_kernel(capacity, groups, *refs):
    *parts, out_ref, done_ref = refs
    me = lax.axis_index("expert")
    done_ref[...] = jnp.zeros_like(done_ref)
    for kept_ref, got_ref, group in zip(parts[::2], parts[1::2], groups):
        for i, k in enumerate(group):
            here = slice(i * capacity, (i + 1) * capacity)
            there = pl.ds(pl.multiple_of((me ^ k) * capacity, capacity), capacity)
            out_ref[there, :] = (kept_ref[here, :] + got_ref[here, :].astype(F32)).astype(BF16)


def grads_kernel(groups, *refs):
    *ins, _, grad_gate_ref, grad_up_ref, grad_down_ref = refs
    by_group = [ins[i :: groups] for i in range(groups)]

    def total(left, right):
        return sum(
            jnp.dot(one[left][...], one[right][...], preferred_element_type=F32)
            for one in by_group
        ).astype(BF16)

    grad_gate_ref[...] = total(0, 3)
    grad_up_ref[...] = total(1, 3)
    grad_down_ref[...] = total(2, 4)


def combine_kernel(capacity, row_ref, back_hbm, out_ref, back_ref, sems):
    slots = back_ref.shape[0]
    step = slots // PIECES
    copies = [
        pltpu.make_async_copy(
            back_hbm.at[i * step : (i + 1) * step],
            back_ref.at[i * step : (i + 1) * step],
            sems.at[i],
        )
        for i in range(PIECES)
    ]
    for copy in copies:
        copy.start()
    route, within = rank_among_same(row_ref[...], 1)
    slot = lax.broadcasted_iota(jnp.int32, (out_ref.shape[0], slots), 1)
    placing = jnp.where(slot == route * capacity + within, 1.0, 0.0).astype(BF16)
    total = jnp.zeros(out_ref.shape, F32)
    for i, copy in enumerate(copies):
        copy.wait()
        total += jnp.dot(
            placing[:, i * step : (i + 1) * step],
            back_ref[i * step : (i + 1) * step],
            preferred_element_type=F32,
        )
    out_ref[...] = total.astype(BF16)


def params(limit):
    return pltpu.CompilerParams(vmem_limit_bytes=limit)


def cost(products, rows, hidden, features):
    return pl.CostEstimate(
        flops=2 * products * rows * hidden * features,
        bytes_accessed=2 * products * (hidden + rows) * features,
        transcendentals=0,
    )


def combine(capacity, ids_row, returned, tok_rows):
    slots, width = returned.shape
    return pl.pallas_call(
        functools.partial(combine_kernel, capacity),
        out_shape=jax.ShapeDtypeStruct((tok_rows, width), BF16),
        in_specs=[IN_VMEM, ANYWHERE],
        out_specs=IN_VMEM,
        scratch_shapes=[pltpu.VMEM((slots, width), BF16), pltpu.SemaphoreType.DMA((PIECES,))],
        compiler_params=params(LARGE),
        name="combine",
    )(ids_row, returned)


def to_experts(rows, experts):
    return lax.all_to_all(
        rows.reshape(experts, rows.shape[0] // experts, rows.shape[1]),
        "expert",
        split_axis=0,
        concat_axis=0,
        tiled=True,
    ).reshape(rows.shape)


def grouped(tokens, upstream, expert_ids, gate_rows, up_rows, down_rows):
    experts = lax.axis_size("expert")
    tok_rows, width = tokens.shape
    units, features = gate_rows.shape
    capacity = max(2, 2 * tok_rows // experts)
    ids_row = expert_ids.reshape(1, tok_rows)
    tile = units // 2 if units % 32 == 0 else units

    far = [k for k in reversed(range(1, experts)) if k >= experts // 2]
    near = [k for k in reversed(range(1, experts)) if k < experts // 2]
    early = experts // 4 - 1
    share = experts // 2 - 1 - early
    turns = [k for pair in zip(far[:early], near[:early]) for k in pair]
    first = [0] + turns + near[early:share]
    second = far[early:] + near[share:]
    late = second[-2:]
    rows = len(first) * capacity

    slabs = list(
        pl.pallas_call(
            functools.partial(place_kernel, capacity),
            out_shape=[jax.ShapeDtypeStruct((2 * capacity, width), BF16)] * experts,
            in_specs=[IN_VMEM, ANYWHERE, ANYWHERE],
            out_specs=[IN_VMEM] * experts,
            scratch_shapes=[
                pltpu.VMEM((tok_rows, width), BF16),
                pltpu.VMEM((tok_rows, width), BF16),
                pltpu.SemaphoreType.DMA((2,)),
            ],
            compiler_params=params(LARGE),
            name="place",
        )(ids_row, tokens, upstream)
    )

    def swap(k):
        return lax.ppermute(slabs[k], "expert", [(e, e ^ k) for e in range(experts)])

    def exchange(values):
        return lax.ppermute(values, "tensor", [(0, 1), (1, 0)])

    def collect(arrived):
        return pl.pallas_call(
            functools.partial(collect_kernel, capacity),
            out_shape=jax.ShapeDtypeStruct((2 * rows, width), BF16),
            in_specs=[IN_VMEM] * len(arrived),
            out_specs=IN_VMEM,
            compiler_params=params(SMALL),
            name="collect",
        )(*arrived)

    def front(own, passed):
        other = exchange(own)
        outs = pl.pallas_call(
            functools.partial(front_kernel, tile),
            out_shape=[jax.ShapeDtypeStruct(one.shape, one.dtype) for one in passed]
            + [jax.ShapeDtypeStruct((rows, features), BF16)] * 2
            + [jax.ShapeDtypeStruct((units, rows), BF16)] * 3
            + [jax.ShapeDtypeStruct((rows, width), BF16)],
            in_specs=[IN_VMEM] * (5 + len(passed)),
            out_specs=[IN_VMEM] * (len(passed) + 6),
            input_output_aliases={5 + i: i for i in range(len(passed))},
            compiler_params=params(SMALL),
            cost_estimate=cost(4, rows, units, features),
            name="front",
        )(own, other, gate_rows, up_rows, down_rows, *passed)
        return outs[: len(passed)], outs[len(passed) :]

    def kept_rows(d_gate, d_up):
        return pl.pallas_call(
            kept_kernel,
            out_shape=jax.ShapeDtypeStruct((rows, width), F32),
            in_specs=[IN_VMEM] * 4,
            out_specs=IN_VMEM,
            compiler_params=params(SMALL),
            cost_estimate=cost(1, rows, units, features),
            name="kept",
        )(d_gate, d_up, gate_rows, up_rows)

    got = {k: swap(k) for k in first + second if k and k not in late}
    got[0] = slabs[0]
    passed, front_a = front(collect([got[k] for k in first]), [slabs[k] for k in late])
    for k, slab in zip(late, passed):
        slabs[k] = slab
        got[k] = swap(k)
    _, front_b = front(collect([got[k] for k in second]), [])
    sums = []
    for _, _, _, d_gate, d_up, sent in (front_a, front_b):
        sums += [kept_rows(d_gate, d_up), exchange(sent)]
    totals, done = pl.pallas_call(
        functools.partial(total_kernel, capacity, (first, second)),
        out_shape=[
            jax.ShapeDtypeStruct((experts * capacity, width), BF16),
            jax.ShapeDtypeStruct((8, 128), F32),
        ],
        in_specs=[IN_VMEM] * 4,
        out_specs=[IN_VMEM] * 2,
        compiler_params=params(SMALL),
        name="total",
    )(*sums)
    returned = to_experts(totals, experts)

    lefts = [front_a[3], front_b[3], front_a[4], front_b[4], front_a[2], front_b[2]]
    rights = [front_a[0], front_b[0], front_a[1], front_b[1]]
    grads = pl.pallas_call(
        functools.partial(grads_kernel, 2),
        grid=(units // tile,),
        out_shape=[jax.ShapeDtypeStruct((units, features), BF16)] * 3,
        in_specs=[pl.BlockSpec((tile, rows), lambda i: (i, 0))] * 6
        + [pl.BlockSpec((rows, features), lambda i: (0, 0))] * 4
        + [pl.BlockSpec((8, 128), lambda i: (0, 0))],
        out_specs=[pl.BlockSpec((tile, features), lambda i: (i, 0))] * 3,
        compiler_params=params(32 * 2**20),
        cost_estimate=cost(6, rows, units, features),
        name="grads",
    )(*lefts, *rights, done)
    return combine(capacity, ids_row, returned, tok_rows), grads


def rows_by_weights(rows, weights):
    return lax.dot_general(rows, weights, (((1,), (1,)), ((), ())), preferred_element_type=F32)


def weight_grad(left, right):
    return lax.dot_general(
        left, right, (((0,), (0,)), ((), ())), preferred_element_type=F32
    ).astype(BF16)


def general(tokens, upstream, expert_ids, gate_rows, up_rows, down_rows):
    experts = lax.axis_size("expert")
    tok_rows, width = tokens.shape
    capacity = max(2, 2 * tok_rows // experts)
    route = expert_ids[:, 0]
    onehot = (route[:, None] == jnp.arange(experts, dtype=jnp.int32)[None, :]).astype(jnp.int32)
    before = jnp.cumsum(onehot, axis=0) - onehot
    target = route * capacity + jnp.sum(before * onehot, axis=1)
    slot = jnp.arange(experts * capacity, dtype=jnp.int32)
    placing = (target[None, :] == slot[:, None]).astype(BF16)
    both = jnp.concatenate([tokens, upstream], axis=1)
    own = to_experts(jnp.dot(placing, both, preferred_element_type=F32).astype(BF16), experts)
    x_all = lax.all_gather(own[:, :width], "tensor", axis=1, tiled=True)
    dy_all = lax.all_gather(own[:, width:], "tensor", axis=1, tiled=True)
    gate_pre = rows_by_weights(x_all, gate_rows)
    up_pre = rows_by_weights(x_all, up_rows)
    d_hidden = rows_by_weights(dy_all, down_rows)
    sig = jax.nn.sigmoid(gate_pre)
    silu = gate_pre * sig
    hidden = (silu * up_pre).astype(BF16)
    d_up = (d_hidden * silu).astype(BF16)
    d_gate = (d_hidden * up_pre * sig * (1.0 + gate_pre * (1.0 - sig))).astype(BF16)
    partial = jnp.dot(d_gate, gate_rows, preferred_element_type=F32) + jnp.dot(
        d_up, up_rows, preferred_element_type=F32
    )
    totals = lax.psum_scatter(partial.astype(BF16), "tensor", scatter_dimension=1, tiled=True)
    returned = to_experts(totals, experts)
    grads = [weight_grad(d_gate, x_all), weight_grad(d_up, x_all), weight_grad(hidden, dy_all)]
    return weight_grad(placing, returned), grads


def on_device(tokens, upstream, expert_ids, w_gate, w_up, w_down):
    experts = lax.axis_size("expert")
    capacity = 2 * tokens.shape[0] // experts
    pairs = lax.axis_size("tensor") == 2 and experts & (experts - 1) == 0 and experts > 4
    run = grouped if pairs and capacity % 16 == 0 else general
    grad_tokens, grads = run(tokens, upstream, expert_ids, w_gate[0], w_up[0], w_down[0])
    return (grad_tokens, *(grad[None] for grad in grads))


def solution(mesh):
    rows = P("expert", "tensor")
    weights = P("expert", "tensor", None)
    return jax.shard_map(
        on_device,
        mesh=mesh,
        in_specs=(rows, rows, P("expert", None), weights, weights, weights),
        out_specs=(rows, weights, weights, weights),
        check_vma=False,
    )
```

time: 117 us -> 112 us (0.957)
  blocking collectives: 55.3 us -> 0 us
  starting transfers between devices: 5.42 us -> 37.3 us
  matrix products: 29.9 us -> 0 us
  waiting for transfers between devices: 15.5 us -> 37.2 us
  Pallas kernels: 3.79 us -> 25 us
  local copies, waits for them, and re-layouts: 2.97 us -> 11 us
  other arithmetic: 2.52 us -> 0 us
    all_to_all x1 -> x0, blocking collectives: 55.3 us -> none  [to_experts(): lax.all_to_all(rows.reshape(experts, capacity, rows.shape[1]), 'expert',...]
    dot_general x13 -> x0, matrix products: 29.9 us -> none  [the longest x6 15 us: rows_by_weights(): lax.dot_general(rows, weights, (((1,), (1,)), ((), ())), preferred_elemen...]
    ppermute x2 -> x19, starting transfers between devices: 0.56 us -> 28.6 us  [the longest x15 27.7 us: swap(): lax.ppermute(slabs[k], 'expert', [(e, e ^ k) for e in range(experts)])]
    pallas_call x2 -> x10, Pallas kernels: 3.79 us -> 25 us  [the longest x2 7.68 us: front(): pl.pallas_call(functools.partial(front_kernel, tile), out_shape=[jax.Shap...]
    ppermute x2 -> x19, waiting for transfers between devices: 1.26 us -> 22.1 us  [the longest x15 19.9 us: swap(): lax.ppermute(slabs[k], 'expert', [(e, e ^ k) for e in range(experts)])]
    unnamed x30 -> x32, local copies, waits for them, and re-layouts: 2.97 us -> 11 us
    all_to_all x1, starting transfers between devices: 4.86 us -> 8.67 us  [to_experts(): lax.all_to_all(rows.reshape(experts, rows.shape[0] // experts, rows.shape...]
    select_n x1 -> x0, other arithmetic: 2.52 us -> none  [in_order(): jnp.where(first, left, right)]
  transfers between devices with their start and end apart: 3 -> 20, of which waited for: 2 -> 12; matrix products, arithmetic and copies ran while one was open for 17% -> 0% of each run, Pallas kernels for 0% -> 15%
where the time goes in v4:
time: 112 us; the launch traced here: 111 us
  starting transfers between devices  37.3 us (33%)
  waiting for transfers between devices  37.2 us (33%)
  Pallas kernels  25 us (22%)
  local copies, waits for them, and re-layouts  11 us (10%)
    ppermute x15, starting transfers between devices, swap(): lax.ppermute(slabs[k], 'expert', [(e, e ^ k) for e in range(experts)])  27.7 us
    ppermute x15, waiting for transfers between devices, swap(): lax.ppermute(slabs[k], 'expert', [(e, e ^ k) for e in range(experts)])  19.9 us
    all_to_all x1, waiting for transfers between devices, to_experts(): lax.all_to_all(rows.reshape(experts, rows.shape[0] // experts, rows.shape...  15.1 us
    unnamed x32, local copies, waits for them, and re-layouts  11 us
    all_to_all x1, starting transfers between devices, to_experts(): lax.all_to_all(rows.reshape(experts, rows.shape[0] // experts, rows.shape...  8.67 us
    pallas_call x2, Pallas kernels, front(): pl.pallas_call(functools.partial(front_kernel, tile), out_shape=[jax.Shap...  7.68 us
    pallas_call x1, Pallas kernels, grouped(): pl.pallas_call(functools.partial(grads_kernel, 2), grid=(units // tile,),...  6.77 us
    pallas_call x1, Pallas kernels, grouped(): pl.pallas_call(functools.partial(place_kernel, capacity), out_shape=[jax....  4 us
  transfers between devices with their start and end apart: 20, of which 12 were waited for; matrix products, arithmetic and copies ran while one was open for 0% of the time, Pallas kernels for 15%

profile of v4, /device:TPU:8, one launch (start us, length us, event | category | flops | bytes accessed | tf_op | source)
XLA Modules:
  0.0 111.2 jit_solution(3267671578344340673)
XLA Ops:
  0.6 4.0 %place.1 = (bf16[64,1024]{1,0:T(8,128)(2,1)}, bf16[64,1024]{1,0:T(8,128)(2,1)}, bf16[64,1024]{1,0:T(8,128)(2,1)}, bf16[64,1024]{1,0:T(8,128)(2,1)}, bf16[64,1024...) custom-call(s32[1,256]{1,0:T(1,128)} %bitcast.19, ...), custom_call_target="tpu_custom_call" | custom-call | tf_op jit(solution)/shard_map/place/pallas_call | solution.py:216
  4.6 3.5 %collective-permute-start = (bf16[64,1024]{1,0:T(8,128)(2,1)}, bf16[64,1024]{1,0:T(8,128)(2,1)S(1)}, u32[]{:S(2)}, u32[]{:S(2)}) collective-permute-start(bf16[64,1024]{1,0:T(8,128)(2,1)} %get-tuple-element.40), channel_id=1, source_target_pairs={{0,30},{2,28},{4,26},{6,24},{8,22},{10,20},{12,18},{14,16},{16,14}... | collective-permute-start | bytes 393224 | tf_op jit(solution)/shard_map/ppermute | solution.py:232
  8.2 2.4 %collective-permute-start.1 = (bf16[64,1024]{1,0:T(8,128)(2,1)}, bf16[64,1024]{1,0:T(8,128)(2,1)S(1)}, u32[]{:S(2)}, u32[]{:S(2)}) collective-permute-start(bf16[64,1024]{1,0:T(8,128)(2,1)} %get-tuple-element.41), channel_id=1, source_target_pairs={{0,14},{2,12},{4,10},{6,8},{8,6},{10,4},{12,2},{14,0},{16,30},{18,... | collective-permute-start | bytes 393224 | tf_op jit(solution)/shard_map/ppermute | solution.py:232
  10.6 0.3 collective-permute-start.2
  10.8 1.5 %collective-permute-start.3 = (bf16[64,1024]{1,0:T(8,128)(2,1)}, bf16[64,1024]{1,0:T(8,128)(2,1)S(1)}, u32[]{:S(2)}, u32[]{:S(2)}) collective-permute-start(bf16[64,1024]{1,0:T(8,128)(2,1)} %get-tuple-element.43), channel_id=1, source_target_pairs={{0,12},{2,14},{4,8},{6,10},{8,4},{10,6},{12,0},{14,2},{16,28},{18,... | collective-permute-start | bytes 393224 | tf_op jit(solution)/shard_map/ppermute | solution.py:232
  12.4 2.5 %collective-permute-start.4 = (bf16[64,1024]{1,0:T(8,128)(2,1)}, bf16[64,1024]{1,0:T(8,128)(2,1)S(1)}, u32[]{:S(2)}, u32[]{:S(2)}) collective-permute-start(bf16[64,1024]{1,0:T(8,128)(2,1)} %get-tuple-element.44), channel_id=1, source_target_pairs={{0,26},{2,24},{4,30},{6,28},{8,18},{10,16},{12,22},{14,20},{16,10}... | collective-permute-start | bytes 393224 | tf_op jit(solution)/shard_map/ppermute | solution.py:232
  14.9 1.1 collective-permute-done.refs_1_
  16.0 1.4 %collective-permute-start.5 = (bf16[64,1024]{1,0:T(8,128)(2,1)}, bf16[64,1024]{1,0:T(8,128)(2,1)S(1)}, u32[]{:S(2)}, u32[]{:S(2)}) collective-permute-start(bf16[64,1024]{1,0:T(8,128)(2,1)} %get-tuple-element.45), channel_id=1, source_target_pairs={{0,10},{2,8},{4,14},{6,12},{8,2},{10,0},{12,6},{14,4},{16,26},{18,... | collective-permute-start | bytes 393224 | tf_op jit(solution)/shard_map/ppermute | solution.py:232
  17.3 1.2 %collective-permute-done.1.refs_2_ = bf16[64,1024]{1,0:T(8,128)(2,1)S(1)} collective-permute-done((bf16[64,1024]{1,0:T(8,128)(2,1)}, bf16[64,1024]{1,0:T(8,128)(2,1)S(1)}, u32[]{:S(2)}, u32[]{:S(2)}) %collective-permute-start.1) | collective-permute-done | bytes 131104 | tf_op jit(solution)/shard_map/ppermute | solution.py:232
  18.5 4.6 %collective-permute-start.6 = (bf16[64,1024]{1,0:T(8,128)(2,1)}, bf16[64,1024]{1,0:T(8,128)(2,1)S(1)}, u32[]{:S(2)}, u32[]{:S(2)}) collective-permute-start(bf16[64,1024]{1,0:T(8,128)(2,1)} %get-tuple-element.46), channel_id=1, source_target_pairs={{0,8},{2,10},{4,12},{6,14},{8,0},{10,2},{12,4},{14,6},{16,24},{18,... | collective-permute-start | bytes 393224 | tf_op jit(solution)/shard_map/ppermute | solution.py:232
  23.1 0.5 collective-permute-done.3.refs_4_
  23.6 2.8 %collective-permute-done.4.refs_5_ = bf16[64,1024]{1,0:T(8,128)(2,1)S(1)} collective-permute-done((bf16[64,1024]{1,0:T(8,128)(2,1)}, bf16[64,1024]{1,0:T(8,128)(2,1)S(1)}, u32[]{:S(2)}, u32[]{:S(2)}) %collective-permute-start.4) | collective-permute-done | bytes 131104 | tf_op jit(solution)/shard_map/ppermute | solution.py:232
  26.4 3.5 %collective-permute-done.5.refs_6_ = bf16[64,1024]{1,0:T(8,128)(2,1)S(1)} collective-permute-done((bf16[64,1024]{1,0:T(8,128)(2,1)}, bf16[64,1024]{1,0:T(8,128)(2,1)S(1)}, u32[]{:S(2)}, u32[]{:S(2)}) %collective-permute-start.5) | collective-permute-done | bytes 131104 | tf_op jit(solution)/shard_map/ppermute | solution.py:232
  29.9 1.1 %collective-permute-done.6.refs_7_ = bf16[64,1024]{1,0:T(8,128)(2,1)S(1)} collective-permute-done((bf16[64,1024]{1,0:T(8,128)(2,1)}, bf16[64,1024]{1,0:T(8,128)(2,1)S(1)}, u32[]{:S(2)}, u32[]{:S(2)}) %collective-permute-start.6) | collective-permute-done | bytes 131104 | tf_op jit(solution)/shard_map/ppermute | solution.py:232
  31.0 0.9 copy-done.6
  32.1 4.1 %collective-permute-start.10 = (bf16[64,1024]{1,0:T(8,128)(2,1)}, bf16[64,1024]{1,0:T(8,128)(2,1)S(1)}, u32[]{:S(2)}, u32[]{:S(2)}) collective-permute-start(bf16[64,1024]{1,0:T(8,128)(2,1)} %get-tuple-element.53), channel_id=1, source_target_pairs={{0,22},{2,20},{4,18},{6,16},{8,30},{10,28},{12,26},{14,24},{16,6},... | collective-permute-start | bytes 393224 | tf_op jit(solution)/shard_map/ppermute | solution.py:232
  36.2 0.4 collective-permute-start.11
  36.6 2.8 %collective-permute-start.12 = (bf16[64,1024]{1,0:T(8,128)(2,1)}, bf16[64,1024]{1,0:T(8,128)(2,1)S(1)}, u32[]{:S(2)}, u32[]{:S(2)}) collective-permute-start(bf16[64,1024]{1,0:T(8,128)(2,1)} %get-tuple-element.55), channel_id=1, source_target_pairs={{0,18},{2,16},{4,22},{6,20},{8,26},{10,24},{12,30},{14,28},{16,2},... | collective-permute-start | bytes 393224 | tf_op jit(solution)/shard_map/ppermute | solution.py:232
  39.5 0.4 collective-permute-start.13
  39.9 1.8 %copy-done.1 = bf16[1,704,2048]{2,1,0:T(8,128)(2,1)S(1)} copy-done((bf16[1,704,2048]{2,1,0:T(8,128)(2,1)S(1)}, bf16[1,704,2048]{2,1,0:T(8,128)(2,1)}, u32[]{:S(2)}) %copy-start.1) | copy-done | bytes 2883608
  41.7 1.8 %copy-done.2 = bf16[1,704,2048]{2,1,0:T(8,128)(2,1)S(1)} copy-done((bf16[1,704,2048]{2,1,0:T(8,128)(2,1)S(1)}, bf16[1,704,2048]{2,1,0:T(8,128)(2,1)}, u32[]{:S(2)}) %copy-start.2) | copy-done | bytes 2883608
  43.5 0.9 copy-done.4
  44.4 0.9 copy-done.5
  45.3 3.8 %front.2 = (bf16[64,1024]{1,0:T(8,128)(2,1)S(1)}, bf16[64,1024]{1,0:T(8,128)(2,1)S(1)}, bf16[256,2048]{1,0:T(8,128)(2,1)S(1)}, bf16[256,2048]{1,0:T(8,128)(2,1)S...) custom-call(bf16[512,1024]{1,0:T(8,128)(2,1)S(1)} %collect.2.own_ref, ...), custom_call_target="tpu_custom_call", output_to_operand_aliasing={{0}: (5, {}), {1}: (6, {})} | custom-call | flops 2952790016 | bytes 15728640 | tf_op jit(solution)/shard_map/front/pallas_call | solution.py:249
  49.2 3.5 %collective-permute-done.9.refs_0_ = bf16[64,1024]{1,0:T(8,128)(2,1)S(1)} collective-permute-done((bf16[64,1024]{1,0:T(8,128)(2,1)}, bf16[64,1024]{1,0:T(8,128)(2,1)S(1)}, u32[]{:S(2)}, u32[]{:S(2)}) %collective-permute-start.9) | collective-permute-done | bytes 131104 | tf_op jit(solution)/shard_map/ppermute | solution.py:232
  52.7 1.1 collective-permute-start.14
  53.7 1.5 %collective-permute-start.15 = (bf16[64,1024]{1,0:T(8,128)(2,1)S(1)}, bf16[64,1024]{1,0:T(8,128)(2,1)S(1)}, u32[]{:S(2)}, u32[]{:S(2)}) collective-permute-start(bf16[64,1024]{1,0:T(8,128)(2,1)S(1)} %get-tuple-element.58), channel_id=1, source_target_pairs={{0,4},{2,6},{4,0},{6,2},{8,12},{10,14},{12,8},{14,10},{16,20},{18,... | collective-permute-start | bytes 393224 | tf_op jit(solution)/shard_map/ppermute | solution.py:232
  55.3 1.7 %collective-permute-done.11.refs_2_ = bf16[64,1024]{1,0:T(8,128)(2,1)S(1)} collective-permute-done((bf16[64,1024]{1,0:T(8,128)(2,1)}, bf16[64,1024]{1,0:T(8,128)(2,1)S(1)}, u32[]{:S(2)}, u32[]{:S(2)}) %collective-permute-start.11) | collective-permute-done | bytes 131104 | tf_op jit(solution)/shard_map/ppermute | solution.py:232
  57.0 1.1 %collective-permute-start.16 = (bf16[64,1024]{1,0:T(8,128)(2,1)S(1)}, bf16[64,1024]{1,0:T(8,128)(2,1)S(1)}, u32[]{:S(2)}, u32[]{:S(2)}) collective-permute-start(bf16[64,1024]{1,0:T(8,128)(2,1)S(1)} %get-tuple-element.59), channel_id=1, source_target_pairs={{0,2},{2,0},{4,6},{6,4},{8,10},{10,8},{12,14},{14,12},{16,18},{18,... | collective-permute-start | bytes 393224 | tf_op jit(solution)/shard_map/ppermute | solution.py:232
  58.1 2.0 %collective-permute-done.12.refs_3_ = bf16[64,1024]{1,0:T(8,128)(2,1)S(1)} collective-permute-done((bf16[64,1024]{1,0:T(8,128)(2,1)}, bf16[64,1024]{1,0:T(8,128)(2,1)S(1)}, u32[]{:S(2)}, u32[]{:S(2)}) %collective-permute-start.12) | collective-permute-done | bytes 131104 | tf_op jit(solution)/shard_map/ppermute | solution.py:232
  60.1 2.6 %collective-permute-done.13.refs_4_ = bf16[64,1024]{1,0:T(8,128)(2,1)S(1)} collective-permute-done((bf16[64,1024]{1,0:T(8,128)(2,1)}, bf16[64,1024]{1,0:T(8,128)(2,1)S(1)}, u32[]{:S(2)}, u32[]{:S(2)}) %collective-permute-start.13) | collective-permute-done | bytes 131104 | tf_op jit(solution)/shard_map/ppermute | solution.py:232
  62.9 0.5 collective-permute-start.8
  63.4 2.1 %collective-permute-done.17.other_ref = bf16[512,1024]{1,0:T(8,128)(2,1)S(1)} collective-permute-done((bf16[512,1024]{1,0:T(8,128)(2,1)S(1)}, bf16[512,1024]{1,0:T(8,128)(2,1)S(1)}, u32[]{:S(2)}, u32[]{:S(2)}) %collective-permute-start.17) | collective-permute-done | bytes 1048608 | tf_op jit(solution)/shard_map/ppermute | solution.py:235
  65.5 3.8 %front.3 = (bf16[256,2048]{1,0:T(8,128)(2,1)S(1)}, bf16[256,2048]{1,0:T(8,128)(2,1)S(1)}, bf16[704,256]{1,0:T(8,128)(2,1)S(1)}, bf16[704,256]{1,0:T(8,128)(2,1)S...) custom-call(bf16[512,1024]{1,0:T(8,128)(2,1)S(1)} %collect.3.own_ref, ...), custom_call_target="tpu_custom_call" | custom-call | flops 2952790016 | bytes 15728640 | tf_op jit(solution)/shard_map/front/pallas_call | solution.py:249
  69.4 0.2 collective-permute-start.18
  69.6 1.0 kept.2.refs_0_
  70.6 0.1 copy-done.11
  70.7 0.1 copy-done.13
  70.8 1.0 kept.3.refs_2_
  71.8 1.1 %total.1 = (bf16[512,1024]{1,0:T(8,128)(2,1)}, f32[8,128]{1,0:T(8,128)S(1)}) custom-call(f32[256,1024]{1,0:T(8,128)S(1)} %kept.2.refs_0_, bf16[256,1024]{1,0:T(8,128)(2,1)S(1)} %collective-permute-done.8.refs_1_, f32[256,1024]{1,0:T(8,128)S(1)} %kept.3.refs_2_, bf16[256,1024]{1,0:T(8,128)(2,1)S(1)} %collective-permute-done.18.refs_3_), custom_call_target="tpu_custom_call" | custom-call | tf_op jit(solution)/shard_map/total/pallas_call | solution.py:285
  73.0 8.7 %all-to-all-start = ((bf16[16,32,1024]{2,1,0:T(8,128)(2,1)}), bf16[16,32,1024]{2,1,0:T(8,128)(2,1)}, u32[]{:S(2)}, u32[]{:S(2)}) async-start(bf16[16,32,1024]{2,1,0:T(8,128)(2,1)} %bitcast.4), calls=%async_computation | async-start | bytes 2097152 | tf_op jit(solution)/shard_map/all_to_all | solution.py:188
  81.6 1.0 copy-done.8
  82.6 1.2 %copy-done.10 = bf16[256,2048]{1,0:T(8,128)(2,1)S(1)} copy-done((bf16[256,2048]{1,0:T(8,128)(2,1)S(1)}, bf16[256,2048]{1,0:T(8,128)(2,1)}, u32[]{:S(2)}) %copy-start.10) | copy-done | bytes 1048600
  83.8 1.2 %copy-done.12 = bf16[256,2048]{1,0:T(8,128)(2,1)S(1)} copy-done((bf16[256,2048]{1,0:T(8,128)(2,1)S(1)}, bf16[256,2048]{1,0:T(8,128)(2,1)}, u32[]{:S(2)}) %copy-start.12) | copy-done | bytes 1048600
  85.1 1.0 copy-done.14
  86.1 6.8 %grads.1 = (bf16[704,2048]{1,0:T(8,128)(2,1)}, bf16[704,2048]{1,0:T(8,128)(2,1)}, bf16[704,2048]{1,0:T(8,128)(2,1)}) custom-call(bf16[704,256]{1,0:T(8,128)(2,1)S(1)} %get-tuple-element.49.d_gate_ref.refs_0_, bf16[704,256]{1,0:T(8,128)(2,1)S(1)} %get-tuple-element.60.d_gate_ref.refs_1_, bf16[704,256]{1,0:T(8,128)(2,1)S(1)} %get-tuple-element.50.d_up_ref.refs_2_, ...), custom_call_target="tpu_custom_call" | custom-call | flops 4429185024 | bytes 23592960 | tf_op jit(solution)/shard_map/grads/pallas_call | solution.py:300
  92.8 15.1 %all-to-all-done = bf16[16,32,1024]{2,1,0:T(8,128)(2,1)} async-done(((bf16[16,32,1024]{2,1,0:T(8,128)(2,1)}), bf16[16,32,1024]{2,1,0:T(8,128)(2,1)}, u32[]{:S(2)}, u32[]{:S(2)}) %all-to-all-start) | async-done | bytes 1048608 | tf_op jit(solution)/shard_map/all_to_all | solution.py:188
  107.9 3.3 %combine.1 = bf16[256,1024]{1,0:T(8,128)(2,1)} custom-call(s32[1,256]{1,0:T(1,128)} %bitcast.20, bf16[512,1024]{1,0:T(8,128)(2,1)} %bitcast.5.back_hbm), custom_call_target="tpu_custom_call" | custom-call | tf_op jit(solution)/shard_map/combine/pallas_call | solution.py:176
  (34 shorter events, 0.4 us)
Async XLA Ops:
  0.6 39.2 %copy-start = (bf16[1,704,2048]{2,1,0:T(8,128)(2,1)S(1)}, bf16[1,704,2048]{2,1,0:T(8,128)(2,1)}, u32[]{:S(2)}) copy-start(bf16[1,704,2048]{2,1,0:T(8,128)(2,1)} %param.9) | copy-start | bytes 8650756
  4.6 11.3 %collective-permute-start = (bf16[64,1024]{1,0:T(8,128)(2,1)}, bf16[64,1024]{1,0:T(8,128)(2,1)S(1)}, u32[]{:S(2)}, u32[]{:S(2)}) collective-permute-start(bf16[64,1024]{1,0:T(8,128)(2,1)} %get-tuple-element.40), channel_id=1, source_target_pairs={{0,30},{2,28},{4,26},{6,24},{8,22},{10,20},{12,18},{14,16},{16,14}... | collective-permute-start | bytes 393224 | tf_op jit(solution)/shard_map/ppermute | solution.py:232
  8.2 10.3 %collective-permute-start.1 = (bf16[64,1024]{1,0:T(8,128)(2,1)}, bf16[64,1024]{1,0:T(8,128)(2,1)S(1)}, u32[]{:S(2)}, u32[]{:S(2)}) collective-permute-start(bf16[64,1024]{1,0:T(8,128)(2,1)} %get-tuple-element.41), channel_id=1, source_target_pairs={{0,14},{2,12},{4,10},{6,8},{8,6},{10,4},{12,2},{14,0},{16,30},{18,... | collective-permute-start | bytes 393224 | tf_op jit(solution)/shard_map/ppermute | solution.py:232
  10.6 12.5 %collective-permute-start.2 = (bf16[64,1024]{1,0:T(8,128)(2,1)}, bf16[64,1024]{1,0:T(8,128)(2,1)S(1)}, u32[]{:S(2)}, u32[]{:S(2)}) collective-permute-start(bf16[64,1024]{1,0:T(8,128)(2,1)} %get-tuple-element.42), channel_id=1, source_target_pairs={{0,28},{2,30},{4,24},{6,26},{8,20},{10,22},{12,16},{14,18},{16,12}... | collective-permute-start | bytes 393224 | tf_op jit(solution)/shard_map/ppermute | solution.py:232
  10.8 12.7 %collective-permute-start.3 = (bf16[64,1024]{1,0:T(8,128)(2,1)}, bf16[64,1024]{1,0:T(8,128)(2,1)S(1)}, u32[]{:S(2)}, u32[]{:S(2)}) collective-permute-start(bf16[64,1024]{1,0:T(8,128)(2,1)} %get-tuple-element.43), channel_id=1, source_target_pairs={{0,12},{2,14},{4,8},{6,10},{8,4},{10,6},{12,0},{14,2},{16,28},{18,... | collective-permute-start | bytes 393224 | tf_op jit(solution)/shard_map/ppermute | solution.py:232
  12.4 14.1 %collective-permute-start.4 = (bf16[64,1024]{1,0:T(8,128)(2,1)}, bf16[64,1024]{1,0:T(8,128)(2,1)S(1)}, u32[]{:S(2)}, u32[]{:S(2)}) collective-permute-start(bf16[64,1024]{1,0:T(8,128)(2,1)} %get-tuple-element.44), channel_id=1, source_target_pairs={{0,26},{2,24},{4,30},{6,28},{8,18},{10,16},{12,22},{14,20},{16,10}... | collective-permute-start | bytes 393224 | tf_op jit(solution)/shard_map/ppermute | solution.py:232
  16.0 13.9 %collective-permute-start.5 = (bf16[64,1024]{1,0:T(8,128)(2,1)}, bf16[64,1024]{1,0:T(8,128)(2,1)S(1)}, u32[]{:S(2)}, u32[]{:S(2)}) collective-permute-start(bf16[64,1024]{1,0:T(8,128)(2,1)} %get-tuple-element.45), channel_id=1, source_target_pairs={{0,10},{2,8},{4,14},{6,12},{8,2},{10,0},{12,6},{14,4},{16,26},{18,... | collective-permute-start | bytes 393224 | tf_op jit(solution)/shard_map/ppermute | solution.py:232
  18.5 12.5 %collective-permute-start.6 = (bf16[64,1024]{1,0:T(8,128)(2,1)}, bf16[64,1024]{1,0:T(8,128)(2,1)S(1)}, u32[]{:S(2)}, u32[]{:S(2)}) collective-permute-start(bf16[64,1024]{1,0:T(8,128)(2,1)} %get-tuple-element.46), channel_id=1, source_target_pairs={{0,8},{2,10},{4,12},{6,14},{8,0},{10,2},{12,4},{14,6},{16,24},{18,... | collective-permute-start | bytes 393224 | tf_op jit(solution)/shard_map/ppermute | solution.py:232
  31.0 0.9 copy-start.6
  32.0 7.5 %collective-permute-start.7 = (bf16[512,1024]{1,0:T(8,128)(2,1)S(1)}, bf16[512,1024]{1,0:T(8,128)(2,1)S(1)}, u32[]{:S(2)}, u32[]{:S(2)}) collective-permute-start(bf16[512,1024]{1,0:T(8,128)(2,1)S(1)} %collect.2.own_ref), channel_id=1, source_target_pairs={{0,1},{1,0},{2,3},{3,2},{4,5},{5,4},{6,7},{7,6},{8,9},{9,8},{10,11... | collective-permute-start | bytes 3145736 | tf_op jit(solution)/shard_map/ppermute | solution.py:235
  32.0 20.6 %collective-permute-start.9 = (bf16[64,1024]{1,0:T(8,128)(2,1)}, bf16[64,1024]{1,0:T(8,128)(2,1)S(1)}, u32[]{:S(2)}, u32[]{:S(2)}) collective-permute-start(bf16[64,1024]{1,0:T(8,128)(2,1)} %get-tuple-element.52), channel_id=1, source_target_pairs={{0,24},{2,26},{4,28},{6,30},{8,16},{10,18},{12,20},{14,22},{16,8},... | collective-permute-start | bytes 393224 | tf_op jit(solution)/shard_map/ppermute | solution.py:232
  32.1 21.6 %collective-permute-start.10 = (bf16[64,1024]{1,0:T(8,128)(2,1)}, bf16[64,1024]{1,0:T(8,128)(2,1)S(1)}, u32[]{:S(2)}, u32[]{:S(2)}) collective-permute-start(bf16[64,1024]{1,0:T(8,128)(2,1)} %get-tuple-element.53), channel_id=1, source_target_pairs={{0,22},{2,20},{4,18},{6,16},{8,30},{10,28},{12,26},{14,24},{16,6},... | collective-permute-start | bytes 393224 | tf_op jit(solution)/shard_map/ppermute | solution.py:232
  36.2 20.8 %collective-permute-start.11 = (bf16[64,1024]{1,0:T(8,128)(2,1)}, bf16[64,1024]{1,0:T(8,128)(2,1)S(1)}, u32[]{:S(2)}, u32[]{:S(2)}) collective-permute-start(bf16[64,1024]{1,0:T(8,128)(2,1)} %get-tuple-element.54), channel_id=1, source_target_pairs={{0,20},{2,22},{4,16},{6,18},{8,28},{10,30},{12,24},{14,26},{16,4},... | collective-permute-start | bytes 393224 | tf_op jit(solution)/shard_map/ppermute | solution.py:232
  36.6 23.5 %collective-permute-start.12 = (bf16[64,1024]{1,0:T(8,128)(2,1)}, bf16[64,1024]{1,0:T(8,128)(2,1)S(1)}, u32[]{:S(2)}, u32[]{:S(2)}) collective-permute-start(bf16[64,1024]{1,0:T(8,128)(2,1)} %get-tuple-element.55), channel_id=1, source_target_pairs={{0,18},{2,16},{4,22},{6,20},{8,26},{10,24},{12,30},{14,28},{16,2},... | collective-permute-start | bytes 393224 | tf_op jit(solution)/shard_map/ppermute | solution.py:232
  39.5 23.2 %collective-permute-start.13 = (bf16[64,1024]{1,0:T(8,128)(2,1)}, bf16[64,1024]{1,0:T(8,128)(2,1)S(1)}, u32[]{:S(2)}, u32[]{:S(2)}) collective-permute-start(bf16[64,1024]{1,0:T(8,128)(2,1)} %get-tuple-element.56), channel_id=1, source_target_pairs={{0,16},{2,18},{4,20},{6,22},{8,24},{10,26},{12,28},{14,30},{16,0},... | collective-permute-start | bytes 393224 | tf_op jit(solution)/shard_map/ppermute | solution.py:232
  39.9 1.8 %copy-start.1 = (bf16[1,704,2048]{2,1,0:T(8,128)(2,1)S(1)}, bf16[1,704,2048]{2,1,0:T(8,128)(2,1)}, u32[]{:S(2)}) copy-start(bf16[1,704,2048]{2,1,0:T(8,128)(2,1)} %param.10) | copy-start | bytes 8650756
  41.7 1.8 %copy-start.2 = (bf16[1,704,2048]{2,1,0:T(8,128)(2,1)S(1)}, bf16[1,704,2048]{2,1,0:T(8,128)(2,1)}, u32[]{:S(2)}) copy-start(bf16[1,704,2048]{2,1,0:T(8,128)(2,1)} %param.11) | copy-start | bytes 8650756
  43.5 0.9 copy-start.4
  44.4 0.9 copy-start.5
  45.3 7.4 %copy-start.15 = (bf16[64,1024]{1,0:T(8,128)(2,1)S(1)}, bf16[64,1024]{1,0:T(8,128)(2,1)}, u32[]{:S(2)}) copy-start(bf16[64,1024]{1,0:T(8,128)(2,1)} %get-tuple-element.57) | copy-start | bytes 393220
  45.3 20.2 %copy-start.3 = (bf16[1,704,2048]{2,1,0:T(8,128)(2,1)S(1)}, bf16[1,704,2048]{2,1,0:T(8,128)(2,1)}, u32[]{:S(2)}) copy-start(bf16[1,704,2048]{2,1,0:T(8,128)(2,1)} %param.11) | copy-start | bytes 8650756
  49.1 14.2 %copy-start.7 = (bf16[704,256]{1,0:T(8,128)(2,1)}, bf16[704,256]{1,0:T(8,128)(2,1)S(1)}, u32[]{:S(2)}) copy-start(bf16[704,256]{1,0:T(8,128)(2,1)S(1)} %get-tuple-element.64.refs_4_) | copy-start | bytes 1081348
  52.7 10.0 %collective-permute-start.14 = (bf16[64,1024]{1,0:T(8,128)(2,1)S(1)}, bf16[64,1024]{1,0:T(8,128)(2,1)S(1)}, u32[]{:S(2)}, u32[]{:S(2)}) collective-permute-start(bf16[64,1024]{1,0:T(8,128)(2,1)S(1)} %copy-done.15), channel_id=1, source_target_pairs={{0,6},{2,4},{4,2},{6,0},{8,14},{10,12},{12,10},{14,8},{16,22},{18,... | collective-permute-start | bytes 393224 | tf_op jit(solution)/shard_map/ppermute | solution.py:232
  53.7 9.0 %collective-permute-start.15 = (bf16[64,1024]{1,0:T(8,128)(2,1)S(1)}, bf16[64,1024]{1,0:T(8,128)(2,1)S(1)}, u32[]{:S(2)}, u32[]{:S(2)}) collective-permute-start(bf16[64,1024]{1,0:T(8,128)(2,1)S(1)} %get-tuple-element.58), channel_id=1, source_target_pairs={{0,4},{2,6},{4,0},{6,2},{8,12},{10,14},{12,8},{14,10},{16,20},{18,... | collective-permute-start | bytes 393224 | tf_op jit(solution)/shard_map/ppermute | solution.py:232
  57.0 5.7 %collective-permute-start.16 = (bf16[64,1024]{1,0:T(8,128)(2,1)S(1)}, bf16[64,1024]{1,0:T(8,128)(2,1)S(1)}, u32[]{:S(2)}, u32[]{:S(2)}) collective-permute-start(bf16[64,1024]{1,0:T(8,128)(2,1)S(1)} %get-tuple-element.59), channel_id=1, source_target_pairs={{0,2},{2,0},{4,6},{6,4},{8,10},{10,8},{12,14},{14,12},{16,18},{18,... | collective-permute-start | bytes 393224 | tf_op jit(solution)/shard_map/ppermute | solution.py:232
  62.8 2.7 %collective-permute-start.17 = (bf16[512,1024]{1,0:T(8,128)(2,1)S(1)}, bf16[512,1024]{1,0:T(8,128)(2,1)S(1)}, u32[]{:S(2)}, u32[]{:S(2)}) collective-permute-start(bf16[512,1024]{1,0:T(8,128)(2,1)S(1)} %collect.3.own_ref), channel_id=1, source_target_pairs={{0,1},{1,0},{2,3},{3,2},{4,5},{5,4},{6,7},{7,6},{8,9},{9,8},{10,11... | collective-permute-start | bytes 3145736 | tf_op jit(solution)/shard_map/ppermute | solution.py:235
  62.9 8.9 %collective-permute-start.8 = (bf16[256,1024]{1,0:T(8,128)(2,1)S(1)}, bf16[256,1024]{1,0:T(8,128)(2,1)S(1)}, u32[]{:S(2)}, u32[]{:S(2)}) collective-permute-start(bf16[256,1024]{1,0:T(8,128)(2,1)S(1)} %get-tuple-element.51), channel_id=1, source_target_pairs={{0,1},{1,0},{2,3},{3,2},{4,5},{5,4},{6,7},{7,6},{8,9},{9,8},{10,11... | collective-permute-start | bytes 1572872 | tf_op jit(solution)/shard_map/ppermute | solution.py:235
  69.4 1.2 %copy-start.9 = (bf16[256,2048]{1,0:T(8,128)(2,1)}, bf16[256,2048]{1,0:T(8,128)(2,1)S(1)}, u32[]{:S(2)}) copy-start(bf16[256,2048]{1,0:T(8,128)(2,1)S(1)} %get-tuple-element.67.refs_7_) | copy-start | bytes 3145732
  69.4 1.3 %copy-start.11 = (bf16[256,2048]{1,0:T(8,128)(2,1)}, bf16[256,2048]{1,0:T(8,128)(2,1)S(1)}, u32[]{:S(2)}) copy-start(bf16[256,2048]{1,0:T(8,128)(2,1)S(1)} %get-tuple-element.69.refs_9_) | copy-start | bytes 3145732
  69.4 1.4 %copy-start.13 = (bf16[704,256]{1,0:T(8,128)(2,1)}, bf16[704,256]{1,0:T(8,128)(2,1)S(1)}, u32[]{:S(2)}) copy-start(bf16[704,256]{1,0:T(8,128)(2,1)S(1)} %get-tuple-element.65.refs_5_) | copy-start | bytes 1081348
  69.4 2.4 %collective-permute-start.18 = (bf16[256,1024]{1,0:T(8,128)(2,1)S(1)}, bf16[256,1024]{1,0:T(8,128)(2,1)S(1)}, u32[]{:S(2)}, u32[]{:S(2)}) collective-permute-start(bf16[256,1024]{1,0:T(8,128)(2,1)S(1)} %get-tuple-element.62), channel_id=1, source_target_pairs={{0,1},{1,0},{2,3},{3,2},{4,5},{5,4},{6,7},{7,6},{8,9},{9,8},{10,11... | collective-permute-start | bytes 1572872 | tf_op jit(solution)/shard_map/ppermute | solution.py:235
  73.0 35.0 %all-to-all-start = ((bf16[16,32,1024]{2,1,0:T(8,128)(2,1)}), bf16[16,32,1024]{2,1,0:T(8,128)(2,1)}, u32[]{:S(2)}, u32[]{:S(2)}) async-start(bf16[16,32,1024]{2,1,0:T(8,128)(2,1)} %bitcast.4), calls=%async_computation | async-start | bytes 2097152 | tf_op jit(solution)/shard_map/all_to_all | solution.py:188
  81.6 1.0 copy-start.8
  82.6 1.2 %copy-start.10 = (bf16[256,2048]{1,0:T(8,128)(2,1)S(1)}, bf16[256,2048]{1,0:T(8,128)(2,1)}, u32[]{:S(2)}) copy-start(bf16[256,2048]{1,0:T(8,128)(2,1)} %copy-done.9) | copy-start | bytes 3145732
  83.8 1.2 %copy-start.12 = (bf16[256,2048]{1,0:T(8,128)(2,1)S(1)}, bf16[256,2048]{1,0:T(8,128)(2,1)}, u32[]{:S(2)}) copy-start(bf16[256,2048]{1,0:T(8,128)(2,1)} %copy-done.11) | copy-start | bytes 3145732
  85.1 1.0 copy-start.14

commit v5 on v4

--- a/solution.py
+++ b/solution.py
@@ -12,6 +12,7 @@
 SMALL = 20 * 2**20
 LARGE = 56 * 2**20
 PIECES = 4
+COLLECT = 16
 IN_VMEM = pl.BlockSpec(memory_space=pltpu.VMEM)
 ANYWHERE = pl.BlockSpec(memory_space=pl.ANY)
 
@@ -28,11 +29,19 @@
 
 def place_kernel(capacity, row_ref, x_hbm, dy_hbm, *refs):
     *slabs, x_ref, dy_ref, sems = refs
+    step = x_ref.shape[0] // PIECES
     copies = [
-        pltpu.make_async_copy(x_hbm, x_ref, sems.at[0]),
-        pltpu.make_async_copy(dy_hbm, dy_ref, sems.at[1]),
+        [
+            pltpu.make_async_copy(
+                from_ref.at[i * step : (i + 1) * step],
+                to_ref.at[i * step : (i + 1) * step],
+                sems.at[which, i],
+            )
+            for i in range(PIECES)
+        ]
+        for which, (from_ref, to_ref) in enumerate(((x_hbm, x_ref), (dy_hbm, dy_ref)))
     ]
-    for copy in copies:
+    for copy in copies[0] + copies[1]:
         copy.start()
     me = lax.axis_index("expert")
     route, within = rank_among_same(row_ref[...], 0)
@@ -40,7 +49,8 @@
     slot = lax.broadcasted_iota(jnp.int32, (slots, x_ref.shape[0]), 0)
     placing = jnp.where(slot == (route ^ me) * capacity + within, 1.0, 0.0).astype(BF16)
     for i, ref in enumerate((x_ref, dy_ref)):
-        copies[i].wait()
+        for copy in copies[i]:
+            copy.wait()
         placed = jnp.dot(placing, ref[...], preferred_element_type=F32).astype(BF16)
         for k, slab in enumerate(slabs):
             slab[i * capacity : (i + 1) * capacity, :] = placed[k * capacity : (k + 1) * capacity]
@@ -68,7 +78,7 @@
 
 
 def front_kernel(tile, own_ref, other_ref, gate_ref, up_ref, down_ref, *refs):
-    x_ref, dy_ref, hidden_ref, d_gate_ref, d_up_ref, sent_ref = refs[-6:]
+    x_ref, dy_ref, hidden_ref, d_gate_ref, d_up_ref, sent_ref = refs
     rows, width = x_ref.shape[0], own_ref.shape[1]
     mine = lax.axis_index("tensor")
     for half, whole_ref in enumerate((x_ref, dy_ref)):
@@ -204,12 +214,8 @@
 
     far = [k for k in reversed(range(1, experts)) if k >= experts // 2]
     near = [k for k in reversed(range(1, experts)) if k < experts // 2]
-    early = experts // 4 - 1
-    share = experts // 2 - 1 - early
-    turns = [k for pair in zip(far[:early], near[:early]) for k in pair]
-    first = [0] + turns + near[early:share]
-    second = far[early:] + near[share:]
-    late = second[-2:]
+    turns = [k for pair in zip(far, near) for k in pair] + far[len(near) :]
+    first, second = [0] + turns[: experts // 2 - 1], turns[experts // 2 - 1 :]
     rows = len(first) * capacity
 
     slabs = list(
@@ -221,7 +227,7 @@
             scratch_shapes=[
                 pltpu.VMEM((tok_rows, width), BF16),
                 pltpu.VMEM((tok_rows, width), BF16),
-                pltpu.SemaphoreType.DMA((2,)),
+                pltpu.SemaphoreType.DMA((2, PIECES)),
             ],
             compiler_params=params(LARGE),
             name="place",
@@ -241,25 +247,23 @@
             in_specs=[IN_VMEM] * len(arrived),
             out_specs=IN_VMEM,
             compiler_params=params(SMALL),
+            cost_estimate=cost(COLLECT, rows, units, features),
             name="collect",
         )(*arrived)
 
-    def front(own, passed):
+    def front(own):
         other = exchange(own)
-        outs = pl.pallas_call(
+        return pl.pallas_call(
             functools.partial(front_kernel, tile),
-            out_shape=[jax.ShapeDtypeStruct(one.shape, one.dtype) for one in passed]
-            + [jax.ShapeDtypeStruct((rows, features), BF16)] * 2
+            out_shape=[jax.ShapeDtypeStruct((rows, features), BF16)] * 2
             + [jax.ShapeDtypeStruct((units, rows), BF16)] * 3
             + [jax.ShapeDtypeStruct((rows, width), BF16)],
-            in_specs=[IN_VMEM] * (5 + len(passed)),
-            out_specs=[IN_VMEM] * (len(passed) + 6),
-            input_output_aliases={5 + i: i for i in range(len(passed))},
+            in_specs=[IN_VMEM] * 5,
+            out_specs=[IN_VMEM] * 6,
             compiler_params=params(SMALL),
             cost_estimate=cost(4, rows, units, features),
             name="front",
-        )(own, other, gate_rows, up_rows, down_rows, *passed)
-        return outs[: len(passed)], outs[len(passed) :]
+        )(own, other, gate_rows, up_rows, down_rows)
 
     def kept_rows(d_gate, d_up):
         return pl.pallas_call(
@@ -272,13 +276,10 @@
             name="kept",
         )(d_gate, d_up, gate_rows, up_rows)
 
-    got = {k: swap(k) for k in first + second if k and k not in late}
+    got = {k: swap(k) for k in turns}
     got[0] = slabs[0]
-    passed, front_a = front(collect([got[k] for k in first]), [slabs[k] for k in late])
-    for k, slab in zip(late, passed):
-        slabs[k] = slab
-        got[k] = swap(k)
-    _, front_b = front(collect([got[k] for k in second]), [])
+    front_a = front(collect([got[k] for k in first]))
+    front_b = front(collect([got[k] for k in second]))
     sums = []
     for _, _, _, d_gate, d_up, sent in (front_a, front_b):
         sums += [kept_rows(d_gate, d_up), exchange(sent)]

time: 112 us -> 104 us (0.929)
  local copies, waits for them, and re-layouts: 11 us -> 7.08 us
  waiting for transfers between devices: 37.2 us -> 34.8 us
  starting transfers between devices: 37.3 us -> 35.4 us
    unnamed x32 -> x24, local copies, waits for them, and re-layouts: 11 us -> 7.08 us
    all_to_all x1, starting transfers between devices: 8.67 us -> 6.33 us  [to_experts(): lax.all_to_all(rows.reshape(experts, rows.shape[0] // experts, rows.shape...]
    ppermute x4, waiting for transfers between devices: 2.15 us -> 0.01 us  [exchange(): return lax.ppermute(values, 'tensor', [(0, 1), (1, 0)])]
  transfers between devices with their start and end apart: 20 -> 20, of which waited for: 12 -> 11; matrix products, arithmetic and copies ran while one was open for 0% -> 0% of each run, Pallas kernels for 15% -> 16%
where the time goes in v5:
time: 104 us; the launch traced here: 103 us
  starting transfers between devices  35.4 us (34%)
  waiting for transfers between devices  34.8 us (33%)
  Pallas kernels  25 us (24%)
  local copies, waits for them, and re-layouts  7.08 us (7%)
    ppermute x15, starting transfers between devices, swap(): lax.ppermute(slabs[k], 'expert', [(e, e ^ k) for e in range(experts)])  28.4 us
    ppermute x15, waiting for transfers between devices, swap(): lax.ppermute(slabs[k], 'expert', [(e, e ^ k) for e in range(experts)])  19.2 us
    all_to_all x1, waiting for transfers between devices, to_experts(): lax.all_to_all(rows.reshape(experts, rows.shape[0] // experts, rows.shape...  15.6 us
    pallas_call x2, Pallas kernels, front(): pl.pallas_call(functools.partial(front_kernel, tile), out_shape=[jax.Shap...  7.7 us
    unnamed x24, local copies, waits for them, and re-layouts  7.08 us
    pallas_call x1, Pallas kernels, grouped(): pl.pallas_call(functools.partial(grads_kernel, 2), grid=(units // tile,),...  6.79 us
    all_to_all x1, starting transfers between devices, to_experts(): lax.all_to_all(rows.reshape(experts, rows.shape[0] // experts, rows.shape...  6.33 us
    pallas_call x1, Pallas kernels, grouped(): pl.pallas_call(functools.partial(place_kernel, capacity), out_shape=[jax....  3.92 us
  transfers between devices with their start and end apart: 20, of which 11 were waited for; matrix products, arithmetic and copies ran while one was open for 0% of the time, Pallas kernels for 16%

profile of v5, /device:TPU:8, one launch (start us, length us, event | category | flops | bytes accessed | tf_op | source)
XLA Modules:
  0.0 103.1 jit_solution(15003342683496399808)
XLA Ops:
  0.6 3.9 %place.1 = (bf16[64,1024]{1,0:T(8,128)(2,1)}, bf16[64,1024]{1,0:T(8,128)(2,1)}, bf16[64,1024]{1,0:T(8,128)(2,1)}, bf16[64,1024]{1,0:T(8,128)(2,1)}, bf16[64,1024...) custom-call(s32[1,256]{1,0:T(1,128)} %bitcast.19, ...), custom_call_target="tpu_custom_call" | custom-call | tf_op jit(solution)/shard_map/place/pallas_call | solution.py:222
  4.6 3.5 %collective-permute-start = (bf16[64,1024]{1,0:T(8,128)(2,1)}, bf16[64,1024]{1,0:T(8,128)(2,1)S(1)}, u32[]{:S(2)}, u32[]{:S(2)}) collective-permute-start(bf16[64,1024]{1,0:T(8,128)(2,1)} %get-tuple-element.38), channel_id=1, source_target_pairs={{0,30},{2,28},{4,26},{6,24},{8,22},{10,20},{12,18},{14,16},{16,14}... | collective-permute-start | bytes 393224 | tf_op jit(solution)/shard_map/ppermute | solution.py:238
  8.1 2.4 %collective-permute-start.1 = (bf16[64,1024]{1,0:T(8,128)(2,1)}, bf16[64,1024]{1,0:T(8,128)(2,1)S(1)}, u32[]{:S(2)}, u32[]{:S(2)}) collective-permute-start(bf16[64,1024]{1,0:T(8,128)(2,1)} %get-tuple-element.39), channel_id=1, source_target_pairs={{0,14},{2,12},{4,10},{6,8},{8,6},{10,4},{12,2},{14,0},{16,30},{18,... | collective-permute-start | bytes 393224 | tf_op jit(solution)/shard_map/ppermute | solution.py:238
  10.5 0.3 collective-permute-start.2
  10.8 1.5 %collective-permute-start.3 = (bf16[64,1024]{1,0:T(8,128)(2,1)}, bf16[64,1024]{1,0:T(8,128)(2,1)S(1)}, u32[]{:S(2)}, u32[]{:S(2)}) collective-permute-start(bf16[64,1024]{1,0:T(8,128)(2,1)} %get-tuple-element.41), channel_id=1, source_target_pairs={{0,12},{2,14},{4,8},{6,10},{8,4},{10,6},{12,0},{14,2},{16,28},{18,... | collective-permute-start | bytes 393224 | tf_op jit(solution)/shard_map/ppermute | solution.py:238
  12.3 2.5 %collective-permute-start.4 = (bf16[64,1024]{1,0:T(8,128)(2,1)}, bf16[64,1024]{1,0:T(8,128)(2,1)S(1)}, u32[]{:S(2)}, u32[]{:S(2)}) collective-permute-start(bf16[64,1024]{1,0:T(8,128)(2,1)} %get-tuple-element.42), channel_id=1, source_target_pairs={{0,26},{2,24},{4,30},{6,28},{8,18},{10,16},{12,22},{14,20},{16,10}... | collective-permute-start | bytes 393224 | tf_op jit(solution)/shard_map/ppermute | solution.py:238
  14.8 1.1 %collective-permute-done.refs_1_ = bf16[64,1024]{1,0:T(8,128)(2,1)S(1)} collective-permute-done((bf16[64,1024]{1,0:T(8,128)(2,1)}, bf16[64,1024]{1,0:T(8,128)(2,1)S(1)}, u32[]{:S(2)}, u32[]{:S(2)}) %collective-permute-start) | collective-permute-done | bytes 131104 | tf_op jit(solution)/shard_map/ppermute | solution.py:238
  15.9 1.4 %collective-permute-start.5 = (bf16[64,1024]{1,0:T(8,128)(2,1)}, bf16[64,1024]{1,0:T(8,128)(2,1)S(1)}, u32[]{:S(2)}, u32[]{:S(2)}) collective-permute-start(bf16[64,1024]{1,0:T(8,128)(2,1)} %get-tuple-element.43), channel_id=1, source_target_pairs={{0,10},{2,8},{4,14},{6,12},{8,2},{10,0},{12,6},{14,4},{16,26},{18,... | collective-permute-start | bytes 393224 | tf_op jit(solution)/shard_map/ppermute | solution.py:238
  17.2 1.2 %collective-permute-done.1.refs_2_ = bf16[64,1024]{1,0:T(8,128)(2,1)S(1)} collective-permute-done((bf16[64,1024]{1,0:T(8,128)(2,1)}, bf16[64,1024]{1,0:T(8,128)(2,1)S(1)}, u32[]{:S(2)}, u32[]{:S(2)}) %collective-permute-start.1) | collective-permute-done | bytes 131104 | tf_op jit(solution)/shard_map/ppermute | solution.py:238
  18.4 0.6 collective-permute-start.6
  19.0 3.4 %collective-permute-done.2.refs_3_ = bf16[64,1024]{1,0:T(8,128)(2,1)S(1)} collective-permute-done((bf16[64,1024]{1,0:T(8,128)(2,1)}, bf16[64,1024]{1,0:T(8,128)(2,1)S(1)}, u32[]{:S(2)}, u32[]{:S(2)}) %collective-permute-start.2) | collective-permute-done | bytes 131104 | tf_op jit(solution)/shard_map/ppermute | solution.py:238
  22.3 0.7 collective-permute-start.9
  23.0 0.5 collective-permute-done.3.refs_4_
  23.5 3.4 %collective-permute-start.10 = (bf16[64,1024]{1,0:T(8,128)(2,1)}, bf16[64,1024]{1,0:T(8,128)(2,1)S(1)}, u32[]{:S(2)}, u32[]{:S(2)}) collective-permute-start(bf16[64,1024]{1,0:T(8,128)(2,1)} %get-tuple-element.49), channel_id=1, source_target_pairs={{0,22},{2,20},{4,18},{6,16},{8,30},{10,28},{12,26},{14,24},{16,6},... | collective-permute-start | bytes 393224 | tf_op jit(solution)/shard_map/ppermute | solution.py:238
  26.9 0.3 collective-permute-done.4.refs_5_
  27.2 3.9 %collective-permute-start.11 = (bf16[64,1024]{1,0:T(8,128)(2,1)}, bf16[64,1024]{1,0:T(8,128)(2,1)S(1)}, u32[]{:S(2)}, u32[]{:S(2)}) collective-permute-start(bf16[64,1024]{1,0:T(8,128)(2,1)} %get-tuple-element.50), channel_id=1, source_target_pairs={{0,6},{2,4},{4,2},{6,0},{8,14},{10,12},{12,10},{14,8},{16,22},{18,... | collective-permute-start | bytes 393224 | tf_op jit(solution)/shard_map/ppermute | solution.py:238
  31.2 2.5 %collective-permute-done.6.refs_7_ = bf16[64,1024]{1,0:T(8,128)(2,1)S(1)} collective-permute-done((bf16[64,1024]{1,0:T(8,128)(2,1)}, bf16[64,1024]{1,0:T(8,128)(2,1)S(1)}, u32[]{:S(2)}, u32[]{:S(2)}) %collective-permute-start.6) | collective-permute-done | bytes 131104 | tf_op jit(solution)/shard_map/ppermute | solution.py:238
  33.6 0.5 collective-permute-start.13
  34.1 0.7 collective-permute-done.9.refs_0_
  34.8 3.2 %collective-permute-start.14 = (bf16[64,1024]{1,0:T(8,128)(2,1)}, bf16[64,1024]{1,0:T(8,128)(2,1)S(1)}, u32[]{:S(2)}, u32[]{:S(2)}) collective-permute-start(bf16[64,1024]{1,0:T(8,128)(2,1)} %get-tuple-element.53), channel_id=1, source_target_pairs={{0,18},{2,16},{4,22},{6,20},{8,26},{10,24},{12,30},{14,28},{16,2},... | collective-permute-start | bytes 393224 | tf_op jit(solution)/shard_map/ppermute | solution.py:238
  37.9 4.9 %collective-permute-done.10.refs_1_ = bf16[64,1024]{1,0:T(8,128)(2,1)S(1)} collective-permute-done((bf16[64,1024]{1,0:T(8,128)(2,1)}, bf16[64,1024]{1,0:T(8,128)(2,1)S(1)}, u32[]{:S(2)}, u32[]{:S(2)}) %collective-permute-start.10) | collective-permute-done | bytes 131104 | tf_op jit(solution)/shard_map/ppermute | solution.py:238
  42.9 0.3 collective-permute-start.15
  43.2 4.3 %collective-permute-start.16 = (bf16[64,1024]{1,0:T(8,128)(2,1)}, bf16[64,1024]{1,0:T(8,128)(2,1)S(1)}, u32[]{:S(2)}, u32[]{:S(2)}) collective-permute-start(bf16[64,1024]{1,0:T(8,128)(2,1)} %get-tuple-element.55), channel_id=1, source_target_pairs={{0,16},{2,18},{4,20},{6,22},{8,24},{10,26},{12,28},{14,30},{16,0},... | collective-permute-start | bytes 393224 | tf_op jit(solution)/shard_map/ppermute | solution.py:238
  47.5 0.9 copy-done.3
  48.4 0.1 collect.2.own_ref
  48.5 0.1 collective-permute-start.7
  48.6 2.7 %collective-permute-done.14.refs_5_ = bf16[64,1024]{1,0:T(8,128)(2,1)S(1)} collective-permute-done((bf16[64,1024]{1,0:T(8,128)(2,1)}, bf16[64,1024]{1,0:T(8,128)(2,1)S(1)}, u32[]{:S(2)}, u32[]{:S(2)}) %collective-permute-start.14) | collective-permute-done | bytes 131104 | tf_op jit(solution)/shard_map/ppermute | solution.py:238
  51.3 2.0 %collective-permute-done.16.refs_7_ = bf16[64,1024]{1,0:T(8,128)(2,1)S(1)} collective-permute-done((bf16[64,1024]{1,0:T(8,128)(2,1)}, bf16[64,1024]{1,0:T(8,128)(2,1)S(1)}, u32[]{:S(2)}, u32[]{:S(2)}) %collective-permute-start.16) | collective-permute-done | bytes 131104 | tf_op jit(solution)/shard_map/ppermute | solution.py:238
  53.3 0.1 collect.3.own_ref
  53.4 0.1 collective-permute-start.17
  53.5 3.9 %front.2 = (bf16[256,2048]{1,0:T(8,128)(2,1)S(1)}, bf16[256,2048]{1,0:T(8,128)(2,1)S(1)}, bf16[704,256]{1,0:T(8,128)(2,1)S(1)}, bf16[704,256]{1,0:T(8,128)(2,1)S...) custom-call(bf16[512,1024]{1,0:T(8,128)(2,1)S(1)} %collect.2.own_ref, ...), custom_call_target="tpu_custom_call" | custom-call | flops 2952790016 | bytes 15728640 | tf_op jit(solution)/shard_map/front/pallas_call | solution.py:256
  57.4 0.7 copy-done.8
  58.1 0.5 collective-permute-start.8
  58.6 3.8 %front.3 = (bf16[256,2048]{1,0:T(8,128)(2,1)S(1)}, bf16[256,2048]{1,0:T(8,128)(2,1)S(1)}, bf16[704,256]{1,0:T(8,128)(2,1)S(1)}, bf16[704,256]{1,0:T(8,128)(2,1)S...) custom-call(bf16[512,1024]{1,0:T(8,128)(2,1)S(1)} %collect.3.own_ref, ...), custom_call_target="tpu_custom_call" | custom-call | flops 2952790016 | bytes 15728640 | tf_op jit(solution)/shard_map/front/pallas_call | solution.py:256
  62.4 1.0 copy-done.4
  63.4 0.0 collective-permute-start.18
  63.4 1.0 kept.2.refs_0_
  64.4 0.0 copy-done.10
  64.5 1.0 kept.3.refs_2_
  65.5 1.2 %total.1 = (bf16[512,1024]{1,0:T(8,128)(2,1)}, f32[8,128]{1,0:T(8,128)S(1)}) custom-call(f32[256,1024]{1,0:T(8,128)S(1)} %kept.2.refs_0_, bf16[256,1024]{1,0:T(8,128)(2,1)S(1)} %collective-permute-done.8.refs_1_, f32[256,1024]{1,0:T(8,128)S(1)} %kept.3.refs_2_, bf16[256,1024]{1,0:T(8,128)(2,1)S(1)} %collective-permute-done.18.refs_3_), custom_call_target="tpu_custom_call" | custom-call | tf_op jit(solution)/shard_map/total/pallas_call | solution.py:286
  66.7 6.3 %all-to-all-start = ((bf16[16,32,1024]{2,1,0:T(8,128)(2,1)}), bf16[16,32,1024]{2,1,0:T(8,128)(2,1)}, u32[]{:S(2)}, u32[]{:S(2)}) async-start(bf16[16,32,1024]{2,1,0:T(8,128)(2,1)} %bitcast.4), calls=%async_computation | async-start | bytes 2097152 | tf_op jit(solution)/shard_map/all_to_all | solution.py:198
  73.0 1.2 %copy-done.5 = bf16[256,2048]{1,0:T(8,128)(2,1)S(1)} copy-done((bf16[256,2048]{1,0:T(8,128)(2,1)S(1)}, bf16[256,2048]{1,0:T(8,128)(2,1)}, u32[]{:S(2)}) %copy-start.5) | copy-done | bytes 1048600
  74.2 1.2 %copy-done.7 = bf16[256,2048]{1,0:T(8,128)(2,1)S(1)} copy-done((bf16[256,2048]{1,0:T(8,128)(2,1)S(1)}, bf16[256,2048]{1,0:T(8,128)(2,1)}, u32[]{:S(2)}) %copy-start.7) | copy-done | bytes 1048600
  75.5 1.0 copy-done.9
  76.4 1.0 copy-done.11
  77.4 6.8 %grads.1 = (bf16[704,2048]{1,0:T(8,128)(2,1)}, bf16[704,2048]{1,0:T(8,128)(2,1)}, bf16[704,2048]{1,0:T(8,128)(2,1)}) custom-call(bf16[704,256]{1,0:T(8,128)(2,1)S(1)} %get-tuple-element.45.d_gate_ref.refs_0_, bf16[704,256]{1,0:T(8,128)(2,1)S(1)} %get-tuple-element.56.d_gate_ref.refs_1_, bf16[704,256]{1,0:T(8,128)(2,1)S(1)} %get-tuple-element.46.d_up_ref.refs_2_, ...), custom_call_target="tpu_custom_call" | custom-call | flops 4429185024 | bytes 23592960 | tf_op jit(solution)/shard_map/grads/pallas_call | solution.py:301
  84.2 15.6 %all-to-all-done = bf16[16,32,1024]{2,1,0:T(8,128)(2,1)} async-done(((bf16[16,32,1024]{2,1,0:T(8,128)(2,1)}), bf16[16,32,1024]{2,1,0:T(8,128)(2,1)}, u32[]{:S(2)}, u32[]{:S(2)}) %all-to-all-start) | async-done | bytes 1048608 | tf_op jit(solution)/shard_map/all_to_all | solution.py:198
  99.8 3.3 %combine.1 = bf16[256,1024]{1,0:T(8,128)(2,1)} custom-call(s32[1,256]{1,0:T(1,128)} %bitcast.20, bf16[512,1024]{1,0:T(8,128)(2,1)} %bitcast.5.back_hbm), custom_call_target="tpu_custom_call" | custom-call | tf_op jit(solution)/shard_map/combine/pallas_call | solution.py:186
  (26 shorter events, 0.1 us)
Async XLA Ops:
  4.6 11.3 %collective-permute-start = (bf16[64,1024]{1,0:T(8,128)(2,1)}, bf16[64,1024]{1,0:T(8,128)(2,1)S(1)}, u32[]{:S(2)}, u32[]{:S(2)}) collective-permute-start(bf16[64,1024]{1,0:T(8,128)(2,1)} %get-tuple-element.38), channel_id=1, source_target_pairs={{0,30},{2,28},{4,26},{6,24},{8,22},{10,20},{12,18},{14,16},{16,14}... | collective-permute-start | bytes 393224 | tf_op jit(solution)/shard_map/ppermute | solution.py:238
  8.1 10.3 %collective-permute-start.1 = (bf16[64,1024]{1,0:T(8,128)(2,1)}, bf16[64,1024]{1,0:T(8,128)(2,1)S(1)}, u32[]{:S(2)}, u32[]{:S(2)}) collective-permute-start(bf16[64,1024]{1,0:T(8,128)(2,1)} %get-tuple-element.39), channel_id=1, source_target_pairs={{0,14},{2,12},{4,10},{6,8},{8,6},{10,4},{12,2},{14,0},{16,30},{18,... | collective-permute-start | bytes 393224 | tf_op jit(solution)/shard_map/ppermute | solution.py:238
  10.5 11.9 %collective-permute-start.2 = (bf16[64,1024]{1,0:T(8,128)(2,1)}, bf16[64,1024]{1,0:T(8,128)(2,1)S(1)}, u32[]{:S(2)}, u32[]{:S(2)}) collective-permute-start(bf16[64,1024]{1,0:T(8,128)(2,1)} %get-tuple-element.40), channel_id=1, source_target_pairs={{0,28},{2,30},{4,24},{6,26},{8,20},{10,22},{12,16},{14,18},{16,12}... | collective-permute-start | bytes 393224 | tf_op jit(solution)/shard_map/ppermute | solution.py:238
  10.8 12.7 %collective-permute-start.3 = (bf16[64,1024]{1,0:T(8,128)(2,1)}, bf16[64,1024]{1,0:T(8,128)(2,1)S(1)}, u32[]{:S(2)}, u32[]{:S(2)}) collective-permute-start(bf16[64,1024]{1,0:T(8,128)(2,1)} %get-tuple-element.41), channel_id=1, source_target_pairs={{0,12},{2,14},{4,8},{6,10},{8,4},{10,6},{12,0},{14,2},{16,28},{18,... | collective-permute-start | bytes 393224 | tf_op jit(solution)/shard_map/ppermute | solution.py:238
  12.3 14.9 %collective-permute-start.4 = (bf16[64,1024]{1,0:T(8,128)(2,1)}, bf16[64,1024]{1,0:T(8,128)(2,1)S(1)}, u32[]{:S(2)}, u32[]{:S(2)}) collective-permute-start(bf16[64,1024]{1,0:T(8,128)(2,1)} %get-tuple-element.42), channel_id=1, source_target_pairs={{0,26},{2,24},{4,30},{6,28},{8,18},{10,16},{12,22},{14,20},{16,10}... | collective-permute-start | bytes 393224 | tf_op jit(solution)/shard_map/ppermute | solution.py:238
  15.9 15.3 %collective-permute-start.5 = (bf16[64,1024]{1,0:T(8,128)(2,1)}, bf16[64,1024]{1,0:T(8,128)(2,1)S(1)}, u32[]{:S(2)}, u32[]{:S(2)}) collective-permute-start(bf16[64,1024]{1,0:T(8,128)(2,1)} %get-tuple-element.43), channel_id=1, source_target_pairs={{0,10},{2,8},{4,14},{6,12},{8,2},{10,0},{12,6},{14,4},{16,26},{18,... | collective-permute-start | bytes 393224 | tf_op jit(solution)/shard_map/ppermute | solution.py:238
  18.4 15.2 %collective-permute-start.6 = (bf16[64,1024]{1,0:T(8,128)(2,1)}, bf16[64,1024]{1,0:T(8,128)(2,1)S(1)}, u32[]{:S(2)}, u32[]{:S(2)}) collective-permute-start(bf16[64,1024]{1,0:T(8,128)(2,1)} %get-tuple-element.44), channel_id=1, source_target_pairs={{0,24},{2,26},{4,28},{6,30},{8,16},{10,18},{12,20},{14,22},{16,8},... | collective-permute-start | bytes 393224 | tf_op jit(solution)/shard_map/ppermute | solution.py:238
  22.3 12.4 %collective-permute-start.9 = (bf16[64,1024]{1,0:T(8,128)(2,1)}, bf16[64,1024]{1,0:T(8,128)(2,1)S(1)}, u32[]{:S(2)}, u32[]{:S(2)}) collective-permute-start(bf16[64,1024]{1,0:T(8,128)(2,1)} %get-tuple-element.48), channel_id=1, source_target_pairs={{0,8},{2,10},{4,12},{6,14},{8,0},{10,2},{12,4},{14,6},{16,24},{18,... | collective-permute-start | bytes 393224 | tf_op jit(solution)/shard_map/ppermute | solution.py:238
  23.5 19.4 %collective-permute-start.10 = (bf16[64,1024]{1,0:T(8,128)(2,1)}, bf16[64,1024]{1,0:T(8,128)(2,1)S(1)}, u32[]{:S(2)}, u32[]{:S(2)}) collective-permute-start(bf16[64,1024]{1,0:T(8,128)(2,1)} %get-tuple-element.49), channel_id=1, source_target_pairs={{0,22},{2,20},{4,18},{6,16},{8,30},{10,28},{12,26},{14,24},{16,6},... | collective-permute-start | bytes 393224 | tf_op jit(solution)/shard_map/ppermute | solution.py:238
  27.2 16.0 %collective-permute-start.11 = (bf16[64,1024]{1,0:T(8,128)(2,1)}, bf16[64,1024]{1,0:T(8,128)(2,1)S(1)}, u32[]{:S(2)}, u32[]{:S(2)}) collective-permute-start(bf16[64,1024]{1,0:T(8,128)(2,1)} %get-tuple-element.50), channel_id=1, source_target_pairs={{0,6},{2,4},{4,2},{6,0},{8,14},{10,12},{12,10},{14,8},{16,22},{18,... | collective-permute-start | bytes 393224 | tf_op jit(solution)/shard_map/ppermute | solution.py:238
  31.2 17.3 %collective-permute-start.12 = (bf16[64,1024]{1,0:T(8,128)(2,1)}, bf16[64,1024]{1,0:T(8,128)(2,1)S(1)}, u32[]{:S(2)}, u32[]{:S(2)}) collective-permute-start(bf16[64,1024]{1,0:T(8,128)(2,1)} %get-tuple-element.51), channel_id=1, source_target_pairs={{0,20},{2,22},{4,16},{6,18},{8,28},{10,30},{12,24},{14,26},{16,4},... | collective-permute-start | bytes 393224 | tf_op jit(solution)/shard_map/ppermute | solution.py:238
  33.6 14.9 %collective-permute-start.13 = (bf16[64,1024]{1,0:T(8,128)(2,1)}, bf16[64,1024]{1,0:T(8,128)(2,1)S(1)}, u32[]{:S(2)}, u32[]{:S(2)}) collective-permute-start(bf16[64,1024]{1,0:T(8,128)(2,1)} %get-tuple-element.52), channel_id=1, source_target_pairs={{0,4},{2,6},{4,0},{6,2},{8,12},{10,14},{12,8},{14,10},{16,20},{18,... | collective-permute-start | bytes 393224 | tf_op jit(solution)/shard_map/ppermute | solution.py:238
  34.8 16.5 %collective-permute-start.14 = (bf16[64,1024]{1,0:T(8,128)(2,1)}, bf16[64,1024]{1,0:T(8,128)(2,1)S(1)}, u32[]{:S(2)}, u32[]{:S(2)}) collective-permute-start(bf16[64,1024]{1,0:T(8,128)(2,1)} %get-tuple-element.53), channel_id=1, source_target_pairs={{0,18},{2,16},{4,22},{6,20},{8,26},{10,24},{12,30},{14,28},{16,2},... | collective-permute-start | bytes 393224 | tf_op jit(solution)/shard_map/ppermute | solution.py:238
  42.9 8.4 %collective-permute-start.15 = (bf16[64,1024]{1,0:T(8,128)(2,1)}, bf16[64,1024]{1,0:T(8,128)(2,1)S(1)}, u32[]{:S(2)}, u32[]{:S(2)}) collective-permute-start(bf16[64,1024]{1,0:T(8,128)(2,1)} %get-tuple-element.54), channel_id=1, source_target_pairs={{0,2},{2,0},{4,6},{6,4},{8,10},{10,8},{12,14},{14,12},{16,18},{18,... | collective-permute-start | bytes 393224 | tf_op jit(solution)/shard_map/ppermute | solution.py:238
  43.2 10.1 %collective-permute-start.16 = (bf16[64,1024]{1,0:T(8,128)(2,1)}, bf16[64,1024]{1,0:T(8,128)(2,1)S(1)}, u32[]{:S(2)}, u32[]{:S(2)}) collective-permute-start(bf16[64,1024]{1,0:T(8,128)(2,1)} %get-tuple-element.55), channel_id=1, source_target_pairs={{0,16},{2,18},{4,20},{6,22},{8,24},{10,26},{12,28},{14,30},{16,0},... | collective-permute-start | bytes 393224 | tf_op jit(solution)/shard_map/ppermute | solution.py:238
  47.5 0.9 copy-start.3
  48.4 5.0 %copy-start = (bf16[1,704,2048]{2,1,0:T(8,128)(2,1)S(1)}, bf16[1,704,2048]{2,1,0:T(8,128)(2,1)}, u32[]{:S(2)}) copy-start(bf16[1,704,2048]{2,1,0:T(8,128)(2,1)} %param.9) | copy-start | bytes 8650756
  48.5 5.0 %copy-start.1 = (bf16[1,704,2048]{2,1,0:T(8,128)(2,1)S(1)}, bf16[1,704,2048]{2,1,0:T(8,128)(2,1)}, u32[]{:S(2)}) copy-start(bf16[1,704,2048]{2,1,0:T(8,128)(2,1)} %param.10) | copy-start | bytes 8650756
  48.5 5.0 %copy-start.2 = (bf16[1,704,2048]{2,1,0:T(8,128)(2,1)S(1)}, bf16[1,704,2048]{2,1,0:T(8,128)(2,1)}, u32[]{:S(2)}) copy-start(bf16[1,704,2048]{2,1,0:T(8,128)(2,1)} %param.11) | copy-start | bytes 8650756
  48.5 4.9 %collective-permute-start.7 = (bf16[512,1024]{1,0:T(8,128)(2,1)S(1)}, bf16[512,1024]{1,0:T(8,128)(2,1)S(1)}, u32[]{:S(2)}, u32[]{:S(2)}) collective-permute-start(bf16[512,1024]{1,0:T(8,128)(2,1)S(1)} %collect.2.own_ref), channel_id=1, source_target_pairs={{0,1},{1,0},{2,3},{3,2},{4,5},{5,4},{6,7},{7,6},{8,9},{9,8},{10,11... | collective-permute-start | bytes 3145736 | tf_op jit(solution)/shard_map/ppermute | solution.py:241
  53.4 5.2 %collective-permute-start.17 = (bf16[512,1024]{1,0:T(8,128)(2,1)S(1)}, bf16[512,1024]{1,0:T(8,128)(2,1)S(1)}, u32[]{:S(2)}, u32[]{:S(2)}) collective-permute-start(bf16[512,1024]{1,0:T(8,128)(2,1)S(1)} %collect.3.own_ref), channel_id=1, source_target_pairs={{0,1},{1,0},{2,3},{3,2},{4,5},{5,4},{6,7},{7,6},{8,9},{9,8},{10,11... | collective-permute-start | bytes 3145736 | tf_op jit(solution)/shard_map/ppermute | solution.py:241
  57.3 0.7 copy-start.8
  58.1 7.4 %collective-permute-start.8 = (bf16[256,1024]{1,0:T(8,128)(2,1)S(1)}, bf16[256,1024]{1,0:T(8,128)(2,1)S(1)}, u32[]{:S(2)}, u32[]{:S(2)}) collective-permute-start(bf16[256,1024]{1,0:T(8,128)(2,1)S(1)} %get-tuple-element.47), channel_id=1, source_target_pairs={{0,1},{1,0},{2,3},{3,2},{4,5},{5,4},{6,7},{7,6},{8,9},{9,8},{10,11... | collective-permute-start | bytes 1572872 | tf_op jit(solution)/shard_map/ppermute | solution.py:241
  62.4 1.0 copy-start.4
  63.4 1.0 copy-start.6
  63.4 1.1 %copy-start.10 = (bf16[704,256]{1,0:T(8,128)(2,1)}, bf16[704,256]{1,0:T(8,128)(2,1)S(1)}, u32[]{:S(2)}) copy-start(bf16[704,256]{1,0:T(8,128)(2,1)S(1)} %get-tuple-element.61.refs_5_) | copy-start | bytes 1081348
  63.4 2.1 %collective-permute-start.18 = (bf16[256,1024]{1,0:T(8,128)(2,1)S(1)}, bf16[256,1024]{1,0:T(8,128)(2,1)S(1)}, u32[]{:S(2)}, u32[]{:S(2)}) collective-permute-start(bf16[256,1024]{1,0:T(8,128)(2,1)S(1)} %get-tuple-element.58), channel_id=1, source_target_pairs={{0,1},{1,0},{2,3},{3,2},{4,5},{5,4},{6,7},{7,6},{8,9},{9,8},{10,11... | collective-permute-start | bytes 1572872 | tf_op jit(solution)/shard_map/ppermute | solution.py:241
  66.7 33.2 %all-to-all-start = ((bf16[16,32,1024]{2,1,0:T(8,128)(2,1)}), bf16[16,32,1024]{2,1,0:T(8,128)(2,1)}, u32[]{:S(2)}, u32[]{:S(2)}) async-start(bf16[16,32,1024]{2,1,0:T(8,128)(2,1)} %bitcast.4), calls=%async_computation | async-start | bytes 2097152 | tf_op jit(solution)/shard_map/all_to_all | solution.py:198
  73.0 1.2 %copy-start.5 = (bf16[256,2048]{1,0:T(8,128)(2,1)S(1)}, bf16[256,2048]{1,0:T(8,128)(2,1)}, u32[]{:S(2)}) copy-start(bf16[256,2048]{1,0:T(8,128)(2,1)} %copy-done.4) | copy-start | bytes 3145732
  74.2 1.2 %copy-start.7 = (bf16[256,2048]{1,0:T(8,128)(2,1)S(1)}, bf16[256,2048]{1,0:T(8,128)(2,1)}, u32[]{:S(2)}) copy-start(bf16[256,2048]{1,0:T(8,128)(2,1)} %copy-done.6) | copy-start | bytes 3145732
  75.5 1.0 copy-start.9
  76.4 1.0 copy-start.11

commit v6 on v5

--- a/solution.py
+++ b/solution.py
@@ -56,8 +56,8 @@
             slab[i * capacity : (i + 1) * capacity, :] = placed[k * capacity : (k + 1) * capacity]
 
 
-def collect_kernel(capacity, *refs):
-    *slabs, out_ref = refs
+def collect_kernel(capacity, count, *refs):
+    slabs, out_ref = refs[:count], refs[-1]
     half = len(slabs) * capacity
     for i, slab in enumerate(slabs):
         out_ref[i * capacity : (i + 1) * capacity, :] = slab[:capacity, :]
@@ -77,27 +77,31 @@
     )
 
 
-def front_kernel(tile, own_ref, other_ref, gate_ref, up_ref, down_ref, *refs):
-    x_ref, dy_ref, hidden_ref, d_gate_ref, d_up_ref, sent_ref = refs
-    rows, width = x_ref.shape[0], own_ref.shape[1]
+def front_kernel(
+    tile, own_ref, other_ref, gate_ref, up_ref, down_ref, hidden_ref, d_gate_ref, d_up_ref, sent_ref
+):
+    rows, width = sent_ref.shape
     mine = lax.axis_index("tensor")
-    for half, whole_ref in enumerate((x_ref, dy_ref)):
-        whole_ref[:, side(mine, width)] = own_ref[half * rows : (half + 1) * rows, :]
-        whole_ref[:, side(1 - mine, width)] = other_ref[half * rows : (half + 1) * rows, :]
     over_features = (((1,), (1,)), ((), ()))
 
     @pl.loop(0, hidden_ref.shape[0] // tile)
     def _(step):
         units = pl.ds(pl.multiple_of(step * tile, tile), tile)
 
-        def product(weight_ref, whole_ref):
-            return lax.dot_general(
-                weight_ref[units, :], whole_ref[...], over_features, preferred_element_type=F32
+        def product(weight_ref, start):
+            return sum(
+                lax.dot_general(
+                    weight_ref[units, side(which, width)],
+                    half_ref[start : start + rows, :],
+                    over_features,
+                    preferred_element_type=F32,
+                )
+                for which, half_ref in ((mine, own_ref), (1 - mine, other_ref))
             )
 
-        gate_pre = product(gate_ref, x_ref)
-        up_pre = product(up_ref, x_ref)
-        d_hidden = product(down_ref, dy_ref)
+        gate_pre = product(gate_ref, 0)
+        up_pre = product(up_ref, 0)
+        d_hidden = product(down_ref, rows)
         sig = jax.nn.sigmoid(gate_pre)
         silu = gate_pre * sig
         hidden_ref[units, :] = (silu * up_pre).astype(BF16)
@@ -127,19 +131,26 @@
             out_ref[there, :] = (kept_ref[here, :] + got_ref[here, :].astype(F32)).astype(BF16)
 
 
-def grads_kernel(groups, *refs):
+def grads_kernel(sizes, *refs):
     *ins, _, grad_gate_ref, grad_up_ref, grad_down_ref = refs
-    by_group = [ins[i :: groups] for i in range(groups)]
-
-    def total(left, right):
+    mine = lax.axis_index("tensor")
+    groups = [(*ins[5 * i : 5 * i + 5], rows) for i, rows in enumerate(sizes)]
+    width = groups[0][0].shape[1]
+
+    def total(left, half, second):
         return sum(
-            jnp.dot(one[left][...], one[right][...], preferred_element_type=F32)
-            for one in by_group
+            jnp.dot(
+                one[left][...],
+                one[half][one[5] * second : one[5] * (second + 1), :],
+                preferred_element_type=F32,
+            )
+            for one in groups
         ).astype(BF16)
 
-    grad_gate_ref[...] = total(0, 3)
-    grad_up_ref[...] = total(1, 3)
-    grad_down_ref[...] = total(2, 4)
+    for half, which in enumerate((mine, 1 - mine)):
+        grad_gate_ref[:, side(which, width)] = total(2, half, 0)
+        grad_up_ref[:, side(which, width)] = total(3, half, 0)
+        grad_down_ref[:, side(which, width)] = total(4, half, 1)
 
 
 def combine_kernel(capacity, row_ref, back_hbm, out_ref, back_ref, sems):
@@ -215,8 +226,8 @@
     far = [k for k in reversed(range(1, experts)) if k >= experts // 2]
     near = [k for k in reversed(range(1, experts)) if k < experts // 2]
     turns = [k for pair in zip(far, near) for k in pair] + far[len(near) :]
-    first, second = [0] + turns[: experts // 2 - 1], turns[experts // 2 - 1 :]
-    rows = len(first) * capacity
+    cut = 3 * experts // 4
+    first, second = turns[:cut], turns[cut:] + [0]
 
     slabs = list(
         pl.pallas_call(
@@ -240,33 +251,31 @@
     def exchange(values):
         return lax.ppermute(values, "tensor", [(0, 1), (1, 0)])
 
-    def collect(arrived):
+    def collect(arrived, after):
         return pl.pallas_call(
-            functools.partial(collect_kernel, capacity),
-            out_shape=jax.ShapeDtypeStruct((2 * rows, width), BF16),
-            in_specs=[IN_VMEM] * len(arrived),
+            functools.partial(collect_kernel, capacity, len(arrived)),
+            out_shape=jax.ShapeDtypeStruct((2 * len(arrived) * capacity, width), BF16),
+            in_specs=[IN_VMEM] * (len(arrived) + len(after)),
             out_specs=IN_VMEM,
             compiler_params=params(SMALL),
-            cost_estimate=cost(COLLECT, rows, units, features),
+            cost_estimate=cost(COLLECT, len(arrived) * capacity, units, features),
             name="collect",
-        )(*arrived)
+        )(*arrived, *after)
 
     def front(own):
         other = exchange(own)
-        return pl.pallas_call(
+        rows = own.shape[0] // 2
+        hidden, d_gate, d_up, sent = pl.pallas_call(
             functools.partial(front_kernel, tile),
-            out_shape=[jax.ShapeDtypeStruct((rows, features), BF16)] * 2
-            + [jax.ShapeDtypeStruct((units, rows), BF16)] * 3
+            out_shape=[jax.ShapeDtypeStruct((units, rows), BF16)] * 3
             + [jax.ShapeDtypeStruct((rows, width), BF16)],
             in_specs=[IN_VMEM] * 5,
-            out_specs=[IN_VMEM] * 6,
+            out_specs=[IN_VMEM] * 4,
             compiler_params=params(SMALL),
             cost_estimate=cost(4, rows, units, features),
             name="front",
         )(own, other, gate_rows, up_rows, down_rows)
-
-    def kept_rows(d_gate, d_up):
-        return pl.pallas_call(
+        kept = pl.pallas_call(
             kept_kernel,
             out_shape=jax.ShapeDtypeStruct((rows, width), F32),
             in_specs=[IN_VMEM] * 4,
@@ -275,14 +284,12 @@
             cost_estimate=cost(1, rows, units, features),
             name="kept",
         )(d_gate, d_up, gate_rows, up_rows)
+        return (own, other, d_gate, d_up, hidden), (kept, exchange(sent))
 
     got = {k: swap(k) for k in turns}
     got[0] = slabs[0]
-    front_a = front(collect([got[k] for k in first]))
-    front_b = front(collect([got[k] for k in second]))
-    sums = []
-    for _, _, _, d_gate, d_up, sent in (front_a, front_b):
-        sums += [kept_rows(d_gate, d_up), exchange(sent)]
+    for_grads_a, sums_a = front(collect([got[k] for k in first], []))
+    for_grads_b, sums_b = front(collect([got[k] for k in second], sums_a[:1]))
     totals, done = pl.pallas_call(
         functools.partial(total_kernel, capacity, (first, second)),
         out_shape=[
@@ -293,23 +300,27 @@
         out_specs=[IN_VMEM] * 2,
         compiler_params=params(SMALL),
         name="total",
-    )(*sums)
+    )(*sums_a, *sums_b)
     returned = to_experts(totals, experts)
 
-    lefts = [front_a[3], front_b[3], front_a[4], front_b[4], front_a[2], front_b[2]]
-    rights = [front_a[0], front_b[0], front_a[1], front_b[1]]
+    def grads_specs(rows):
+        return [pl.BlockSpec((2 * rows, width), lambda i: (0, 0))] * 2 + [
+            pl.BlockSpec((tile, rows), lambda i: (i, 0))
+        ] * 3
+
+    sizes = [len(group) * capacity for group in (first, second)]
     grads = pl.pallas_call(
-        functools.partial(grads_kernel, 2),
+        functools.partial(grads_kernel, sizes),
         grid=(units // tile,),
         out_shape=[jax.ShapeDtypeStruct((units, features), BF16)] * 3,
-        in_specs=[pl.BlockSpec((tile, rows), lambda i: (i, 0))] * 6
-        + [pl.BlockSpec((rows, features), lambda i: (0, 0))] * 4
+        in_specs=grads_specs(sizes[0])
+        + grads_specs(sizes[1])
         + [pl.BlockSpec((8, 128), lambda i: (0, 0))],
         out_specs=[pl.BlockSpec((tile, features), lambda i: (i, 0))] * 3,
         compiler_params=params(32 * 2**20),
-        cost_estimate=cost(6, rows, units, features),
+        cost_estimate=cost(3, sum(sizes), units, features),
         name="grads",
-    )(*lefts, *rights, done)
+    )(*for_grads_a, *for_grads_b, done)
     return combine(capacity, ids_row, returned, tok_rows), grads
 
 

time: 104 us -> 102 us (0.981)
  local copies, waits for them, and re-layouts: 7.08 us -> 2.85 us
  Pallas kernels: 25 us -> 29 us
  starting transfers between devices: 35.4 us -> 33.9 us
    unnamed x24 -> x22, local copies, waits for them, and re-layouts: 7.08 us -> 2.85 us
    ppermute x15, starting transfers between devices: 28.4 us -> 25.1 us  [swap(): lax.ppermute(slabs[k], 'expert', [(e, e ^ k) for e in range(experts)])]
    ppermute x4, waiting for transfers between devices: 0.01 us -> 2.19 us  [exchange(): return lax.ppermute(values, 'tensor', [(0, 1), (1, 0)])]
    pallas_call x5, Pallas kernels: 8.91 us -> 11.1 us  [the longest x1 8.92 us: grouped(): pl.pallas_call(functools.partial(grads_kernel, sizes), grid=(units // til...]
    pallas_call x2, Pallas kernels: 7.7 us -> 9.51 us  [front(): pl.pallas_call(functools.partial(front_kernel, tile), out_shape=[jax.Shap...]
    all_to_all x1, starting transfers between devices: 6.33 us -> 7.9 us  [to_experts(): lax.all_to_all(rows.reshape(experts, rows.shape[0] // experts, rows.shape...]
    all_to_all x1, waiting for transfers between devices: 15.6 us -> 14.1 us  [to_experts(): lax.all_to_all(rows.reshape(experts, rows.shape[0] // experts, rows.shape...]
  transfers between devices with their start and end apart: 20 -> 20, of which waited for: 11 -> 14; matrix products, arithmetic and copies ran while one was open for 0% -> 0% of each run, Pallas kernels for 16% -> 20%
where the time goes in v6:
time: 102 us; the launch traced here: 101 us
  waiting for transfers between devices  34.9 us (34%)
  starting transfers between devices  33.9 us (33%)
  Pallas kernels  29 us (28%)
  local copies, waits for them, and re-layouts  2.85 us (3%)
    ppermute x15, starting transfers between devices, swap(): lax.ppermute(slabs[k], 'expert', [(e, e ^ k) for e in range(experts)])  25.1 us
    ppermute x15, waiting for transfers between devices, swap(): lax.ppermute(slabs[k], 'expert', [(e, e ^ k) for e in range(experts)])  18.6 us
    all_to_all x1, waiting for transfers between devices, to_experts(): lax.all_to_all(rows.reshape(experts, rows.shape[0] // experts, rows.shape...  14.1 us
    pallas_call x2, Pallas kernels, front(): pl.pallas_call(functools.partial(front_kernel, tile), out_shape=[jax.Shap...  9.51 us
    pallas_call x1, Pallas kernels, grouped(): pl.pallas_call(functools.partial(grads_kernel, sizes), grid=(units // til...  8.92 us
    all_to_all x1, starting transfers between devices, to_experts(): lax.all_to_all(rows.reshape(experts, rows.shape[0] // experts, rows.shape...  7.9 us
    pallas_call x1, Pallas kernels, grouped(): pl.pallas_call(functools.partial(place_kernel, capacity), out_shape=[jax....  3.93 us
    pallas_call x1, Pallas kernels, combine(): pl.pallas_call(functools.partial(combine_kernel, capacity), out_shape=jax...  3.28 us
  transfers between devices with their start and end apart: 20, of which 14 were waited for; matrix products, arithmetic and copies ran while one was open for 0% of the time, Pallas kernels for 20%

profile of v6, /device:TPU:8, one launch (start us, length us, event | category | flops | bytes accessed | tf_op | source)
XLA Modules:
  0.0 101.5 jit_solution(12138912607036437411)
XLA Ops:
  0.6 3.9 %place.1 = (bf16[64,1024]{1,0:T(8,128)(2,1)}, bf16[64,1024]{1,0:T(8,128)(2,1)}, bf16[64,1024]{1,0:T(8,128)(2,1)}, bf16[64,1024]{1,0:T(8,128)(2,1)}, bf16[64,1024...) custom-call(s32[1,256]{1,0:T(1,128)} %bitcast.19, ...), custom_call_target="tpu_custom_call" | custom-call | tf_op jit(solution)/shard_map/place/pallas_call | solution.py:233
  4.6 3.5 %collective-permute-start = (bf16[64,1024]{1,0:T(8,128)(2,1)}, bf16[64,1024]{1,0:T(8,128)(2,1)S(1)}, u32[]{:S(2)}, u32[]{:S(2)}) collective-permute-start(bf16[64,1024]{1,0:T(8,128)(2,1)} %get-tuple-element.33), channel_id=1, source_target_pairs={{0,30},{2,28},{4,26},{6,24},{8,22},{10,20},{12,18},{14,16},{16,14}... | collective-permute-start | bytes 393224 | tf_op jit(solution)/shard_map/ppermute | solution.py:249
  8.1 2.4 %collective-permute-start.1 = (bf16[64,1024]{1,0:T(8,128)(2,1)}, bf16[64,1024]{1,0:T(8,128)(2,1)S(1)}, u32[]{:S(2)}, u32[]{:S(2)}) collective-permute-start(bf16[64,1024]{1,0:T(8,128)(2,1)} %get-tuple-element.34), channel_id=1, source_target_pairs={{0,14},{2,12},{4,10},{6,8},{8,6},{10,4},{12,2},{14,0},{16,30},{18,... | collective-permute-start | bytes 393224 | tf_op jit(solution)/shard_map/ppermute | solution.py:249
  10.5 0.3 collective-permute-start.2
  10.8 1.5 %collective-permute-start.3 = (bf16[64,1024]{1,0:T(8,128)(2,1)}, bf16[64,1024]{1,0:T(8,128)(2,1)S(1)}, u32[]{:S(2)}, u32[]{:S(2)}) collective-permute-start(bf16[64,1024]{1,0:T(8,128)(2,1)} %get-tuple-element.36), channel_id=1, source_target_pairs={{0,12},{2,14},{4,8},{6,10},{8,4},{10,6},{12,0},{14,2},{16,28},{18,... | collective-permute-start | bytes 393224 | tf_op jit(solution)/shard_map/ppermute | solution.py:249
  12.3 2.5 %collective-permute-start.4 = (bf16[64,1024]{1,0:T(8,128)(2,1)}, bf16[64,1024]{1,0:T(8,128)(2,1)S(1)}, u32[]{:S(2)}, u32[]{:S(2)}) collective-permute-start(bf16[64,1024]{1,0:T(8,128)(2,1)} %get-tuple-element.37), channel_id=1, source_target_pairs={{0,26},{2,24},{4,30},{6,28},{8,18},{10,16},{12,22},{14,20},{16,10}... | collective-permute-start | bytes 393224 | tf_op jit(solution)/shard_map/ppermute | solution.py:249
  14.8 1.1 %collective-permute-done.refs_0_ = bf16[64,1024]{1,0:T(8,128)(2,1)S(1)} collective-permute-done((bf16[64,1024]{1,0:T(8,128)(2,1)}, bf16[64,1024]{1,0:T(8,128)(2,1)S(1)}, u32[]{:S(2)}, u32[]{:S(2)}) %collective-permute-start) | collective-permute-done | bytes 131104 | tf_op jit(solution)/shard_map/ppermute | solution.py:249
  15.9 1.4 %collective-permute-start.5 = (bf16[64,1024]{1,0:T(8,128)(2,1)}, bf16[64,1024]{1,0:T(8,128)(2,1)S(1)}, u32[]{:S(2)}, u32[]{:S(2)}) collective-permute-start(bf16[64,1024]{1,0:T(8,128)(2,1)} %get-tuple-element.38), channel_id=1, source_target_pairs={{0,10},{2,8},{4,14},{6,12},{8,2},{10,0},{12,6},{14,4},{16,26},{18,... | collective-permute-start | bytes 393224 | tf_op jit(solution)/shard_map/ppermute | solution.py:249
  17.2 1.2 %collective-permute-done.1.refs_1_ = bf16[64,1024]{1,0:T(8,128)(2,1)S(1)} collective-permute-done((bf16[64,1024]{1,0:T(8,128)(2,1)}, bf16[64,1024]{1,0:T(8,128)(2,1)S(1)}, u32[]{:S(2)}, u32[]{:S(2)}) %collective-permute-start.1) | collective-permute-done | bytes 131104 | tf_op jit(solution)/shard_map/ppermute | solution.py:249
  18.4 0.6 collective-permute-start.6
  19.0 3.4 %collective-permute-done.2.refs_2_ = bf16[64,1024]{1,0:T(8,128)(2,1)S(1)} collective-permute-done((bf16[64,1024]{1,0:T(8,128)(2,1)}, bf16[64,1024]{1,0:T(8,128)(2,1)S(1)}, u32[]{:S(2)}, u32[]{:S(2)}) %collective-permute-start.2) | collective-permute-done | bytes 131104 | tf_op jit(solution)/shard_map/ppermute | solution.py:249
  22.4 0.7 collective-permute-start.7
  23.0 0.5 collective-permute-done.3.refs_3_
  23.5 3.4 %collective-permute-start.8 = (bf16[64,1024]{1,0:T(8,128)(2,1)}, bf16[64,1024]{1,0:T(8,128)(2,1)S(1)}, u32[]{:S(2)}, u32[]{:S(2)}) collective-permute-start(bf16[64,1024]{1,0:T(8,128)(2,1)} %get-tuple-element.41), channel_id=1, source_target_pairs={{0,22},{2,20},{4,18},{6,16},{8,30},{10,28},{12,26},{14,24},{16,6},... | collective-permute-start | bytes 393224 | tf_op jit(solution)/shard_map/ppermute | solution.py:249
  26.9 0.3 collective-permute-done.4.refs_4_
  27.2 3.9 %collective-permute-start.9 = (bf16[64,1024]{1,0:T(8,128)(2,1)}, bf16[64,1024]{1,0:T(8,128)(2,1)S(1)}, u32[]{:S(2)}, u32[]{:S(2)}) collective-permute-start(bf16[64,1024]{1,0:T(8,128)(2,1)} %get-tuple-element.42), channel_id=1, source_target_pairs={{0,6},{2,4},{4,2},{6,0},{8,14},{10,12},{12,10},{14,8},{16,22},{18,... | collective-permute-start | bytes 393224 | tf_op jit(solution)/shard_map/ppermute | solution.py:249
  31.2 2.5 %collective-permute-done.6.refs_6_ = bf16[64,1024]{1,0:T(8,128)(2,1)S(1)} collective-permute-done((bf16[64,1024]{1,0:T(8,128)(2,1)}, bf16[64,1024]{1,0:T(8,128)(2,1)S(1)}, u32[]{:S(2)}, u32[]{:S(2)}) %collective-permute-start.6) | collective-permute-done | bytes 131104 | tf_op jit(solution)/shard_map/ppermute | solution.py:249
  33.7 0.0 copy-start.1
  33.7 0.0 copy-start.2
  33.7 0.6 collective-permute-start.11
  34.2 0.6 collective-permute-done.7.refs_7_
  34.8 5.3 %collective-permute-done.8.refs_8_ = bf16[64,1024]{1,0:T(8,128)(2,1)S(1)} collective-permute-done((bf16[64,1024]{1,0:T(8,128)(2,1)}, bf16[64,1024]{1,0:T(8,128)(2,1)S(1)}, u32[]{:S(2)}, u32[]{:S(2)}) %collective-permute-start.8) | collective-permute-done | bytes 131104 | tf_op jit(solution)/shard_map/ppermute | solution.py:249
  40.1 2.0 %collective-permute-done.10.refs_10_ = bf16[64,1024]{1,0:T(8,128)(2,1)S(1)} collective-permute-done((bf16[64,1024]{1,0:T(8,128)(2,1)}, bf16[64,1024]{1,0:T(8,128)(2,1)S(1)}, u32[]{:S(2)}, u32[]{:S(2)}) %collective-permute-start.10) | collective-permute-done | bytes 131104 | tf_op jit(solution)/shard_map/ppermute | solution.py:249
  42.1 0.6 collective-permute-done.11.refs_11_
  42.7 0.1 collect.2.own_ref.refs_0_
  42.8 0.0 copy-start.3
  42.8 0.1 collective-permute-start.12
  42.9 2.8 %collective-permute-start.14 = (bf16[64,1024]{1,0:T(8,128)(2,1)S(1)}, bf16[64,1024]{1,0:T(8,128)(2,1)S(1)}, u32[]{:S(2)}, u32[]{:S(2)}) collective-permute-start(bf16[64,1024]{1,0:T(8,128)(2,1)S(1)} %copy-done.10), channel_id=1, source_target_pairs={{0,18},{2,16},{4,22},{6,20},{8,26},{10,24},{12,30},{14,28},{16,2},... | collective-permute-start | bytes 393224 | tf_op jit(solution)/shard_map/ppermute | solution.py:249
  45.7 1.6 %collective-permute-start.15 = (bf16[64,1024]{1,0:T(8,128)(2,1)S(1)}, bf16[64,1024]{1,0:T(8,128)(2,1)S(1)}, u32[]{:S(2)}, u32[]{:S(2)}) collective-permute-start(bf16[64,1024]{1,0:T(8,128)(2,1)S(1)} %copy-done.9), channel_id=1, source_target_pairs={{0,2},{2,0},{4,6},{6,4},{8,10},{10,8},{12,14},{14,12},{16,18},{18,... | collective-permute-start | bytes 393224 | tf_op jit(solution)/shard_map/ppermute | solution.py:249
  47.3 0.0 collective-permute-start.16
  47.4 6.3 %front.2 = (bf16[704,384]{1,0:T(8,128)(2,1)S(1)}, bf16[704,384]{1,0:T(8,128)(2,1)S(1)}, bf16[704,384]{1,0:T(8,128)(2,1)S(1)}, bf16[384,1024]{1,0:T(8,128)(2,1)S(1)}) custom-call(bf16[768,1024]{1,0:T(8,128)(2,1)S(1)} %collect.2.own_ref.refs_0_, bf16[768,1024]{1,0:T(8,128)(2,1)S(1)} %collective-permute-done.12.other_ref.refs_1_, ...), custom_call_target="tpu_custom_call" | custom-call | flops 4429185024 | bytes 17825792 | tf_op jit(solution)/shard_map/front/pallas_call | solution.py:268
  53.7 0.0 copy-start.7
  53.8 1.4 %kept.2.refs_4_.refs_0_ = f32[384,1024]{1,0:T(8,128)S(1)} custom-call(bf16[704,384]{1,0:T(8,128)(2,1)S(1)} %get-tuple-element.45.d_gate_ref.refs_2_, bf16[704,384]{1,0:T(8,128)(2,1)S(1)} %get-tuple-element.46.d_up_ref.refs_3_, bf16[704,2048]{1,0:T(8,128)(2,1)S(1)} %bitcast.10, bf16[704,2048]{1,0:T(8,128)(2,1)S(1)} %bitcast.14), custom_call_target="tpu_custom_call" | custom-call | flops 1107296256 | bytes 4456448 | tf_op jit(solution)/shard_map/kept/pallas_call | solution.py:278
  55.2 1.2 %collective-permute-done.16.refs_2_ = bf16[64,1024]{1,0:T(8,128)(2,1)S(1)} collective-permute-done((bf16[64,1024]{1,0:T(8,128)(2,1)S(1)}, bf16[64,1024]{1,0:T(8,128)(2,1)S(1)}, u32[]{:S(2)}, u32[]{:S(2)}) %collective-permute-start.16) | collective-permute-done | bytes 131104 | tf_op jit(solution)/shard_map/ppermute | solution.py:249
  56.5 0.1 collective-permute-start.17
  56.6 0.5 collective-permute-start.13
  57.0 1.4 %collective-permute-done.17.other_ref.refs_6_ = bf16[256,1024]{1,0:T(8,128)(2,1)S(1)} collective-permute-done((bf16[256,1024]{1,0:T(8,128)(2,1)S(1)}, bf16[256,1024]{1,0:T(8,128)(2,1)S(1)}, u32[]{:S(2)}, u32[]{:S(2)}) %collective-permute-start.17) | collective-permute-done | bytes 524320 | tf_op jit(solution)/shard_map/ppermute | solution.py:252
  58.4 3.2 %front.3 = (bf16[704,128]{1,0:T(8,128)(2,1)S(1)}, bf16[704,128]{1,0:T(8,128)(2,1)S(1)}, bf16[704,128]{1,0:T(8,128)(2,1)S(1)}, bf16[128,1024]{1,0:T(8,128)(2,1)S(1)}) custom-call(bf16[256,1024]{1,0:T(8,128)(2,1)S(1)} %collect.3.own_ref.refs_5_, bf16[256,1024]{1,0:T(8,128)(2,1)S(1)} %collective-permute-done.17.other_ref.refs_6_, ...), custom_call_target="tpu_custom_call" | custom-call | flops 1476395008 | bytes 13631488 | tf_op jit(solution)/shard_map/front/pallas_call | solution.py:268
  61.6 0.2 collective-permute-start.18
  61.8 0.6 kept.3.refs_2_
  62.4 0.8 collective-permute-done.18.refs_3_
  63.2 1.2 %total.1 = (bf16[512,1024]{1,0:T(8,128)(2,1)}, f32[8,128]{1,0:T(8,128)S(1)}) custom-call(f32[384,1024]{1,0:T(8,128)S(1)} %kept.2.refs_4_.refs_0_, bf16[384,1024]{1,0:T(8,128)(2,1)S(1)} %collective-permute-done.13.refs_1_, f32[128,1024]{1,0:T(8,128)S(1)} %kept.3.refs_2_, bf16[128,1024]{1,0:T(8,128)(2,1)S(1)} %collective-permute-done.18.refs_3_), custom_call_target="tpu_custom_call" | custom-call | tf_op jit(solution)/shard_map/total/pallas_call | solution.py:293
  64.5 7.9 %all-to-all-start = ((bf16[16,32,1024]{2,1,0:T(8,128)(2,1)}), bf16[16,32,1024]{2,1,0:T(8,128)(2,1)}, u32[]{:S(2)}, u32[]{:S(2)}) async-start(bf16[16,32,1024]{2,1,0:T(8,128)(2,1)} %bitcast.4), calls=%async_computation | async-start | bytes 2097152 | tf_op jit(solution)/shard_map/all_to_all | solution.py:209
  72.4 1.4 %copy-done.4 = bf16[768,1024]{1,0:T(8,128)(2,1)S(1)} copy-done((bf16[768,1024]{1,0:T(8,128)(2,1)S(1)}, bf16[768,1024]{1,0:T(8,128)(2,1)}, u32[]{:S(2)}) %copy-start.4) | copy-done | bytes 1572888
  73.8 1.4 %copy-done.6 = bf16[768,1024]{1,0:T(8,128)(2,1)S(1)} copy-done((bf16[768,1024]{1,0:T(8,128)(2,1)S(1)}, bf16[768,1024]{1,0:T(8,128)(2,1)}, u32[]{:S(2)}) %copy-start.6) | copy-done | bytes 1572888
  75.2 8.9 %grads.1 = (bf16[704,2048]{1,0:T(8,128)(2,1)}, bf16[704,2048]{1,0:T(8,128)(2,1)}, bf16[704,2048]{1,0:T(8,128)(2,1)}) custom-call(bf16[768,1024]{1,0:T(8,128)(2,1)S(1)} %copy-done.4, bf16[768,1024]{1,0:T(8,128)(2,1)S(1)} %copy-done.6, bf16[704,384]{1,0:T(8,128)(2,1)S(1)} %get-tuple-element.45.d_gate_ref.refs_2_, ...), custom_call_target="tpu_custom_call" | custom-call | flops 4429185024 | bytes 14942208 | tf_op jit(solution)/shard_map/grads/pallas_call | solution.py:312
  84.1 14.1 %all-to-all-done = bf16[16,32,1024]{2,1,0:T(8,128)(2,1)} async-done(((bf16[16,32,1024]{2,1,0:T(8,128)(2,1)}), bf16[16,32,1024]{2,1,0:T(8,128)(2,1)}, u32[]{:S(2)}, u32[]{:S(2)}) %all-to-all-start) | async-done | bytes 1048608 | tf_op jit(solution)/shard_map/all_to_all | solution.py:209
  98.2 3.3 %combine.1 = bf16[256,1024]{1,0:T(8,128)(2,1)} custom-call(s32[1,256]{1,0:T(1,128)} %bitcast.20, bf16[512,1024]{1,0:T(8,128)(2,1)} %bitcast.5.back_hbm), custom_call_target="tpu_custom_call" | custom-call | tf_op jit(solution)/shard_map/combine/pallas_call | solution.py:197
  (24 shorter events, 0.1 us)
Async XLA Ops:
  4.6 11.3 %collective-permute-start = (bf16[64,1024]{1,0:T(8,128)(2,1)}, bf16[64,1024]{1,0:T(8,128)(2,1)S(1)}, u32[]{:S(2)}, u32[]{:S(2)}) collective-permute-start(bf16[64,1024]{1,0:T(8,128)(2,1)} %get-tuple-element.33), channel_id=1, source_target_pairs={{0,30},{2,28},{4,26},{6,24},{8,22},{10,20},{12,18},{14,16},{16,14}... | collective-permute-start | bytes 393224 | tf_op jit(solution)/shard_map/ppermute | solution.py:249
  8.1 10.3 %collective-permute-start.1 = (bf16[64,1024]{1,0:T(8,128)(2,1)}, bf16[64,1024]{1,0:T(8,128)(2,1)S(1)}, u32[]{:S(2)}, u32[]{:S(2)}) collective-permute-start(bf16[64,1024]{1,0:T(8,128)(2,1)} %get-tuple-element.34), channel_id=1, source_target_pairs={{0,14},{2,12},{4,10},{6,8},{8,6},{10,4},{12,2},{14,0},{16,30},{18,... | collective-permute-start | bytes 393224 | tf_op jit(solution)/shard_map/ppermute | solution.py:249
  10.5 11.9 %collective-permute-start.2 = (bf16[64,1024]{1,0:T(8,128)(2,1)}, bf16[64,1024]{1,0:T(8,128)(2,1)S(1)}, u32[]{:S(2)}, u32[]{:S(2)}) collective-permute-start(bf16[64,1024]{1,0:T(8,128)(2,1)} %get-tuple-element.35), channel_id=1, source_target_pairs={{0,28},{2,30},{4,24},{6,26},{8,20},{10,22},{12,16},{14,18},{16,12}... | collective-permute-start | bytes 393224 | tf_op jit(solution)/shard_map/ppermute | solution.py:249
  10.8 12.7 %collective-permute-start.3 = (bf16[64,1024]{1,0:T(8,128)(2,1)}, bf16[64,1024]{1,0:T(8,128)(2,1)S(1)}, u32[]{:S(2)}, u32[]{:S(2)}) collective-permute-start(bf16[64,1024]{1,0:T(8,128)(2,1)} %get-tuple-element.36), channel_id=1, source_target_pairs={{0,12},{2,14},{4,8},{6,10},{8,4},{10,6},{12,0},{14,2},{16,28},{18,... | collective-permute-start | bytes 393224 | tf_op jit(solution)/shard_map/ppermute | solution.py:249
  12.3 14.9 %collective-permute-start.4 = (bf16[64,1024]{1,0:T(8,128)(2,1)}, bf16[64,1024]{1,0:T(8,128)(2,1)S(1)}, u32[]{:S(2)}, u32[]{:S(2)}) collective-permute-start(bf16[64,1024]{1,0:T(8,128)(2,1)} %get-tuple-element.37), channel_id=1, source_target_pairs={{0,26},{2,24},{4,30},{6,28},{8,18},{10,16},{12,22},{14,20},{16,10}... | collective-permute-start | bytes 393224 | tf_op jit(solution)/shard_map/ppermute | solution.py:249
  15.9 15.3 %collective-permute-start.5 = (bf16[64,1024]{1,0:T(8,128)(2,1)}, bf16[64,1024]{1,0:T(8,128)(2,1)S(1)}, u32[]{:S(2)}, u32[]{:S(2)}) collective-permute-start(bf16[64,1024]{1,0:T(8,128)(2,1)} %get-tuple-element.38), channel_id=1, source_target_pairs={{0,10},{2,8},{4,14},{6,12},{8,2},{10,0},{12,6},{14,4},{16,26},{18,... | collective-permute-start | bytes 393224 | tf_op jit(solution)/shard_map/ppermute | solution.py:249
  18.4 15.2 %collective-permute-start.6 = (bf16[64,1024]{1,0:T(8,128)(2,1)}, bf16[64,1024]{1,0:T(8,128)(2,1)S(1)}, u32[]{:S(2)}, u32[]{:S(2)}) collective-permute-start(bf16[64,1024]{1,0:T(8,128)(2,1)} %get-tuple-element.39), channel_id=1, source_target_pairs={{0,24},{2,26},{4,28},{6,30},{8,16},{10,18},{12,20},{14,22},{16,8},... | collective-permute-start | bytes 393224 | tf_op jit(solution)/shard_map/ppermute | solution.py:249
  22.4 12.4 %collective-permute-start.7 = (bf16[64,1024]{1,0:T(8,128)(2,1)}, bf16[64,1024]{1,0:T(8,128)(2,1)S(1)}, u32[]{:S(2)}, u32[]{:S(2)}) collective-permute-start(bf16[64,1024]{1,0:T(8,128)(2,1)} %get-tuple-element.40), channel_id=1, source_target_pairs={{0,8},{2,10},{4,12},{6,14},{8,0},{10,2},{12,4},{14,6},{16,24},{18,... | collective-permute-start | bytes 393224 | tf_op jit(solution)/shard_map/ppermute | solution.py:249
  23.5 16.5 %collective-permute-start.8 = (bf16[64,1024]{1,0:T(8,128)(2,1)}, bf16[64,1024]{1,0:T(8,128)(2,1)S(1)}, u32[]{:S(2)}, u32[]{:S(2)}) collective-permute-start(bf16[64,1024]{1,0:T(8,128)(2,1)} %get-tuple-element.41), channel_id=1, source_target_pairs={{0,22},{2,20},{4,18},{6,16},{8,30},{10,28},{12,26},{14,24},{16,6},... | collective-permute-start | bytes 393224 | tf_op jit(solution)/shard_map/ppermute | solution.py:249
  27.2 12.8 %collective-permute-start.9 = (bf16[64,1024]{1,0:T(8,128)(2,1)}, bf16[64,1024]{1,0:T(8,128)(2,1)S(1)}, u32[]{:S(2)}, u32[]{:S(2)}) collective-permute-start(bf16[64,1024]{1,0:T(8,128)(2,1)} %get-tuple-element.42), channel_id=1, source_target_pairs={{0,6},{2,4},{4,2},{6,0},{8,14},{10,12},{12,10},{14,8},{16,22},{18,... | collective-permute-start | bytes 393224 | tf_op jit(solution)/shard_map/ppermute | solution.py:249
  31.2 10.9 %collective-permute-start.10 = (bf16[64,1024]{1,0:T(8,128)(2,1)}, bf16[64,1024]{1,0:T(8,128)(2,1)S(1)}, u32[]{:S(2)}, u32[]{:S(2)}) collective-permute-start(bf16[64,1024]{1,0:T(8,128)(2,1)} %get-tuple-element.43), channel_id=1, source_target_pairs={{0,20},{2,22},{4,16},{6,18},{8,28},{10,30},{12,24},{14,26},{16,4},... | collective-permute-start | bytes 393224 | tf_op jit(solution)/shard_map/ppermute | solution.py:249
  33.6 9.2 %copy-start.10 = (bf16[64,1024]{1,0:T(8,128)(2,1)S(1)}, bf16[64,1024]{1,0:T(8,128)(2,1)}, u32[]{:S(2)}) copy-start(bf16[64,1024]{1,0:T(8,128)(2,1)} %get-tuple-element.48) | copy-start | bytes 393220
  33.6 12.1 %copy-start.9 = (bf16[64,1024]{1,0:T(8,128)(2,1)S(1)}, bf16[64,1024]{1,0:T(8,128)(2,1)}, u32[]{:S(2)}) copy-start(bf16[64,1024]{1,0:T(8,128)(2,1)} %get-tuple-element.49) | copy-start | bytes 393220
  33.6 13.7 %copy-start.8 = (bf16[64,1024]{1,0:T(8,128)(2,1)S(1)}, bf16[64,1024]{1,0:T(8,128)(2,1)}, u32[]{:S(2)}) copy-start(bf16[64,1024]{1,0:T(8,128)(2,1)} %get-tuple-element.50) | copy-start | bytes 393220
  33.6 13.7 %copy-start = (bf16[1,704,2048]{2,1,0:T(8,128)(2,1)S(1)}, bf16[1,704,2048]{2,1,0:T(8,128)(2,1)}, u32[]{:S(2)}) copy-start(bf16[1,704,2048]{2,1,0:T(8,128)(2,1)} %param.9) | copy-start | bytes 8650756
  33.7 13.7 %copy-start.1 = (bf16[1,704,2048]{2,1,0:T(8,128)(2,1)S(1)}, bf16[1,704,2048]{2,1,0:T(8,128)(2,1)}, u32[]{:S(2)}) copy-start(bf16[1,704,2048]{2,1,0:T(8,128)(2,1)} %param.10) | copy-start | bytes 8650756
  33.7 13.7 %copy-start.2 = (bf16[1,704,2048]{2,1,0:T(8,128)(2,1)S(1)}, bf16[1,704,2048]{2,1,0:T(8,128)(2,1)}, u32[]{:S(2)}) copy-start(bf16[1,704,2048]{2,1,0:T(8,128)(2,1)} %param.11) | copy-start | bytes 8650756
  33.7 9.0 %collective-permute-start.11 = (bf16[64,1024]{1,0:T(8,128)(2,1)}, bf16[64,1024]{1,0:T(8,128)(2,1)S(1)}, u32[]{:S(2)}, u32[]{:S(2)}) collective-permute-start(bf16[64,1024]{1,0:T(8,128)(2,1)} %get-tuple-element.44), channel_id=1, source_target_pairs={{0,4},{2,6},{4,0},{6,2},{8,12},{10,14},{12,8},{14,10},{16,20},{18,... | collective-permute-start | bytes 393224 | tf_op jit(solution)/shard_map/ppermute | solution.py:249
  42.8 10.9 %copy-start.3 = (bf16[768,1024]{1,0:T(8,128)(2,1)}, bf16[768,1024]{1,0:T(8,128)(2,1)S(1)}, u32[]{:S(2)}) copy-start(bf16[768,1024]{1,0:T(8,128)(2,1)S(1)} %collect.2.own_ref.refs_0_) | copy-start | bytes 4718596
  42.8 4.6 %collective-permute-start.12 = (bf16[768,1024]{1,0:T(8,128)(2,1)S(1)}, bf16[768,1024]{1,0:T(8,128)(2,1)S(1)}, u32[]{:S(2)}, u32[]{:S(2)}) collective-permute-start(bf16[768,1024]{1,0:T(8,128)(2,1)S(1)} %collect.2.own_ref.refs_0_), channel_id=1, source_target_pairs={{0,1},{1,0},{2,3},{3,2},{4,5},{5,4},{6,7},{7,6},{8,9},{9,8},{10,11... | collective-permute-start | bytes 4718600 | tf_op jit(solution)/shard_map/ppermute | solution.py:252
  42.9 12.3 %collective-permute-start.14 = (bf16[64,1024]{1,0:T(8,128)(2,1)S(1)}, bf16[64,1024]{1,0:T(8,128)(2,1)S(1)}, u32[]{:S(2)}, u32[]{:S(2)}) collective-permute-start(bf16[64,1024]{1,0:T(8,128)(2,1)S(1)} %copy-done.10), channel_id=1, source_target_pairs={{0,18},{2,16},{4,22},{6,20},{8,26},{10,24},{12,30},{14,28},{16,2},... | collective-permute-start | bytes 393224 | tf_op jit(solution)/shard_map/ppermute | solution.py:249
  45.7 9.5 %collective-permute-start.15 = (bf16[64,1024]{1,0:T(8,128)(2,1)S(1)}, bf16[64,1024]{1,0:T(8,128)(2,1)S(1)}, u32[]{:S(2)}, u32[]{:S(2)}) collective-permute-start(bf16[64,1024]{1,0:T(8,128)(2,1)S(1)} %copy-done.9), channel_id=1, source_target_pairs={{0,2},{2,0},{4,6},{6,4},{8,10},{10,8},{12,14},{14,12},{16,18},{18,... | collective-permute-start | bytes 393224 | tf_op jit(solution)/shard_map/ppermute | solution.py:249
  47.3 9.1 %collective-permute-start.16 = (bf16[64,1024]{1,0:T(8,128)(2,1)S(1)}, bf16[64,1024]{1,0:T(8,128)(2,1)S(1)}, u32[]{:S(2)}, u32[]{:S(2)}) collective-permute-start(bf16[64,1024]{1,0:T(8,128)(2,1)S(1)} %copy-done.8), channel_id=1, source_target_pairs={{0,16},{2,18},{4,20},{6,22},{8,24},{10,26},{12,28},{14,30},{16,0},... | collective-permute-start | bytes 393224 | tf_op jit(solution)/shard_map/ppermute | solution.py:249
  47.4 6.4 %copy-start.5 = (bf16[768,1024]{1,0:T(8,128)(2,1)}, bf16[768,1024]{1,0:T(8,128)(2,1)S(1)}, u32[]{:S(2)}) copy-start(bf16[768,1024]{1,0:T(8,128)(2,1)S(1)} %collective-permute-done.12.other_ref.refs_1_) | copy-start | bytes 4718596
  53.7 2.7 %copy-start.7 = (bf16[64,1024]{1,0:T(8,128)(2,1)S(1)}, bf16[64,1024]{1,0:T(8,128)(2,1)}, u32[]{:S(2)}) copy-start(bf16[64,1024]{1,0:T(8,128)(2,1)} %get-tuple-element.51.refs_3_) | copy-start | bytes 393220
  56.5 2.0 %collective-permute-start.17 = (bf16[256,1024]{1,0:T(8,128)(2,1)S(1)}, bf16[256,1024]{1,0:T(8,128)(2,1)S(1)}, u32[]{:S(2)}, u32[]{:S(2)}) collective-permute-start(bf16[256,1024]{1,0:T(8,128)(2,1)S(1)} %collect.3.own_ref.refs_5_), channel_id=1, source_target_pairs={{0,1},{1,0},{2,3},{3,2},{4,5},{5,4},{6,7},{7,6},{8,9},{9,8},{10,11... | collective-permute-start | bytes 1572872 | tf_op jit(solution)/shard_map/ppermute | solution.py:252
  56.6 5.8 %collective-permute-start.13 = (bf16[384,1024]{1,0:T(8,128)(2,1)S(1)}, bf16[384,1024]{1,0:T(8,128)(2,1)S(1)}, u32[]{:S(2)}, u32[]{:S(2)}) collective-permute-start(bf16[384,1024]{1,0:T(8,128)(2,1)S(1)} %get-tuple-element.47), channel_id=1, source_target_pairs={{0,1},{1,0},{2,3},{3,2},{4,5},{5,4},{6,7},{7,6},{8,9},{9,8},{10,11... | collective-permute-start | bytes 2359304 | tf_op jit(solution)/shard_map/ppermute | solution.py:252
  61.6 1.6 %collective-permute-start.18 = (bf16[128,1024]{1,0:T(8,128)(2,1)S(1)}, bf16[128,1024]{1,0:T(8,128)(2,1)S(1)}, u32[]{:S(2)}, u32[]{:S(2)}) collective-permute-start(bf16[128,1024]{1,0:T(8,128)(2,1)S(1)} %get-tuple-element.54), channel_id=1, source_target_pairs={{0,1},{1,0},{2,3},{3,2},{4,5},{5,4},{6,7},{7,6},{8,9},{9,8},{10,11... | collective-permute-start | bytes 786440 | tf_op jit(solution)/shard_map/ppermute | solution.py:252
  64.5 33.8 %all-to-all-start = ((bf16[16,32,1024]{2,1,0:T(8,128)(2,1)}), bf16[16,32,1024]{2,1,0:T(8,128)(2,1)}, u32[]{:S(2)}, u32[]{:S(2)}) async-start(bf16[16,32,1024]{2,1,0:T(8,128)(2,1)} %bitcast.4), calls=%async_computation | async-start | bytes 2097152 | tf_op jit(solution)/shard_map/all_to_all | solution.py:209
  72.3 1.4 %copy-start.4 = (bf16[768,1024]{1,0:T(8,128)(2,1)S(1)}, bf16[768,1024]{1,0:T(8,128)(2,1)}, u32[]{:S(2)}) copy-start(bf16[768,1024]{1,0:T(8,128)(2,1)} %copy-done.3) | copy-start | bytes 4718596
  73.8 1.4 %copy-start.6 = (bf16[768,1024]{1,0:T(8,128)(2,1)S(1)}, bf16[768,1024]{1,0:T(8,128)(2,1)}, u32[]{:S(2)}) copy-start(bf16[768,1024]{1,0:T(8,128)(2,1)} %copy-done.5) | copy-start | bytes 4718596

commit v7 on v6

--- a/solution.py
+++ b/solution.py
@@ -9,12 +9,12 @@
 
 F32 = jnp.float32
 BF16 = jnp.bfloat16
-SMALL = 20 * 2**20
+SMALL = 16 * 2**20
 LARGE = 56 * 2**20
 PIECES = 4
 COLLECT = 16
 IN_VMEM = pl.BlockSpec(memory_space=pltpu.VMEM)
-ANYWHERE = pl.BlockSpec(memory_space=pl.ANY)
+IN_HBM = pl.BlockSpec(memory_space=pltpu.HBM)
 
 
 def rank_among_same(row, axis):
@@ -27,15 +27,17 @@
     return (col if axis else row), jnp.sum(same, axis=axis, keepdims=True)
 
 
-def place_kernel(capacity, row_ref, x_hbm, dy_hbm, *refs):
-    *slabs, x_ref, dy_ref, sems = refs
+def place_kernel(capacity, row_hbm, x_hbm, dy_hbm, *refs):
+    *slabs, row_ref, x_ref, dy_ref, placed_ref, row_sem, in_sems, out_sems = refs
+    row_copy = pltpu.make_async_copy(row_hbm, row_ref, row_sem)
+    row_copy.start()
     step = x_ref.shape[0] // PIECES
     copies = [
         [
             pltpu.make_async_copy(
                 from_ref.at[i * step : (i + 1) * step],
                 to_ref.at[i * step : (i + 1) * step],
-                sems.at[which, i],
+                in_sems.at[which, i],
             )
             for i in range(PIECES)
         ]
@@ -44,16 +46,27 @@
     for copy in copies[0] + copies[1]:
         copy.start()
     me = lax.axis_index("expert")
+    row_copy.wait()
     route, within = rank_among_same(row_ref[...], 0)
     slots = len(slabs) * capacity
     slot = lax.broadcasted_iota(jnp.int32, (slots, x_ref.shape[0]), 0)
     placing = jnp.where(slot == (route ^ me) * capacity + within, 1.0, 0.0).astype(BF16)
+    out_copies = []
     for i, ref in enumerate((x_ref, dy_ref)):
         for copy in copies[i]:
             copy.wait()
-        placed = jnp.dot(placing, ref[...], preferred_element_type=F32).astype(BF16)
+        placed_ref[i] = jnp.dot(placing, ref[...], preferred_element_type=F32).astype(BF16)
         for k, slab in enumerate(slabs):
-            slab[i * capacity : (i + 1) * capacity, :] = placed[k * capacity : (k + 1) * capacity]
+            out_copies.append(
+                pltpu.make_async_copy(
+                    placed_ref.at[i, k * capacity : (k + 1) * capacity],
+                    slab.at[i * capacity : (i + 1) * capacity],
+                    out_sems.at[i, k],
+                )
+            )
+            out_copies[-1].start()
+    for copy in out_copies:
+        copy.wait()
 
 
 def collect_kernel(capacity, count, *refs):
@@ -115,20 +128,26 @@
     ).astype(BF16)
 
 
-def kept_kernel(d_gate_ref, d_up_ref, gate_ref, up_ref, out_ref):
+def sum_kernel(d_gate_ref, d_up_ref, gate_ref, up_ref, got_ref, out_ref):
     columns = side(lax.axis_index("tensor"), out_ref.shape[1])
-    out_ref[...] = input_rows(d_gate_ref, d_up_ref, gate_ref, up_ref, columns)
-
-
-def total_kernel(capacity, groups, *refs):
-    *parts, out_ref, done_ref = refs
+    own = input_rows(d_gate_ref, d_up_ref, gate_ref, up_ref, columns)
+    out_ref[...] = (own + got_ref[...].astype(F32)).astype(BF16)
+
+
+def last_sum_kernel(capacity, groups, *refs):
+    *earlier_refs, d_gate_ref, d_up_ref, gate_ref, up_ref, got_ref = refs[:-3]
+    out_ref, done_ref, sum_ref = refs[-3:]
+    done_ref[...] = jnp.zeros_like(done_ref)
     me = lax.axis_index("expert")
-    done_ref[...] = jnp.zeros_like(done_ref)
-    for kept_ref, got_ref, group in zip(parts[::2], parts[1::2], groups):
+
+    def put(rows_ref, group):
         for i, k in enumerate(group):
-            here = slice(i * capacity, (i + 1) * capacity)
             there = pl.ds(pl.multiple_of((me ^ k) * capacity, capacity), capacity)
-            out_ref[there, :] = (kept_ref[here, :] + got_ref[here, :].astype(F32)).astype(BF16)
+            out_ref[there, :] = rows_ref[i * capacity : (i + 1) * capacity, :]
+
+    sum_kernel(d_gate_ref, d_up_ref, gate_ref, up_ref, got_ref, sum_ref)
+    for rows_ref, group in zip((*earlier_refs, sum_ref), groups):
+        put(rows_ref, group)
 
 
 def grads_kernel(sizes, *refs):
@@ -197,10 +216,10 @@
     return pl.pallas_call(
         functools.partial(combine_kernel, capacity),
         out_shape=jax.ShapeDtypeStruct((tok_rows, width), BF16),
-        in_specs=[IN_VMEM, ANYWHERE],
+        in_specs=[IN_VMEM, IN_HBM],
         out_specs=IN_VMEM,
         scratch_shapes=[pltpu.VMEM((slots, width), BF16), pltpu.SemaphoreType.DMA((PIECES,))],
-        compiler_params=params(LARGE),
+        compiler_params=params(SMALL),
         name="combine",
     )(ids_row, returned)
 
@@ -226,19 +245,23 @@
     far = [k for k in reversed(range(1, experts)) if k >= experts // 2]
     near = [k for k in reversed(range(1, experts)) if k < experts // 2]
     turns = [k for pair in zip(far, near) for k in pair] + far[len(near) :]
-    cut = 3 * experts // 4
+    cut = experts // 2
     first, second = turns[:cut], turns[cut:] + [0]
 
     slabs = list(
         pl.pallas_call(
             functools.partial(place_kernel, capacity),
             out_shape=[jax.ShapeDtypeStruct((2 * capacity, width), BF16)] * experts,
-            in_specs=[IN_VMEM, ANYWHERE, ANYWHERE],
-            out_specs=[IN_VMEM] * experts,
+            in_specs=[IN_HBM] * 3,
+            out_specs=[IN_HBM] * experts,
             scratch_shapes=[
+                pltpu.VMEM((1, tok_rows), jnp.int32),
                 pltpu.VMEM((tok_rows, width), BF16),
                 pltpu.VMEM((tok_rows, width), BF16),
+                pltpu.VMEM((2, experts * capacity, width), BF16),
+                pltpu.SemaphoreType.DMA,
                 pltpu.SemaphoreType.DMA((2, PIECES)),
+                pltpu.SemaphoreType.DMA((2, experts)),
             ],
             compiler_params=params(LARGE),
             name="place",
@@ -251,16 +274,16 @@
     def exchange(values):
         return lax.ppermute(values, "tensor", [(0, 1), (1, 0)])
 
-    def collect(arrived, after):
+    def collect(arrived):
         return pl.pallas_call(
             functools.partial(collect_kernel, capacity, len(arrived)),
             out_shape=jax.ShapeDtypeStruct((2 * len(arrived) * capacity, width), BF16),
-            in_specs=[IN_VMEM] * (len(arrived) + len(after)),
+            in_specs=[IN_VMEM] * len(arrived),
             out_specs=IN_VMEM,
             compiler_params=params(SMALL),
             cost_estimate=cost(COLLECT, len(arrived) * capacity, units, features),
             name="collect",
-        )(*arrived, *after)
+        )(*arrived)
 
     def front(own):
         other = exchange(own)
@@ -275,32 +298,35 @@
             cost_estimate=cost(4, rows, units, features),
             name="front",
         )(own, other, gate_rows, up_rows, down_rows)
-        kept = pl.pallas_call(
-            kept_kernel,
-            out_shape=jax.ShapeDtypeStruct((rows, width), F32),
-            in_specs=[IN_VMEM] * 4,
-            out_specs=IN_VMEM,
-            compiler_params=params(SMALL),
-            cost_estimate=cost(1, rows, units, features),
-            name="kept",
-        )(d_gate, d_up, gate_rows, up_rows)
-        return (own, other, d_gate, d_up, hidden), (kept, exchange(sent))
+        for_sum = (d_gate, d_up, gate_rows, up_rows, exchange(sent))
+        return (own, other, d_gate, d_up, hidden), for_sum
 
     got = {k: swap(k) for k in turns}
     got[0] = slabs[0]
-    for_grads_a, sums_a = front(collect([got[k] for k in first], []))
-    for_grads_b, sums_b = front(collect([got[k] for k in second], sums_a[:1]))
+    for_grads_a, for_sum_a = front(collect([got[k] for k in first]))
+    for_grads_b, for_sum_b = front(collect([got[k] for k in second]))
+    sum_a = pl.pallas_call(
+        sum_kernel,
+        out_shape=jax.ShapeDtypeStruct((len(first) * capacity, width), BF16),
+        in_specs=[IN_VMEM] * 5,
+        out_specs=IN_VMEM,
+        compiler_params=params(SMALL),
+        cost_estimate=cost(1, len(first) * capacity, units, features),
+        name="sum",
+    )(*for_sum_a)
     totals, done = pl.pallas_call(
-        functools.partial(total_kernel, capacity, (first, second)),
+        functools.partial(last_sum_kernel, capacity, (first, second)),
         out_shape=[
             jax.ShapeDtypeStruct((experts * capacity, width), BF16),
             jax.ShapeDtypeStruct((8, 128), F32),
         ],
-        in_specs=[IN_VMEM] * 4,
+        in_specs=[IN_VMEM] * 6,
         out_specs=[IN_VMEM] * 2,
+        scratch_shapes=[pltpu.VMEM((len(second) * capacity, width), BF16)],
         compiler_params=params(SMALL),
-        name="total",
-    )(*sums_a, *sums_b)
+        cost_estimate=cost(1, len(second) * capacity, units, features),
+        name="last_sum",
+    )(sum_a, *for_sum_b)
     returned = to_experts(totals, experts)
 
     def grads_specs(rows):
@@ -317,7 +343,7 @@
         + grads_specs(sizes[1])
         + [pl.BlockSpec((8, 128), lambda i: (0, 0))],
         out_specs=[pl.BlockSpec((tile, features), lambda i: (i, 0))] * 3,
-        compiler_params=params(32 * 2**20),
+        compiler_params=params(2 * SMALL),
         cost_estimate=cost(3, sum(sizes), units, features),
         name="grads",
     )(*for_grads_a, *for_grads_b, done)

time: 102 us -> 104 us (1.020)
  local copies, waits for them, and re-layouts: 2.85 us -> 10.5 us
  Pallas kernels: 29 us -> 22.6 us
  starting transfers between devices: 33.9 us -> 35.1 us
    unnamed x22 -> x30, local copies, waits for them, and re-layouts: 2.85 us -> 10.5 us
    ppermute x15, starting transfers between devices: 25.1 us -> 28.4 us  [swap(): lax.ppermute(slabs[k], 'expert', [(e, e ^ k) for e in range(experts)])]
    pallas_call x1, Pallas kernels: 8.92 us -> 6.64 us  [grouped(): pl.pallas_call(functools.partial(grads_kernel, sizes), grid=(units // til...]
    pallas_call x2, Pallas kernels: 9.51 us -> 7.4 us  [front(): pl.pallas_call(functools.partial(front_kernel, tile), out_shape=[jax.Shap...]
    all_to_all x1, starting transfers between devices: 7.9 us -> 6.04 us  [to_experts(): lax.all_to_all(rows.reshape(experts, rows.shape[0] // experts, rows.shape...]
    ppermute x4, waiting for transfers between devices: 2.19 us -> 0.53 us  [exchange(): return lax.ppermute(values, 'tensor', [(0, 1), (1, 0)])]
    ppermute x15, waiting for transfers between devices: 18.6 us -> 20.2 us  [swap(): lax.ppermute(slabs[k], 'expert', [(e, e ^ k) for e in range(experts)])]
    pallas_call x1, Pallas kernels: 3.28 us -> 1.93 us  [combine(): pl.pallas_call(functools.partial(combine_kernel, capacity), out_shape=jax...]
  transfers between devices with their start and end apart: 20 -> 20, of which waited for: 14 -> 12; matrix products, arithmetic and copies ran while one was open for 0% -> 0% of each run, Pallas kernels for 20% -> 15%
where the time goes in v7:
time: 104 us; the launch traced here: 103 us
  starting transfers between devices  35.1 us (34%)
  waiting for transfers between devices  34.4 us (33%)
  Pallas kernels  22.6 us (22%)
  local copies, waits for them, and re-layouts  10.5 us (10%)
    ppermute x15, starting transfers between devices, swap(): lax.ppermute(slabs[k], 'expert', [(e, e ^ k) for e in range(experts)])  28.4 us
    ppermute x15, waiting for transfers between devices, swap(): lax.ppermute(slabs[k], 'expert', [(e, e ^ k) for e in range(experts)])  20.2 us
    all_to_all x1, waiting for transfers between devices, to_experts(): lax.all_to_all(rows.reshape(experts, rows.shape[0] // experts, rows.shape...  13.7 us
    unnamed x30, local copies, waits for them, and re-layouts  10.5 us
    pallas_call x2, Pallas kernels, front(): pl.pallas_call(functools.partial(front_kernel, tile), out_shape=[jax.Shap...  7.4 us
    pallas_call x1, Pallas kernels, grouped(): pl.pallas_call(functools.partial(grads_kernel, sizes), grid=(units // til...  6.64 us
    all_to_all x1, starting transfers between devices, to_experts(): lax.all_to_all(rows.reshape(experts, rows.shape[0] // experts, rows.shape...  6.04 us
    pallas_call x1, Pallas kernels, grouped(): pl.pallas_call(functools.partial(place_kernel, capacity), out_shape=[jax....  3.49 us
  transfers between devices with their start and end apart: 20, of which 12 were waited for; matrix products, arithmetic and copies ran while one was open for 0% of the time, Pallas kernels for 15%

profile of v7, /device:TPU:8, one launch (start us, length us, event | category | flops | bytes accessed | tf_op | source)
XLA Modules:
  0.0 103.4 jit_solution(13699579100702784121)
XLA Ops:
  0.6 3.5 %place.1 = (bf16[64,1024]{1,0:T(8,128)(2,1)}, bf16[64,1024]{1,0:T(8,128)(2,1)}, bf16[64,1024]{1,0:T(8,128)(2,1)}, bf16[64,1024]{1,0:T(8,128)(2,1)}, bf16[64,1024...) custom-call(s32[1,256]{1,0:T(1,128)} %bitcast.18, ...), custom_call_target="tpu_custom_call" | custom-call | tf_op jit(solution)/shard_map/place/pallas_call | solution.py:252
  4.1 3.5 %collective-permute-start = (bf16[64,1024]{1,0:T(8,128)(2,1)}, bf16[64,1024]{1,0:T(8,128)(2,1)S(1)}, u32[]{:S(2)}, u32[]{:S(2)}) collective-permute-start(bf16[64,1024]{1,0:T(8,128)(2,1)} %get-tuple-element.33), channel_id=1, source_target_pairs={{0,30},{2,28},{4,26},{6,24},{8,22},{10,20},{12,18},{14,16},{16,14}... | collective-permute-start | bytes 393224 | tf_op jit(solution)/shard_map/ppermute | solution.py:272
  7.7 2.4 %collective-permute-start.1 = (bf16[64,1024]{1,0:T(8,128)(2,1)}, bf16[64,1024]{1,0:T(8,128)(2,1)S(1)}, u32[]{:S(2)}, u32[]{:S(2)}) collective-permute-start(bf16[64,1024]{1,0:T(8,128)(2,1)} %get-tuple-element.34), channel_id=1, source_target_pairs={{0,14},{2,12},{4,10},{6,8},{8,6},{10,4},{12,2},{14,0},{16,30},{18,... | collective-permute-start | bytes 393224 | tf_op jit(solution)/shard_map/ppermute | solution.py:272
  10.0 0.3 collective-permute-start.2
  10.3 1.5 %collective-permute-start.3 = (bf16[64,1024]{1,0:T(8,128)(2,1)}, bf16[64,1024]{1,0:T(8,128)(2,1)S(1)}, u32[]{:S(2)}, u32[]{:S(2)}) collective-permute-start(bf16[64,1024]{1,0:T(8,128)(2,1)} %get-tuple-element.36), channel_id=1, source_target_pairs={{0,12},{2,14},{4,8},{6,10},{8,4},{10,6},{12,0},{14,2},{16,28},{18,... | collective-permute-start | bytes 393224 | tf_op jit(solution)/shard_map/ppermute | solution.py:272
  11.8 2.5 %collective-permute-start.4 = (bf16[64,1024]{1,0:T(8,128)(2,1)}, bf16[64,1024]{1,0:T(8,128)(2,1)S(1)}, u32[]{:S(2)}, u32[]{:S(2)}) collective-permute-start(bf16[64,1024]{1,0:T(8,128)(2,1)} %get-tuple-element.37), channel_id=1, source_target_pairs={{0,26},{2,24},{4,30},{6,28},{8,18},{10,16},{12,22},{14,20},{16,10}... | collective-permute-start | bytes 393224 | tf_op jit(solution)/shard_map/ppermute | solution.py:272
  14.4 1.1 %collective-permute-done.refs_0_ = bf16[64,1024]{1,0:T(8,128)(2,1)S(1)} collective-permute-done((bf16[64,1024]{1,0:T(8,128)(2,1)}, bf16[64,1024]{1,0:T(8,128)(2,1)S(1)}, u32[]{:S(2)}, u32[]{:S(2)}) %collective-permute-start) | collective-permute-done | bytes 131104 | tf_op jit(solution)/shard_map/ppermute | solution.py:272
  15.5 1.3 %collective-permute-start.5 = (bf16[64,1024]{1,0:T(8,128)(2,1)}, bf16[64,1024]{1,0:T(8,128)(2,1)S(1)}, u32[]{:S(2)}, u32[]{:S(2)}) collective-permute-start(bf16[64,1024]{1,0:T(8,128)(2,1)} %get-tuple-element.38), channel_id=1, source_target_pairs={{0,10},{2,8},{4,14},{6,12},{8,2},{10,0},{12,6},{14,4},{16,26},{18,... | collective-permute-start | bytes 393224 | tf_op jit(solution)/shard_map/ppermute | solution.py:272
  16.8 1.2 %collective-permute-done.1.refs_1_ = bf16[64,1024]{1,0:T(8,128)(2,1)S(1)} collective-permute-done((bf16[64,1024]{1,0:T(8,128)(2,1)}, bf16[64,1024]{1,0:T(8,128)(2,1)S(1)}, u32[]{:S(2)}, u32[]{:S(2)}) %collective-permute-start.1) | collective-permute-done | bytes 131104 | tf_op jit(solution)/shard_map/ppermute | solution.py:272
  18.0 0.6 collective-permute-start.6
  18.5 3.4 %collective-permute-done.2.refs_2_ = bf16[64,1024]{1,0:T(8,128)(2,1)S(1)} collective-permute-done((bf16[64,1024]{1,0:T(8,128)(2,1)}, bf16[64,1024]{1,0:T(8,128)(2,1)S(1)}, u32[]{:S(2)}, u32[]{:S(2)}) %collective-permute-start.2) | collective-permute-done | bytes 131104 | tf_op jit(solution)/shard_map/ppermute | solution.py:272
  21.9 0.7 collective-permute-start.7
  22.6 0.5 collective-permute-done.3.refs_3_
  23.1 3.4 %collective-permute-start.10 = (bf16[64,1024]{1,0:T(8,128)(2,1)}, bf16[64,1024]{1,0:T(8,128)(2,1)S(1)}, u32[]{:S(2)}, u32[]{:S(2)}) collective-permute-start(bf16[64,1024]{1,0:T(8,128)(2,1)} %get-tuple-element.44), channel_id=1, source_target_pairs={{0,22},{2,20},{4,18},{6,16},{8,30},{10,28},{12,26},{14,24},{16,6},... | collective-permute-start | bytes 393224 | tf_op jit(solution)/shard_map/ppermute | solution.py:272
  26.4 0.3 collective-permute-done.4.refs_4_
  26.8 3.9 %collective-permute-start.11 = (bf16[64,1024]{1,0:T(8,128)(2,1)}, bf16[64,1024]{1,0:T(8,128)(2,1)S(1)}, u32[]{:S(2)}, u32[]{:S(2)}) collective-permute-start(bf16[64,1024]{1,0:T(8,128)(2,1)} %get-tuple-element.45), channel_id=1, source_target_pairs={{0,6},{2,4},{4,2},{6,0},{8,14},{10,12},{12,10},{14,8},{16,22},{18,... | collective-permute-start | bytes 393224 | tf_op jit(solution)/shard_map/ppermute | solution.py:272
  30.7 2.5 %collective-permute-done.6.refs_6_ = bf16[64,1024]{1,0:T(8,128)(2,1)S(1)} collective-permute-done((bf16[64,1024]{1,0:T(8,128)(2,1)}, bf16[64,1024]{1,0:T(8,128)(2,1)S(1)}, u32[]{:S(2)}, u32[]{:S(2)}) %collective-permute-start.6) | collective-permute-done | bytes 131104 | tf_op jit(solution)/shard_map/ppermute | solution.py:272
  33.2 0.5 collective-permute-start.13
  33.7 0.7 collective-permute-done.7.refs_7_
  34.4 3.1 %collective-permute-start.14 = (bf16[64,1024]{1,0:T(8,128)(2,1)}, bf16[64,1024]{1,0:T(8,128)(2,1)S(1)}, u32[]{:S(2)}, u32[]{:S(2)}) collective-permute-start(bf16[64,1024]{1,0:T(8,128)(2,1)} %get-tuple-element.48), channel_id=1, source_target_pairs={{0,18},{2,16},{4,22},{6,20},{8,26},{10,24},{12,30},{14,28},{16,2},... | collective-permute-start | bytes 393224 | tf_op jit(solution)/shard_map/ppermute | solution.py:272
  37.5 4.9 %collective-permute-done.10.refs_0_ = bf16[64,1024]{1,0:T(8,128)(2,1)S(1)} collective-permute-done((bf16[64,1024]{1,0:T(8,128)(2,1)}, bf16[64,1024]{1,0:T(8,128)(2,1)S(1)}, u32[]{:S(2)}, u32[]{:S(2)}) %collective-permute-start.10) | collective-permute-done | bytes 131104 | tf_op jit(solution)/shard_map/ppermute | solution.py:272
  42.4 0.3 collective-permute-start.15
  42.8 4.3 %collective-permute-start.16 = (bf16[64,1024]{1,0:T(8,128)(2,1)}, bf16[64,1024]{1,0:T(8,128)(2,1)S(1)}, u32[]{:S(2)}, u32[]{:S(2)}) collective-permute-start(bf16[64,1024]{1,0:T(8,128)(2,1)} %get-tuple-element.50), channel_id=1, source_target_pairs={{0,16},{2,18},{4,20},{6,22},{8,24},{10,26},{12,28},{14,30},{16,0},... | collective-permute-start | bytes 393224 | tf_op jit(solution)/shard_map/ppermute | solution.py:272
  47.0 0.1 collect.2.own_ref.refs_0_
  47.1 0.1 collective-permute-start.8
  47.2 3.6 %collective-permute-done.14.refs_4_ = bf16[64,1024]{1,0:T(8,128)(2,1)S(1)} collective-permute-done((bf16[64,1024]{1,0:T(8,128)(2,1)}, bf16[64,1024]{1,0:T(8,128)(2,1)S(1)}, u32[]{:S(2)}, u32[]{:S(2)}) %collective-permute-start.14) | collective-permute-done | bytes 131104 | tf_op jit(solution)/shard_map/ppermute | solution.py:272
  50.9 2.0 %collective-permute-done.16.refs_6_ = bf16[64,1024]{1,0:T(8,128)(2,1)S(1)} collective-permute-done((bf16[64,1024]{1,0:T(8,128)(2,1)}, bf16[64,1024]{1,0:T(8,128)(2,1)S(1)}, u32[]{:S(2)}, u32[]{:S(2)}) %collective-permute-start.16) | collective-permute-done | bytes 131104 | tf_op jit(solution)/shard_map/ppermute | solution.py:272
  52.9 0.1 collect.3.own_ref.refs_5_
  53.0 0.1 collective-permute-start.17
  53.1 2.4 %copy-done = bf16[1,704,2048]{2,1,0:T(8,128)(2,1)S(1)} copy-done((bf16[1,704,2048]{2,1,0:T(8,128)(2,1)S(1)}, bf16[1,704,2048]{2,1,0:T(8,128)(2,1)}, u32[]{:S(2)}) %copy-start) | copy-done | bytes 2883608
  55.4 0.9 copy-done.1
  56.3 0.8 copy-done.3
  57.2 3.7 %front.2 = (bf16[704,256]{1,0:T(8,128)(2,1)S(1)}, bf16[704,256]{1,0:T(8,128)(2,1)S(1)}, bf16[704,256]{1,0:T(8,128)(2,1)S(1)}, bf16[256,1024]{1,0:T(8,128)(2,1)S(1)}) custom-call(bf16[512,1024]{1,0:T(8,128)(2,1)S(1)} %collect.2.own_ref.refs_0_, bf16[512,1024]{1,0:T(8,128)(2,1)S(1)} %collective-permute-done.8.other_ref.refs_1_, bf16[704,2048]{1,0:T(8,128)(2,1)S(1)} %bitcast.9, ...), custom_call_target="tpu_custom_call" | custom-call | flops 2952790016 | bytes 15728640 | tf_op jit(solution)/shard_map/front/pallas_call | solution.py:291
  60.9 0.7 copy-done.11
  61.6 3.7 %front.3 = (bf16[704,256]{1,0:T(8,128)(2,1)S(1)}, bf16[704,256]{1,0:T(8,128)(2,1)S(1)}, bf16[704,256]{1,0:T(8,128)(2,1)S(1)}, bf16[256,1024]{1,0:T(8,128)(2,1)S(1)}) custom-call(bf16[512,1024]{1,0:T(8,128)(2,1)S(1)} %collect.3.own_ref.refs_5_, bf16[512,1024]{1,0:T(8,128)(2,1)S(1)} %collective-permute-done.17.other_ref.refs_6_, ...), custom_call_target="tpu_custom_call" | custom-call | flops 2952790016 | bytes 15728640 | tf_op jit(solution)/shard_map/front/pallas_call | solution.py:291
  65.4 0.6 collective-permute-start.18
  65.9 1.0 sum.1.refs_0_
  66.9 0.5 collective-permute-done.18.refs_5_
  67.5 2.0 %last_sum.1 = (bf16[512,1024]{1,0:T(8,128)(2,1)}, f32[8,128]{1,0:T(8,128)S(1)}) custom-call(bf16[256,1024]{1,0:T(8,128)(2,1)S(1)} %sum.1.refs_0_, bf16[704,256]{1,0:T(8,128)(2,1)S(1)} %get-tuple-element.52.refs_1_.refs_7_, bf16[704,256]{1,0:T(8,128)(2,1)S(1)} %get-tuple-element.53.refs_2_.refs_8_, bf16[704,2048]{1,0:T(8,128)(2,1)S(1)} %bitcast.12, ...), custom_call_target="tpu_custom_call" | custom-call | flops 738197504 | bytes 3932160 | tf_op jit(solution)/shard_map/last_sum/pallas_call | solution.py:317
  69.4 6.0 %all-to-all-start = ((bf16[16,32,1024]{2,1,0:T(8,128)(2,1)}), bf16[16,32,1024]{2,1,0:T(8,128)(2,1)S(1)}, u32[]{:S(2)}, u32[]{:S(2)}) async-start(bf16[16,32,1024]{2,1,0:T(8,128)(2,1)} %bitcast.4), calls=%async_computation | async-start | bytes 2097152 | tf_op jit(solution)/shard_map/all_to_all | solution.py:228
  75.5 1.2 %copy-done.5 = bf16[512,1024]{1,0:T(8,128)(2,1)S(1)} copy-done((bf16[512,1024]{1,0:T(8,128)(2,1)S(1)}, bf16[512,1024]{1,0:T(8,128)(2,1)}, u32[]{:S(2)}) %copy-start.5) | copy-done | bytes 1048600
  76.7 1.2 %copy-done.7 = bf16[512,1024]{1,0:T(8,128)(2,1)S(1)} copy-done((bf16[512,1024]{1,0:T(8,128)(2,1)S(1)}, bf16[512,1024]{1,0:T(8,128)(2,1)}, u32[]{:S(2)}) %copy-start.7) | copy-done | bytes 1048600
  77.9 1.2 %copy-done.9 = bf16[512,1024]{1,0:T(8,128)(2,1)S(1)} copy-done((bf16[512,1024]{1,0:T(8,128)(2,1)S(1)}, bf16[512,1024]{1,0:T(8,128)(2,1)}, u32[]{:S(2)}) %copy-start.9) | copy-done | bytes 1048600
  79.2 1.0 copy-done.12
  80.1 1.0 copy-done.14
  81.1 6.6 %grads.1 = (bf16[704,2048]{1,0:T(8,128)(2,1)}, bf16[704,2048]{1,0:T(8,128)(2,1)}, bf16[704,2048]{1,0:T(8,128)(2,1)}) custom-call(bf16[512,1024]{1,0:T(8,128)(2,1)S(1)} %collect.2.own_ref.refs_0_, bf16[512,1024]{1,0:T(8,128)(2,1)S(1)} %copy-done.5, bf16[704,256]{1,0:T(8,128)(2,1)S(1)} %get-tuple-element.41.d_gate_ref.refs_2_, ...), custom_call_target="tpu_custom_call" | custom-call | flops 4429185024 | bytes 14942208 | tf_op jit(solution)/shard_map/grads/pallas_call | solution.py:338
  87.8 13.7 %all-to-all-done = bf16[16,32,1024]{2,1,0:T(8,128)(2,1)S(1)} async-done(((bf16[16,32,1024]{2,1,0:T(8,128)(2,1)}), bf16[16,32,1024]{2,1,0:T(8,128)(2,1)S(1)}, u32[]{:S(2)}, u32[]{:S(2)}) %all-to-all-start) | async-done | bytes 1048608 | tf_op jit(solution)/shard_map/all_to_all | solution.py:228
  101.5 1.9 %combine.1 = bf16[256,1024]{1,0:T(8,128)(2,1)} custom-call(s32[1,256]{1,0:T(1,128)S(1)} %bitcast.19, bf16[512,1024]{1,0:T(8,128)(2,1)S(1)} %bitcast.17), custom_call_target="tpu_custom_call" | custom-call | tf_op jit(solution)/shard_map/combine/pallas_call | solution.py:216
  (31 shorter events, 0.1 us)
Async XLA Ops:
  4.1 11.3 %collective-permute-start = (bf16[64,1024]{1,0:T(8,128)(2,1)}, bf16[64,1024]{1,0:T(8,128)(2,1)S(1)}, u32[]{:S(2)}, u32[]{:S(2)}) collective-permute-start(bf16[64,1024]{1,0:T(8,128)(2,1)} %get-tuple-element.33), channel_id=1, source_target_pairs={{0,30},{2,28},{4,26},{6,24},{8,22},{10,20},{12,18},{14,16},{16,14}... | collective-permute-start | bytes 393224 | tf_op jit(solution)/shard_map/ppermute | solution.py:272
  7.7 10.3 %collective-permute-start.1 = (bf16[64,1024]{1,0:T(8,128)(2,1)}, bf16[64,1024]{1,0:T(8,128)(2,1)S(1)}, u32[]{:S(2)}, u32[]{:S(2)}) collective-permute-start(bf16[64,1024]{1,0:T(8,128)(2,1)} %get-tuple-element.34), channel_id=1, source_target_pairs={{0,14},{2,12},{4,10},{6,8},{8,6},{10,4},{12,2},{14,0},{16,30},{18,... | collective-permute-start | bytes 393224 | tf_op jit(solution)/shard_map/ppermute | solution.py:272
  10.0 11.9 %collective-permute-start.2 = (bf16[64,1024]{1,0:T(8,128)(2,1)}, bf16[64,1024]{1,0:T(8,128)(2,1)S(1)}, u32[]{:S(2)}, u32[]{:S(2)}) collective-permute-start(bf16[64,1024]{1,0:T(8,128)(2,1)} %get-tuple-element.35), channel_id=1, source_target_pairs={{0,28},{2,30},{4,24},{6,26},{8,20},{10,22},{12,16},{14,18},{16,12}... | collective-permute-start | bytes 393224 | tf_op jit(solution)/shard_map/ppermute | solution.py:272
  10.3 12.7 %collective-permute-start.3 = (bf16[64,1024]{1,0:T(8,128)(2,1)}, bf16[64,1024]{1,0:T(8,128)(2,1)S(1)}, u32[]{:S(2)}, u32[]{:S(2)}) collective-permute-start(bf16[64,1024]{1,0:T(8,128)(2,1)} %get-tuple-element.36), channel_id=1, source_target_pairs={{0,12},{2,14},{4,8},{6,10},{8,4},{10,6},{12,0},{14,2},{16,28},{18,... | collective-permute-start | bytes 393224 | tf_op jit(solution)/shard_map/ppermute | solution.py:272
  11.8 14.9 %collective-permute-start.4 = (bf16[64,1024]{1,0:T(8,128)(2,1)}, bf16[64,1024]{1,0:T(8,128)(2,1)S(1)}, u32[]{:S(2)}, u32[]{:S(2)}) collective-permute-start(bf16[64,1024]{1,0:T(8,128)(2,1)} %get-tuple-element.37), channel_id=1, source_target_pairs={{0,26},{2,24},{4,30},{6,28},{8,18},{10,16},{12,22},{14,20},{16,10}... | collective-permute-start | bytes 393224 | tf_op jit(solution)/shard_map/ppermute | solution.py:272
  15.5 15.3 %collective-permute-start.5 = (bf16[64,1024]{1,0:T(8,128)(2,1)}, bf16[64,1024]{1,0:T(8,128)(2,1)S(1)}, u32[]{:S(2)}, u32[]{:S(2)}) collective-permute-start(bf16[64,1024]{1,0:T(8,128)(2,1)} %get-tuple-element.38), channel_id=1, source_target_pairs={{0,10},{2,8},{4,14},{6,12},{8,2},{10,0},{12,6},{14,4},{16,26},{18,... | collective-permute-start | bytes 393224 | tf_op jit(solution)/shard_map/ppermute | solution.py:272
  18.0 15.2 %collective-permute-start.6 = (bf16[64,1024]{1,0:T(8,128)(2,1)}, bf16[64,1024]{1,0:T(8,128)(2,1)S(1)}, u32[]{:S(2)}, u32[]{:S(2)}) collective-permute-start(bf16[64,1024]{1,0:T(8,128)(2,1)} %get-tuple-element.39), channel_id=1, source_target_pairs={{0,24},{2,26},{4,28},{6,30},{8,16},{10,18},{12,20},{14,22},{16,8},... | collective-permute-start | bytes 393224 | tf_op jit(solution)/shard_map/ppermute | solution.py:272
  21.9 12.4 %collective-permute-start.7 = (bf16[64,1024]{1,0:T(8,128)(2,1)}, bf16[64,1024]{1,0:T(8,128)(2,1)S(1)}, u32[]{:S(2)}, u32[]{:S(2)}) collective-permute-start(bf16[64,1024]{1,0:T(8,128)(2,1)} %get-tuple-element.40), channel_id=1, source_target_pairs={{0,8},{2,10},{4,12},{6,14},{8,0},{10,2},{12,4},{14,6},{16,24},{18,... | collective-permute-start | bytes 393224 | tf_op jit(solution)/shard_map/ppermute | solution.py:272
  23.1 19.4 %collective-permute-start.10 = (bf16[64,1024]{1,0:T(8,128)(2,1)}, bf16[64,1024]{1,0:T(8,128)(2,1)S(1)}, u32[]{:S(2)}, u32[]{:S(2)}) collective-permute-start(bf16[64,1024]{1,0:T(8,128)(2,1)} %get-tuple-element.44), channel_id=1, source_target_pairs={{0,22},{2,20},{4,18},{6,16},{8,30},{10,28},{12,26},{14,24},{16,6},... | collective-permute-start | bytes 393224 | tf_op jit(solution)/shard_map/ppermute | solution.py:272
  26.8 16.0 %collective-permute-start.11 = (bf16[64,1024]{1,0:T(8,128)(2,1)}, bf16[64,1024]{1,0:T(8,128)(2,1)S(1)}, u32[]{:S(2)}, u32[]{:S(2)}) collective-permute-start(bf16[64,1024]{1,0:T(8,128)(2,1)} %get-tuple-element.45), channel_id=1, source_target_pairs={{0,6},{2,4},{4,2},{6,0},{8,14},{10,12},{12,10},{14,8},{16,22},{18,... | collective-permute-start | bytes 393224 | tf_op jit(solution)/shard_map/ppermute | solution.py:272
  30.7 16.4 %collective-permute-start.12 = (bf16[64,1024]{1,0:T(8,128)(2,1)}, bf16[64,1024]{1,0:T(8,128)(2,1)S(1)}, u32[]{:S(2)}, u32[]{:S(2)}) collective-permute-start(bf16[64,1024]{1,0:T(8,128)(2,1)} %get-tuple-element.46), channel_id=1, source_target_pairs={{0,20},{2,22},{4,16},{6,18},{8,28},{10,30},{12,24},{14,26},{16,4},... | collective-permute-start | bytes 393224 | tf_op jit(solution)/shard_map/ppermute | solution.py:272
  33.2 14.0 %collective-permute-start.13 = (bf16[64,1024]{1,0:T(8,128)(2,1)}, bf16[64,1024]{1,0:T(8,128)(2,1)S(1)}, u32[]{:S(2)}, u32[]{:S(2)}) collective-permute-start(bf16[64,1024]{1,0:T(8,128)(2,1)} %get-tuple-element.47), channel_id=1, source_target_pairs={{0,4},{2,6},{4,0},{6,2},{8,12},{10,14},{12,8},{14,10},{16,20},{18,... | collective-permute-start | bytes 393224 | tf_op jit(solution)/shard_map/ppermute | solution.py:272
  34.4 16.5 %collective-permute-start.14 = (bf16[64,1024]{1,0:T(8,128)(2,1)}, bf16[64,1024]{1,0:T(8,128)(2,1)S(1)}, u32[]{:S(2)}, u32[]{:S(2)}) collective-permute-start(bf16[64,1024]{1,0:T(8,128)(2,1)} %get-tuple-element.48), channel_id=1, source_target_pairs={{0,18},{2,16},{4,22},{6,20},{8,26},{10,24},{12,30},{14,28},{16,2},... | collective-permute-start | bytes 393224 | tf_op jit(solution)/shard_map/ppermute | solution.py:272
  42.4 8.4 %collective-permute-start.15 = (bf16[64,1024]{1,0:T(8,128)(2,1)}, bf16[64,1024]{1,0:T(8,128)(2,1)S(1)}, u32[]{:S(2)}, u32[]{:S(2)}) collective-permute-start(bf16[64,1024]{1,0:T(8,128)(2,1)} %get-tuple-element.49), channel_id=1, source_target_pairs={{0,2},{2,0},{4,6},{6,4},{8,10},{10,8},{12,14},{14,12},{16,18},{18,... | collective-permute-start | bytes 393224 | tf_op jit(solution)/shard_map/ppermute | solution.py:272
  42.8 10.1 %copy-start.10 = (bf16[64,1024]{1,0:T(8,128)(2,1)S(1)}, bf16[64,1024]{1,0:T(8,128)(2,1)}, u32[]{:S(2)}) copy-start(bf16[64,1024]{1,0:T(8,128)(2,1)} %get-tuple-element.51.refs_7_) | copy-start | bytes 393220
  42.8 10.1 %collective-permute-start.16 = (bf16[64,1024]{1,0:T(8,128)(2,1)}, bf16[64,1024]{1,0:T(8,128)(2,1)S(1)}, u32[]{:S(2)}, u32[]{:S(2)}) collective-permute-start(bf16[64,1024]{1,0:T(8,128)(2,1)} %get-tuple-element.50), channel_id=1, source_target_pairs={{0,16},{2,18},{4,20},{6,22},{8,24},{10,26},{12,28},{14,30},{16,0},... | collective-permute-start | bytes 393224 | tf_op jit(solution)/shard_map/ppermute | solution.py:272
  47.1 5.9 %collective-permute-start.8 = (bf16[512,1024]{1,0:T(8,128)(2,1)S(1)}, bf16[512,1024]{1,0:T(8,128)(2,1)S(1)}, u32[]{:S(2)}, u32[]{:S(2)}) collective-permute-start(bf16[512,1024]{1,0:T(8,128)(2,1)S(1)} %collect.2.own_ref.refs_0_), channel_id=1, source_target_pairs={{0,1},{1,0},{2,3},{3,2},{4,5},{5,4},{6,7},{7,6},{8,9},{9,8},{10,11... | collective-permute-start | bytes 3145736 | tf_op jit(solution)/shard_map/ppermute | solution.py:275
  52.9 2.6 %copy-start = (bf16[1,704,2048]{2,1,0:T(8,128)(2,1)S(1)}, bf16[1,704,2048]{2,1,0:T(8,128)(2,1)}, u32[]{:S(2)}) copy-start(bf16[1,704,2048]{2,1,0:T(8,128)(2,1)} %param.9) | copy-start | bytes 8650756
  52.9 3.4 %copy-start.1 = (bf16[1,704,2048]{2,1,0:T(8,128)(2,1)S(1)}, bf16[1,704,2048]{2,1,0:T(8,128)(2,1)}, u32[]{:S(2)}) copy-start(bf16[1,704,2048]{2,1,0:T(8,128)(2,1)} %param.10) | copy-start | bytes 8650756
  52.9 4.3 %copy-start.3 = (bf16[1,704,2048]{2,1,0:T(8,128)(2,1)S(1)}, bf16[1,704,2048]{2,1,0:T(8,128)(2,1)}, u32[]{:S(2)}) copy-start(bf16[1,704,2048]{2,1,0:T(8,128)(2,1)} %param.11) | copy-start | bytes 8650756
  53.0 8.7 %copy-start.6 = (bf16[512,1024]{1,0:T(8,128)(2,1)}, bf16[512,1024]{1,0:T(8,128)(2,1)S(1)}, u32[]{:S(2)}) copy-start(bf16[512,1024]{1,0:T(8,128)(2,1)S(1)} %collect.3.own_ref.refs_5_) | copy-start | bytes 3145732
  53.0 8.7 %collective-permute-start.17 = (bf16[512,1024]{1,0:T(8,128)(2,1)S(1)}, bf16[512,1024]{1,0:T(8,128)(2,1)S(1)}, u32[]{:S(2)}, u32[]{:S(2)}) collective-permute-start(bf16[512,1024]{1,0:T(8,128)(2,1)S(1)} %collect.3.own_ref.refs_5_), channel_id=1, source_target_pairs={{0,1},{1,0},{2,3},{3,2},{4,5},{5,4},{6,7},{7,6},{8,9},{9,8},{10,11... | collective-permute-start | bytes 3145736 | tf_op jit(solution)/shard_map/ppermute | solution.py:275
  53.1 7.8 %copy-start.4 = (bf16[512,1024]{1,0:T(8,128)(2,1)}, bf16[512,1024]{1,0:T(8,128)(2,1)S(1)}, u32[]{:S(2)}) copy-start(bf16[512,1024]{1,0:T(8,128)(2,1)S(1)} %collective-permute-done.8.other_ref.refs_1_) | copy-start | bytes 3145732
  60.9 0.7 copy-start.11
  61.6 4.3 %collective-permute-start.9 = (bf16[256,1024]{1,0:T(8,128)(2,1)S(1)}, bf16[256,1024]{1,0:T(8,128)(2,1)S(1)}, u32[]{:S(2)}, u32[]{:S(2)}) collective-permute-start(bf16[256,1024]{1,0:T(8,128)(2,1)S(1)} %get-tuple-element.43), channel_id=1, source_target_pairs={{0,1},{1,0},{2,3},{3,2},{4,5},{5,4},{6,7},{7,6},{8,9},{9,8},{10,11... | collective-permute-start | bytes 1572872 | tf_op jit(solution)/shard_map/ppermute | solution.py:275
  61.6 3.7 %copy-start.8 = (bf16[512,1024]{1,0:T(8,128)(2,1)}, bf16[512,1024]{1,0:T(8,128)(2,1)S(1)}, u32[]{:S(2)}) copy-start(bf16[512,1024]{1,0:T(8,128)(2,1)S(1)} %collective-permute-done.17.other_ref.refs_6_) | copy-start | bytes 3145732
  65.4 1.6 %copy-start.13 = (bf16[704,256]{1,0:T(8,128)(2,1)}, bf16[704,256]{1,0:T(8,128)(2,1)S(1)}, u32[]{:S(2)}) copy-start(bf16[704,256]{1,0:T(8,128)(2,1)S(1)} %get-tuple-element.57.refs_9_) | copy-start | bytes 1081348
  65.4 2.1 %collective-permute-start.18 = (bf16[256,1024]{1,0:T(8,128)(2,1)S(1)}, bf16[256,1024]{1,0:T(8,128)(2,1)S(1)}, u32[]{:S(2)}, u32[]{:S(2)}) collective-permute-start(bf16[256,1024]{1,0:T(8,128)(2,1)S(1)} %get-tuple-element.54), channel_id=1, source_target_pairs={{0,1},{1,0},{2,3},{3,2},{4,5},{5,4},{6,7},{7,6},{8,9},{9,8},{10,11... | collective-permute-start | bytes 1572872 | tf_op jit(solution)/shard_map/ppermute | solution.py:275
  69.4 32.0 %all-to-all-start = ((bf16[16,32,1024]{2,1,0:T(8,128)(2,1)}), bf16[16,32,1024]{2,1,0:T(8,128)(2,1)S(1)}, u32[]{:S(2)}, u32[]{:S(2)}) async-start(bf16[16,32,1024]{2,1,0:T(8,128)(2,1)} %bitcast.4), calls=%async_computation | async-start | bytes 2097152 | tf_op jit(solution)/shard_map/all_to_all | solution.py:228
  75.5 1.2 %copy-start.5 = (bf16[512,1024]{1,0:T(8,128)(2,1)S(1)}, bf16[512,1024]{1,0:T(8,128)(2,1)}, u32[]{:S(2)}) copy-start(bf16[512,1024]{1,0:T(8,128)(2,1)} %copy-done.4) | copy-start | bytes 3145732
  76.7 1.2 %copy-start.7 = (bf16[512,1024]{1,0:T(8,128)(2,1)S(1)}, bf16[512,1024]{1,0:T(8,128)(2,1)}, u32[]{:S(2)}) copy-start(bf16[512,1024]{1,0:T(8,128)(2,1)} %copy-done.6) | copy-start | bytes 3145732
  77.9 1.2 %copy-start.9 = (bf16[512,1024]{1,0:T(8,128)(2,1)S(1)}, bf16[512,1024]{1,0:T(8,128)(2,1)}, u32[]{:S(2)}) copy-start(bf16[512,1024]{1,0:T(8,128)(2,1)} %copy-done.8) | copy-start | bytes 3145732
  79.2 1.0 copy-start.12
  80.1 1.0 copy-start.14
  81.1 20.4 %copy-start.2 = (s32[256,1]{0,1:T(1,128)S(1)}, s32[256,1]{0,1:T(1,128)}, u32[]{:S(2)}) copy-start(s32[256,1]{0,1:T(1,128)} %param.8) | copy-start | bytes 3076

commit v8 on v7

--- a/solution.py
+++ b/solution.py
@@ -128,26 +128,27 @@
     ).astype(BF16)
 
 
-def sum_kernel(d_gate_ref, d_up_ref, gate_ref, up_ref, got_ref, out_ref):
+def kept_kernel(d_gate_ref, d_up_ref, gate_ref, up_ref, out_ref):
     columns = side(lax.axis_index("tensor"), out_ref.shape[1])
-    own = input_rows(d_gate_ref, d_up_ref, gate_ref, up_ref, columns)
-    out_ref[...] = (own + got_ref[...].astype(F32)).astype(BF16)
-
-
-def last_sum_kernel(capacity, groups, *refs):
-    *earlier_refs, d_gate_ref, d_up_ref, gate_ref, up_ref, got_ref = refs[:-3]
-    out_ref, done_ref, sum_ref = refs[-3:]
+    out_ref[...] = input_rows(d_gate_ref, d_up_ref, gate_ref, up_ref, columns)
+
+
+def sum_kernel(kept_ref, got_ref, out_ref):
+    out_ref[...] = (kept_ref[...] + got_ref[...].astype(F32)).astype(BF16)
+
+
+def last_sum_kernel(capacity, groups, sum_ref, kept_ref, got_ref, out_ref, done_ref):
     done_ref[...] = jnp.zeros_like(done_ref)
     me = lax.axis_index("expert")
-
-    def put(rows_ref, group):
+    for last, group in enumerate(groups):
         for i, k in enumerate(group):
+            here = slice(i * capacity, (i + 1) * capacity)
             there = pl.ds(pl.multiple_of((me ^ k) * capacity, capacity), capacity)
-            out_ref[there, :] = rows_ref[i * capacity : (i + 1) * capacity, :]
-
-    sum_kernel(d_gate_ref, d_up_ref, gate_ref, up_ref, got_ref, sum_ref)
-    for rows_ref, group in zip((*earlier_refs, sum_ref), groups):
-        put(rows_ref, group)
+            if last:
+                both = kept_ref[here, :] + got_ref[here, :].astype(F32)
+                out_ref[there, :] = both.astype(BF16)
+            else:
+                out_ref[there, :] = sum_ref[here, :]
 
 
 def grads_kernel(sizes, *refs):
@@ -245,7 +246,7 @@
     far = [k for k in reversed(range(1, experts)) if k >= experts // 2]
     near = [k for k in reversed(range(1, experts)) if k < experts // 2]
     turns = [k for pair in zip(far, near) for k in pair] + far[len(near) :]
-    cut = experts // 2
+    cut = 3 * experts // 4
     first, second = turns[:cut], turns[cut:] + [0]
 
     slabs = list(
@@ -274,16 +275,16 @@
     def exchange(values):
         return lax.ppermute(values, "tensor", [(0, 1), (1, 0)])
 
-    def collect(arrived):
+    def collect(arrived, after):
         return pl.pallas_call(
             functools.partial(collect_kernel, capacity, len(arrived)),
             out_shape=jax.ShapeDtypeStruct((2 * len(arrived) * capacity, width), BF16),
-            in_specs=[IN_VMEM] * len(arrived),
+            in_specs=[IN_VMEM] * (len(arrived) + len(after)),
             out_specs=IN_VMEM,
             compiler_params=params(SMALL),
             cost_estimate=cost(COLLECT, len(arrived) * capacity, units, features),
             name="collect",
-        )(*arrived)
+        )(*arrived, *after)
 
     def front(own):
         other = exchange(own)
@@ -298,20 +299,27 @@
             cost_estimate=cost(4, rows, units, features),
             name="front",
         )(own, other, gate_rows, up_rows, down_rows)
-        for_sum = (d_gate, d_up, gate_rows, up_rows, exchange(sent))
-        return (own, other, d_gate, d_up, hidden), for_sum
+        kept = pl.pallas_call(
+            kept_kernel,
+            out_shape=jax.ShapeDtypeStruct((rows, width), F32),
+            in_specs=[IN_VMEM] * 4,
+            out_specs=IN_VMEM,
+            compiler_params=params(SMALL),
+            cost_estimate=cost(1, rows, units, features),
+            name="kept",
+        )(d_gate, d_up, gate_rows, up_rows)
+        return (own, other, d_gate, d_up, hidden), (kept, exchange(sent))
 
     got = {k: swap(k) for k in turns}
     got[0] = slabs[0]
-    for_grads_a, for_sum_a = front(collect([got[k] for k in first]))
-    for_grads_b, for_sum_b = front(collect([got[k] for k in second]))
+    for_grads_a, for_sum_a = front(collect([got[k] for k in first], []))
+    for_grads_b, for_sum_b = front(collect([got[k] for k in second], for_sum_a[:1]))
     sum_a = pl.pallas_call(
         sum_kernel,
         out_shape=jax.ShapeDtypeStruct((len(first) * capacity, width), BF16),
-        in_specs=[IN_VMEM] * 5,
+        in_specs=[IN_VMEM] * 2,
         out_specs=IN_VMEM,
         compiler_params=params(SMALL),
-        cost_estimate=cost(1, len(first) * capacity, units, features),
         name="sum",
     )(*for_sum_a)
     totals, done = pl.pallas_call(
@@ -320,11 +328,9 @@
             jax.ShapeDtypeStruct((experts * capacity, width), BF16),
             jax.ShapeDtypeStruct((8, 128), F32),
         ],
-        in_specs=[IN_VMEM] * 6,
+        in_specs=[IN_VMEM] * 3,
         out_specs=[IN_VMEM] * 2,
-        scratch_shapes=[pltpu.VMEM((len(second) * capacity, width), BF16)],
         compiler_params=params(SMALL),
-        cost_estimate=cost(1, len(second) * capacity, units, features),
         name="last_sum",
     )(sum_a, *for_sum_b)
     returned = to_experts(totals, experts)

time: 104 us -> 99.8 us (0.960)
  local copies, waits for them, and re-layouts: 10.5 us -> 5.62 us
  Pallas kernels: 22.6 us -> 27.2 us
  waiting for transfers between devices: 34.4 us -> 32 us
  starting transfers between devices: 35.1 us -> 33.9 us
    unnamed x30 -> x32, local copies, waits for them, and re-layouts: 10.5 us -> 5.62 us
    ppermute x15, starting transfers between devices: 28.4 us -> 25.1 us  [swap(): lax.ppermute(slabs[k], 'expert', [(e, e ^ k) for e in range(experts)])]
    ppermute x15, waiting for transfers between devices: 20.2 us -> 17.9 us  [swap(): lax.ppermute(slabs[k], 'expert', [(e, e ^ k) for e in range(experts)])]
    pallas_call x1, Pallas kernels: 6.64 us -> 8.91 us  [grouped(): pl.pallas_call(functools.partial(grads_kernel, sizes), grid=(units // til...]
    pallas_call x2, Pallas kernels: 7.4 us -> 9.51 us  [front(): pl.pallas_call(functools.partial(front_kernel, tile), out_shape=[jax.Shap...]
    pallas_call x0 -> x2, Pallas kernels: none -> 2 us  [front(): pl.pallas_call(kept_kernel, out_shape=jax.ShapeDtypeStruct((rows, width),...]
    all_to_all x1, starting transfers between devices: 6.04 us -> 7.9 us  [to_experts(): lax.all_to_all(rows.reshape(experts, rows.shape[0] // experts, rows.shape...]
    all_to_all x1, waiting for transfers between devices: 13.7 us -> 12.1 us  [to_experts(): lax.all_to_all(rows.reshape(experts, rows.shape[0] // experts, rows.shape...]
  transfers between devices with their start and end apart: 20 -> 20, of which waited for: 12 -> 14; matrix products, arithmetic and copies ran while one was open for 0% -> 0% of each run, Pallas kernels for 15% -> 21%
where the time goes in v8:
time: 99.8 us; the launch traced here: 99.5 us
  starting transfers between devices  33.9 us (34%)
  waiting for transfers between devices  32 us (32%)
  Pallas kernels  27.2 us (27%)
  local copies, waits for them, and re-layouts  5.62 us (6%)
    ppermute x15, starting transfers between devices, swap(): lax.ppermute(slabs[k], 'expert', [(e, e ^ k) for e in range(experts)])  25.1 us
    ppermute x15, waiting for transfers between devices, swap(): lax.ppermute(slabs[k], 'expert', [(e, e ^ k) for e in range(experts)])  17.9 us
    all_to_all x1, waiting for transfers between devices, to_experts(): lax.all_to_all(rows.reshape(experts, rows.shape[0] // experts, rows.shape...  12.1 us
    pallas_call x2, Pallas kernels, front(): pl.pallas_call(functools.partial(front_kernel, tile), out_shape=[jax.Shap...  9.51 us
    pallas_call x1, Pallas kernels, grouped(): pl.pallas_call(functools.partial(grads_kernel, sizes), grid=(units // til...  8.91 us
    all_to_all x1, starting transfers between devices, to_experts(): lax.all_to_all(rows.reshape(experts, rows.shape[0] // experts, rows.shape...  7.9 us
    unnamed x32, local copies, waits for them, and re-layouts  5.62 us
    pallas_call x1, Pallas kernels, grouped(): pl.pallas_call(functools.partial(place_kernel, capacity), out_shape=[jax....  3.48 us
  transfers between devices with their start and end apart: 20, of which 14 were waited for; matrix products, arithmetic and copies ran while one was open for 0% of the time, Pallas kernels for 21%

profile of v8, /device:TPU:8, one launch (start us, length us, event | category | flops | bytes accessed | tf_op | source)
XLA Modules:
  0.0 99.5 jit_solution(166267524063986905)
XLA Ops:
  0.6 3.5 %place.1 = (bf16[64,1024]{1,0:T(8,128)(2,1)}, bf16[64,1024]{1,0:T(8,128)(2,1)}, bf16[64,1024]{1,0:T(8,128)(2,1)}, bf16[64,1024]{1,0:T(8,128)(2,1)}, bf16[64,1024...) custom-call(s32[1,256]{1,0:T(1,128)} %bitcast.20, ...), custom_call_target="tpu_custom_call" | custom-call | tf_op jit(solution)/shard_map/place/pallas_call | solution.py:253
  4.1 3.5 %collective-permute-start = (bf16[64,1024]{1,0:T(8,128)(2,1)}, bf16[64,1024]{1,0:T(8,128)(2,1)S(1)}, u32[]{:S(2)}, u32[]{:S(2)}) collective-permute-start(bf16[64,1024]{1,0:T(8,128)(2,1)} %get-tuple-element.33), channel_id=1, source_target_pairs={{0,30},{2,28},{4,26},{6,24},{8,22},{10,20},{12,18},{14,16},{16,14}... | collective-permute-start | bytes 393224 | tf_op jit(solution)/shard_map/ppermute | solution.py:273
  7.6 2.4 %collective-permute-start.1 = (bf16[64,1024]{1,0:T(8,128)(2,1)}, bf16[64,1024]{1,0:T(8,128)(2,1)S(1)}, u32[]{:S(2)}, u32[]{:S(2)}) collective-permute-start(bf16[64,1024]{1,0:T(8,128)(2,1)} %get-tuple-element.34), channel_id=1, source_target_pairs={{0,14},{2,12},{4,10},{6,8},{8,6},{10,4},{12,2},{14,0},{16,30},{18,... | collective-permute-start | bytes 393224 | tf_op jit(solution)/shard_map/ppermute | solution.py:273
  10.0 0.3 collective-permute-start.2
  10.3 1.5 %collective-permute-start.3 = (bf16[64,1024]{1,0:T(8,128)(2,1)}, bf16[64,1024]{1,0:T(8,128)(2,1)S(1)}, u32[]{:S(2)}, u32[]{:S(2)}) collective-permute-start(bf16[64,1024]{1,0:T(8,128)(2,1)} %get-tuple-element.36), channel_id=1, source_target_pairs={{0,12},{2,14},{4,8},{6,10},{8,4},{10,6},{12,0},{14,2},{16,28},{18,... | collective-permute-start | bytes 393224 | tf_op jit(solution)/shard_map/ppermute | solution.py:273
  11.8 2.5 %collective-permute-start.4 = (bf16[64,1024]{1,0:T(8,128)(2,1)}, bf16[64,1024]{1,0:T(8,128)(2,1)S(1)}, u32[]{:S(2)}, u32[]{:S(2)}) collective-permute-start(bf16[64,1024]{1,0:T(8,128)(2,1)} %get-tuple-element.37), channel_id=1, source_target_pairs={{0,26},{2,24},{4,30},{6,28},{8,18},{10,16},{12,22},{14,20},{16,10}... | collective-permute-start | bytes 393224 | tf_op jit(solution)/shard_map/ppermute | solution.py:273
  14.3 1.1 %collective-permute-done.refs_0_ = bf16[64,1024]{1,0:T(8,128)(2,1)S(1)} collective-permute-done((bf16[64,1024]{1,0:T(8,128)(2,1)}, bf16[64,1024]{1,0:T(8,128)(2,1)S(1)}, u32[]{:S(2)}, u32[]{:S(2)}) %collective-permute-start) | collective-permute-done | bytes 131104 | tf_op jit(solution)/shard_map/ppermute | solution.py:273
  15.4 1.3 %collective-permute-start.5 = (bf16[64,1024]{1,0:T(8,128)(2,1)}, bf16[64,1024]{1,0:T(8,128)(2,1)S(1)}, u32[]{:S(2)}, u32[]{:S(2)}) collective-permute-start(bf16[64,1024]{1,0:T(8,128)(2,1)} %get-tuple-element.38), channel_id=1, source_target_pairs={{0,10},{2,8},{4,14},{6,12},{8,2},{10,0},{12,6},{14,4},{16,26},{18,... | collective-permute-start | bytes 393224 | tf_op jit(solution)/shard_map/ppermute | solution.py:273
  16.8 1.2 %collective-permute-done.1.refs_1_ = bf16[64,1024]{1,0:T(8,128)(2,1)S(1)} collective-permute-done((bf16[64,1024]{1,0:T(8,128)(2,1)}, bf16[64,1024]{1,0:T(8,128)(2,1)S(1)}, u32[]{:S(2)}, u32[]{:S(2)}) %collective-permute-start.1) | collective-permute-done | bytes 131104 | tf_op jit(solution)/shard_map/ppermute | solution.py:273
  17.9 0.6 collective-permute-start.6
  18.5 3.4 %collective-permute-done.2.refs_2_ = bf16[64,1024]{1,0:T(8,128)(2,1)S(1)} collective-permute-done((bf16[64,1024]{1,0:T(8,128)(2,1)}, bf16[64,1024]{1,0:T(8,128)(2,1)S(1)}, u32[]{:S(2)}, u32[]{:S(2)}) %collective-permute-start.2) | collective-permute-done | bytes 131104 | tf_op jit(solution)/shard_map/ppermute | solution.py:273
  21.9 0.7 collective-permute-start.7
  22.6 0.5 collective-permute-done.3.refs_3_
  23.1 3.4 %collective-permute-start.8 = (bf16[64,1024]{1,0:T(8,128)(2,1)}, bf16[64,1024]{1,0:T(8,128)(2,1)S(1)}, u32[]{:S(2)}, u32[]{:S(2)}) collective-permute-start(bf16[64,1024]{1,0:T(8,128)(2,1)} %get-tuple-element.41), channel_id=1, source_target_pairs={{0,22},{2,20},{4,18},{6,16},{8,30},{10,28},{12,26},{14,24},{16,6},... | collective-permute-start | bytes 393224 | tf_op jit(solution)/shard_map/ppermute | solution.py:273
  26.4 0.3 collective-permute-done.4.refs_4_
  26.8 3.9 %collective-permute-start.9 = (bf16[64,1024]{1,0:T(8,128)(2,1)}, bf16[64,1024]{1,0:T(8,128)(2,1)S(1)}, u32[]{:S(2)}, u32[]{:S(2)}) collective-permute-start(bf16[64,1024]{1,0:T(8,128)(2,1)} %get-tuple-element.42), channel_id=1, source_target_pairs={{0,6},{2,4},{4,2},{6,0},{8,14},{10,12},{12,10},{14,8},{16,22},{18,... | collective-permute-start | bytes 393224 | tf_op jit(solution)/shard_map/ppermute | solution.py:273
  30.7 2.5 %collective-permute-done.6.refs_6_ = bf16[64,1024]{1,0:T(8,128)(2,1)S(1)} collective-permute-done((bf16[64,1024]{1,0:T(8,128)(2,1)}, bf16[64,1024]{1,0:T(8,128)(2,1)S(1)}, u32[]{:S(2)}, u32[]{:S(2)}) %collective-permute-start.6) | collective-permute-done | bytes 131104 | tf_op jit(solution)/shard_map/ppermute | solution.py:273
  33.2 0.6 collective-permute-start.11
  33.8 0.6 collective-permute-done.7.refs_7_
  34.4 5.3 %collective-permute-done.8.refs_8_ = bf16[64,1024]{1,0:T(8,128)(2,1)S(1)} collective-permute-done((bf16[64,1024]{1,0:T(8,128)(2,1)}, bf16[64,1024]{1,0:T(8,128)(2,1)S(1)}, u32[]{:S(2)}, u32[]{:S(2)}) %collective-permute-start.8) | collective-permute-done | bytes 131104 | tf_op jit(solution)/shard_map/ppermute | solution.py:273
  39.6 2.0 %collective-permute-done.10.refs_10_ = bf16[64,1024]{1,0:T(8,128)(2,1)S(1)} collective-permute-done((bf16[64,1024]{1,0:T(8,128)(2,1)}, bf16[64,1024]{1,0:T(8,128)(2,1)S(1)}, u32[]{:S(2)}, u32[]{:S(2)}) %collective-permute-start.10) | collective-permute-done | bytes 131104 | tf_op jit(solution)/shard_map/ppermute | solution.py:273
  41.6 0.6 collective-permute-done.11.refs_11_
  42.2 0.1 collect.2.own_ref.refs_0_
  42.3 0.1 collective-permute-start.12
  42.4 2.8 %collective-permute-start.14 = (bf16[64,1024]{1,0:T(8,128)(2,1)S(1)}, bf16[64,1024]{1,0:T(8,128)(2,1)S(1)}, u32[]{:S(2)}, u32[]{:S(2)}) collective-permute-start(bf16[64,1024]{1,0:T(8,128)(2,1)S(1)} %copy-done.15), channel_id=1, source_target_pairs={{0,18},{2,16},{4,22},{6,20},{8,26},{10,24},{12,30},{14,28},{16,2},... | collective-permute-start | bytes 393224 | tf_op jit(solution)/shard_map/ppermute | solution.py:273
  45.3 1.6 %collective-permute-start.15 = (bf16[64,1024]{1,0:T(8,128)(2,1)S(1)}, bf16[64,1024]{1,0:T(8,128)(2,1)S(1)}, u32[]{:S(2)}, u32[]{:S(2)}) collective-permute-start(bf16[64,1024]{1,0:T(8,128)(2,1)S(1)} %copy-done.14), channel_id=1, source_target_pairs={{0,2},{2,0},{4,6},{6,4},{8,10},{10,8},{12,14},{14,12},{16,18},{18,... | collective-permute-start | bytes 393224 | tf_op jit(solution)/shard_map/ppermute | solution.py:273
  46.9 0.0 collective-permute-start.16
  46.9 6.3 %front.2 = (bf16[704,384]{1,0:T(8,128)(2,1)S(1)}, bf16[704,384]{1,0:T(8,128)(2,1)S(1)}, bf16[704,384]{1,0:T(8,128)(2,1)S(1)}, bf16[384,1024]{1,0:T(8,128)(2,1)S(1)}) custom-call(bf16[768,1024]{1,0:T(8,128)(2,1)S(1)} %collect.2.own_ref.refs_0_, bf16[768,1024]{1,0:T(8,128)(2,1)S(1)} %collective-permute-done.12.other_ref.refs_1_, ...), custom_call_target="tpu_custom_call" | custom-call | flops 4429185024 | bytes 17825792 | tf_op jit(solution)/shard_map/front/pallas_call | solution.py:292
  53.3 0.8 copy-done.11
  54.1 1.4 %kept.2.kept_ref.refs_4_ = f32[384,1024]{1,0:T(8,128)S(1)} custom-call(bf16[704,384]{1,0:T(8,128)(2,1)S(1)} %get-tuple-element.45.d_gate_ref.refs_2_, bf16[704,384]{1,0:T(8,128)(2,1)S(1)} %get-tuple-element.46.d_up_ref.refs_3_, bf16[704,2048]{1,0:T(8,128)(2,1)S(1)} %bitcast.10, bf16[704,2048]{1,0:T(8,128)(2,1)S(1)} %bitcast.14), custom_call_target="tpu_custom_call" | custom-call | flops 1107296256 | bytes 4456448 | tf_op jit(solution)/shard_map/kept/pallas_call | solution.py:302
  55.5 0.5 collective-permute-done.16.refs_2_
  56.0 0.1 collective-permute-start.17
  56.1 0.5 collective-permute-start.13
  56.6 1.4 %collective-permute-done.17.other_ref.refs_6_ = bf16[256,1024]{1,0:T(8,128)(2,1)S(1)} collective-permute-done((bf16[256,1024]{1,0:T(8,128)(2,1)S(1)}, bf16[256,1024]{1,0:T(8,128)(2,1)S(1)}, u32[]{:S(2)}, u32[]{:S(2)}) %collective-permute-start.17) | collective-permute-done | bytes 524320 | tf_op jit(solution)/shard_map/ppermute | solution.py:276
  58.0 3.2 %front.3 = (bf16[704,128]{1,0:T(8,128)(2,1)S(1)}, bf16[704,128]{1,0:T(8,128)(2,1)S(1)}, bf16[704,128]{1,0:T(8,128)(2,1)S(1)}, bf16[128,1024]{1,0:T(8,128)(2,1)S(1)}) custom-call(bf16[256,1024]{1,0:T(8,128)(2,1)S(1)} %collect.3.own_ref.refs_5_, bf16[256,1024]{1,0:T(8,128)(2,1)S(1)} %collective-permute-done.17.other_ref.refs_6_, ...), custom_call_target="tpu_custom_call" | custom-call | flops 1476395008 | bytes 13631488 | tf_op jit(solution)/shard_map/front/pallas_call | solution.py:292
  61.2 0.2 collective-permute-start.18
  61.4 0.6 kept.3.kept_ref
  62.0 0.1 sum.1.sum_ref
  62.2 0.6 collective-permute-done.18.got_ref
  62.8 1.1 %last_sum.1 = (bf16[512,1024]{1,0:T(8,128)(2,1)}, f32[8,128]{1,0:T(8,128)S(1)}) custom-call(bf16[384,1024]{1,0:T(8,128)(2,1)S(1)} %sum.1.sum_ref, f32[128,1024]{1,0:T(8,128)S(1)} %kept.3.kept_ref, bf16[128,1024]{1,0:T(8,128)(2,1)S(1)} %collective-permute-done.18.got_ref), custom_call_target="tpu_custom_call" | custom-call | tf_op jit(solution)/shard_map/last_sum/pallas_call | solution.py:325
  63.9 7.9 %all-to-all-start = ((bf16[16,32,1024]{2,1,0:T(8,128)(2,1)}), bf16[16,32,1024]{2,1,0:T(8,128)(2,1)S(1)}, u32[]{:S(2)}, u32[]{:S(2)}) async-start(bf16[16,32,1024]{2,1,0:T(8,128)(2,1)} %bitcast.4), calls=%async_computation | async-start | bytes 2097152 | tf_op jit(solution)/shard_map/all_to_all | solution.py:229
  71.8 1.4 %copy-done.5 = bf16[768,1024]{1,0:T(8,128)(2,1)S(1)} copy-done((bf16[768,1024]{1,0:T(8,128)(2,1)S(1)}, bf16[768,1024]{1,0:T(8,128)(2,1)}, u32[]{:S(2)}) %copy-start.5) | copy-done | bytes 1572888
  73.2 1.4 %copy-done.7 = bf16[768,1024]{1,0:T(8,128)(2,1)S(1)} copy-done((bf16[768,1024]{1,0:T(8,128)(2,1)S(1)}, bf16[768,1024]{1,0:T(8,128)(2,1)}, u32[]{:S(2)}) %copy-start.7) | copy-done | bytes 1572888
  74.6 0.9 copy-done.9
  75.5 1.0 %copy-done.12 = bf16[704,384]{1,0:T(8,128)(2,1)S(1)} copy-done((bf16[704,384]{1,0:T(8,128)(2,1)S(1)}, bf16[704,384]{1,0:T(8,128)(2,1)}, u32[]{:S(2)}) %copy-start.12) | copy-done | bytes 540696
  76.6 8.9 %grads.1 = (bf16[704,2048]{1,0:T(8,128)(2,1)}, bf16[704,2048]{1,0:T(8,128)(2,1)}, bf16[704,2048]{1,0:T(8,128)(2,1)}) custom-call(bf16[768,1024]{1,0:T(8,128)(2,1)S(1)} %copy-done.5, bf16[768,1024]{1,0:T(8,128)(2,1)S(1)} %copy-done.7, bf16[704,384]{1,0:T(8,128)(2,1)S(1)} %get-tuple-element.45.d_gate_ref.refs_2_, ...), custom_call_target="tpu_custom_call" | custom-call | flops 4429185024 | bytes 14942208 | tf_op jit(solution)/shard_map/grads/pallas_call | solution.py:344
  85.5 12.1 %all-to-all-done = bf16[16,32,1024]{2,1,0:T(8,128)(2,1)S(1)} async-done(((bf16[16,32,1024]{2,1,0:T(8,128)(2,1)}), bf16[16,32,1024]{2,1,0:T(8,128)(2,1)S(1)}, u32[]{:S(2)}, u32[]{:S(2)}) %all-to-all-start) | async-done | bytes 1048608 | tf_op jit(solution)/shard_map/all_to_all | solution.py:229
  97.6 1.9 %combine.1 = bf16[256,1024]{1,0:T(8,128)(2,1)} custom-call(s32[1,256]{1,0:T(1,128)S(1)} %bitcast.21, bf16[512,1024]{1,0:T(8,128)(2,1)S(1)} %bitcast.17), custom_call_target="tpu_custom_call" | custom-call | tf_op jit(solution)/shard_map/combine/pallas_call | solution.py:217
  (35 shorter events, 0.1 us)
Async XLA Ops:
  4.1 11.3 %collective-permute-start = (bf16[64,1024]{1,0:T(8,128)(2,1)}, bf16[64,1024]{1,0:T(8,128)(2,1)S(1)}, u32[]{:S(2)}, u32[]{:S(2)}) collective-permute-start(bf16[64,1024]{1,0:T(8,128)(2,1)} %get-tuple-element.33), channel_id=1, source_target_pairs={{0,30},{2,28},{4,26},{6,24},{8,22},{10,20},{12,18},{14,16},{16,14}... | collective-permute-start | bytes 393224 | tf_op jit(solution)/shard_map/ppermute | solution.py:273
  7.6 10.3 %collective-permute-start.1 = (bf16[64,1024]{1,0:T(8,128)(2,1)}, bf16[64,1024]{1,0:T(8,128)(2,1)S(1)}, u32[]{:S(2)}, u32[]{:S(2)}) collective-permute-start(bf16[64,1024]{1,0:T(8,128)(2,1)} %get-tuple-element.34), channel_id=1, source_target_pairs={{0,14},{2,12},{4,10},{6,8},{8,6},{10,4},{12,2},{14,0},{16,30},{18,... | collective-permute-start | bytes 393224 | tf_op jit(solution)/shard_map/ppermute | solution.py:273
  10.0 11.9 %collective-permute-start.2 = (bf16[64,1024]{1,0:T(8,128)(2,1)}, bf16[64,1024]{1,0:T(8,128)(2,1)S(1)}, u32[]{:S(2)}, u32[]{:S(2)}) collective-permute-start(bf16[64,1024]{1,0:T(8,128)(2,1)} %get-tuple-element.35), channel_id=1, source_target_pairs={{0,28},{2,30},{4,24},{6,26},{8,20},{10,22},{12,16},{14,18},{16,12}... | collective-permute-start | bytes 393224 | tf_op jit(solution)/shard_map/ppermute | solution.py:273
  10.3 12.7 %collective-permute-start.3 = (bf16[64,1024]{1,0:T(8,128)(2,1)}, bf16[64,1024]{1,0:T(8,128)(2,1)S(1)}, u32[]{:S(2)}, u32[]{:S(2)}) collective-permute-start(bf16[64,1024]{1,0:T(8,128)(2,1)} %get-tuple-element.36), channel_id=1, source_target_pairs={{0,12},{2,14},{4,8},{6,10},{8,4},{10,6},{12,0},{14,2},{16,28},{18,... | collective-permute-start | bytes 393224 | tf_op jit(solution)/shard_map/ppermute | solution.py:273
  11.8 14.9 %collective-permute-start.4 = (bf16[64,1024]{1,0:T(8,128)(2,1)}, bf16[64,1024]{1,0:T(8,128)(2,1)S(1)}, u32[]{:S(2)}, u32[]{:S(2)}) collective-permute-start(bf16[64,1024]{1,0:T(8,128)(2,1)} %get-tuple-element.37), channel_id=1, source_target_pairs={{0,26},{2,24},{4,30},{6,28},{8,18},{10,16},{12,22},{14,20},{16,10}... | collective-permute-start | bytes 393224 | tf_op jit(solution)/shard_map/ppermute | solution.py:273
  15.4 15.3 %collective-permute-start.5 = (bf16[64,1024]{1,0:T(8,128)(2,1)}, bf16[64,1024]{1,0:T(8,128)(2,1)S(1)}, u32[]{:S(2)}, u32[]{:S(2)}) collective-permute-start(bf16[64,1024]{1,0:T(8,128)(2,1)} %get-tuple-element.38), channel_id=1, source_target_pairs={{0,10},{2,8},{4,14},{6,12},{8,2},{10,0},{12,6},{14,4},{16,26},{18,... | collective-permute-start | bytes 393224 | tf_op jit(solution)/shard_map/ppermute | solution.py:273
  17.9 15.2 %collective-permute-start.6 = (bf16[64,1024]{1,0:T(8,128)(2,1)}, bf16[64,1024]{1,0:T(8,128)(2,1)S(1)}, u32[]{:S(2)}, u32[]{:S(2)}) collective-permute-start(bf16[64,1024]{1,0:T(8,128)(2,1)} %get-tuple-element.39), channel_id=1, source_target_pairs={{0,24},{2,26},{4,28},{6,30},{8,16},{10,18},{12,20},{14,22},{16,8},... | collective-permute-start | bytes 393224 | tf_op jit(solution)/shard_map/ppermute | solution.py:273
  21.9 12.4 %collective-permute-start.7 = (bf16[64,1024]{1,0:T(8,128)(2,1)}, bf16[64,1024]{1,0:T(8,128)(2,1)S(1)}, u32[]{:S(2)}, u32[]{:S(2)}) collective-permute-start(bf16[64,1024]{1,0:T(8,128)(2,1)} %get-tuple-element.40), channel_id=1, source_target_pairs={{0,8},{2,10},{4,12},{6,14},{8,0},{10,2},{12,4},{14,6},{16,24},{18,... | collective-permute-start | bytes 393224 | tf_op jit(solution)/shard_map/ppermute | solution.py:273
  23.1 16.5 %collective-permute-start.8 = (bf16[64,1024]{1,0:T(8,128)(2,1)}, bf16[64,1024]{1,0:T(8,128)(2,1)S(1)}, u32[]{:S(2)}, u32[]{:S(2)}) collective-permute-start(bf16[64,1024]{1,0:T(8,128)(2,1)} %get-tuple-element.41), channel_id=1, source_target_pairs={{0,22},{2,20},{4,18},{6,16},{8,30},{10,28},{12,26},{14,24},{16,6},... | collective-permute-start | bytes 393224 | tf_op jit(solution)/shard_map/ppermute | solution.py:273
  26.8 12.8 %collective-permute-start.9 = (bf16[64,1024]{1,0:T(8,128)(2,1)}, bf16[64,1024]{1,0:T(8,128)(2,1)S(1)}, u32[]{:S(2)}, u32[]{:S(2)}) collective-permute-start(bf16[64,1024]{1,0:T(8,128)(2,1)} %get-tuple-element.42), channel_id=1, source_target_pairs={{0,6},{2,4},{4,2},{6,0},{8,14},{10,12},{12,10},{14,8},{16,22},{18,... | collective-permute-start | bytes 393224 | tf_op jit(solution)/shard_map/ppermute | solution.py:273
  30.7 10.9 %collective-permute-start.10 = (bf16[64,1024]{1,0:T(8,128)(2,1)}, bf16[64,1024]{1,0:T(8,128)(2,1)S(1)}, u32[]{:S(2)}, u32[]{:S(2)}) collective-permute-start(bf16[64,1024]{1,0:T(8,128)(2,1)} %get-tuple-element.43), channel_id=1, source_target_pairs={{0,20},{2,22},{4,16},{6,18},{8,28},{10,30},{12,24},{14,26},{16,4},... | collective-permute-start | bytes 393224 | tf_op jit(solution)/shard_map/ppermute | solution.py:273
  33.2 9.2 %copy-start.15 = (bf16[64,1024]{1,0:T(8,128)(2,1)S(1)}, bf16[64,1024]{1,0:T(8,128)(2,1)}, u32[]{:S(2)}) copy-start(bf16[64,1024]{1,0:T(8,128)(2,1)} %get-tuple-element.48) | copy-start | bytes 393220
  33.2 12.1 %copy-start.14 = (bf16[64,1024]{1,0:T(8,128)(2,1)S(1)}, bf16[64,1024]{1,0:T(8,128)(2,1)}, u32[]{:S(2)}) copy-start(bf16[64,1024]{1,0:T(8,128)(2,1)} %get-tuple-element.49) | copy-start | bytes 393220
  33.2 13.7 %copy-start.13 = (bf16[64,1024]{1,0:T(8,128)(2,1)S(1)}, bf16[64,1024]{1,0:T(8,128)(2,1)}, u32[]{:S(2)}) copy-start(bf16[64,1024]{1,0:T(8,128)(2,1)} %get-tuple-element.50) | copy-start | bytes 393220
  33.2 13.7 %copy-start = (bf16[1,704,2048]{2,1,0:T(8,128)(2,1)S(1)}, bf16[1,704,2048]{2,1,0:T(8,128)(2,1)}, u32[]{:S(2)}) copy-start(bf16[1,704,2048]{2,1,0:T(8,128)(2,1)} %param.9) | copy-start | bytes 8650756
  33.2 13.7 %copy-start.1 = (bf16[1,704,2048]{2,1,0:T(8,128)(2,1)S(1)}, bf16[1,704,2048]{2,1,0:T(8,128)(2,1)}, u32[]{:S(2)}) copy-start(bf16[1,704,2048]{2,1,0:T(8,128)(2,1)} %param.10) | copy-start | bytes 8650756
  33.2 13.7 %copy-start.2 = (bf16[1,704,2048]{2,1,0:T(8,128)(2,1)S(1)}, bf16[1,704,2048]{2,1,0:T(8,128)(2,1)}, u32[]{:S(2)}) copy-start(bf16[1,704,2048]{2,1,0:T(8,128)(2,1)} %param.11) | copy-start | bytes 8650756
  33.2 9.0 %collective-permute-start.11 = (bf16[64,1024]{1,0:T(8,128)(2,1)}, bf16[64,1024]{1,0:T(8,128)(2,1)S(1)}, u32[]{:S(2)}, u32[]{:S(2)}) collective-permute-start(bf16[64,1024]{1,0:T(8,128)(2,1)} %get-tuple-element.44), channel_id=1, source_target_pairs={{0,4},{2,6},{4,0},{6,2},{8,12},{10,14},{12,8},{14,10},{16,20},{18,... | collective-permute-start | bytes 393224 | tf_op jit(solution)/shard_map/ppermute | solution.py:273
  42.3 10.9 %copy-start.4 = (bf16[768,1024]{1,0:T(8,128)(2,1)}, bf16[768,1024]{1,0:T(8,128)(2,1)S(1)}, u32[]{:S(2)}) copy-start(bf16[768,1024]{1,0:T(8,128)(2,1)S(1)} %collect.2.own_ref.refs_0_) | copy-start | bytes 4718596
  42.3 4.6 %collective-permute-start.12 = (bf16[768,1024]{1,0:T(8,128)(2,1)S(1)}, bf16[768,1024]{1,0:T(8,128)(2,1)S(1)}, u32[]{:S(2)}, u32[]{:S(2)}) collective-permute-start(bf16[768,1024]{1,0:T(8,128)(2,1)S(1)} %collect.2.own_ref.refs_0_), channel_id=1, source_target_pairs={{0,1},{1,0},{2,3},{3,2},{4,5},{5,4},{6,7},{7,6},{8,9},{9,8},{10,11... | collective-permute-start | bytes 4718600 | tf_op jit(solution)/shard_map/ppermute | solution.py:276
  42.4 13.1 %collective-permute-start.14 = (bf16[64,1024]{1,0:T(8,128)(2,1)S(1)}, bf16[64,1024]{1,0:T(8,128)(2,1)S(1)}, u32[]{:S(2)}, u32[]{:S(2)}) collective-permute-start(bf16[64,1024]{1,0:T(8,128)(2,1)S(1)} %copy-done.15), channel_id=1, source_target_pairs={{0,18},{2,16},{4,22},{6,20},{8,26},{10,24},{12,30},{14,28},{16,2},... | collective-permute-start | bytes 393224 | tf_op jit(solution)/shard_map/ppermute | solution.py:273
  45.3 10.2 %collective-permute-start.15 = (bf16[64,1024]{1,0:T(8,128)(2,1)S(1)}, bf16[64,1024]{1,0:T(8,128)(2,1)S(1)}, u32[]{:S(2)}, u32[]{:S(2)}) collective-permute-start(bf16[64,1024]{1,0:T(8,128)(2,1)S(1)} %copy-done.14), channel_id=1, source_target_pairs={{0,2},{2,0},{4,6},{6,4},{8,10},{10,8},{12,14},{14,12},{16,18},{18,... | collective-permute-start | bytes 393224 | tf_op jit(solution)/shard_map/ppermute | solution.py:273
  46.9 9.1 %collective-permute-start.16 = (bf16[64,1024]{1,0:T(8,128)(2,1)S(1)}, bf16[64,1024]{1,0:T(8,128)(2,1)S(1)}, u32[]{:S(2)}, u32[]{:S(2)}) collective-permute-start(bf16[64,1024]{1,0:T(8,128)(2,1)S(1)} %copy-done.13), channel_id=1, source_target_pairs={{0,16},{2,18},{4,20},{6,22},{8,24},{10,26},{12,28},{14,30},{16,0},... | collective-permute-start | bytes 393224 | tf_op jit(solution)/shard_map/ppermute | solution.py:273
  46.9 6.4 %copy-start.6 = (bf16[768,1024]{1,0:T(8,128)(2,1)}, bf16[768,1024]{1,0:T(8,128)(2,1)S(1)}, u32[]{:S(2)}) copy-start(bf16[768,1024]{1,0:T(8,128)(2,1)S(1)} %collective-permute-done.12.other_ref.refs_1_) | copy-start | bytes 4718596
  53.3 0.8 copy-start.11
  54.1 1.9 %copy-start.10 = (bf16[64,1024]{1,0:T(8,128)(2,1)S(1)}, bf16[64,1024]{1,0:T(8,128)(2,1)}, u32[]{:S(2)}) copy-start(bf16[64,1024]{1,0:T(8,128)(2,1)} %get-tuple-element.51.refs_3_) | copy-start | bytes 393220
  56.0 2.0 %collective-permute-start.17 = (bf16[256,1024]{1,0:T(8,128)(2,1)S(1)}, bf16[256,1024]{1,0:T(8,128)(2,1)S(1)}, u32[]{:S(2)}, u32[]{:S(2)}) collective-permute-start(bf16[256,1024]{1,0:T(8,128)(2,1)S(1)} %collect.3.own_ref.refs_5_), channel_id=1, source_target_pairs={{0,1},{1,0},{2,3},{3,2},{4,5},{5,4},{6,7},{7,6},{8,9},{9,8},{10,11... | collective-permute-start | bytes 1572872 | tf_op jit(solution)/shard_map/ppermute | solution.py:276
  56.1 5.9 %collective-permute-start.13 = (bf16[384,1024]{1,0:T(8,128)(2,1)S(1)}, bf16[384,1024]{1,0:T(8,128)(2,1)S(1)}, u32[]{:S(2)}, u32[]{:S(2)}) collective-permute-start(bf16[384,1024]{1,0:T(8,128)(2,1)S(1)} %get-tuple-element.47), channel_id=1, source_target_pairs={{0,1},{1,0},{2,3},{3,2},{4,5},{5,4},{6,7},{7,6},{8,9},{9,8},{10,11... | collective-permute-start | bytes 2359304 | tf_op jit(solution)/shard_map/ppermute | solution.py:276
  61.2 0.8 copy-start.8
  61.2 1.6 %collective-permute-start.18 = (bf16[128,1024]{1,0:T(8,128)(2,1)S(1)}, bf16[128,1024]{1,0:T(8,128)(2,1)S(1)}, u32[]{:S(2)}, u32[]{:S(2)}) collective-permute-start(bf16[128,1024]{1,0:T(8,128)(2,1)S(1)} %get-tuple-element.54), channel_id=1, source_target_pairs={{0,1},{1,0},{2,3},{3,2},{4,5},{5,4},{6,7},{7,6},{8,9},{9,8},{10,11... | collective-permute-start | bytes 786440 | tf_op jit(solution)/shard_map/ppermute | solution.py:276
  63.9 33.7 %all-to-all-start = ((bf16[16,32,1024]{2,1,0:T(8,128)(2,1)}), bf16[16,32,1024]{2,1,0:T(8,128)(2,1)S(1)}, u32[]{:S(2)}, u32[]{:S(2)}) async-start(bf16[16,32,1024]{2,1,0:T(8,128)(2,1)} %bitcast.4), calls=%async_computation | async-start | bytes 2097152 | tf_op jit(solution)/shard_map/all_to_all | solution.py:229
  71.8 1.4 %copy-start.5 = (bf16[768,1024]{1,0:T(8,128)(2,1)S(1)}, bf16[768,1024]{1,0:T(8,128)(2,1)}, u32[]{:S(2)}) copy-start(bf16[768,1024]{1,0:T(8,128)(2,1)} %copy-done.4) | copy-start | bytes 4718596
  73.2 1.4 %copy-start.7 = (bf16[768,1024]{1,0:T(8,128)(2,1)S(1)}, bf16[768,1024]{1,0:T(8,128)(2,1)}, u32[]{:S(2)}) copy-start(bf16[768,1024]{1,0:T(8,128)(2,1)} %copy-done.6) | copy-start | bytes 4718596
  74.6 0.9 copy-start.9
  75.5 1.0 %copy-start.12 = (bf16[704,384]{1,0:T(8,128)(2,1)S(1)}, bf16[704,384]{1,0:T(8,128)(2,1)}, u32[]{:S(2)}) copy-start(bf16[704,384]{1,0:T(8,128)(2,1)} %copy-done.11) | copy-start | bytes 1622020
  76.6 21.0 %copy-start.3 = (s32[256,1]{0,1:T(1,128)S(1)}, s32[256,1]{0,1:T(1,128)}, u32[]{:S(2)}) copy-start(s32[256,1]{0,1:T(1,128)} %param.8) | copy-start | bytes 3076

commit v9 on v8

--- a/solution.py
+++ b/solution.py
@@ -90,31 +90,51 @@
     )
 
 
-def front_kernel(
-    tile, own_ref, other_ref, gate_ref, up_ref, down_ref, hidden_ref, d_gate_ref, d_up_ref, sent_ref
-):
+OVER_FEATURES = (((1,), (1,)), ((), ()))
+
+
+def begin_kernel(tile, own_ref, gate_ref, up_ref, down_ref, *out_refs):
+    rows, width = out_refs[0].shape[1], own_ref.shape[1]
+    columns = side(lax.axis_index("tensor"), width)
+
+    @pl.loop(0, gate_ref.shape[0] // tile)
+    def _(step):
+        units = pl.ds(pl.multiple_of(step * tile, tile), tile)
+        for weight_ref, out_ref, start in zip(
+            (gate_ref, up_ref, down_ref), out_refs, (0, 0, rows)
+        ):
+            out_ref[units, :] = lax.dot_general(
+                weight_ref[units, columns],
+                own_ref[start : start + rows, :],
+                OVER_FEATURES,
+                preferred_element_type=F32,
+            )
+
+
+def front_kernel(tile, own_ref, other_ref, gate_ref, up_ref, down_ref, *refs):
+    *begun_refs, hidden_ref, d_gate_ref, d_up_ref, sent_ref = refs
     rows, width = sent_ref.shape
     mine = lax.axis_index("tensor")
-    over_features = (((1,), (1,)), ((), ()))
 
     @pl.loop(0, hidden_ref.shape[0] // tile)
     def _(step):
         units = pl.ds(pl.multiple_of(step * tile, tile), tile)
 
-        def product(weight_ref, start):
-            return sum(
-                lax.dot_general(
-                    weight_ref[units, side(which, width)],
+        def product(which, weight_ref, start):
+            def share(half_ref, half):
+                return lax.dot_general(
+                    weight_ref[units, side(half, width)],
                     half_ref[start : start + rows, :],
-                    over_features,
+                    OVER_FEATURES,
                     preferred_element_type=F32,
                 )
-                for which, half_ref in ((mine, own_ref), (1 - mine, other_ref))
-            )
-
-        gate_pre = product(gate_ref, 0)
-        up_pre = product(up_ref, 0)
-        d_hidden = product(down_ref, rows)
+
+            own = begun_refs[which][units, :] if begun_refs else share(own_ref, mine)
+            return own + share(other_ref, 1 - mine)
+
+        gate_pre = product(0, gate_ref, 0)
+        up_pre = product(1, up_ref, 0)
+        d_hidden = product(2, down_ref, rows)
         sig = jax.nn.sigmoid(gate_pre)
         silu = gate_pre * sig
         hidden_ref[units, :] = (silu * up_pre).astype(BF16)
@@ -173,9 +193,14 @@
         grad_down_ref[:, side(which, width)] = total(4, half, 1)
 
 
-def combine_kernel(capacity, row_ref, back_hbm, out_ref, back_ref, sems):
-    slots = back_ref.shape[0]
-    step = slots // PIECES
+def placing_kernel(capacity, row_ref, _, placing_ref):
+    route, within = rank_among_same(row_ref[...], 1)
+    slot = lax.broadcasted_iota(jnp.int32, placing_ref.shape, 1)
+    placing_ref[...] = jnp.where(slot == route * capacity + within, 1.0, 0.0).astype(BF16)
+
+
+def combine_kernel(placing_ref, back_hbm, out_ref, back_ref, sems):
+    step = back_ref.shape[0] // PIECES
     copies = [
         pltpu.make_async_copy(
             back_hbm.at[i * step : (i + 1) * step],
@@ -186,14 +211,11 @@
     ]
     for copy in copies:
         copy.start()
-    route, within = rank_among_same(row_ref[...], 1)
-    slot = lax.broadcasted_iota(jnp.int32, (out_ref.shape[0], slots), 1)
-    placing = jnp.where(slot == route * capacity + within, 1.0, 0.0).astype(BF16)
     total = jnp.zeros(out_ref.shape, F32)
     for i, copy in enumerate(copies):
         copy.wait()
         total += jnp.dot(
-            placing[:, i * step : (i + 1) * step],
+            placing_ref[:, i * step : (i + 1) * step],
             back_ref[i * step : (i + 1) * step],
             preferred_element_type=F32,
         )
@@ -212,17 +234,28 @@
     )
 
 
-def combine(capacity, ids_row, returned, tok_rows):
+def placing_of(capacity, ids_row, slots, after):
+    return pl.pallas_call(
+        functools.partial(placing_kernel, capacity),
+        out_shape=jax.ShapeDtypeStruct((ids_row.shape[1], slots), BF16),
+        in_specs=[IN_VMEM] * 2,
+        out_specs=IN_VMEM,
+        compiler_params=params(SMALL),
+        name="placing",
+    )(ids_row, after)
+
+
+def combine(placing, returned):
     slots, width = returned.shape
     return pl.pallas_call(
-        functools.partial(combine_kernel, capacity),
-        out_shape=jax.ShapeDtypeStruct((tok_rows, width), BF16),
+        combine_kernel,
+        out_shape=jax.ShapeDtypeStruct((placing.shape[0], width), BF16),
         in_specs=[IN_VMEM, IN_HBM],
         out_specs=IN_VMEM,
         scratch_shapes=[pltpu.VMEM((slots, width), BF16), pltpu.SemaphoreType.DMA((PIECES,))],
         compiler_params=params(SMALL),
         name="combine",
-    )(ids_row, returned)
+    )(placing, returned)
 
 
 def to_experts(rows, experts):
@@ -286,19 +319,31 @@
             name="collect",
         )(*arrived, *after)
 
-    def front(own):
+    def begin(own):
+        rows = own.shape[0] // 2
+        return pl.pallas_call(
+            functools.partial(begin_kernel, tile),
+            out_shape=[jax.ShapeDtypeStruct((units, rows), F32)] * 3,
+            in_specs=[IN_VMEM] * 4,
+            out_specs=[IN_VMEM] * 3,
+            compiler_params=params(SMALL),
+            cost_estimate=cost(2, rows, units, features),
+            name="begin",
+        )(own, gate_rows, up_rows, down_rows)
+
+    def front(own, begun):
         other = exchange(own)
         rows = own.shape[0] // 2
         hidden, d_gate, d_up, sent = pl.pallas_call(
             functools.partial(front_kernel, tile),
             out_shape=[jax.ShapeDtypeStruct((units, rows), BF16)] * 3
             + [jax.ShapeDtypeStruct((rows, width), BF16)],
-            in_specs=[IN_VMEM] * 5,
+            in_specs=[IN_VMEM] * (5 + len(begun)),
             out_specs=[IN_VMEM] * 4,
             compiler_params=params(SMALL),
             cost_estimate=cost(4, rows, units, features),
             name="front",
-        )(own, other, gate_rows, up_rows, down_rows)
+        )(own, other, gate_rows, up_rows, down_rows, *begun)
         kept = pl.pallas_call(
             kept_kernel,
             out_shape=jax.ShapeDtypeStruct((rows, width), F32),
@@ -312,8 +357,9 @@
 
     got = {k: swap(k) for k in turns}
     got[0] = slabs[0]
-    for_grads_a, for_sum_a = front(collect([got[k] for k in first], []))
-    for_grads_b, for_sum_b = front(collect([got[k] for k in second], for_sum_a[:1]))
+    for_grads_a, for_sum_a = front(collect([got[k] for k in first], []), [])
+    own_b = collect([got[k] for k in second], for_sum_a[:1])
+    for_grads_b, for_sum_b = front(own_b, begin(own_b))
     sum_a = pl.pallas_call(
         sum_kernel,
         out_shape=jax.ShapeDtypeStruct((len(first) * capacity, width), BF16),
@@ -334,6 +380,7 @@
         name="last_sum",
     )(sum_a, *for_sum_b)
     returned = to_experts(totals, experts)
+    placing = placing_of(capacity, ids_row, experts * capacity, done)
 
     def grads_specs(rows):
         return [pl.BlockSpec((2 * rows, width), lambda i: (0, 0))] * 2 + [
@@ -347,13 +394,13 @@
         out_shape=[jax.ShapeDtypeStruct((units, features), BF16)] * 3,
         in_specs=grads_specs(sizes[0])
         + grads_specs(sizes[1])
-        + [pl.BlockSpec((8, 128), lambda i: (0, 0))],
+        + [pl.BlockSpec(placing.shape, lambda i: (0, 0))],
         out_specs=[pl.BlockSpec((tile, features), lambda i: (i, 0))] * 3,
         compiler_params=params(2 * SMALL),
         cost_estimate=cost(3, sum(sizes), units, features),
         name="grads",
-    )(*for_grads_a, *for_grads_b, done)
-    return combine(capacity, ids_row, returned, tok_rows), grads
+    )(*for_grads_a, *for_grads_b, placing)
+    return combine(placing, returned), grads
 
 
 def rows_by_weights(rows, weights):

time: 99.8 us -> 99.3 us (level)
  waiting for transfers between devices: 32 us -> 29.2 us
  local copies, waits for them, and re-layouts: 5.62 us -> 7.37 us
    all_to_all x1, waiting for transfers between devices: 12.1 us -> 9.92 us  [to_experts(): lax.all_to_all(rows.reshape(experts, rows.shape[0] // experts, rows.shape...]
    unnamed x32 -> x40, local copies, waits for them, and re-layouts: 5.62 us -> 7.37 us
    pallas_call x1 -> x3, Pallas kernels: 1.93 us -> 3.37 us  [the longest x1 1.67 us: combine(): pl.pallas_call(combine_kernel, out_shape=jax.ShapeDtypeStruct((placing.sh...]
    ppermute x4, waiting for transfers between devices: 2.05 us -> 0.68 us  [exchange(): return lax.ppermute(values, 'tensor', [(0, 1), (1, 0)])]
    pallas_call x2, Pallas kernels: 9.51 us -> 8.41 us  [front(): pl.pallas_call(functools.partial(front_kernel, tile), out_shape=[jax.Shap...]
  transfers between devices with their start and end apart: 20 -> 20, of which waited for: 14 -> 13; matrix products, arithmetic and copies ran while one was open for 0% -> 0% of each run, Pallas kernels for 21% -> 21%
where the time goes in v9:
time: 99.3 us; the launch traced here: 98.9 us
  starting transfers between devices  33.8 us (34%)
  waiting for transfers between devices  29.2 us (29%)
  Pallas kernels  27.6 us (28%)
  local copies, waits for them, and re-layouts  7.37 us (7%)
  between operations  1.02 us (1%)
    ppermute x15, starting transfers between devices, swap(): lax.ppermute(slabs[k], 'expert', [(e, e ^ k) for e in range(experts)])  25.1 us
    ppermute x15, waiting for transfers between devices, swap(): lax.ppermute(slabs[k], 'expert', [(e, e ^ k) for e in range(experts)])  18.6 us
    all_to_all x1, waiting for transfers between devices, to_experts(): lax.all_to_all(rows.reshape(experts, rows.shape[0] // experts, rows.shape...  9.92 us
    pallas_call x1, Pallas kernels, grouped(): pl.pallas_call(functools.partial(grads_kernel, sizes), grid=(units // til...  8.91 us
    pallas_call x2, Pallas kernels, front(): pl.pallas_call(functools.partial(front_kernel, tile), out_shape=[jax.Shap...  8.41 us
    all_to_all x1, starting transfers between devices, to_experts(): lax.all_to_all(rows.reshape(experts, rows.shape[0] // experts, rows.shape...  7.89 us
    unnamed x40, local copies, waits for them, and re-layouts  7.37 us
    pallas_call x1, Pallas kernels, grouped(): pl.pallas_call(functools.partial(place_kernel, capacity), out_shape=[jax....  3.5 us
  transfers between devices with their start and end apart: 20, of which 13 were waited for; matrix products, arithmetic and copies ran while one was open for 0% of the time, Pallas kernels for 21%

profile of v9, /device:TPU:8, one launch (start us, length us, event | category | flops | bytes accessed | tf_op | source)
XLA Modules:
  0.0 98.9 jit_solution(12807456701802941461)
XLA Ops:
  0.6 3.5 %place.1 = (bf16[64,1024]{1,0:T(8,128)(2,1)}, bf16[64,1024]{1,0:T(8,128)(2,1)}, bf16[64,1024]{1,0:T(8,128)(2,1)}, bf16[64,1024]{1,0:T(8,128)(2,1)}, bf16[64,1024...) custom-call(s32[1,256]{1,0:T(1,128)} %bitcast.23, ...), custom_call_target="tpu_custom_call" | custom-call | tf_op jit(solution)/shard_map/place/pallas_call | solution.py:286
  4.1 3.5 %collective-permute-start = (bf16[64,1024]{1,0:T(8,128)(2,1)}, bf16[64,1024]{1,0:T(8,128)(2,1)S(1)}, u32[]{:S(2)}, u32[]{:S(2)}) collective-permute-start(bf16[64,1024]{1,0:T(8,128)(2,1)} %get-tuple-element.36), channel_id=1, source_target_pairs={{0,30},{2,28},{4,26},{6,24},{8,22},{10,20},{12,18},{14,16},{16,14}... | collective-permute-start | bytes 393224 | tf_op jit(solution)/shard_map/ppermute | solution.py:306
  7.7 2.4 %collective-permute-start.1 = (bf16[64,1024]{1,0:T(8,128)(2,1)}, bf16[64,1024]{1,0:T(8,128)(2,1)S(1)}, u32[]{:S(2)}, u32[]{:S(2)}) collective-permute-start(bf16[64,1024]{1,0:T(8,128)(2,1)} %get-tuple-element.37), channel_id=1, source_target_pairs={{0,14},{2,12},{4,10},{6,8},{8,6},{10,4},{12,2},{14,0},{16,30},{18,... | collective-permute-start | bytes 393224 | tf_op jit(solution)/shard_map/ppermute | solution.py:306
  10.1 0.3 collective-permute-start.2
  10.3 1.5 %collective-permute-start.3 = (bf16[64,1024]{1,0:T(8,128)(2,1)}, bf16[64,1024]{1,0:T(8,128)(2,1)S(1)}, u32[]{:S(2)}, u32[]{:S(2)}) collective-permute-start(bf16[64,1024]{1,0:T(8,128)(2,1)} %get-tuple-element.39), channel_id=1, source_target_pairs={{0,12},{2,14},{4,8},{6,10},{8,4},{10,6},{12,0},{14,2},{16,28},{18,... | collective-permute-start | bytes 393224 | tf_op jit(solution)/shard_map/ppermute | solution.py:306
  11.8 2.5 %collective-permute-start.4 = (bf16[64,1024]{1,0:T(8,128)(2,1)}, bf16[64,1024]{1,0:T(8,128)(2,1)S(1)}, u32[]{:S(2)}, u32[]{:S(2)}) collective-permute-start(bf16[64,1024]{1,0:T(8,128)(2,1)} %get-tuple-element.40), channel_id=1, source_target_pairs={{0,26},{2,24},{4,30},{6,28},{8,18},{10,16},{12,22},{14,20},{16,10}... | collective-permute-start | bytes 393224 | tf_op jit(solution)/shard_map/ppermute | solution.py:306
  14.4 1.1 %collective-permute-done.refs_0_ = bf16[64,1024]{1,0:T(8,128)(2,1)S(1)} collective-permute-done((bf16[64,1024]{1,0:T(8,128)(2,1)}, bf16[64,1024]{1,0:T(8,128)(2,1)S(1)}, u32[]{:S(2)}, u32[]{:S(2)}) %collective-permute-start) | collective-permute-done | bytes 131104 | tf_op jit(solution)/shard_map/ppermute | solution.py:306
  15.5 1.4 %collective-permute-start.5 = (bf16[64,1024]{1,0:T(8,128)(2,1)}, bf16[64,1024]{1,0:T(8,128)(2,1)S(1)}, u32[]{:S(2)}, u32[]{:S(2)}) collective-permute-start(bf16[64,1024]{1,0:T(8,128)(2,1)} %get-tuple-element.41), channel_id=1, source_target_pairs={{0,10},{2,8},{4,14},{6,12},{8,2},{10,0},{12,6},{14,4},{16,26},{18,... | collective-permute-start | bytes 393224 | tf_op jit(solution)/shard_map/ppermute | solution.py:306
  16.8 1.2 %collective-permute-done.1.refs_1_ = bf16[64,1024]{1,0:T(8,128)(2,1)S(1)} collective-permute-done((bf16[64,1024]{1,0:T(8,128)(2,1)}, bf16[64,1024]{1,0:T(8,128)(2,1)S(1)}, u32[]{:S(2)}, u32[]{:S(2)}) %collective-permute-start.1) | collective-permute-done | bytes 131104 | tf_op jit(solution)/shard_map/ppermute | solution.py:306
  18.0 0.6 collective-permute-start.6
  18.5 3.4 %collective-permute-done.2.refs_2_ = bf16[64,1024]{1,0:T(8,128)(2,1)S(1)} collective-permute-done((bf16[64,1024]{1,0:T(8,128)(2,1)}, bf16[64,1024]{1,0:T(8,128)(2,1)S(1)}, u32[]{:S(2)}, u32[]{:S(2)}) %collective-permute-start.2) | collective-permute-done | bytes 131104 | tf_op jit(solution)/shard_map/ppermute | solution.py:306
  21.9 0.7 collective-permute-start.7
  22.6 0.5 collective-permute-done.3.refs_3_
  23.1 3.4 %collective-permute-start.8 = (bf16[64,1024]{1,0:T(8,128)(2,1)}, bf16[64,1024]{1,0:T(8,128)(2,1)S(1)}, u32[]{:S(2)}, u32[]{:S(2)}) collective-permute-start(bf16[64,1024]{1,0:T(8,128)(2,1)} %get-tuple-element.44), channel_id=1, source_target_pairs={{0,22},{2,20},{4,18},{6,16},{8,30},{10,28},{12,26},{14,24},{16,6},... | collective-permute-start | bytes 393224 | tf_op jit(solution)/shard_map/ppermute | solution.py:306
  26.5 0.3 collective-permute-done.4.refs_4_
  26.8 3.9 %collective-permute-start.9 = (bf16[64,1024]{1,0:T(8,128)(2,1)}, bf16[64,1024]{1,0:T(8,128)(2,1)S(1)}, u32[]{:S(2)}, u32[]{:S(2)}) collective-permute-start(bf16[64,1024]{1,0:T(8,128)(2,1)} %get-tuple-element.45), channel_id=1, source_target_pairs={{0,6},{2,4},{4,2},{6,0},{8,14},{10,12},{12,10},{14,8},{16,22},{18,... | collective-permute-start | bytes 393224 | tf_op jit(solution)/shard_map/ppermute | solution.py:306
  30.7 2.5 %collective-permute-done.6.refs_6_ = bf16[64,1024]{1,0:T(8,128)(2,1)S(1)} collective-permute-done((bf16[64,1024]{1,0:T(8,128)(2,1)}, bf16[64,1024]{1,0:T(8,128)(2,1)S(1)}, u32[]{:S(2)}, u32[]{:S(2)}) %collective-permute-start.6) | collective-permute-done | bytes 131104 | tf_op jit(solution)/shard_map/ppermute | solution.py:306
  33.2 0.6 collective-permute-start.11
  33.8 0.6 collective-permute-done.7.refs_7_
  34.4 5.3 %collective-permute-done.8.refs_8_ = bf16[64,1024]{1,0:T(8,128)(2,1)S(1)} collective-permute-done((bf16[64,1024]{1,0:T(8,128)(2,1)}, bf16[64,1024]{1,0:T(8,128)(2,1)S(1)}, u32[]{:S(2)}, u32[]{:S(2)}) %collective-permute-start.8) | collective-permute-done | bytes 131104 | tf_op jit(solution)/shard_map/ppermute | solution.py:306
  39.6 2.0 %collective-permute-done.10.refs_10_ = bf16[64,1024]{1,0:T(8,128)(2,1)S(1)} collective-permute-done((bf16[64,1024]{1,0:T(8,128)(2,1)}, bf16[64,1024]{1,0:T(8,128)(2,1)S(1)}, u32[]{:S(2)}, u32[]{:S(2)}) %collective-permute-start.10) | collective-permute-done | bytes 131104 | tf_op jit(solution)/shard_map/ppermute | solution.py:306
  41.6 0.6 collective-permute-done.11.refs_11_
  42.3 0.1 collect.2.own_ref.refs_0_
  42.5 2.8 %collective-permute-start.14 = (bf16[64,1024]{1,0:T(8,128)(2,1)S(1)}, bf16[64,1024]{1,0:T(8,128)(2,1)S(1)}, u32[]{:S(2)}, u32[]{:S(2)}) collective-permute-start(bf16[64,1024]{1,0:T(8,128)(2,1)S(1)} %copy-done.19), channel_id=1, source_target_pairs={{0,18},{2,16},{4,22},{6,20},{8,26},{10,24},{12,30},{14,28},{16,2},... | collective-permute-start | bytes 393224 | tf_op jit(solution)/shard_map/ppermute | solution.py:306
  45.3 1.6 %collective-permute-start.15 = (bf16[64,1024]{1,0:T(8,128)(2,1)S(1)}, bf16[64,1024]{1,0:T(8,128)(2,1)S(1)}, u32[]{:S(2)}, u32[]{:S(2)}) collective-permute-start(bf16[64,1024]{1,0:T(8,128)(2,1)S(1)} %copy-done.18), channel_id=1, source_target_pairs={{0,2},{2,0},{4,6},{6,4},{8,10},{10,8},{12,14},{14,12},{16,18},{18,... | collective-permute-start | bytes 393224 | tf_op jit(solution)/shard_map/ppermute | solution.py:306
  46.9 6.3 %front.2 = (bf16[704,384]{1,0:T(8,128)(2,1)S(1)}, bf16[704,384]{1,0:T(8,128)(2,1)S(1)}, bf16[704,384]{1,0:T(8,128)(2,1)S(1)}, bf16[384,1024]{1,0:T(8,128)(2,1)S(1)}) custom-call(bf16[768,1024]{1,0:T(8,128)(2,1)S(1)} %collect.2.own_ref.refs_0_, bf16[768,1024]{1,0:T(8,128)(2,1)S(1)} %collective-permute-done.12.other_ref.refs_1_, ...), custom_call_target="tpu_custom_call" | custom-call | flops 4429185024 | bytes 17825792 | tf_op jit(solution)/shard_map/front/pallas_call | solution.py:337
  53.3 1.4 %kept.2.kept_ref.refs_4_ = f32[384,1024]{1,0:T(8,128)S(1)} custom-call(bf16[704,384]{1,0:T(8,128)(2,1)S(1)} %get-tuple-element.48.d_gate_ref.refs_2_, bf16[704,384]{1,0:T(8,128)(2,1)S(1)} %get-tuple-element.49.d_up_ref.refs_3_, bf16[704,2048]{1,0:T(8,128)(2,1)S(1)} %bitcast.10, bf16[704,2048]{1,0:T(8,128)(2,1)S(1)} %bitcast.15), custom_call_target="tpu_custom_call" | custom-call | flops 1107296256 | bytes 4456448 | tf_op jit(solution)/shard_map/kept/pallas_call | solution.py:347
  54.8 1.2 %collective-permute-done.16.refs_2_ = bf16[64,1024]{1,0:T(8,128)(2,1)S(1)} collective-permute-done((bf16[64,1024]{1,0:T(8,128)(2,1)S(1)}, bf16[64,1024]{1,0:T(8,128)(2,1)S(1)}, u32[]{:S(2)}, u32[]{:S(2)}) %collective-permute-start.16) | collective-permute-done | bytes 131104 | tf_op jit(solution)/shard_map/ppermute | solution.py:306
  56.0 0.1 collective-permute-start.17
  56.2 0.5 collective-permute-start.13
  56.6 1.4 %begin.1 = (f32[704,128]{1,0:T(8,128)S(1)}, f32[704,128]{1,0:T(8,128)S(1)}, f32[704,128]{1,0:T(8,128)S(1)}) custom-call(bf16[256,1024]{1,0:T(8,128)(2,1)S(1)} %collect.3.own_ref.refs_5_, bf16[704,2048]{1,0:T(8,128)(2,1)S(1)} %bitcast.11, bf16[704,2048]{1,0:T(8,128)(2,1)S(1)} %bitcast.16, bf16[704,2048]{1,0:T(8,128)(2,1)S(1)} %bitcast.20), custom_call_target="tpu_custom_call" | custom-call | flops 738197504 | bytes 6815744 | tf_op jit(solution)/shard_map/begin/pallas_call | solution.py:324
  58.1 2.1 %front.3 = (bf16[704,128]{1,0:T(8,128)(2,1)S(1)}, bf16[704,128]{1,0:T(8,128)(2,1)S(1)}, bf16[704,128]{1,0:T(8,128)(2,1)S(1)}, bf16[128,1024]{1,0:T(8,128)(2,1)S(1)}) custom-call(bf16[256,1024]{1,0:T(8,128)(2,1)S(1)} %collect.3.own_ref.refs_5_, bf16[256,1024]{1,0:T(8,128)(2,1)S(1)} %collective-permute-done.17.other_ref.refs_6_, ...), custom_call_target="tpu_custom_call" | custom-call | flops 1476395008 | bytes 13631488 | tf_op jit(solution)/shard_map/front/pallas_call | solution.py:337
  60.2 0.7 copy-done.12
  60.9 0.6 kept.3.kept_ref
  61.6 0.1 sum.1.sum_ref
  61.7 0.7 collective-permute-done.18.got_ref
  62.4 1.1 %last_sum.1 = (bf16[512,1024]{1,0:T(8,128)(2,1)}, f32[8,128]{1,0:T(8,128)S(1)}) custom-call(bf16[384,1024]{1,0:T(8,128)(2,1)S(1)} %sum.1.sum_ref, f32[128,1024]{1,0:T(8,128)S(1)} %kept.3.kept_ref, bf16[128,1024]{1,0:T(8,128)(2,1)S(1)} %collective-permute-done.18.got_ref), custom_call_target="tpu_custom_call" | custom-call | tf_op jit(solution)/shard_map/last_sum/pallas_call | solution.py:371
  63.5 7.9 %all-to-all-start = ((bf16[16,32,1024]{2,1,0:T(8,128)(2,1)}), bf16[16,32,1024]{2,1,0:T(8,128)(2,1)S(1)}, u32[]{:S(2)}, u32[]{:S(2)}) async-start(bf16[16,32,1024]{2,1,0:T(8,128)(2,1)} %bitcast.4), calls=%async_computation | async-start | bytes 2097152 | tf_op jit(solution)/shard_map/all_to_all | solution.py:262
  71.4 0.3 placing.1.placing_ref.refs_10_
  71.7 0.9 copy-done.4
  72.6 0.9 copy-done.6
  73.5 1.4 %copy-done.9 = bf16[768,1024]{1,0:T(8,128)(2,1)S(1)} copy-done((bf16[768,1024]{1,0:T(8,128)(2,1)S(1)}, bf16[768,1024]{1,0:T(8,128)(2,1)}, u32[]{:S(2)}) %copy-start.9) | copy-done | bytes 1572888
  74.9 1.4 %copy-done.11 = bf16[768,1024]{1,0:T(8,128)(2,1)S(1)} copy-done((bf16[768,1024]{1,0:T(8,128)(2,1)S(1)}, bf16[768,1024]{1,0:T(8,128)(2,1)}, u32[]{:S(2)}) %copy-start.11) | copy-done | bytes 1572888
  76.3 0.9 copy-done.13
  77.2 1.0 %copy-done.16 = bf16[704,384]{1,0:T(8,128)(2,1)S(1)} copy-done((bf16[704,384]{1,0:T(8,128)(2,1)S(1)}, bf16[704,384]{1,0:T(8,128)(2,1)}, u32[]{:S(2)}) %copy-start.16) | copy-done | bytes 540696
  78.3 8.9 %grads.1 = (bf16[704,2048]{1,0:T(8,128)(2,1)}, bf16[704,2048]{1,0:T(8,128)(2,1)}, bf16[704,2048]{1,0:T(8,128)(2,1)}) custom-call(bf16[768,1024]{1,0:T(8,128)(2,1)S(1)} %copy-done.9, bf16[768,1024]{1,0:T(8,128)(2,1)S(1)} %copy-done.11, bf16[704,384]{1,0:T(8,128)(2,1)S(1)} %get-tuple-element.48.d_gate_ref.refs_2_, ...), custom_call_target="tpu_custom_call" | custom-call | flops 4429185024 | bytes 14942208 | tf_op jit(solution)/shard_map/grads/pallas_call | solution.py:391
  87.2 9.9 %all-to-all-done = bf16[16,32,1024]{2,1,0:T(8,128)(2,1)S(1)} async-done(((bf16[16,32,1024]{2,1,0:T(8,128)(2,1)}), bf16[16,32,1024]{2,1,0:T(8,128)(2,1)S(1)}, u32[]{:S(2)}, u32[]{:S(2)}) %all-to-all-start) | async-done | bytes 1048608 | tf_op jit(solution)/shard_map/all_to_all | solution.py:262
  97.1 1.7 %combine.1 = bf16[256,1024]{1,0:T(8,128)(2,1)} custom-call(bf16[256,512]{1,0:T(8,128)(2,1)S(1)} %placing.1.placing_ref.refs_10_, bf16[512,1024]{1,0:T(8,128)(2,1)S(1)} %bitcast.22), custom_call_target="tpu_custom_call" | custom-call | tf_op jit(solution)/shard_map/combine/pallas_call | solution.py:250
  (45 shorter events, 0.4 us)
Async XLA Ops:
  4.1 11.3 %collective-permute-start = (bf16[64,1024]{1,0:T(8,128)(2,1)}, bf16[64,1024]{1,0:T(8,128)(2,1)S(1)}, u32[]{:S(2)}, u32[]{:S(2)}) collective-permute-start(bf16[64,1024]{1,0:T(8,128)(2,1)} %get-tuple-element.36), channel_id=1, source_target_pairs={{0,30},{2,28},{4,26},{6,24},{8,22},{10,20},{12,18},{14,16},{16,14}... | collective-permute-start | bytes 393224 | tf_op jit(solution)/shard_map/ppermute | solution.py:306
  7.7 10.3 %collective-permute-start.1 = (bf16[64,1024]{1,0:T(8,128)(2,1)}, bf16[64,1024]{1,0:T(8,128)(2,1)S(1)}, u32[]{:S(2)}, u32[]{:S(2)}) collective-permute-start(bf16[64,1024]{1,0:T(8,128)(2,1)} %get-tuple-element.37), channel_id=1, source_target_pairs={{0,14},{2,12},{4,10},{6,8},{8,6},{10,4},{12,2},{14,0},{16,30},{18,... | collective-permute-start | bytes 393224 | tf_op jit(solution)/shard_map/ppermute | solution.py:306
  10.1 11.9 %collective-permute-start.2 = (bf16[64,1024]{1,0:T(8,128)(2,1)}, bf16[64,1024]{1,0:T(8,128)(2,1)S(1)}, u32[]{:S(2)}, u32[]{:S(2)}) collective-permute-start(bf16[64,1024]{1,0:T(8,128)(2,1)} %get-tuple-element.38), channel_id=1, source_target_pairs={{0,28},{2,30},{4,24},{6,26},{8,20},{10,22},{12,16},{14,18},{16,12}... | collective-permute-start | bytes 393224 | tf_op jit(solution)/shard_map/ppermute | solution.py:306
  10.3 12.7 %collective-permute-start.3 = (bf16[64,1024]{1,0:T(8,128)(2,1)}, bf16[64,1024]{1,0:T(8,128)(2,1)S(1)}, u32[]{:S(2)}, u32[]{:S(2)}) collective-permute-start(bf16[64,1024]{1,0:T(8,128)(2,1)} %get-tuple-element.39), channel_id=1, source_target_pairs={{0,12},{2,14},{4,8},{6,10},{8,4},{10,6},{12,0},{14,2},{16,28},{18,... | collective-permute-start | bytes 393224 | tf_op jit(solution)/shard_map/ppermute | solution.py:306
  11.8 14.9 %collective-permute-start.4 = (bf16[64,1024]{1,0:T(8,128)(2,1)}, bf16[64,1024]{1,0:T(8,128)(2,1)S(1)}, u32[]{:S(2)}, u32[]{:S(2)}) collective-permute-start(bf16[64,1024]{1,0:T(8,128)(2,1)} %get-tuple-element.40), channel_id=1, source_target_pairs={{0,26},{2,24},{4,30},{6,28},{8,18},{10,16},{12,22},{14,20},{16,10}... | collective-permute-start | bytes 393224 | tf_op jit(solution)/shard_map/ppermute | solution.py:306
  15.5 15.3 %collective-permute-start.5 = (bf16[64,1024]{1,0:T(8,128)(2,1)}, bf16[64,1024]{1,0:T(8,128)(2,1)S(1)}, u32[]{:S(2)}, u32[]{:S(2)}) collective-permute-start(bf16[64,1024]{1,0:T(8,128)(2,1)} %get-tuple-element.41), channel_id=1, source_target_pairs={{0,10},{2,8},{4,14},{6,12},{8,2},{10,0},{12,6},{14,4},{16,26},{18,... | collective-permute-start | bytes 393224 | tf_op jit(solution)/shard_map/ppermute | solution.py:306
  18.0 15.2 %collective-permute-start.6 = (bf16[64,1024]{1,0:T(8,128)(2,1)}, bf16[64,1024]{1,0:T(8,128)(2,1)S(1)}, u32[]{:S(2)}, u32[]{:S(2)}) collective-permute-start(bf16[64,1024]{1,0:T(8,128)(2,1)} %get-tuple-element.42), channel_id=1, source_target_pairs={{0,24},{2,26},{4,28},{6,30},{8,16},{10,18},{12,20},{14,22},{16,8},... | collective-permute-start | bytes 393224 | tf_op jit(solution)/shard_map/ppermute | solution.py:306
  21.9 12.4 %collective-permute-start.7 = (bf16[64,1024]{1,0:T(8,128)(2,1)}, bf16[64,1024]{1,0:T(8,128)(2,1)S(1)}, u32[]{:S(2)}, u32[]{:S(2)}) collective-permute-start(bf16[64,1024]{1,0:T(8,128)(2,1)} %get-tuple-element.43), channel_id=1, source_target_pairs={{0,8},{2,10},{4,12},{6,14},{8,0},{10,2},{12,4},{14,6},{16,24},{18,... | collective-permute-start | bytes 393224 | tf_op jit(solution)/shard_map/ppermute | solution.py:306
  23.1 16.5 %collective-permute-start.8 = (bf16[64,1024]{1,0:T(8,128)(2,1)}, bf16[64,1024]{1,0:T(8,128)(2,1)S(1)}, u32[]{:S(2)}, u32[]{:S(2)}) collective-permute-start(bf16[64,1024]{1,0:T(8,128)(2,1)} %get-tuple-element.44), channel_id=1, source_target_pairs={{0,22},{2,20},{4,18},{6,16},{8,30},{10,28},{12,26},{14,24},{16,6},... | collective-permute-start | bytes 393224 | tf_op jit(solution)/shard_map/ppermute | solution.py:306
  26.8 12.8 %collective-permute-start.9 = (bf16[64,1024]{1,0:T(8,128)(2,1)}, bf16[64,1024]{1,0:T(8,128)(2,1)S(1)}, u32[]{:S(2)}, u32[]{:S(2)}) collective-permute-start(bf16[64,1024]{1,0:T(8,128)(2,1)} %get-tuple-element.45), channel_id=1, source_target_pairs={{0,6},{2,4},{4,2},{6,0},{8,14},{10,12},{12,10},{14,8},{16,22},{18,... | collective-permute-start | bytes 393224 | tf_op jit(solution)/shard_map/ppermute | solution.py:306
  30.7 10.9 %collective-permute-start.10 = (bf16[64,1024]{1,0:T(8,128)(2,1)}, bf16[64,1024]{1,0:T(8,128)(2,1)S(1)}, u32[]{:S(2)}, u32[]{:S(2)}) collective-permute-start(bf16[64,1024]{1,0:T(8,128)(2,1)} %get-tuple-element.46), channel_id=1, source_target_pairs={{0,20},{2,22},{4,16},{6,18},{8,28},{10,30},{12,24},{14,26},{16,4},... | collective-permute-start | bytes 393224 | tf_op jit(solution)/shard_map/ppermute | solution.py:306
  33.2 9.2 %copy-start.19 = (bf16[64,1024]{1,0:T(8,128)(2,1)S(1)}, bf16[64,1024]{1,0:T(8,128)(2,1)}, u32[]{:S(2)}) copy-start(bf16[64,1024]{1,0:T(8,128)(2,1)} %get-tuple-element.51) | copy-start | bytes 393220
  33.2 12.1 %copy-start.18 = (bf16[64,1024]{1,0:T(8,128)(2,1)S(1)}, bf16[64,1024]{1,0:T(8,128)(2,1)}, u32[]{:S(2)}) copy-start(bf16[64,1024]{1,0:T(8,128)(2,1)} %get-tuple-element.52) | copy-start | bytes 393220
  33.2 13.7 %copy-start.17 = (bf16[64,1024]{1,0:T(8,128)(2,1)S(1)}, bf16[64,1024]{1,0:T(8,128)(2,1)}, u32[]{:S(2)}) copy-start(bf16[64,1024]{1,0:T(8,128)(2,1)} %get-tuple-element.53) | copy-start | bytes 393220
  33.2 13.7 %copy-start = (bf16[1,704,2048]{2,1,0:T(8,128)(2,1)S(1)}, bf16[1,704,2048]{2,1,0:T(8,128)(2,1)}, u32[]{:S(2)}) copy-start(bf16[1,704,2048]{2,1,0:T(8,128)(2,1)} %param.9) | copy-start | bytes 8650756
  33.2 13.7 %copy-start.1 = (bf16[1,704,2048]{2,1,0:T(8,128)(2,1)S(1)}, bf16[1,704,2048]{2,1,0:T(8,128)(2,1)}, u32[]{:S(2)}) copy-start(bf16[1,704,2048]{2,1,0:T(8,128)(2,1)} %param.10) | copy-start | bytes 8650756
  33.2 13.7 %copy-start.2 = (bf16[1,704,2048]{2,1,0:T(8,128)(2,1)S(1)}, bf16[1,704,2048]{2,1,0:T(8,128)(2,1)}, u32[]{:S(2)}) copy-start(bf16[1,704,2048]{2,1,0:T(8,128)(2,1)} %param.11) | copy-start | bytes 8650756
  33.2 9.0 %collective-permute-start.11 = (bf16[64,1024]{1,0:T(8,128)(2,1)}, bf16[64,1024]{1,0:T(8,128)(2,1)S(1)}, u32[]{:S(2)}, u32[]{:S(2)}) collective-permute-start(bf16[64,1024]{1,0:T(8,128)(2,1)} %get-tuple-element.47), channel_id=1, source_target_pairs={{0,4},{2,6},{4,0},{6,2},{8,12},{10,14},{12,8},{14,10},{16,20},{18,... | collective-permute-start | bytes 393224 | tf_op jit(solution)/shard_map/ppermute | solution.py:306
  42.4 10.9 %copy-start.8 = (bf16[768,1024]{1,0:T(8,128)(2,1)}, bf16[768,1024]{1,0:T(8,128)(2,1)S(1)}, u32[]{:S(2)}) copy-start(bf16[768,1024]{1,0:T(8,128)(2,1)S(1)} %collect.2.own_ref.refs_0_) | copy-start | bytes 4718596
  42.4 4.6 %collective-permute-start.12 = (bf16[768,1024]{1,0:T(8,128)(2,1)S(1)}, bf16[768,1024]{1,0:T(8,128)(2,1)S(1)}, u32[]{:S(2)}, u32[]{:S(2)}) collective-permute-start(bf16[768,1024]{1,0:T(8,128)(2,1)S(1)} %collect.2.own_ref.refs_0_), channel_id=1, source_target_pairs={{0,1},{1,0},{2,3},{3,2},{4,5},{5,4},{6,7},{7,6},{8,9},{9,8},{10,11... | collective-permute-start | bytes 4718600 | tf_op jit(solution)/shard_map/ppermute | solution.py:309
  42.5 12.3 %collective-permute-start.14 = (bf16[64,1024]{1,0:T(8,128)(2,1)S(1)}, bf16[64,1024]{1,0:T(8,128)(2,1)S(1)}, u32[]{:S(2)}, u32[]{:S(2)}) collective-permute-start(bf16[64,1024]{1,0:T(8,128)(2,1)S(1)} %copy-done.19), channel_id=1, source_target_pairs={{0,18},{2,16},{4,22},{6,20},{8,26},{10,24},{12,30},{14,28},{16,2},... | collective-permute-start | bytes 393224 | tf_op jit(solution)/shard_map/ppermute | solution.py:306
  45.3 9.5 %collective-permute-start.15 = (bf16[64,1024]{1,0:T(8,128)(2,1)S(1)}, bf16[64,1024]{1,0:T(8,128)(2,1)S(1)}, u32[]{:S(2)}, u32[]{:S(2)}) collective-permute-start(bf16[64,1024]{1,0:T(8,128)(2,1)S(1)} %copy-done.18), channel_id=1, source_target_pairs={{0,2},{2,0},{4,6},{6,4},{8,10},{10,8},{12,14},{14,12},{16,18},{18,... | collective-permute-start | bytes 393224 | tf_op jit(solution)/shard_map/ppermute | solution.py:306
  46.9 9.1 %collective-permute-start.16 = (bf16[64,1024]{1,0:T(8,128)(2,1)S(1)}, bf16[64,1024]{1,0:T(8,128)(2,1)S(1)}, u32[]{:S(2)}, u32[]{:S(2)}) collective-permute-start(bf16[64,1024]{1,0:T(8,128)(2,1)S(1)} %copy-done.17), channel_id=1, source_target_pairs={{0,16},{2,18},{4,20},{6,22},{8,24},{10,26},{12,28},{14,30},{16,0},... | collective-permute-start | bytes 393224 | tf_op jit(solution)/shard_map/ppermute | solution.py:306
  46.9 6.4 %copy-start.10 = (bf16[768,1024]{1,0:T(8,128)(2,1)}, bf16[768,1024]{1,0:T(8,128)(2,1)S(1)}, u32[]{:S(2)}) copy-start(bf16[768,1024]{1,0:T(8,128)(2,1)S(1)} %collective-permute-done.12.other_ref.refs_1_) | copy-start | bytes 4718596
  53.3 1.4 %copy-start.15 = (bf16[704,384]{1,0:T(8,128)(2,1)}, bf16[704,384]{1,0:T(8,128)(2,1)S(1)}, u32[]{:S(2)}) copy-start(bf16[704,384]{1,0:T(8,128)(2,1)S(1)} %get-tuple-element.63.refs_4_) | copy-start | bytes 1622020
  53.3 2.7 %copy-start.14 = (bf16[64,1024]{1,0:T(8,128)(2,1)S(1)}, bf16[64,1024]{1,0:T(8,128)(2,1)}, u32[]{:S(2)}) copy-start(bf16[64,1024]{1,0:T(8,128)(2,1)} %get-tuple-element.54.refs_3_) | copy-start | bytes 393220
  56.0 2.0 %collective-permute-start.17 = (bf16[256,1024]{1,0:T(8,128)(2,1)S(1)}, bf16[256,1024]{1,0:T(8,128)(2,1)S(1)}, u32[]{:S(2)}, u32[]{:S(2)}) collective-permute-start(bf16[256,1024]{1,0:T(8,128)(2,1)S(1)} %collect.3.own_ref.refs_5_), channel_id=1, source_target_pairs={{0,1},{1,0},{2,3},{3,2},{4,5},{5,4},{6,7},{7,6},{8,9},{9,8},{10,11... | collective-permute-start | bytes 1572872 | tf_op jit(solution)/shard_map/ppermute | solution.py:309
  56.2 5.4 %collective-permute-start.13 = (bf16[384,1024]{1,0:T(8,128)(2,1)S(1)}, bf16[384,1024]{1,0:T(8,128)(2,1)S(1)}, u32[]{:S(2)}, u32[]{:S(2)}) collective-permute-start(bf16[384,1024]{1,0:T(8,128)(2,1)S(1)} %get-tuple-element.50), channel_id=1, source_target_pairs={{0,1},{1,0},{2,3},{3,2},{4,5},{5,4},{6,7},{7,6},{8,9},{9,8},{10,11... | collective-permute-start | bytes 2359304 | tf_op jit(solution)/shard_map/ppermute | solution.py:309
  60.2 0.7 copy-start.12
  60.8 0.7 copy-start.3
  60.8 0.7 copy-start.5
  60.8 1.5 %collective-permute-start.18 = (bf16[128,1024]{1,0:T(8,128)(2,1)S(1)}, bf16[128,1024]{1,0:T(8,128)(2,1)S(1)}, u32[]{:S(2)}, u32[]{:S(2)}) collective-permute-start(bf16[128,1024]{1,0:T(8,128)(2,1)S(1)} %get-tuple-element.60), channel_id=1, source_target_pairs={{0,1},{1,0},{2,3},{3,2},{4,5},{5,4},{6,7},{7,6},{8,9},{9,8},{10,11... | collective-permute-start | bytes 786440 | tf_op jit(solution)/shard_map/ppermute | solution.py:309
  61.5 9.8 %copy-start.7 = (s32[256,1]{0,1:T(1,128)S(1)}, s32[256,1]{0,1:T(1,128)}, u32[]{:S(2)}) copy-start(s32[256,1]{0,1:T(1,128)} %param.8) | copy-start | bytes 3076
  63.5 33.6 %all-to-all-start = ((bf16[16,32,1024]{2,1,0:T(8,128)(2,1)}), bf16[16,32,1024]{2,1,0:T(8,128)(2,1)S(1)}, u32[]{:S(2)}, u32[]{:S(2)}) async-start(bf16[16,32,1024]{2,1,0:T(8,128)(2,1)} %bitcast.4), calls=%async_computation | async-start | bytes 2097152 | tf_op jit(solution)/shard_map/all_to_all | solution.py:262
  71.7 0.9 copy-start.4
  72.6 0.9 copy-start.6
  73.5 1.4 %copy-start.9 = (bf16[768,1024]{1,0:T(8,128)(2,1)S(1)}, bf16[768,1024]{1,0:T(8,128)(2,1)}, u32[]{:S(2)}) copy-start(bf16[768,1024]{1,0:T(8,128)(2,1)} %copy-done.8) | copy-start | bytes 4718596
  74.9 1.4 %copy-start.11 = (bf16[768,1024]{1,0:T(8,128)(2,1)S(1)}, bf16[768,1024]{1,0:T(8,128)(2,1)}, u32[]{:S(2)}) copy-start(bf16[768,1024]{1,0:T(8,128)(2,1)} %copy-done.10) | copy-start | bytes 4718596
  76.3 0.9 copy-start.13
  77.2 1.0 %copy-start.16 = (bf16[704,384]{1,0:T(8,128)(2,1)S(1)}, bf16[704,384]{1,0:T(8,128)(2,1)}, u32[]{:S(2)}) copy-start(bf16[704,384]{1,0:T(8,128)(2,1)} %copy-done.15) | copy-start | bytes 1622020

commit v10 on v9

--- a/solution.py
+++ b/solution.py
@@ -112,7 +112,7 @@
 
 
 def front_kernel(tile, own_ref, other_ref, gate_ref, up_ref, down_ref, *refs):
-    *begun_refs, hidden_ref, d_gate_ref, d_up_ref, sent_ref = refs
+    *begun_refs, hidden_hbm, d_gate_ref, d_up_ref, sent_ref, hidden_ref, sem = refs
     rows, width = sent_ref.shape
     mine = lax.axis_index("tensor")
 
@@ -143,9 +143,12 @@
             d_hidden * up_pre * sig * (1.0 + gate_pre * (1.0 - sig))
         ).astype(BF16)
 
+    copy = pltpu.make_async_copy(hidden_ref, hidden_hbm, sem)
+    copy.start()
     sent_ref[...] = input_rows(
         d_gate_ref, d_up_ref, gate_ref, up_ref, side(1 - mine, width)
     ).astype(BF16)
+    copy.wait()
 
 
 def kept_kernel(d_gate_ref, d_up_ref, gate_ref, up_ref, out_ref):
@@ -153,22 +156,21 @@
     out_ref[...] = input_rows(d_gate_ref, d_up_ref, gate_ref, up_ref, columns)
 
 
-def sum_kernel(kept_ref, got_ref, out_ref):
-    out_ref[...] = (kept_ref[...] + got_ref[...].astype(F32)).astype(BF16)
-
-
-def last_sum_kernel(capacity, groups, sum_ref, kept_ref, got_ref, out_ref, done_ref):
+def sum_kernel(capacity, group, kept_ref, got_ref, *refs):
+    out_hbm, done_ref, sum_ref, sems = refs[-4:]
     done_ref[...] = jnp.zeros_like(done_ref)
     me = lax.axis_index("expert")
-    for last, group in enumerate(groups):
-        for i, k in enumerate(group):
-            here = slice(i * capacity, (i + 1) * capacity)
-            there = pl.ds(pl.multiple_of((me ^ k) * capacity, capacity), capacity)
-            if last:
-                both = kept_ref[here, :] + got_ref[here, :].astype(F32)
-                out_ref[there, :] = both.astype(BF16)
-            else:
-                out_ref[there, :] = sum_ref[here, :]
+    copies = []
+    for i, k in enumerate(group):
+        here = slice(i * capacity, (i + 1) * capacity)
+        there = pl.ds(pl.multiple_of((me ^ k) * capacity, capacity), capacity)
+        sum_ref[here, :] = (kept_ref[here, :] + got_ref[here, :].astype(F32)).astype(BF16)
+        copies.append(
+            pltpu.make_async_copy(sum_ref.at[here], out_hbm.at[there], sems.at[i])
+        )
+        copies[-1].start()
+    for copy in copies:
+        copy.wait()
 
 
 def grads_kernel(sizes, *refs):
@@ -339,7 +341,8 @@
             out_shape=[jax.ShapeDtypeStruct((units, rows), BF16)] * 3
             + [jax.ShapeDtypeStruct((rows, width), BF16)],
             in_specs=[IN_VMEM] * (5 + len(begun)),
-            out_specs=[IN_VMEM] * 4,
+            out_specs=[IN_HBM] + [IN_VMEM] * 3,
+            scratch_shapes=[pltpu.VMEM((units, rows), BF16), pltpu.SemaphoreType.DMA],
             compiler_params=params(SMALL),
             cost_estimate=cost(4, rows, units, features),
             name="front",
@@ -360,25 +363,27 @@
     for_grads_a, for_sum_a = front(collect([got[k] for k in first], []), [])
     own_b = collect([got[k] for k in second], for_sum_a[:1])
     for_grads_b, for_sum_b = front(own_b, begin(own_b))
-    sum_a = pl.pallas_call(
-        sum_kernel,
-        out_shape=jax.ShapeDtypeStruct((len(first) * capacity, width), BF16),
-        in_specs=[IN_VMEM] * 2,
-        out_specs=IN_VMEM,
-        compiler_params=params(SMALL),
-        name="sum",
-    )(*for_sum_a)
-    totals, done = pl.pallas_call(
-        functools.partial(last_sum_kernel, capacity, (first, second)),
-        out_shape=[
-            jax.ShapeDtypeStruct((experts * capacity, width), BF16),
-            jax.ShapeDtypeStruct((8, 128), F32),
-        ],
-        in_specs=[IN_VMEM] * 3,
-        out_specs=[IN_VMEM] * 2,
-        compiler_params=params(SMALL),
-        name="last_sum",
-    )(sum_a, *for_sum_b)
+
+    def add_rows(group, kept, got_rows, earlier):
+        return pl.pallas_call(
+            functools.partial(sum_kernel, capacity, group),
+            out_shape=[
+                jax.ShapeDtypeStruct((experts * capacity, width), BF16),
+                jax.ShapeDtypeStruct((8, 128), F32),
+            ],
+            in_specs=[IN_VMEM] * 2 + [IN_HBM] * len(earlier),
+            out_specs=[IN_HBM, IN_VMEM],
+            input_output_aliases={2: 0} if earlier else {},
+            scratch_shapes=[
+                pltpu.VMEM((len(group) * capacity, width), BF16),
+                pltpu.SemaphoreType.DMA((len(group),)),
+            ],
+            compiler_params=params(SMALL),
+            name="sum",
+        )(kept, got_rows, *earlier)
+
+    totals, _ = add_rows(first, *for_sum_a, [])
+    totals, done = add_rows(second, *for_sum_b, [totals])
     returned = to_experts(totals, experts)
     placing = placing_of(capacity, ids_row, experts * capacity, done)
 

time: 99.3 us -> 100 us (level)
  Pallas kernels: 27.6 us -> 29 us
    pallas_call x2, Pallas kernels: 1.25 us -> 2.38 us  [add_rows(): pl.pallas_call(functools.partial(sum_kernel, capacity, group), out_shape=...]
  transfers between devices with their start and end apart: 20 -> 20, of which waited for: 13 -> 12; matrix products, arithmetic and copies ran while one was open for 0% -> 0% of each run, Pallas kernels for 21% -> 23%
where the time goes in v10:
time: 100 us
  starting transfers between devices  33.8 us (34%)
  Pallas kernels  29 us (29%)
  waiting for transfers between devices  28.9 us (29%)
  local copies, waits for them, and re-layouts  7.38 us (7%)
  between operations  1.04 us (1%)
    ppermute x15, starting transfers between devices, swap(): lax.ppermute(slabs[k], 'expert', [(e, e ^ k) for e in range(experts)])  25.1 us
    ppermute x15, waiting for transfers between devices, swap(): lax.ppermute(slabs[k], 'expert', [(e, e ^ k) for e in range(experts)])  18.5 us
    all_to_all x1, waiting for transfers between devices, to_experts(): lax.all_to_all(rows.reshape(experts, rows.shape[0] // experts, rows.shape...  10.3 us
    pallas_call x1, Pallas kernels, grouped(): pl.pallas_call(functools.partial(grads_kernel, sizes), grid=(units // til...  8.91 us
    pallas_call x2, Pallas kernels, front(): pl.pallas_call(functools.partial(front_kernel, tile), out_shape=[jax.Shap...  8.74 us
    all_to_all x1, starting transfers between devices, to_experts(): lax.all_to_all(rows.reshape(experts, rows.shape[0] // experts, rows.shape...  7.88 us
    unnamed x40, local copies, waits for them, and re-layouts  7.38 us
    pallas_call x1, Pallas kernels, grouped(): pl.pallas_call(functools.partial(place_kernel, capacity), out_shape=[jax....  3.49 us
  transfers between devices with their start and end apart: 20, of which 12 were waited for; matrix products, arithmetic and copies ran while one was open for 0% of the time, Pallas kernels for 23%

profile of v10, /device:TPU:8, one launch (start us, length us, event | category | flops | bytes accessed | tf_op | source)
XLA Modules:
  0.0 100.1 jit_solution(5507437395120730115)
XLA Ops:
  0.6 3.5 %place.1 = (bf16[64,1024]{1,0:T(8,128)(2,1)}, bf16[64,1024]{1,0:T(8,128)(2,1)}, bf16[64,1024]{1,0:T(8,128)(2,1)}, bf16[64,1024]{1,0:T(8,128)(2,1)}, bf16[64,1024...) custom-call(s32[1,256]{1,0:T(1,128)} %bitcast.23, ...), custom_call_target="tpu_custom_call" | custom-call | tf_op jit(solution)/shard_map/place/pallas_call | solution.py:288
  4.1 3.5 %collective-permute-start.3 = (bf16[64,1024]{1,0:T(8,128)(2,1)}, bf16[64,1024]{1,0:T(8,128)(2,1)S(1)}, u32[]{:S(2)}, u32[]{:S(2)}) collective-permute-start(bf16[64,1024]{1,0:T(8,128)(2,1)} %get-tuple-element.41), channel_id=1, source_target_pairs={{0,30},{2,28},{4,26},{6,24},{8,22},{10,20},{12,18},{14,16},{16,14}... | collective-permute-start | bytes 393224 | tf_op jit(solution)/shard_map/ppermute | solution.py:308
  7.6 2.4 %collective-permute-start.4 = (bf16[64,1024]{1,0:T(8,128)(2,1)}, bf16[64,1024]{1,0:T(8,128)(2,1)S(1)}, u32[]{:S(2)}, u32[]{:S(2)}) collective-permute-start(bf16[64,1024]{1,0:T(8,128)(2,1)} %get-tuple-element.42), channel_id=1, source_target_pairs={{0,14},{2,12},{4,10},{6,8},{8,6},{10,4},{12,2},{14,0},{16,30},{18,... | collective-permute-start | bytes 393224 | tf_op jit(solution)/shard_map/ppermute | solution.py:308
  10.0 0.3 collective-permute-start.5
  10.3 1.5 %collective-permute-start.6 = (bf16[64,1024]{1,0:T(8,128)(2,1)}, bf16[64,1024]{1,0:T(8,128)(2,1)S(1)}, u32[]{:S(2)}, u32[]{:S(2)}) collective-permute-start(bf16[64,1024]{1,0:T(8,128)(2,1)} %get-tuple-element.44), channel_id=1, source_target_pairs={{0,12},{2,14},{4,8},{6,10},{8,4},{10,6},{12,0},{14,2},{16,28},{18,... | collective-permute-start | bytes 393224 | tf_op jit(solution)/shard_map/ppermute | solution.py:308
  11.8 2.5 %collective-permute-start.7 = (bf16[64,1024]{1,0:T(8,128)(2,1)}, bf16[64,1024]{1,0:T(8,128)(2,1)S(1)}, u32[]{:S(2)}, u32[]{:S(2)}) collective-permute-start(bf16[64,1024]{1,0:T(8,128)(2,1)} %get-tuple-element.45), channel_id=1, source_target_pairs={{0,26},{2,24},{4,30},{6,28},{8,18},{10,16},{12,22},{14,20},{16,10}... | collective-permute-start | bytes 393224 | tf_op jit(solution)/shard_map/ppermute | solution.py:308
  14.3 1.1 %collective-permute-done.3.refs_0_ = bf16[64,1024]{1,0:T(8,128)(2,1)S(1)} collective-permute-done((bf16[64,1024]{1,0:T(8,128)(2,1)}, bf16[64,1024]{1,0:T(8,128)(2,1)S(1)}, u32[]{:S(2)}, u32[]{:S(2)}) %collective-permute-start.3) | collective-permute-done | bytes 131104 | tf_op jit(solution)/shard_map/ppermute | solution.py:308
  15.4 1.4 %collective-permute-start.8 = (bf16[64,1024]{1,0:T(8,128)(2,1)}, bf16[64,1024]{1,0:T(8,128)(2,1)S(1)}, u32[]{:S(2)}, u32[]{:S(2)}) collective-permute-start(bf16[64,1024]{1,0:T(8,128)(2,1)} %get-tuple-element.46), channel_id=1, source_target_pairs={{0,10},{2,8},{4,14},{6,12},{8,2},{10,0},{12,6},{14,4},{16,26},{18,... | collective-permute-start | bytes 393224 | tf_op jit(solution)/shard_map/ppermute | solution.py:308
  16.8 1.2 %collective-permute-done.4.refs_1_ = bf16[64,1024]{1,0:T(8,128)(2,1)S(1)} collective-permute-done((bf16[64,1024]{1,0:T(8,128)(2,1)}, bf16[64,1024]{1,0:T(8,128)(2,1)S(1)}, u32[]{:S(2)}, u32[]{:S(2)}) %collective-permute-start.4) | collective-permute-done | bytes 131104 | tf_op jit(solution)/shard_map/ppermute | solution.py:308
  17.9 0.6 collective-permute-start.9
  18.5 3.4 %collective-permute-done.5.refs_2_ = bf16[64,1024]{1,0:T(8,128)(2,1)S(1)} collective-permute-done((bf16[64,1024]{1,0:T(8,128)(2,1)}, bf16[64,1024]{1,0:T(8,128)(2,1)S(1)}, u32[]{:S(2)}, u32[]{:S(2)}) %collective-permute-start.5) | collective-permute-done | bytes 131104 | tf_op jit(solution)/shard_map/ppermute | solution.py:308
  21.9 0.7 collective-permute-start.10
  22.6 0.5 collective-permute-done.6.refs_3_
  23.1 3.4 %collective-permute-start.11 = (bf16[64,1024]{1,0:T(8,128)(2,1)}, bf16[64,1024]{1,0:T(8,128)(2,1)S(1)}, u32[]{:S(2)}, u32[]{:S(2)}) collective-permute-start(bf16[64,1024]{1,0:T(8,128)(2,1)} %get-tuple-element.49), channel_id=1, source_target_pairs={{0,22},{2,20},{4,18},{6,16},{8,30},{10,28},{12,26},{14,24},{16,6},... | collective-permute-start | bytes 393224 | tf_op jit(solution)/shard_map/ppermute | solution.py:308
  26.4 0.3 collective-permute-done.7.refs_4_
  26.8 3.9 %collective-permute-start.12 = (bf16[64,1024]{1,0:T(8,128)(2,1)}, bf16[64,1024]{1,0:T(8,128)(2,1)S(1)}, u32[]{:S(2)}, u32[]{:S(2)}) collective-permute-start(bf16[64,1024]{1,0:T(8,128)(2,1)} %get-tuple-element.50), channel_id=1, source_target_pairs={{0,6},{2,4},{4,2},{6,0},{8,14},{10,12},{12,10},{14,8},{16,22},{18,... | collective-permute-start | bytes 393224 | tf_op jit(solution)/shard_map/ppermute | solution.py:308
  30.7 2.5 %collective-permute-done.9.refs_6_ = bf16[64,1024]{1,0:T(8,128)(2,1)S(1)} collective-permute-done((bf16[64,1024]{1,0:T(8,128)(2,1)}, bf16[64,1024]{1,0:T(8,128)(2,1)S(1)}, u32[]{:S(2)}, u32[]{:S(2)}) %collective-permute-start.9) | collective-permute-done | bytes 131104 | tf_op jit(solution)/shard_map/ppermute | solution.py:308
  33.2 0.6 collective-permute-start.14
  33.8 0.6 collective-permute-done.10.refs_7_
  34.4 5.3 %collective-permute-done.11.refs_8_ = bf16[64,1024]{1,0:T(8,128)(2,1)S(1)} collective-permute-done((bf16[64,1024]{1,0:T(8,128)(2,1)}, bf16[64,1024]{1,0:T(8,128)(2,1)S(1)}, u32[]{:S(2)}, u32[]{:S(2)}) %collective-permute-start.11) | collective-permute-done | bytes 131104 | tf_op jit(solution)/shard_map/ppermute | solution.py:308
  39.6 2.0 %collective-permute-done.13.refs_10_ = bf16[64,1024]{1,0:T(8,128)(2,1)S(1)} collective-permute-done((bf16[64,1024]{1,0:T(8,128)(2,1)}, bf16[64,1024]{1,0:T(8,128)(2,1)S(1)}, u32[]{:S(2)}, u32[]{:S(2)}) %collective-permute-start.13) | collective-permute-done | bytes 131104 | tf_op jit(solution)/shard_map/ppermute | solution.py:308
  41.6 0.6 collective-permute-done.14.refs_11_
  42.2 0.1 collect.2.own_ref.refs_0_
  42.4 0.1 collective-permute-start.15
  42.4 2.8 %collective-permute-start = (bf16[64,1024]{1,0:T(8,128)(2,1)S(1)}, bf16[64,1024]{1,0:T(8,128)(2,1)S(1)}, u32[]{:S(2)}, u32[]{:S(2)}) collective-permute-start(bf16[64,1024]{1,0:T(8,128)(2,1)S(1)} %copy-done.19), channel_id=1, source_target_pairs={{0,18},{2,16},{4,22},{6,20},{8,26},{10,24},{12,30},{14,28},{16,2},... | collective-permute-start | bytes 393224 | tf_op jit(solution)/shard_map/ppermute | solution.py:308
  45.3 1.6 %collective-permute-start.1 = (bf16[64,1024]{1,0:T(8,128)(2,1)S(1)}, bf16[64,1024]{1,0:T(8,128)(2,1)S(1)}, u32[]{:S(2)}, u32[]{:S(2)}) collective-permute-start(bf16[64,1024]{1,0:T(8,128)(2,1)S(1)} %copy-done.18), channel_id=1, source_target_pairs={{0,2},{2,0},{4,6},{6,4},{8,10},{10,8},{12,14},{14,12},{16,18},{18,... | collective-permute-start | bytes 393224 | tf_op jit(solution)/shard_map/ppermute | solution.py:308
  46.9 6.4 %front.2 = (bf16[704,384]{1,0:T(8,128)(2,1)S(1)}, bf16[704,384]{1,0:T(8,128)(2,1)S(1)}, bf16[704,384]{1,0:T(8,128)(2,1)S(1)}, bf16[384,1024]{1,0:T(8,128)(2,1)S(1)}) custom-call(bf16[768,1024]{1,0:T(8,128)(2,1)S(1)} %collect.2.own_ref.refs_0_, bf16[768,1024]{1,0:T(8,128)(2,1)S(1)} %collective-permute-done.15.other_ref.refs_1_, ...), custom_call_target="tpu_custom_call" | custom-call | flops 4429185024 | bytes 17825792 | tf_op jit(solution)/shard_map/front/pallas_call | solution.py:339
  53.4 1.4 %kept.2.refs_4_.kept_ref = f32[384,1024]{1,0:T(8,128)S(1)} custom-call(bf16[704,384]{1,0:T(8,128)(2,1)S(1)} %get-tuple-element.53.d_gate_ref.refs_2_, bf16[704,384]{1,0:T(8,128)(2,1)S(1)} %get-tuple-element.54.d_up_ref.refs_3_, bf16[704,2048]{1,0:T(8,128)(2,1)S(1)} %bitcast.10, bf16[704,2048]{1,0:T(8,128)(2,1)S(1)} %bitcast.15), custom_call_target="tpu_custom_call" | custom-call | flops 1107296256 | bytes 4456448 | tf_op jit(solution)/shard_map/kept/pallas_call | solution.py:350
  54.8 1.2 %collective-permute-done.2.refs_2_ = bf16[64,1024]{1,0:T(8,128)(2,1)S(1)} collective-permute-done((bf16[64,1024]{1,0:T(8,128)(2,1)S(1)}, bf16[64,1024]{1,0:T(8,128)(2,1)S(1)}, u32[]{:S(2)}, u32[]{:S(2)}) %collective-permute-start.2) | collective-permute-done | bytes 131104 | tf_op jit(solution)/shard_map/ppermute | solution.py:308
  56.0 0.1 collective-permute-start.16
  56.1 0.5 collective-permute-start.18
  56.6 1.4 %begin.1 = (f32[704,128]{1,0:T(8,128)S(1)}, f32[704,128]{1,0:T(8,128)S(1)}, f32[704,128]{1,0:T(8,128)S(1)}) custom-call(bf16[256,1024]{1,0:T(8,128)(2,1)S(1)} %collect.3.own_ref.refs_5_, bf16[704,2048]{1,0:T(8,128)(2,1)S(1)} %bitcast.11, bf16[704,2048]{1,0:T(8,128)(2,1)S(1)} %bitcast.16, bf16[704,2048]{1,0:T(8,128)(2,1)S(1)} %bitcast.20), custom_call_target="tpu_custom_call" | custom-call | flops 738197504 | bytes 6815744 | tf_op jit(solution)/shard_map/begin/pallas_call | solution.py:326
  58.1 2.3 %front.3 = (bf16[704,128]{1,0:T(8,128)(2,1)S(1)}, bf16[704,128]{1,0:T(8,128)(2,1)S(1)}, bf16[704,128]{1,0:T(8,128)(2,1)S(1)}, bf16[128,1024]{1,0:T(8,128)(2,1)S(1)}) custom-call(bf16[256,1024]{1,0:T(8,128)(2,1)S(1)} %collect.3.own_ref.refs_5_, bf16[256,1024]{1,0:T(8,128)(2,1)S(1)} %collective-permute-done.16.other_ref.refs_6_, ...), custom_call_target="tpu_custom_call" | custom-call | flops 1476395008 | bytes 13631488 | tf_op jit(solution)/shard_map/front/pallas_call | solution.py:339
  60.4 0.7 copy-done.12
  61.2 0.6 kept.3.kept_ref
  61.8 1.6 %sum.2 = (bf16[512,1024]{1,0:T(8,128)(2,1)}, f32[8,128]{1,0:T(8,128)}) custom-call(f32[384,1024]{1,0:T(8,128)S(1)} %kept.2.refs_4_.kept_ref, bf16[384,1024]{1,0:T(8,128)(2,1)S(1)} %collective-permute-done.18.got_ref), custom_call_target="tpu_custom_call" | custom-call | tf_op jit(solution)/shard_map/sum/pallas_call | solution.py:368
  63.5 0.7 sum.3
  64.2 7.9 %all-to-all-start = ((bf16[16,32,1024]{2,1,0:T(8,128)(2,1)}), bf16[16,32,1024]{2,1,0:T(8,128)(2,1)S(1)}, u32[]{:S(2)}, u32[]{:S(2)}) async-start(bf16[16,32,1024]{2,1,0:T(8,128)(2,1)} %bitcast.4), calls=%async_computation | async-start | bytes 2097152 | tf_op jit(solution)/shard_map/all_to_all | solution.py:264
  72.1 0.3 placing.1.placing_ref.refs_10_
  72.4 0.9 copy-done.4
  73.3 0.9 copy-done.6
  74.2 1.4 %copy-done.9 = bf16[768,1024]{1,0:T(8,128)(2,1)S(1)} copy-done((bf16[768,1024]{1,0:T(8,128)(2,1)S(1)}, bf16[768,1024]{1,0:T(8,128)(2,1)}, u32[]{:S(2)}) %copy-start.9) | copy-done | bytes 1572888
  75.6 1.4 %copy-done.11 = bf16[768,1024]{1,0:T(8,128)(2,1)S(1)} copy-done((bf16[768,1024]{1,0:T(8,128)(2,1)S(1)}, bf16[768,1024]{1,0:T(8,128)(2,1)}, u32[]{:S(2)}) %copy-start.11) | copy-done | bytes 1572888
  77.0 0.9 copy-done.13
  78.0 1.0 %copy-done.16 = bf16[704,384]{1,0:T(8,128)(2,1)S(1)} copy-done((bf16[704,384]{1,0:T(8,128)(2,1)S(1)}, bf16[704,384]{1,0:T(8,128)(2,1)}, u32[]{:S(2)}) %copy-start.16) | copy-done | bytes 540696
  79.0 8.9 %grads.1 = (bf16[704,2048]{1,0:T(8,128)(2,1)}, bf16[704,2048]{1,0:T(8,128)(2,1)}, bf16[704,2048]{1,0:T(8,128)(2,1)}) custom-call(bf16[768,1024]{1,0:T(8,128)(2,1)S(1)} %copy-done.9, bf16[768,1024]{1,0:T(8,128)(2,1)S(1)} %copy-done.11, bf16[704,384]{1,0:T(8,128)(2,1)S(1)} %get-tuple-element.53.d_gate_ref.refs_2_, ...), custom_call_target="tpu_custom_call" | custom-call | flops 4429185024 | bytes 14942208 | tf_op jit(solution)/shard_map/grads/pallas_call | solution.py:396
  87.9 10.3 %all-to-all-done = bf16[16,32,1024]{2,1,0:T(8,128)(2,1)S(1)} async-done(((bf16[16,32,1024]{2,1,0:T(8,128)(2,1)}), bf16[16,32,1024]{2,1,0:T(8,128)(2,1)S(1)}, u32[]{:S(2)}, u32[]{:S(2)}) %all-to-all-start) | async-done | bytes 1048608 | tf_op jit(solution)/shard_map/all_to_all | solution.py:264
  98.3 1.7 %combine.1 = bf16[256,1024]{1,0:T(8,128)(2,1)} custom-call(bf16[256,512]{1,0:T(8,128)(2,1)S(1)} %placing.1.placing_ref.refs_10_, bf16[512,1024]{1,0:T(8,128)(2,1)S(1)} %bitcast.22), custom_call_target="tpu_custom_call" | custom-call | tf_op jit(solution)/shard_map/combine/pallas_call | solution.py:252
  (45 shorter events, 0.3 us)
Async XLA Ops:
  4.1 11.3 %collective-permute-start.3 = (bf16[64,1024]{1,0:T(8,128)(2,1)}, bf16[64,1024]{1,0:T(8,128)(2,1)S(1)}, u32[]{:S(2)}, u32[]{:S(2)}) collective-permute-start(bf16[64,1024]{1,0:T(8,128)(2,1)} %get-tuple-element.41), channel_id=1, source_target_pairs={{0,30},{2,28},{4,26},{6,24},{8,22},{10,20},{12,18},{14,16},{16,14}... | collective-permute-start | bytes 393224 | tf_op jit(solution)/shard_map/ppermute | solution.py:308
  7.6 10.3 %collective-permute-start.4 = (bf16[64,1024]{1,0:T(8,128)(2,1)}, bf16[64,1024]{1,0:T(8,128)(2,1)S(1)}, u32[]{:S(2)}, u32[]{:S(2)}) collective-permute-start(bf16[64,1024]{1,0:T(8,128)(2,1)} %get-tuple-element.42), channel_id=1, source_target_pairs={{0,14},{2,12},{4,10},{6,8},{8,6},{10,4},{12,2},{14,0},{16,30},{18,... | collective-permute-start | bytes 393224 | tf_op jit(solution)/shard_map/ppermute | solution.py:308
  10.0 11.9 %collective-permute-start.5 = (bf16[64,1024]{1,0:T(8,128)(2,1)}, bf16[64,1024]{1,0:T(8,128)(2,1)S(1)}, u32[]{:S(2)}, u32[]{:S(2)}) collective-permute-start(bf16[64,1024]{1,0:T(8,128)(2,1)} %get-tuple-element.43), channel_id=1, source_target_pairs={{0,28},{2,30},{4,24},{6,26},{8,20},{10,22},{12,16},{14,18},{16,12}... | collective-permute-start | bytes 393224 | tf_op jit(solution)/shard_map/ppermute | solution.py:308
  10.3 12.7 %collective-permute-start.6 = (bf16[64,1024]{1,0:T(8,128)(2,1)}, bf16[64,1024]{1,0:T(8,128)(2,1)S(1)}, u32[]{:S(2)}, u32[]{:S(2)}) collective-permute-start(bf16[64,1024]{1,0:T(8,128)(2,1)} %get-tuple-element.44), channel_id=1, source_target_pairs={{0,12},{2,14},{4,8},{6,10},{8,4},{10,6},{12,0},{14,2},{16,28},{18,... | collective-permute-start | bytes 393224 | tf_op jit(solution)/shard_map/ppermute | solution.py:308
  11.8 14.9 %collective-permute-start.7 = (bf16[64,1024]{1,0:T(8,128)(2,1)}, bf16[64,1024]{1,0:T(8,128)(2,1)S(1)}, u32[]{:S(2)}, u32[]{:S(2)}) collective-permute-start(bf16[64,1024]{1,0:T(8,128)(2,1)} %get-tuple-element.45), channel_id=1, source_target_pairs={{0,26},{2,24},{4,30},{6,28},{8,18},{10,16},{12,22},{14,20},{16,10}... | collective-permute-start | bytes 393224 | tf_op jit(solution)/shard_map/ppermute | solution.py:308
  15.4 15.3 %collective-permute-start.8 = (bf16[64,1024]{1,0:T(8,128)(2,1)}, bf16[64,1024]{1,0:T(8,128)(2,1)S(1)}, u32[]{:S(2)}, u32[]{:S(2)}) collective-permute-start(bf16[64,1024]{1,0:T(8,128)(2,1)} %get-tuple-element.46), channel_id=1, source_target_pairs={{0,10},{2,8},{4,14},{6,12},{8,2},{10,0},{12,6},{14,4},{16,26},{18,... | collective-permute-start | bytes 393224 | tf_op jit(solution)/shard_map/ppermute | solution.py:308
  17.9 15.2 %collective-permute-start.9 = (bf16[64,1024]{1,0:T(8,128)(2,1)}, bf16[64,1024]{1,0:T(8,128)(2,1)S(1)}, u32[]{:S(2)}, u32[]{:S(2)}) collective-permute-start(bf16[64,1024]{1,0:T(8,128)(2,1)} %get-tuple-element.47), channel_id=1, source_target_pairs={{0,24},{2,26},{4,28},{6,30},{8,16},{10,18},{12,20},{14,22},{16,8},... | collective-permute-start | bytes 393224 | tf_op jit(solution)/shard_map/ppermute | solution.py:308
  21.9 12.4 %collective-permute-start.10 = (bf16[64,1024]{1,0:T(8,128)(2,1)}, bf16[64,1024]{1,0:T(8,128)(2,1)S(1)}, u32[]{:S(2)}, u32[]{:S(2)}) collective-permute-start(bf16[64,1024]{1,0:T(8,128)(2,1)} %get-tuple-element.48), channel_id=1, source_target_pairs={{0,8},{2,10},{4,12},{6,14},{8,0},{10,2},{12,4},{14,6},{16,24},{18,... | collective-permute-start | bytes 393224 | tf_op jit(solution)/shard_map/ppermute | solution.py:308
  23.1 16.5 %collective-permute-start.11 = (bf16[64,1024]{1,0:T(8,128)(2,1)}, bf16[64,1024]{1,0:T(8,128)(2,1)S(1)}, u32[]{:S(2)}, u32[]{:S(2)}) collective-permute-start(bf16[64,1024]{1,0:T(8,128)(2,1)} %get-tuple-element.49), channel_id=1, source_target_pairs={{0,22},{2,20},{4,18},{6,16},{8,30},{10,28},{12,26},{14,24},{16,6},... | collective-permute-start | bytes 393224 | tf_op jit(solution)/shard_map/ppermute | solution.py:308
  26.8 12.8 %collective-permute-start.12 = (bf16[64,1024]{1,0:T(8,128)(2,1)}, bf16[64,1024]{1,0:T(8,128)(2,1)S(1)}, u32[]{:S(2)}, u32[]{:S(2)}) collective-permute-start(bf16[64,1024]{1,0:T(8,128)(2,1)} %get-tuple-element.50), channel_id=1, source_target_pairs={{0,6},{2,4},{4,2},{6,0},{8,14},{10,12},{12,10},{14,8},{16,22},{18,... | collective-permute-start | bytes 393224 | tf_op jit(solution)/shard_map/ppermute | solution.py:308
  30.7 10.9 %collective-permute-start.13 = (bf16[64,1024]{1,0:T(8,128)(2,1)}, bf16[64,1024]{1,0:T(8,128)(2,1)S(1)}, u32[]{:S(2)}, u32[]{:S(2)}) collective-permute-start(bf16[64,1024]{1,0:T(8,128)(2,1)} %get-tuple-element.51), channel_id=1, source_target_pairs={{0,20},{2,22},{4,16},{6,18},{8,28},{10,30},{12,24},{14,26},{16,4},... | collective-permute-start | bytes 393224 | tf_op jit(solution)/shard_map/ppermute | solution.py:308
  33.2 9.2 %copy-start.19 = (bf16[64,1024]{1,0:T(8,128)(2,1)S(1)}, bf16[64,1024]{1,0:T(8,128)(2,1)}, u32[]{:S(2)}) copy-start(bf16[64,1024]{1,0:T(8,128)(2,1)} %get-tuple-element.37) | copy-start | bytes 393220
  33.2 12.1 %copy-start.18 = (bf16[64,1024]{1,0:T(8,128)(2,1)S(1)}, bf16[64,1024]{1,0:T(8,128)(2,1)}, u32[]{:S(2)}) copy-start(bf16[64,1024]{1,0:T(8,128)(2,1)} %get-tuple-element.38) | copy-start | bytes 393220
  33.2 13.7 %copy-start.17 = (bf16[64,1024]{1,0:T(8,128)(2,1)S(1)}, bf16[64,1024]{1,0:T(8,128)(2,1)}, u32[]{:S(2)}) copy-start(bf16[64,1024]{1,0:T(8,128)(2,1)} %get-tuple-element.39) | copy-start | bytes 393220
  33.2 13.7 %copy-start = (bf16[1,704,2048]{2,1,0:T(8,128)(2,1)S(1)}, bf16[1,704,2048]{2,1,0:T(8,128)(2,1)}, u32[]{:S(2)}) copy-start(bf16[1,704,2048]{2,1,0:T(8,128)(2,1)} %param.9) | copy-start | bytes 8650756
  33.2 13.7 %copy-start.1 = (bf16[1,704,2048]{2,1,0:T(8,128)(2,1)S(1)}, bf16[1,704,2048]{2,1,0:T(8,128)(2,1)}, u32[]{:S(2)}) copy-start(bf16[1,704,2048]{2,1,0:T(8,128)(2,1)} %param.10) | copy-start | bytes 8650756
  33.2 13.7 %copy-start.2 = (bf16[1,704,2048]{2,1,0:T(8,128)(2,1)S(1)}, bf16[1,704,2048]{2,1,0:T(8,128)(2,1)}, u32[]{:S(2)}) copy-start(bf16[1,704,2048]{2,1,0:T(8,128)(2,1)} %param.11) | copy-start | bytes 8650756
  33.2 9.0 %collective-permute-start.14 = (bf16[64,1024]{1,0:T(8,128)(2,1)}, bf16[64,1024]{1,0:T(8,128)(2,1)S(1)}, u32[]{:S(2)}, u32[]{:S(2)}) collective-permute-start(bf16[64,1024]{1,0:T(8,128)(2,1)} %get-tuple-element.52), channel_id=1, source_target_pairs={{0,4},{2,6},{4,0},{6,2},{8,12},{10,14},{12,8},{14,10},{16,20},{18,... | collective-permute-start | bytes 393224 | tf_op jit(solution)/shard_map/ppermute | solution.py:308
  42.3 11.0 %copy-start.8 = (bf16[768,1024]{1,0:T(8,128)(2,1)}, bf16[768,1024]{1,0:T(8,128)(2,1)S(1)}, u32[]{:S(2)}) copy-start(bf16[768,1024]{1,0:T(8,128)(2,1)S(1)} %collect.2.own_ref.refs_0_) | copy-start | bytes 4718596
  42.4 4.6 %collective-permute-start.15 = (bf16[768,1024]{1,0:T(8,128)(2,1)S(1)}, bf16[768,1024]{1,0:T(8,128)(2,1)S(1)}, u32[]{:S(2)}, u32[]{:S(2)}) collective-permute-start(bf16[768,1024]{1,0:T(8,128)(2,1)S(1)} %collect.2.own_ref.refs_0_), channel_id=1, source_target_pairs={{0,1},{1,0},{2,3},{3,2},{4,5},{5,4},{6,7},{7,6},{8,9},{9,8},{10,11... | collective-permute-start | bytes 4718600 | tf_op jit(solution)/shard_map/ppermute | solution.py:311
  42.4 12.4 %collective-permute-start = (bf16[64,1024]{1,0:T(8,128)(2,1)S(1)}, bf16[64,1024]{1,0:T(8,128)(2,1)S(1)}, u32[]{:S(2)}, u32[]{:S(2)}) collective-permute-start(bf16[64,1024]{1,0:T(8,128)(2,1)S(1)} %copy-done.19), channel_id=1, source_target_pairs={{0,18},{2,16},{4,22},{6,20},{8,26},{10,24},{12,30},{14,28},{16,2},... | collective-permute-start | bytes 393224 | tf_op jit(solution)/shard_map/ppermute | solution.py:308
  45.3 9.6 %collective-permute-start.1 = (bf16[64,1024]{1,0:T(8,128)(2,1)S(1)}, bf16[64,1024]{1,0:T(8,128)(2,1)S(1)}, u32[]{:S(2)}, u32[]{:S(2)}) collective-permute-start(bf16[64,1024]{1,0:T(8,128)(2,1)S(1)} %copy-done.18), channel_id=1, source_target_pairs={{0,2},{2,0},{4,6},{6,4},{8,10},{10,8},{12,14},{14,12},{16,18},{18,... | collective-permute-start | bytes 393224 | tf_op jit(solution)/shard_map/ppermute | solution.py:308
  46.9 9.1 %collective-permute-start.2 = (bf16[64,1024]{1,0:T(8,128)(2,1)S(1)}, bf16[64,1024]{1,0:T(8,128)(2,1)S(1)}, u32[]{:S(2)}, u32[]{:S(2)}) collective-permute-start(bf16[64,1024]{1,0:T(8,128)(2,1)S(1)} %copy-done.17), channel_id=1, source_target_pairs={{0,16},{2,18},{4,20},{6,22},{8,24},{10,26},{12,28},{14,30},{16,0},... | collective-permute-start | bytes 393224 | tf_op jit(solution)/shard_map/ppermute | solution.py:308
  46.9 6.4 %copy-start.10 = (bf16[768,1024]{1,0:T(8,128)(2,1)}, bf16[768,1024]{1,0:T(8,128)(2,1)S(1)}, u32[]{:S(2)}) copy-start(bf16[768,1024]{1,0:T(8,128)(2,1)S(1)} %collective-permute-done.15.other_ref.refs_1_) | copy-start | bytes 4718596
  53.4 1.4 %copy-start.15 = (bf16[704,384]{1,0:T(8,128)(2,1)}, bf16[704,384]{1,0:T(8,128)(2,1)S(1)}, u32[]{:S(2)}) copy-start(bf16[704,384]{1,0:T(8,128)(2,1)S(1)} %get-tuple-element.65.refs_4_) | copy-start | bytes 1622020
  53.4 2.6 %copy-start.14 = (bf16[64,1024]{1,0:T(8,128)(2,1)S(1)}, bf16[64,1024]{1,0:T(8,128)(2,1)}, u32[]{:S(2)}) copy-start(bf16[64,1024]{1,0:T(8,128)(2,1)} %get-tuple-element.40.refs_3_) | copy-start | bytes 393220
  56.0 2.0 %collective-permute-start.16 = (bf16[256,1024]{1,0:T(8,128)(2,1)S(1)}, bf16[256,1024]{1,0:T(8,128)(2,1)S(1)}, u32[]{:S(2)}, u32[]{:S(2)}) collective-permute-start(bf16[256,1024]{1,0:T(8,128)(2,1)S(1)} %collect.3.own_ref.refs_5_), channel_id=1, source_target_pairs={{0,1},{1,0},{2,3},{3,2},{4,5},{5,4},{6,7},{7,6},{8,9},{9,8},{10,11... | collective-permute-start | bytes 1572872 | tf_op jit(solution)/shard_map/ppermute | solution.py:311
  56.1 5.7 %collective-permute-start.18 = (bf16[384,1024]{1,0:T(8,128)(2,1)S(1)}, bf16[384,1024]{1,0:T(8,128)(2,1)S(1)}, u32[]{:S(2)}, u32[]{:S(2)}) collective-permute-start(bf16[384,1024]{1,0:T(8,128)(2,1)S(1)} %get-tuple-element.61), channel_id=1, source_target_pairs={{0,1},{1,0},{2,3},{3,2},{4,5},{5,4},{6,7},{7,6},{8,9},{9,8},{10,11... | collective-permute-start | bytes 2359304 | tf_op jit(solution)/shard_map/ppermute | solution.py:311
  60.4 0.7 copy-start.12
  61.1 0.7 copy-start.3
  61.1 0.7 copy-start.5
  61.1 2.4 %collective-permute-start.17 = (bf16[128,1024]{1,0:T(8,128)(2,1)S(1)}, bf16[128,1024]{1,0:T(8,128)(2,1)S(1)}, u32[]{:S(2)}, u32[]{:S(2)}) collective-permute-start(bf16[128,1024]{1,0:T(8,128)(2,1)S(1)} %get-tuple-element.60), channel_id=1, source_target_pairs={{0,1},{1,0},{2,3},{3,2},{4,5},{5,4},{6,7},{7,6},{8,9},{9,8},{10,11... | collective-permute-start | bytes 786440 | tf_op jit(solution)/shard_map/ppermute | solution.py:311
  61.8 10.3 %copy-start.7 = (s32[256,1]{0,1:T(1,128)S(1)}, s32[256,1]{0,1:T(1,128)}, u32[]{:S(2)}) copy-start(s32[256,1]{0,1:T(1,128)} %param.8) | copy-start | bytes 3076
  64.2 34.0 %all-to-all-start = ((bf16[16,32,1024]{2,1,0:T(8,128)(2,1)}), bf16[16,32,1024]{2,1,0:T(8,128)(2,1)S(1)}, u32[]{:S(2)}, u32[]{:S(2)}) async-start(bf16[16,32,1024]{2,1,0:T(8,128)(2,1)} %bitcast.4), calls=%async_computation | async-start | bytes 2097152 | tf_op jit(solution)/shard_map/all_to_all | solution.py:264
  72.4 0.9 copy-start.4
  73.3 0.9 copy-start.6
  74.2 1.4 %copy-start.9 = (bf16[768,1024]{1,0:T(8,128)(2,1)S(1)}, bf16[768,1024]{1,0:T(8,128)(2,1)}, u32[]{:S(2)}) copy-start(bf16[768,1024]{1,0:T(8,128)(2,1)} %copy-done.8) | copy-start | bytes 4718596
  75.6 1.4 %copy-start.11 = (bf16[768,1024]{1,0:T(8,128)(2,1)S(1)}, bf16[768,1024]{1,0:T(8,128)(2,1)}, u32[]{:S(2)}) copy-start(bf16[768,1024]{1,0:T(8,128)(2,1)} %copy-done.10) | copy-start | bytes 4718596
  77.0 0.9 copy-start.13
  78.0 1.0 %copy-start.16 = (bf16[704,384]{1,0:T(8,128)(2,1)S(1)}, bf16[704,384]{1,0:T(8,128)(2,1)}, u32[]{:S(2)}) copy-start(bf16[704,384]{1,0:T(8,128)(2,1)} %copy-done.15) | copy-start | bytes 1622020

commit v11 on v9

--- a/solution.py
+++ b/solution.py
@@ -27,7 +27,7 @@
     return (col if axis else row), jnp.sum(same, axis=axis, keepdims=True)
 
 
-def place_kernel(capacity, row_hbm, x_hbm, dy_hbm, *refs):
+def place_kernel(capacity, partners, row_hbm, x_hbm, dy_hbm, *refs):
     *slabs, row_ref, x_ref, dy_ref, placed_ref, row_sem, in_sems, out_sems = refs
     row_copy = pltpu.make_async_copy(row_hbm, row_ref, row_sem)
     row_copy.start()
@@ -48,20 +48,20 @@
     me = lax.axis_index("expert")
     row_copy.wait()
     route, within = rank_among_same(row_ref[...], 0)
-    slots = len(slabs) * capacity
-    slot = lax.broadcasted_iota(jnp.int32, (slots, x_ref.shape[0]), 0)
+    within_slab = lax.broadcasted_iota(jnp.int32, (capacity, x_ref.shape[0]), 0)
+    slot = jnp.concatenate([within_slab + k * capacity for k in partners], axis=0)
     placing = jnp.where(slot == (route ^ me) * capacity + within, 1.0, 0.0).astype(BF16)
     out_copies = []
     for i, ref in enumerate((x_ref, dy_ref)):
         for copy in copies[i]:
             copy.wait()
         placed_ref[i] = jnp.dot(placing, ref[...], preferred_element_type=F32).astype(BF16)
-        for k, slab in enumerate(slabs):
+        for j, slab in enumerate(slabs):
             out_copies.append(
                 pltpu.make_async_copy(
-                    placed_ref.at[i, k * capacity : (k + 1) * capacity],
+                    placed_ref.at[i, j * capacity : (j + 1) * capacity],
                     slab.at[i * capacity : (i + 1) * capacity],
-                    out_sems.at[i, k],
+                    out_sems.at[i, j],
                 )
             )
             out_copies[-1].start()
@@ -282,25 +282,29 @@
     cut = 3 * experts // 4
     first, second = turns[:cut], turns[cut:] + [0]
 
-    slabs = list(
-        pl.pallas_call(
-            functools.partial(place_kernel, capacity),
-            out_shape=[jax.ShapeDtypeStruct((2 * capacity, width), BF16)] * experts,
+    def place(partners):
+        return pl.pallas_call(
+            functools.partial(place_kernel, capacity, partners),
+            out_shape=[jax.ShapeDtypeStruct((2 * capacity, width), BF16)] * len(partners),
             in_specs=[IN_HBM] * 3,
-            out_specs=[IN_HBM] * experts,
+            out_specs=[IN_HBM] * len(partners),
             scratch_shapes=[
                 pltpu.VMEM((1, tok_rows), jnp.int32),
                 pltpu.VMEM((tok_rows, width), BF16),
                 pltpu.VMEM((tok_rows, width), BF16),
-                pltpu.VMEM((2, experts * capacity, width), BF16),
+                pltpu.VMEM((2, len(partners) * capacity, width), BF16),
                 pltpu.SemaphoreType.DMA,
                 pltpu.SemaphoreType.DMA((2, PIECES)),
-                pltpu.SemaphoreType.DMA((2, experts)),
+                pltpu.SemaphoreType.DMA((2, len(partners))),
             ],
             compiler_params=params(LARGE),
             name="place",
         )(ids_row, tokens, upstream)
-    )
+
+    early = experts // 2 - 1
+    slabs = {}
+    for partners in (turns[:early], turns[early:] + [0]):
+        slabs.update(zip(partners, place(partners)))
 
     def swap(k):
         return lax.ppermute(slabs[k], "expert", [(e, e ^ k) for e in range(experts)])

time: 99.3 us -> 98.6 us (level)
  waiting for transfers between devices: 29.2 us -> 24 us
  starting transfers between devices: 33.8 us -> 36.1 us
  Pallas kernels: 27.6 us -> 29.7 us
    ppermute x15, waiting for transfers between devices: 18.6 us -> 13.4 us  [swap(): lax.ppermute(slabs[k], 'expert', [(e, e ^ k) for e in range(experts)])]
    ppermute x15, starting transfers between devices: 25.1 us -> 27.5 us  [swap(): lax.ppermute(slabs[k], 'expert', [(e, e ^ k) for e in range(experts)])]
    pallas_call x1 -> x2, Pallas kernels: 3.5 us -> 5.65 us  [place(): pl.pallas_call(functools.partial(place_kernel, capacity, partners), out_s...]
  transfers between devices with their start and end apart: 20 -> 20, of which waited for: 13 -> 11; matrix products, arithmetic and copies ran while one was open for 0% -> 0% of each run, Pallas kernels for 21% -> 24%
where the time goes in v11:
time: 98.6 us; the launch traced here: 98.2 us
  starting transfers between devices  36.1 us (37%)
  Pallas kernels  29.7 us (30%)
  waiting for transfers between devices  24 us (24%)
  local copies, waits for them, and re-layouts  7.36 us (7%)
  between operations  1.04 us (1%)
    ppermute x15, starting transfers between devices, swap(): lax.ppermute(slabs[k], 'expert', [(e, e ^ k) for e in range(experts)])  27.5 us
    ppermute x15, waiting for transfers between devices, swap(): lax.ppermute(slabs[k], 'expert', [(e, e ^ k) for e in range(experts)])  13.4 us
    all_to_all x1, waiting for transfers between devices, to_experts(): lax.all_to_all(rows.reshape(experts, rows.shape[0] // experts, rows.shape...  9.92 us
    pallas_call x1, Pallas kernels, grouped(): pl.pallas_call(functools.partial(grads_kernel, sizes), grid=(units // til...  8.91 us
    pallas_call x2, Pallas kernels, front(): pl.pallas_call(functools.partial(front_kernel, tile), out_shape=[jax.Shap...  8.41 us
    all_to_all x1, starting transfers between devices, to_experts(): lax.all_to_all(rows.reshape(experts, rows.shape[0] // experts, rows.shape...  7.9 us
    unnamed x40, local copies, waits for them, and re-layouts  7.36 us
    pallas_call x2, Pallas kernels, place(): pl.pallas_call(functools.partial(place_kernel, capacity, partners), out_s...  5.65 us
  transfers between devices with their start and end apart: 20, of which 11 were waited for; matrix products, arithmetic and copies ran while one was open for 0% of the time, Pallas kernels for 24%

profile of v11, /device:TPU:8, one launch (start us, length us, event | category | flops | bytes accessed | tf_op | source)
XLA Modules:
  0.0 98.2 jit_solution(18103387624962076189)
XLA Ops:
  0.6 2.8 %place.2 = (bf16[64,1024]{1,0:T(8,128)(2,1)}, bf16[64,1024]{1,0:T(8,128)(2,1)}, bf16[64,1024]{1,0:T(8,128)(2,1)}, bf16[64,1024]{1,0:T(8,128)(2,1)}, bf16[64,1024...) custom-call(s32[1,256]{1,0:T(1,128)} %bitcast.23, bf16[256,1024]{1,0:T(8,128)(2,1)} %x_hbm.3, ...), custom_call_target="tpu_custom_call" | custom-call | tf_op jit(solution)/shard_map/place/pallas_call | solution.py:286
  3.4 3.5 %collective-permute-start = (bf16[64,1024]{1,0:T(8,128)(2,1)}, bf16[64,1024]{1,0:T(8,128)(2,1)S(1)}, u32[]{:S(2)}, u32[]{:S(2)}) collective-permute-start(bf16[64,1024]{1,0:T(8,128)(2,1)} %get-tuple-element.36), channel_id=1, source_target_pairs={{0,30},{2,28},{4,26},{6,24},{8,22},{10,20},{12,18},{14,16},{16,14}... | collective-permute-start | bytes 393224 | tf_op jit(solution)/shard_map/ppermute | solution.py:310
  6.9 2.4 %collective-permute-start.1 = (bf16[64,1024]{1,0:T(8,128)(2,1)}, bf16[64,1024]{1,0:T(8,128)(2,1)S(1)}, u32[]{:S(2)}, u32[]{:S(2)}) collective-permute-start(bf16[64,1024]{1,0:T(8,128)(2,1)} %get-tuple-element.37), channel_id=1, source_target_pairs={{0,14},{2,12},{4,10},{6,8},{8,6},{10,4},{12,2},{14,0},{16,30},{18,... | collective-permute-start | bytes 393224 | tf_op jit(solution)/shard_map/ppermute | solution.py:310
  9.3 0.3 collective-permute-start.2
  9.6 1.5 %collective-permute-start.3 = (bf16[64,1024]{1,0:T(8,128)(2,1)}, bf16[64,1024]{1,0:T(8,128)(2,1)S(1)}, u32[]{:S(2)}, u32[]{:S(2)}) collective-permute-start(bf16[64,1024]{1,0:T(8,128)(2,1)} %get-tuple-element.39), channel_id=1, source_target_pairs={{0,12},{2,14},{4,8},{6,10},{8,4},{10,6},{12,0},{14,2},{16,28},{18,... | collective-permute-start | bytes 393224 | tf_op jit(solution)/shard_map/ppermute | solution.py:310
  11.1 2.5 %collective-permute-start.4 = (bf16[64,1024]{1,0:T(8,128)(2,1)}, bf16[64,1024]{1,0:T(8,128)(2,1)S(1)}, u32[]{:S(2)}, u32[]{:S(2)}) collective-permute-start(bf16[64,1024]{1,0:T(8,128)(2,1)} %get-tuple-element.40), channel_id=1, source_target_pairs={{0,26},{2,24},{4,30},{6,28},{8,18},{10,16},{12,22},{14,20},{16,10}... | collective-permute-start | bytes 393224 | tf_op jit(solution)/shard_map/ppermute | solution.py:310
  13.6 1.1 %collective-permute-done.refs_0_ = bf16[64,1024]{1,0:T(8,128)(2,1)S(1)} collective-permute-done((bf16[64,1024]{1,0:T(8,128)(2,1)}, bf16[64,1024]{1,0:T(8,128)(2,1)S(1)}, u32[]{:S(2)}, u32[]{:S(2)}) %collective-permute-start) | collective-permute-done | bytes 131104 | tf_op jit(solution)/shard_map/ppermute | solution.py:310
  14.7 1.4 %collective-permute-start.5 = (bf16[64,1024]{1,0:T(8,128)(2,1)}, bf16[64,1024]{1,0:T(8,128)(2,1)S(1)}, u32[]{:S(2)}, u32[]{:S(2)}) collective-permute-start(bf16[64,1024]{1,0:T(8,128)(2,1)} %get-tuple-element.41), channel_id=1, source_target_pairs={{0,10},{2,8},{4,14},{6,12},{8,2},{10,0},{12,6},{14,4},{16,26},{18,... | collective-permute-start | bytes 393224 | tf_op jit(solution)/shard_map/ppermute | solution.py:310
  16.1 1.2 %collective-permute-done.1.refs_1_ = bf16[64,1024]{1,0:T(8,128)(2,1)S(1)} collective-permute-done((bf16[64,1024]{1,0:T(8,128)(2,1)}, bf16[64,1024]{1,0:T(8,128)(2,1)S(1)}, u32[]{:S(2)}, u32[]{:S(2)}) %collective-permute-start.1) | collective-permute-done | bytes 131104 | tf_op jit(solution)/shard_map/ppermute | solution.py:310
  17.2 0.6 collective-permute-start.6
  17.8 2.9 %place.3 = (bf16[64,1024]{1,0:T(8,128)(2,1)}, bf16[64,1024]{1,0:T(8,128)(2,1)}, bf16[64,1024]{1,0:T(8,128)(2,1)}, bf16[64,1024]{1,0:T(8,128)(2,1)}, bf16[64,1024...) custom-call(s32[1,256]{1,0:T(1,128)} %bitcast.24, ...), custom_call_target="tpu_custom_call" | custom-call | tf_op jit(solution)/shard_map/place/pallas_call | solution.py:286
  20.7 0.5 collective-permute-done.2.refs_2_
  21.2 3.6 %collective-permute-start.7 = (bf16[64,1024]{1,0:T(8,128)(2,1)}, bf16[64,1024]{1,0:T(8,128)(2,1)S(1)}, u32[]{:S(2)}, u32[]{:S(2)}) collective-permute-start(bf16[64,1024]{1,0:T(8,128)(2,1)} %get-tuple-element.43), channel_id=1, source_target_pairs={{0,8},{2,10},{4,12},{6,14},{8,0},{10,2},{12,4},{14,6},{16,24},{18,... | collective-permute-start | bytes 393224 | tf_op jit(solution)/shard_map/ppermute | solution.py:310
  24.8 1.5 %collective-permute-start.8 = (bf16[64,1024]{1,0:T(8,128)(2,1)}, bf16[64,1024]{1,0:T(8,128)(2,1)S(1)}, u32[]{:S(2)}, u32[]{:S(2)}) collective-permute-start(bf16[64,1024]{1,0:T(8,128)(2,1)} %get-tuple-element.44), channel_id=1, source_target_pairs={{0,22},{2,20},{4,18},{6,16},{8,30},{10,28},{12,26},{14,24},{16,6},... | collective-permute-start | bytes 393224 | tf_op jit(solution)/shard_map/ppermute | solution.py:310
  26.3 3.7 %collective-permute-start.9 = (bf16[64,1024]{1,0:T(8,128)(2,1)}, bf16[64,1024]{1,0:T(8,128)(2,1)S(1)}, u32[]{:S(2)}, u32[]{:S(2)}) collective-permute-start(bf16[64,1024]{1,0:T(8,128)(2,1)} %get-tuple-element.45), channel_id=1, source_target_pairs={{0,6},{2,4},{4,2},{6,0},{8,14},{10,12},{12,10},{14,8},{16,22},{18,... | collective-permute-start | bytes 393224 | tf_op jit(solution)/shard_map/ppermute | solution.py:310
  30.0 1.5 %collective-permute-start.10 = (bf16[64,1024]{1,0:T(8,128)(2,1)}, bf16[64,1024]{1,0:T(8,128)(2,1)S(1)}, u32[]{:S(2)}, u32[]{:S(2)}) collective-permute-start(bf16[64,1024]{1,0:T(8,128)(2,1)} %get-tuple-element.46), channel_id=1, source_target_pairs={{0,20},{2,22},{4,16},{6,18},{8,28},{10,30},{12,24},{14,26},{16,4},... | collective-permute-start | bytes 393224 | tf_op jit(solution)/shard_map/ppermute | solution.py:310
  31.5 0.9 collective-permute-done.6.refs_6_
  32.5 0.6 collective-permute-start.11
  33.1 0.6 collective-permute-done.7.refs_7_
  33.6 5.1 %collective-permute-done.8.refs_8_ = bf16[64,1024]{1,0:T(8,128)(2,1)S(1)} collective-permute-done((bf16[64,1024]{1,0:T(8,128)(2,1)}, bf16[64,1024]{1,0:T(8,128)(2,1)S(1)}, u32[]{:S(2)}, u32[]{:S(2)}) %collective-permute-start.8) | collective-permute-done | bytes 131104 | tf_op jit(solution)/shard_map/ppermute | solution.py:310
  38.7 2.1 %collective-permute-done.10.refs_10_ = bf16[64,1024]{1,0:T(8,128)(2,1)S(1)} collective-permute-done((bf16[64,1024]{1,0:T(8,128)(2,1)}, bf16[64,1024]{1,0:T(8,128)(2,1)S(1)}, u32[]{:S(2)}, u32[]{:S(2)}) %collective-permute-start.10) | collective-permute-done | bytes 131104 | tf_op jit(solution)/shard_map/ppermute | solution.py:310
  40.9 0.6 collective-permute-done.11.refs_11_
  41.5 0.1 collect.2.own_ref.refs_0_
  41.7 2.8 %collective-permute-start.14 = (bf16[64,1024]{1,0:T(8,128)(2,1)S(1)}, bf16[64,1024]{1,0:T(8,128)(2,1)S(1)}, u32[]{:S(2)}, u32[]{:S(2)}) collective-permute-start(bf16[64,1024]{1,0:T(8,128)(2,1)S(1)} %copy-done.19), channel_id=1, source_target_pairs={{0,18},{2,16},{4,22},{6,20},{8,26},{10,24},{12,30},{14,28},{16,2},... | collective-permute-start | bytes 393224 | tf_op jit(solution)/shard_map/ppermute | solution.py:310
  44.5 1.6 %collective-permute-start.15 = (bf16[64,1024]{1,0:T(8,128)(2,1)S(1)}, bf16[64,1024]{1,0:T(8,128)(2,1)S(1)}, u32[]{:S(2)}, u32[]{:S(2)}) collective-permute-start(bf16[64,1024]{1,0:T(8,128)(2,1)S(1)} %copy-done.18), channel_id=1, source_target_pairs={{0,2},{2,0},{4,6},{6,4},{8,10},{10,8},{12,14},{14,12},{16,18},{18,... | collective-permute-start | bytes 393224 | tf_op jit(solution)/shard_map/ppermute | solution.py:310
  46.2 6.3 %front.2 = (bf16[704,384]{1,0:T(8,128)(2,1)S(1)}, bf16[704,384]{1,0:T(8,128)(2,1)S(1)}, bf16[704,384]{1,0:T(8,128)(2,1)S(1)}, bf16[384,1024]{1,0:T(8,128)(2,1)S(1)}) custom-call(bf16[768,1024]{1,0:T(8,128)(2,1)S(1)} %collect.2.own_ref.refs_0_, bf16[768,1024]{1,0:T(8,128)(2,1)S(1)} %collective-permute-done.12.other_ref.refs_1_, ...), custom_call_target="tpu_custom_call" | custom-call | flops 4429185024 | bytes 17825792 | tf_op jit(solution)/shard_map/front/pallas_call | solution.py:341
  52.6 1.4 %kept.2.kept_ref.refs_4_ = f32[384,1024]{1,0:T(8,128)S(1)} custom-call(bf16[704,384]{1,0:T(8,128)(2,1)S(1)} %get-tuple-element.48.d_gate_ref.refs_2_, bf16[704,384]{1,0:T(8,128)(2,1)S(1)} %get-tuple-element.49.d_up_ref.refs_3_, bf16[704,2048]{1,0:T(8,128)(2,1)S(1)} %bitcast.10, bf16[704,2048]{1,0:T(8,128)(2,1)S(1)} %bitcast.15), custom_call_target="tpu_custom_call" | custom-call | flops 1107296256 | bytes 4456448 | tf_op jit(solution)/shard_map/kept/pallas_call | solution.py:351
  54.0 1.3 %collective-permute-done.16.refs_2_ = bf16[64,1024]{1,0:T(8,128)(2,1)S(1)} collective-permute-done((bf16[64,1024]{1,0:T(8,128)(2,1)S(1)}, bf16[64,1024]{1,0:T(8,128)(2,1)S(1)}, u32[]{:S(2)}, u32[]{:S(2)}) %collective-permute-start.16) | collective-permute-done | bytes 131104 | tf_op jit(solution)/shard_map/ppermute | solution.py:310
  55.3 0.1 collective-permute-start.17
  55.4 0.5 collective-permute-start.13
  55.9 1.4 %begin.1 = (f32[704,128]{1,0:T(8,128)S(1)}, f32[704,128]{1,0:T(8,128)S(1)}, f32[704,128]{1,0:T(8,128)S(1)}) custom-call(bf16[256,1024]{1,0:T(8,128)(2,1)S(1)} %collect.3.own_ref.refs_5_, bf16[704,2048]{1,0:T(8,128)(2,1)S(1)} %bitcast.11, bf16[704,2048]{1,0:T(8,128)(2,1)S(1)} %bitcast.16, bf16[704,2048]{1,0:T(8,128)(2,1)S(1)} %bitcast.20), custom_call_target="tpu_custom_call" | custom-call | flops 738197504 | bytes 6815744 | tf_op jit(solution)/shard_map/begin/pallas_call | solution.py:328
  57.3 2.1 %front.3 = (bf16[704,128]{1,0:T(8,128)(2,1)S(1)}, bf16[704,128]{1,0:T(8,128)(2,1)S(1)}, bf16[704,128]{1,0:T(8,128)(2,1)S(1)}, bf16[128,1024]{1,0:T(8,128)(2,1)S(1)}) custom-call(bf16[256,1024]{1,0:T(8,128)(2,1)S(1)} %collect.3.own_ref.refs_5_, bf16[256,1024]{1,0:T(8,128)(2,1)S(1)} %collective-permute-done.17.other_ref.refs_6_, ...), custom_call_target="tpu_custom_call" | custom-call | flops 1476395008 | bytes 13631488 | tf_op jit(solution)/shard_map/front/pallas_call | solution.py:341
  59.4 0.7 copy-done.12
  60.2 0.6 kept.3.kept_ref
  60.8 0.1 sum.1.sum_ref
  61.0 0.7 collective-permute-done.18.got_ref
  61.6 1.1 %last_sum.1 = (bf16[512,1024]{1,0:T(8,128)(2,1)}, f32[8,128]{1,0:T(8,128)S(1)}) custom-call(bf16[384,1024]{1,0:T(8,128)(2,1)S(1)} %sum.1.sum_ref, f32[128,1024]{1,0:T(8,128)S(1)} %kept.3.kept_ref, bf16[128,1024]{1,0:T(8,128)(2,1)S(1)} %collective-permute-done.18.got_ref), custom_call_target="tpu_custom_call" | custom-call | tf_op jit(solution)/shard_map/last_sum/pallas_call | solution.py:375
  62.7 7.9 %all-to-all-start = ((bf16[16,32,1024]{2,1,0:T(8,128)(2,1)}), bf16[16,32,1024]{2,1,0:T(8,128)(2,1)S(1)}, u32[]{:S(2)}, u32[]{:S(2)}) async-start(bf16[16,32,1024]{2,1,0:T(8,128)(2,1)} %bitcast.4), calls=%async_computation | async-start | bytes 2097152 | tf_op jit(solution)/shard_map/all_to_all | solution.py:262
  70.6 0.3 placing.1.placing_ref.refs_10_
  70.9 0.9 copy-done.4
  71.9 0.9 copy-done.6
  72.8 1.4 %copy-done.9 = bf16[768,1024]{1,0:T(8,128)(2,1)S(1)} copy-done((bf16[768,1024]{1,0:T(8,128)(2,1)S(1)}, bf16[768,1024]{1,0:T(8,128)(2,1)}, u32[]{:S(2)}) %copy-start.9) | copy-done | bytes 1572888
  74.2 1.4 %copy-done.11 = bf16[768,1024]{1,0:T(8,128)(2,1)S(1)} copy-done((bf16[768,1024]{1,0:T(8,128)(2,1)S(1)}, bf16[768,1024]{1,0:T(8,128)(2,1)}, u32[]{:S(2)}) %copy-start.11) | copy-done | bytes 1572888
  75.6 0.9 copy-done.13
  76.5 1.0 %copy-done.16 = bf16[704,384]{1,0:T(8,128)(2,1)S(1)} copy-done((bf16[704,384]{1,0:T(8,128)(2,1)S(1)}, bf16[704,384]{1,0:T(8,128)(2,1)}, u32[]{:S(2)}) %copy-start.16) | copy-done | bytes 540696
  77.6 8.9 %grads.1 = (bf16[704,2048]{1,0:T(8,128)(2,1)}, bf16[704,2048]{1,0:T(8,128)(2,1)}, bf16[704,2048]{1,0:T(8,128)(2,1)}) custom-call(bf16[768,1024]{1,0:T(8,128)(2,1)S(1)} %copy-done.9, bf16[768,1024]{1,0:T(8,128)(2,1)S(1)} %copy-done.11, bf16[704,384]{1,0:T(8,128)(2,1)S(1)} %get-tuple-element.48.d_gate_ref.refs_2_, ...), custom_call_target="tpu_custom_call" | custom-call | flops 4429185024 | bytes 14942208 | tf_op jit(solution)/shard_map/grads/pallas_call | solution.py:395
  86.5 9.9 %all-to-all-done = bf16[16,32,1024]{2,1,0:T(8,128)(2,1)S(1)} async-done(((bf16[16,32,1024]{2,1,0:T(8,128)(2,1)}), bf16[16,32,1024]{2,1,0:T(8,128)(2,1)S(1)}, u32[]{:S(2)}, u32[]{:S(2)}) %all-to-all-start) | async-done | bytes 1048608 | tf_op jit(solution)/shard_map/all_to_all | solution.py:262
  96.4 1.7 %combine.1 = bf16[256,1024]{1,0:T(8,128)(2,1)} custom-call(bf16[256,512]{1,0:T(8,128)(2,1)S(1)} %placing.1.placing_ref.refs_10_, bf16[512,1024]{1,0:T(8,128)(2,1)S(1)} %bitcast.22), custom_call_target="tpu_custom_call" | custom-call | tf_op jit(solution)/shard_map/combine/pallas_call | solution.py:250
  (46 shorter events, 0.4 us)
Async XLA Ops:
  3.4 11.3 %collective-permute-start = (bf16[64,1024]{1,0:T(8,128)(2,1)}, bf16[64,1024]{1,0:T(8,128)(2,1)S(1)}, u32[]{:S(2)}, u32[]{:S(2)}) collective-permute-start(bf16[64,1024]{1,0:T(8,128)(2,1)} %get-tuple-element.36), channel_id=1, source_target_pairs={{0,30},{2,28},{4,26},{6,24},{8,22},{10,20},{12,18},{14,16},{16,14}... | collective-permute-start | bytes 393224 | tf_op jit(solution)/shard_map/ppermute | solution.py:310
  6.9 10.3 %collective-permute-start.1 = (bf16[64,1024]{1,0:T(8,128)(2,1)}, bf16[64,1024]{1,0:T(8,128)(2,1)S(1)}, u32[]{:S(2)}, u32[]{:S(2)}) collective-permute-start(bf16[64,1024]{1,0:T(8,128)(2,1)} %get-tuple-element.37), channel_id=1, source_target_pairs={{0,14},{2,12},{4,10},{6,8},{8,6},{10,4},{12,2},{14,0},{16,30},{18,... | collective-permute-start | bytes 393224 | tf_op jit(solution)/shard_map/ppermute | solution.py:310
  9.3 11.9 %collective-permute-start.2 = (bf16[64,1024]{1,0:T(8,128)(2,1)}, bf16[64,1024]{1,0:T(8,128)(2,1)S(1)}, u32[]{:S(2)}, u32[]{:S(2)}) collective-permute-start(bf16[64,1024]{1,0:T(8,128)(2,1)} %get-tuple-element.38), channel_id=1, source_target_pairs={{0,28},{2,30},{4,24},{6,26},{8,20},{10,22},{12,16},{14,18},{16,12}... | collective-permute-start | bytes 393224 | tf_op jit(solution)/shard_map/ppermute | solution.py:310
  9.6 15.2 %collective-permute-start.3 = (bf16[64,1024]{1,0:T(8,128)(2,1)}, bf16[64,1024]{1,0:T(8,128)(2,1)S(1)}, u32[]{:S(2)}, u32[]{:S(2)}) collective-permute-start(bf16[64,1024]{1,0:T(8,128)(2,1)} %get-tuple-element.39), channel_id=1, source_target_pairs={{0,12},{2,14},{4,8},{6,10},{8,4},{10,6},{12,0},{14,2},{16,28},{18,... | collective-permute-start | bytes 393224 | tf_op jit(solution)/shard_map/ppermute | solution.py:310
  11.1 15.2 %collective-permute-start.4 = (bf16[64,1024]{1,0:T(8,128)(2,1)}, bf16[64,1024]{1,0:T(8,128)(2,1)S(1)}, u32[]{:S(2)}, u32[]{:S(2)}) collective-permute-start(bf16[64,1024]{1,0:T(8,128)(2,1)} %get-tuple-element.40), channel_id=1, source_target_pairs={{0,26},{2,24},{4,30},{6,28},{8,18},{10,16},{12,22},{14,20},{16,10}... | collective-permute-start | bytes 393224 | tf_op jit(solution)/shard_map/ppermute | solution.py:310
  14.7 15.3 %collective-permute-start.5 = (bf16[64,1024]{1,0:T(8,128)(2,1)}, bf16[64,1024]{1,0:T(8,128)(2,1)S(1)}, u32[]{:S(2)}, u32[]{:S(2)}) collective-permute-start(bf16[64,1024]{1,0:T(8,128)(2,1)} %get-tuple-element.41), channel_id=1, source_target_pairs={{0,10},{2,8},{4,14},{6,12},{8,2},{10,0},{12,6},{14,4},{16,26},{18,... | collective-permute-start | bytes 393224 | tf_op jit(solution)/shard_map/ppermute | solution.py:310
  17.2 15.2 %collective-permute-start.6 = (bf16[64,1024]{1,0:T(8,128)(2,1)}, bf16[64,1024]{1,0:T(8,128)(2,1)S(1)}, u32[]{:S(2)}, u32[]{:S(2)}) collective-permute-start(bf16[64,1024]{1,0:T(8,128)(2,1)} %get-tuple-element.42), channel_id=1, source_target_pairs={{0,24},{2,26},{4,28},{6,30},{8,16},{10,18},{12,20},{14,22},{16,8},... | collective-permute-start | bytes 393224 | tf_op jit(solution)/shard_map/ppermute | solution.py:310
  21.2 12.4 %collective-permute-start.7 = (bf16[64,1024]{1,0:T(8,128)(2,1)}, bf16[64,1024]{1,0:T(8,128)(2,1)S(1)}, u32[]{:S(2)}, u32[]{:S(2)}) collective-permute-start(bf16[64,1024]{1,0:T(8,128)(2,1)} %get-tuple-element.43), channel_id=1, source_target_pairs={{0,8},{2,10},{4,12},{6,14},{8,0},{10,2},{12,4},{14,6},{16,24},{18,... | collective-permute-start | bytes 393224 | tf_op jit(solution)/shard_map/ppermute | solution.py:310
  24.8 13.9 %collective-permute-start.8 = (bf16[64,1024]{1,0:T(8,128)(2,1)}, bf16[64,1024]{1,0:T(8,128)(2,1)S(1)}, u32[]{:S(2)}, u32[]{:S(2)}) collective-permute-start(bf16[64,1024]{1,0:T(8,128)(2,1)} %get-tuple-element.44), channel_id=1, source_target_pairs={{0,22},{2,20},{4,18},{6,16},{8,30},{10,28},{12,26},{14,24},{16,6},... | collective-permute-start | bytes 393224 | tf_op jit(solution)/shard_map/ppermute | solution.py:310
  26.3 12.4 %collective-permute-start.9 = (bf16[64,1024]{1,0:T(8,128)(2,1)}, bf16[64,1024]{1,0:T(8,128)(2,1)S(1)}, u32[]{:S(2)}, u32[]{:S(2)}) collective-permute-start(bf16[64,1024]{1,0:T(8,128)(2,1)} %get-tuple-element.45), channel_id=1, source_target_pairs={{0,6},{2,4},{4,2},{6,0},{8,14},{10,12},{12,10},{14,8},{16,22},{18,... | collective-permute-start | bytes 393224 | tf_op jit(solution)/shard_map/ppermute | solution.py:310
  30.0 10.9 %collective-permute-start.10 = (bf16[64,1024]{1,0:T(8,128)(2,1)}, bf16[64,1024]{1,0:T(8,128)(2,1)S(1)}, u32[]{:S(2)}, u32[]{:S(2)}) collective-permute-start(bf16[64,1024]{1,0:T(8,128)(2,1)} %get-tuple-element.46), channel_id=1, source_target_pairs={{0,20},{2,22},{4,16},{6,18},{8,28},{10,30},{12,24},{14,26},{16,4},... | collective-permute-start | bytes 393224 | tf_op jit(solution)/shard_map/ppermute | solution.py:310
  32.5 9.2 %copy-start.19 = (bf16[64,1024]{1,0:T(8,128)(2,1)S(1)}, bf16[64,1024]{1,0:T(8,128)(2,1)}, u32[]{:S(2)}) copy-start(bf16[64,1024]{1,0:T(8,128)(2,1)} %get-tuple-element.51) | copy-start | bytes 393220
  32.5 12.1 %copy-start.18 = (bf16[64,1024]{1,0:T(8,128)(2,1)S(1)}, bf16[64,1024]{1,0:T(8,128)(2,1)}, u32[]{:S(2)}) copy-start(bf16[64,1024]{1,0:T(8,128)(2,1)} %get-tuple-element.52) | copy-start | bytes 393220
  32.5 13.7 %copy-start.17 = (bf16[64,1024]{1,0:T(8,128)(2,1)S(1)}, bf16[64,1024]{1,0:T(8,128)(2,1)}, u32[]{:S(2)}) copy-start(bf16[64,1024]{1,0:T(8,128)(2,1)} %get-tuple-element.53) | copy-start | bytes 393220
  32.5 13.7 %copy-start = (bf16[1,704,2048]{2,1,0:T(8,128)(2,1)S(1)}, bf16[1,704,2048]{2,1,0:T(8,128)(2,1)}, u32[]{:S(2)}) copy-start(bf16[1,704,2048]{2,1,0:T(8,128)(2,1)} %param.9) | copy-start | bytes 8650756
  32.5 13.7 %copy-start.1 = (bf16[1,704,2048]{2,1,0:T(8,128)(2,1)S(1)}, bf16[1,704,2048]{2,1,0:T(8,128)(2,1)}, u32[]{:S(2)}) copy-start(bf16[1,704,2048]{2,1,0:T(8,128)(2,1)} %param.10) | copy-start | bytes 8650756
  32.5 13.7 %copy-start.2 = (bf16[1,704,2048]{2,1,0:T(8,128)(2,1)S(1)}, bf16[1,704,2048]{2,1,0:T(8,128)(2,1)}, u32[]{:S(2)}) copy-start(bf16[1,704,2048]{2,1,0:T(8,128)(2,1)} %param.11) | copy-start | bytes 8650756
  32.5 9.0 %collective-permute-start.11 = (bf16[64,1024]{1,0:T(8,128)(2,1)}, bf16[64,1024]{1,0:T(8,128)(2,1)S(1)}, u32[]{:S(2)}, u32[]{:S(2)}) collective-permute-start(bf16[64,1024]{1,0:T(8,128)(2,1)} %get-tuple-element.47), channel_id=1, source_target_pairs={{0,4},{2,6},{4,0},{6,2},{8,12},{10,14},{12,8},{14,10},{16,20},{18,... | collective-permute-start | bytes 393224 | tf_op jit(solution)/shard_map/ppermute | solution.py:310
  41.6 10.9 %copy-start.8 = (bf16[768,1024]{1,0:T(8,128)(2,1)}, bf16[768,1024]{1,0:T(8,128)(2,1)S(1)}, u32[]{:S(2)}) copy-start(bf16[768,1024]{1,0:T(8,128)(2,1)S(1)} %collect.2.own_ref.refs_0_) | copy-start | bytes 4718596
  41.6 4.6 %collective-permute-start.12 = (bf16[768,1024]{1,0:T(8,128)(2,1)S(1)}, bf16[768,1024]{1,0:T(8,128)(2,1)S(1)}, u32[]{:S(2)}, u32[]{:S(2)}) collective-permute-start(bf16[768,1024]{1,0:T(8,128)(2,1)S(1)} %collect.2.own_ref.refs_0_), channel_id=1, source_target_pairs={{0,1},{1,0},{2,3},{3,2},{4,5},{5,4},{6,7},{7,6},{8,9},{9,8},{10,11... | collective-permute-start | bytes 4718600 | tf_op jit(solution)/shard_map/ppermute | solution.py:313
  41.7 12.3 %collective-permute-start.14 = (bf16[64,1024]{1,0:T(8,128)(2,1)S(1)}, bf16[64,1024]{1,0:T(8,128)(2,1)S(1)}, u32[]{:S(2)}, u32[]{:S(2)}) collective-permute-start(bf16[64,1024]{1,0:T(8,128)(2,1)S(1)} %copy-done.19), channel_id=1, source_target_pairs={{0,18},{2,16},{4,22},{6,20},{8,26},{10,24},{12,30},{14,28},{16,2},... | collective-permute-start | bytes 393224 | tf_op jit(solution)/shard_map/ppermute | solution.py:310
  44.5 9.5 %collective-permute-start.15 = (bf16[64,1024]{1,0:T(8,128)(2,1)S(1)}, bf16[64,1024]{1,0:T(8,128)(2,1)S(1)}, u32[]{:S(2)}, u32[]{:S(2)}) collective-permute-start(bf16[64,1024]{1,0:T(8,128)(2,1)S(1)} %copy-done.18), channel_id=1, source_target_pairs={{0,2},{2,0},{4,6},{6,4},{8,10},{10,8},{12,14},{14,12},{16,18},{18,... | collective-permute-start | bytes 393224 | tf_op jit(solution)/shard_map/ppermute | solution.py:310
  46.1 9.1 %collective-permute-start.16 = (bf16[64,1024]{1,0:T(8,128)(2,1)S(1)}, bf16[64,1024]{1,0:T(8,128)(2,1)S(1)}, u32[]{:S(2)}, u32[]{:S(2)}) collective-permute-start(bf16[64,1024]{1,0:T(8,128)(2,1)S(1)} %copy-done.17), channel_id=1, source_target_pairs={{0,16},{2,18},{4,20},{6,22},{8,24},{10,26},{12,28},{14,30},{16,0},... | collective-permute-start | bytes 393224 | tf_op jit(solution)/shard_map/ppermute | solution.py:310
  46.2 6.4 %copy-start.10 = (bf16[768,1024]{1,0:T(8,128)(2,1)}, bf16[768,1024]{1,0:T(8,128)(2,1)S(1)}, u32[]{:S(2)}) copy-start(bf16[768,1024]{1,0:T(8,128)(2,1)S(1)} %collective-permute-done.12.other_ref.refs_1_) | copy-start | bytes 4718596
  52.5 1.4 %copy-start.15 = (bf16[704,384]{1,0:T(8,128)(2,1)}, bf16[704,384]{1,0:T(8,128)(2,1)S(1)}, u32[]{:S(2)}) copy-start(bf16[704,384]{1,0:T(8,128)(2,1)S(1)} %get-tuple-element.63.refs_4_) | copy-start | bytes 1622020
  52.6 2.7 %copy-start.14 = (bf16[64,1024]{1,0:T(8,128)(2,1)S(1)}, bf16[64,1024]{1,0:T(8,128)(2,1)}, u32[]{:S(2)}) copy-start(bf16[64,1024]{1,0:T(8,128)(2,1)} %get-tuple-element.54.refs_3_) | copy-start | bytes 393220
  55.3 2.0 %collective-permute-start.17 = (bf16[256,1024]{1,0:T(8,128)(2,1)S(1)}, bf16[256,1024]{1,0:T(8,128)(2,1)S(1)}, u32[]{:S(2)}, u32[]{:S(2)}) collective-permute-start(bf16[256,1024]{1,0:T(8,128)(2,1)S(1)} %collect.3.own_ref.refs_5_), channel_id=1, source_target_pairs={{0,1},{1,0},{2,3},{3,2},{4,5},{5,4},{6,7},{7,6},{8,9},{9,8},{10,11... | collective-permute-start | bytes 1572872 | tf_op jit(solution)/shard_map/ppermute | solution.py:313
  55.4 5.4 %collective-permute-start.13 = (bf16[384,1024]{1,0:T(8,128)(2,1)S(1)}, bf16[384,1024]{1,0:T(8,128)(2,1)S(1)}, u32[]{:S(2)}, u32[]{:S(2)}) collective-permute-start(bf16[384,1024]{1,0:T(8,128)(2,1)S(1)} %get-tuple-element.50), channel_id=1, source_target_pairs={{0,1},{1,0},{2,3},{3,2},{4,5},{5,4},{6,7},{7,6},{8,9},{9,8},{10,11... | collective-permute-start | bytes 2359304 | tf_op jit(solution)/shard_map/ppermute | solution.py:313
  59.4 0.7 copy-start.12
  60.1 0.7 copy-start.3
  60.1 0.7 copy-start.5
  60.1 1.5 %collective-permute-start.18 = (bf16[128,1024]{1,0:T(8,128)(2,1)S(1)}, bf16[128,1024]{1,0:T(8,128)(2,1)S(1)}, u32[]{:S(2)}, u32[]{:S(2)}) collective-permute-start(bf16[128,1024]{1,0:T(8,128)(2,1)S(1)} %get-tuple-element.60), channel_id=1, source_target_pairs={{0,1},{1,0},{2,3},{3,2},{4,5},{5,4},{6,7},{7,6},{8,9},{9,8},{10,11... | collective-permute-start | bytes 786440 | tf_op jit(solution)/shard_map/ppermute | solution.py:313
  60.8 9.8 %copy-start.7 = (s32[256,1]{0,1:T(1,128)S(1)}, s32[256,1]{0,1:T(1,128)}, u32[]{:S(2)}) copy-start(s32[256,1]{0,1:T(1,128)} %param.8) | copy-start | bytes 3076
  62.7 33.6 %all-to-all-start = ((bf16[16,32,1024]{2,1,0:T(8,128)(2,1)}), bf16[16,32,1024]{2,1,0:T(8,128)(2,1)S(1)}, u32[]{:S(2)}, u32[]{:S(2)}) async-start(bf16[16,32,1024]{2,1,0:T(8,128)(2,1)} %bitcast.4), calls=%async_computation | async-start | bytes 2097152 | tf_op jit(solution)/shard_map/all_to_all | solution.py:262
  70.9 0.9 copy-start.4
  71.9 0.9 copy-start.6
  72.8 1.4 %copy-start.9 = (bf16[768,1024]{1,0:T(8,128)(2,1)S(1)}, bf16[768,1024]{1,0:T(8,128)(2,1)}, u32[]{:S(2)}) copy-start(bf16[768,1024]{1,0:T(8,128)(2,1)} %copy-done.8) | copy-start | bytes 4718596
  74.2 1.4 %copy-start.11 = (bf16[768,1024]{1,0:T(8,128)(2,1)S(1)}, bf16[768,1024]{1,0:T(8,128)(2,1)}, u32[]{:S(2)}) copy-start(bf16[768,1024]{1,0:T(8,128)(2,1)} %copy-done.10) | copy-start | bytes 4718596
  75.6 0.9 copy-start.13
  76.5 1.0 %copy-start.16 = (bf16[704,384]{1,0:T(8,128)(2,1)S(1)}, bf16[704,384]{1,0:T(8,128)(2,1)}, u32[]{:S(2)}) copy-start(bf16[704,384]{1,0:T(8,128)(2,1)} %copy-done.15) | copy-start | bytes 1622020

commit v12 on v11

--- a/solution.py
+++ b/solution.py
@@ -280,6 +280,7 @@
     near = [k for k in reversed(range(1, experts)) if k < experts // 2]
     turns = [k for pair in zip(far, near) for k in pair] + far[len(near) :]
     cut = 3 * experts // 4
+    turns = turns[:cut] + sorted(turns[cut:], key=lambda k: k < experts // 2)
     first, second = turns[:cut], turns[cut:] + [0]
 
     def place(partners):
@@ -301,7 +302,7 @@
             name="place",
         )(ids_row, tokens, upstream)
 
-    early = experts // 2 - 1
+    early = experts // 4 + 1
     slabs = {}
     for partners in (turns[:early], turns[early:] + [0]):
         slabs.update(zip(partners, place(partners)))

time: 98.6 us -> 98.5 us (level)
  starting transfers between devices: 36.1 us -> 34.4 us
  waiting for transfers between devices: 24 us -> 25.4 us
    ppermute x15, starting transfers between devices: 27.5 us -> 25.8 us  [swap(): lax.ppermute(slabs[k], 'expert', [(e, e ^ k) for e in range(experts)])]
    ppermute x15, waiting for transfers between devices: 13.4 us -> 14.8 us  [swap(): lax.ppermute(slabs[k], 'expert', [(e, e ^ k) for e in range(experts)])]
  transfers between devices with their start and end apart: 20 -> 20, of which waited for: 11 -> 11; matrix products, arithmetic and copies ran while one was open for 0% -> 0% of each run, Pallas kernels for 24% -> 25%
where the time goes in v12:
time: 98.5 us; the launch traced here: 98.1 us
  starting transfers between devices  34.4 us (35%)
  Pallas kernels  29.8 us (30%)
  waiting for transfers between devices  25.4 us (26%)
  local copies, waits for them, and re-layouts  7.38 us (7%)
  between operations  1.03 us (1%)
    ppermute x15, starting transfers between devices, swap(): lax.ppermute(slabs[k], 'expert', [(e, e ^ k) for e in range(experts)])  25.8 us
    ppermute x15, waiting for transfers between devices, swap(): lax.ppermute(slabs[k], 'expert', [(e, e ^ k) for e in range(experts)])  14.8 us
    all_to_all x1, waiting for transfers between devices, to_experts(): lax.all_to_all(rows.reshape(experts, rows.shape[0] // experts, rows.shape...  9.92 us
    pallas_call x1, Pallas kernels, grouped(): pl.pallas_call(functools.partial(grads_kernel, sizes), grid=(units // til...  8.91 us
    pallas_call x2, Pallas kernels, front(): pl.pallas_call(functools.partial(front_kernel, tile), out_shape=[jax.Shap...  8.41 us
    all_to_all x1, starting transfers between devices, to_experts(): lax.all_to_all(rows.reshape(experts, rows.shape[0] // experts, rows.shape...  7.89 us
    unnamed x40, local copies, waits for them, and re-layouts  7.38 us
    pallas_call x2, Pallas kernels, place(): pl.pallas_call(functools.partial(place_kernel, capacity, partners), out_s...  5.76 us
  transfers between devices with their start and end apart: 20, of which 11 were waited for; matrix products, arithmetic and copies ran while one was open for 0% of the time, Pallas kernels for 25%

profile of v12, /device:TPU:8, one launch (start us, length us, event | category | flops | bytes accessed | tf_op | source)
XLA Modules:
  0.0 98.1 jit_solution(2517266184936726537)
XLA Ops:
  0.6 2.6 %place.2 = (bf16[64,1024]{1,0:T(8,128)(2,1)}, bf16[64,1024]{1,0:T(8,128)(2,1)}, bf16[64,1024]{1,0:T(8,128)(2,1)}, bf16[64,1024]{1,0:T(8,128)(2,1)}, bf16[64,1024]{1,0:T(8,128)(2,1)}) custom-call(s32[1,256]{1,0:T(1,128)} %bitcast.23, bf16[256,1024]{1,0:T(8,128)(2,1)} %x_hbm.3, bf16[256,1024]{1,0:T(8,128)(2,1)} %dy_hbm.3), custom_call_target="tpu_custom_call" | custom-call | tf_op jit(solution)/shard_map/place/pallas_call | solution.py:287
  3.2 3.5 %collective-permute-start = (bf16[64,1024]{1,0:T(8,128)(2,1)}, bf16[64,1024]{1,0:T(8,128)(2,1)S(1)}, u32[]{:S(2)}, u32[]{:S(2)}) collective-permute-start(bf16[64,1024]{1,0:T(8,128)(2,1)} %get-tuple-element.36), channel_id=1, source_target_pairs={{0,30},{2,28},{4,26},{6,24},{8,22},{10,20},{12,18},{14,16},{16,14}... | collective-permute-start | bytes 393224 | tf_op jit(solution)/shard_map/ppermute | solution.py:311
  6.8 2.4 %collective-permute-start.1 = (bf16[64,1024]{1,0:T(8,128)(2,1)}, bf16[64,1024]{1,0:T(8,128)(2,1)S(1)}, u32[]{:S(2)}, u32[]{:S(2)}) collective-permute-start(bf16[64,1024]{1,0:T(8,128)(2,1)} %get-tuple-element.37), channel_id=1, source_target_pairs={{0,14},{2,12},{4,10},{6,8},{8,6},{10,4},{12,2},{14,0},{16,30},{18,... | collective-permute-start | bytes 393224 | tf_op jit(solution)/shard_map/ppermute | solution.py:311
  9.2 0.3 collective-permute-start.2
  9.4 1.5 %collective-permute-start.3 = (bf16[64,1024]{1,0:T(8,128)(2,1)}, bf16[64,1024]{1,0:T(8,128)(2,1)S(1)}, u32[]{:S(2)}, u32[]{:S(2)}) collective-permute-start(bf16[64,1024]{1,0:T(8,128)(2,1)} %get-tuple-element.39), channel_id=1, source_target_pairs={{0,12},{2,14},{4,8},{6,10},{8,4},{10,6},{12,0},{14,2},{16,28},{18,... | collective-permute-start | bytes 393224 | tf_op jit(solution)/shard_map/ppermute | solution.py:311
  11.0 2.5 %collective-permute-start.4 = (bf16[64,1024]{1,0:T(8,128)(2,1)}, bf16[64,1024]{1,0:T(8,128)(2,1)S(1)}, u32[]{:S(2)}, u32[]{:S(2)}) collective-permute-start(bf16[64,1024]{1,0:T(8,128)(2,1)} %get-tuple-element.40), channel_id=1, source_target_pairs={{0,26},{2,24},{4,30},{6,28},{8,18},{10,16},{12,22},{14,20},{16,10}... | collective-permute-start | bytes 393224 | tf_op jit(solution)/shard_map/ppermute | solution.py:311
  13.5 3.1 %place.3 = (bf16[64,1024]{1,0:T(8,128)(2,1)}, bf16[64,1024]{1,0:T(8,128)(2,1)}, bf16[64,1024]{1,0:T(8,128)(2,1)}, bf16[64,1024]{1,0:T(8,128)(2,1)}, bf16[64,1024...) custom-call(s32[1,256]{1,0:T(1,128)} %bitcast.24, ...), custom_call_target="tpu_custom_call" | custom-call | tf_op jit(solution)/shard_map/place/pallas_call | solution.py:287
  16.6 2.5 %collective-permute-start.5 = (bf16[64,1024]{1,0:T(8,128)(2,1)}, bf16[64,1024]{1,0:T(8,128)(2,1)S(1)}, u32[]{:S(2)}, u32[]{:S(2)}) collective-permute-start(bf16[64,1024]{1,0:T(8,128)(2,1)} %get-tuple-element.41), channel_id=1, source_target_pairs={{0,10},{2,8},{4,14},{6,12},{8,2},{10,0},{12,6},{14,4},{16,26},{18,... | collective-permute-start | bytes 393224 | tf_op jit(solution)/shard_map/ppermute | solution.py:311
  19.2 1.8 %collective-permute-done.2.refs_2_ = bf16[64,1024]{1,0:T(8,128)(2,1)S(1)} collective-permute-done((bf16[64,1024]{1,0:T(8,128)(2,1)}, bf16[64,1024]{1,0:T(8,128)(2,1)S(1)}, u32[]{:S(2)}, u32[]{:S(2)}) %collective-permute-start.2) | collective-permute-done | bytes 131104 | tf_op jit(solution)/shard_map/ppermute | solution.py:311
  21.0 0.7 collective-permute-start.7
  21.7 0.5 collective-permute-done.3.refs_3_
  22.2 3.4 %collective-permute-start.8 = (bf16[64,1024]{1,0:T(8,128)(2,1)}, bf16[64,1024]{1,0:T(8,128)(2,1)S(1)}, u32[]{:S(2)}, u32[]{:S(2)}) collective-permute-start(bf16[64,1024]{1,0:T(8,128)(2,1)} %get-tuple-element.44), channel_id=1, source_target_pairs={{0,22},{2,20},{4,18},{6,16},{8,30},{10,28},{12,26},{14,24},{16,6},... | collective-permute-start | bytes 393224 | tf_op jit(solution)/shard_map/ppermute | solution.py:311
  25.6 0.3 collective-permute-done.4.refs_4_
  25.9 3.9 %collective-permute-start.9 = (bf16[64,1024]{1,0:T(8,128)(2,1)}, bf16[64,1024]{1,0:T(8,128)(2,1)S(1)}, u32[]{:S(2)}, u32[]{:S(2)}) collective-permute-start(bf16[64,1024]{1,0:T(8,128)(2,1)} %get-tuple-element.45), channel_id=1, source_target_pairs={{0,6},{2,4},{4,2},{6,0},{8,14},{10,12},{12,10},{14,8},{16,22},{18,... | collective-permute-start | bytes 393224 | tf_op jit(solution)/shard_map/ppermute | solution.py:311
  29.8 2.5 %collective-permute-done.6.refs_6_ = bf16[64,1024]{1,0:T(8,128)(2,1)S(1)} collective-permute-done((bf16[64,1024]{1,0:T(8,128)(2,1)}, bf16[64,1024]{1,0:T(8,128)(2,1)S(1)}, u32[]{:S(2)}, u32[]{:S(2)}) %collective-permute-start.6) | collective-permute-done | bytes 131104 | tf_op jit(solution)/shard_map/ppermute | solution.py:311
  32.4 0.6 collective-permute-start.11
  32.9 0.6 collective-permute-done.7.refs_7_
  33.5 5.3 %collective-permute-done.8.refs_8_ = bf16[64,1024]{1,0:T(8,128)(2,1)S(1)} collective-permute-done((bf16[64,1024]{1,0:T(8,128)(2,1)}, bf16[64,1024]{1,0:T(8,128)(2,1)S(1)}, u32[]{:S(2)}, u32[]{:S(2)}) %collective-permute-start.8) | collective-permute-done | bytes 131104 | tf_op jit(solution)/shard_map/ppermute | solution.py:311
  38.7 2.0 %collective-permute-done.10.refs_10_ = bf16[64,1024]{1,0:T(8,128)(2,1)S(1)} collective-permute-done((bf16[64,1024]{1,0:T(8,128)(2,1)}, bf16[64,1024]{1,0:T(8,128)(2,1)S(1)}, u32[]{:S(2)}, u32[]{:S(2)}) %collective-permute-start.10) | collective-permute-done | bytes 131104 | tf_op jit(solution)/shard_map/ppermute | solution.py:311
  40.7 0.6 collective-permute-done.11.refs_11_
  41.3 0.1 collect.2.own_ref.refs_0_
  41.5 0.1 collective-permute-start.12
  41.6 2.8 %collective-permute-start.14 = (bf16[64,1024]{1,0:T(8,128)(2,1)S(1)}, bf16[64,1024]{1,0:T(8,128)(2,1)S(1)}, u32[]{:S(2)}, u32[]{:S(2)}) collective-permute-start(bf16[64,1024]{1,0:T(8,128)(2,1)S(1)} %copy-done.19), channel_id=1, source_target_pairs={{0,18},{2,16},{4,22},{6,20},{8,26},{10,24},{12,30},{14,28},{16,2},... | collective-permute-start | bytes 393224 | tf_op jit(solution)/shard_map/ppermute | solution.py:311
  44.4 0.3 collective-permute-start.15
  44.7 1.4 %collective-permute-start.16 = (bf16[64,1024]{1,0:T(8,128)(2,1)S(1)}, bf16[64,1024]{1,0:T(8,128)(2,1)S(1)}, u32[]{:S(2)}, u32[]{:S(2)}) collective-permute-start(bf16[64,1024]{1,0:T(8,128)(2,1)S(1)} %copy-done.17), channel_id=1, source_target_pairs={{0,2},{2,0},{4,6},{6,4},{8,10},{10,8},{12,14},{14,12},{16,18},{18,... | collective-permute-start | bytes 393224 | tf_op jit(solution)/shard_map/ppermute | solution.py:311
  46.1 6.3 %front.2 = (bf16[704,384]{1,0:T(8,128)(2,1)S(1)}, bf16[704,384]{1,0:T(8,128)(2,1)S(1)}, bf16[704,384]{1,0:T(8,128)(2,1)S(1)}, bf16[384,1024]{1,0:T(8,128)(2,1)S(1)}) custom-call(bf16[768,1024]{1,0:T(8,128)(2,1)S(1)} %collect.2.own_ref.refs_0_, bf16[768,1024]{1,0:T(8,128)(2,1)S(1)} %collective-permute-done.12.other_ref.refs_1_, ...), custom_call_target="tpu_custom_call" | custom-call | flops 4429185024 | bytes 17825792 | tf_op jit(solution)/shard_map/front/pallas_call | solution.py:342
  52.5 1.4 %kept.2.kept_ref.refs_4_ = f32[384,1024]{1,0:T(8,128)S(1)} custom-call(bf16[704,384]{1,0:T(8,128)(2,1)S(1)} %get-tuple-element.48.d_gate_ref.refs_2_, bf16[704,384]{1,0:T(8,128)(2,1)S(1)} %get-tuple-element.49.d_up_ref.refs_3_, bf16[704,2048]{1,0:T(8,128)(2,1)S(1)} %bitcast.10, bf16[704,2048]{1,0:T(8,128)(2,1)S(1)} %bitcast.15), custom_call_target="tpu_custom_call" | custom-call | flops 1107296256 | bytes 4456448 | tf_op jit(solution)/shard_map/kept/pallas_call | solution.py:352
  53.9 1.2 %collective-permute-done.15.refs_1_ = bf16[64,1024]{1,0:T(8,128)(2,1)S(1)} collective-permute-done((bf16[64,1024]{1,0:T(8,128)(2,1)S(1)}, bf16[64,1024]{1,0:T(8,128)(2,1)S(1)}, u32[]{:S(2)}, u32[]{:S(2)}) %collective-permute-start.15) | collective-permute-done | bytes 131104 | tf_op jit(solution)/shard_map/ppermute | solution.py:311
  55.2 0.1 collective-permute-start.17
  55.3 0.5 collective-permute-start.13
  55.7 1.4 %begin.1 = (f32[704,128]{1,0:T(8,128)S(1)}, f32[704,128]{1,0:T(8,128)S(1)}, f32[704,128]{1,0:T(8,128)S(1)}) custom-call(bf16[256,1024]{1,0:T(8,128)(2,1)S(1)} %collect.3.own_ref.refs_5_, bf16[704,2048]{1,0:T(8,128)(2,1)S(1)} %bitcast.11, bf16[704,2048]{1,0:T(8,128)(2,1)S(1)} %bitcast.16, bf16[704,2048]{1,0:T(8,128)(2,1)S(1)} %bitcast.20), custom_call_target="tpu_custom_call" | custom-call | flops 738197504 | bytes 6815744 | tf_op jit(solution)/shard_map/begin/pallas_call | solution.py:329
  57.2 2.1 %front.3 = (bf16[704,128]{1,0:T(8,128)(2,1)S(1)}, bf16[704,128]{1,0:T(8,128)(2,1)S(1)}, bf16[704,128]{1,0:T(8,128)(2,1)S(1)}, bf16[128,1024]{1,0:T(8,128)(2,1)S(1)}) custom-call(bf16[256,1024]{1,0:T(8,128)(2,1)S(1)} %collect.3.own_ref.refs_5_, bf16[256,1024]{1,0:T(8,128)(2,1)S(1)} %collective-permute-done.17.other_ref.refs_6_, ...), custom_call_target="tpu_custom_call" | custom-call | flops 1476395008 | bytes 13631488 | tf_op jit(solution)/shard_map/front/pallas_call | solution.py:342
  59.3 0.7 copy-done.12
  60.0 0.6 kept.3.kept_ref
  60.7 0.1 sum.1.sum_ref
  60.8 0.7 collective-permute-done.18.got_ref
  61.5 1.1 %last_sum.1 = (bf16[512,1024]{1,0:T(8,128)(2,1)}, f32[8,128]{1,0:T(8,128)S(1)}) custom-call(bf16[384,1024]{1,0:T(8,128)(2,1)S(1)} %sum.1.sum_ref, f32[128,1024]{1,0:T(8,128)S(1)} %kept.3.kept_ref, bf16[128,1024]{1,0:T(8,128)(2,1)S(1)} %collective-permute-done.18.got_ref), custom_call_target="tpu_custom_call" | custom-call | tf_op jit(solution)/shard_map/last_sum/pallas_call | solution.py:376
  62.6 7.9 %all-to-all-start = ((bf16[16,32,1024]{2,1,0:T(8,128)(2,1)}), bf16[16,32,1024]{2,1,0:T(8,128)(2,1)S(1)}, u32[]{:S(2)}, u32[]{:S(2)}) async-start(bf16[16,32,1024]{2,1,0:T(8,128)(2,1)} %bitcast.4), calls=%async_computation | async-start | bytes 2097152 | tf_op jit(solution)/shard_map/all_to_all | solution.py:262
  70.5 0.3 placing.1.placing_ref.refs_10_
  70.8 0.9 copy-done.4
  71.7 0.9 copy-done.6
  72.6 1.4 %copy-done.9 = bf16[768,1024]{1,0:T(8,128)(2,1)S(1)} copy-done((bf16[768,1024]{1,0:T(8,128)(2,1)S(1)}, bf16[768,1024]{1,0:T(8,128)(2,1)}, u32[]{:S(2)}) %copy-start.9) | copy-done | bytes 1572888
  74.0 1.4 %copy-done.11 = bf16[768,1024]{1,0:T(8,128)(2,1)S(1)} copy-done((bf16[768,1024]{1,0:T(8,128)(2,1)S(1)}, bf16[768,1024]{1,0:T(8,128)(2,1)}, u32[]{:S(2)}) %copy-start.11) | copy-done | bytes 1572888
  75.5 0.9 copy-done.13
  76.4 1.0 %copy-done.16 = bf16[704,384]{1,0:T(8,128)(2,1)S(1)} copy-done((bf16[704,384]{1,0:T(8,128)(2,1)S(1)}, bf16[704,384]{1,0:T(8,128)(2,1)}, u32[]{:S(2)}) %copy-start.16) | copy-done | bytes 540696
  77.4 8.9 %grads.1 = (bf16[704,2048]{1,0:T(8,128)(2,1)}, bf16[704,2048]{1,0:T(8,128)(2,1)}, bf16[704,2048]{1,0:T(8,128)(2,1)}) custom-call(bf16[768,1024]{1,0:T(8,128)(2,1)S(1)} %copy-done.9, bf16[768,1024]{1,0:T(8,128)(2,1)S(1)} %copy-done.11, bf16[704,384]{1,0:T(8,128)(2,1)S(1)} %get-tuple-element.48.d_gate_ref.refs_2_, ...), custom_call_target="tpu_custom_call" | custom-call | flops 4429185024 | bytes 14942208 | tf_op jit(solution)/shard_map/grads/pallas_call | solution.py:396
  86.3 9.9 %all-to-all-done = bf16[16,32,1024]{2,1,0:T(8,128)(2,1)S(1)} async-done(((bf16[16,32,1024]{2,1,0:T(8,128)(2,1)}), bf16[16,32,1024]{2,1,0:T(8,128)(2,1)S(1)}, u32[]{:S(2)}, u32[]{:S(2)}) %all-to-all-start) | async-done | bytes 1048608 | tf_op jit(solution)/shard_map/all_to_all | solution.py:262
  96.3 1.7 %combine.1 = bf16[256,1024]{1,0:T(8,128)(2,1)} custom-call(bf16[256,512]{1,0:T(8,128)(2,1)S(1)} %placing.1.placing_ref.refs_10_, bf16[512,1024]{1,0:T(8,128)(2,1)S(1)} %bitcast.22), custom_call_target="tpu_custom_call" | custom-call | tf_op jit(solution)/shard_map/combine/pallas_call | solution.py:250
  (46 shorter events, 0.3 us)
Async XLA Ops:
  3.2 13.4 %collective-permute-start = (bf16[64,1024]{1,0:T(8,128)(2,1)}, bf16[64,1024]{1,0:T(8,128)(2,1)S(1)}, u32[]{:S(2)}, u32[]{:S(2)}) collective-permute-start(bf16[64,1024]{1,0:T(8,128)(2,1)} %get-tuple-element.36), channel_id=1, source_target_pairs={{0,30},{2,28},{4,26},{6,24},{8,22},{10,20},{12,18},{14,16},{16,14}... | collective-permute-start | bytes 393224 | tf_op jit(solution)/shard_map/ppermute | solution.py:311
  6.8 12.4 %collective-permute-start.1 = (bf16[64,1024]{1,0:T(8,128)(2,1)}, bf16[64,1024]{1,0:T(8,128)(2,1)S(1)}, u32[]{:S(2)}, u32[]{:S(2)}) collective-permute-start(bf16[64,1024]{1,0:T(8,128)(2,1)} %get-tuple-element.37), channel_id=1, source_target_pairs={{0,14},{2,12},{4,10},{6,8},{8,6},{10,4},{12,2},{14,0},{16,30},{18,... | collective-permute-start | bytes 393224 | tf_op jit(solution)/shard_map/ppermute | solution.py:311
  9.2 11.9 %collective-permute-start.2 = (bf16[64,1024]{1,0:T(8,128)(2,1)}, bf16[64,1024]{1,0:T(8,128)(2,1)S(1)}, u32[]{:S(2)}, u32[]{:S(2)}) collective-permute-start(bf16[64,1024]{1,0:T(8,128)(2,1)} %get-tuple-element.38), channel_id=1, source_target_pairs={{0,28},{2,30},{4,24},{6,26},{8,20},{10,22},{12,16},{14,18},{16,12}... | collective-permute-start | bytes 393224 | tf_op jit(solution)/shard_map/ppermute | solution.py:311
  9.4 12.7 %collective-permute-start.3 = (bf16[64,1024]{1,0:T(8,128)(2,1)}, bf16[64,1024]{1,0:T(8,128)(2,1)S(1)}, u32[]{:S(2)}, u32[]{:S(2)}) collective-permute-start(bf16[64,1024]{1,0:T(8,128)(2,1)} %get-tuple-element.39), channel_id=1, source_target_pairs={{0,12},{2,14},{4,8},{6,10},{8,4},{10,6},{12,0},{14,2},{16,28},{18,... | collective-permute-start | bytes 393224 | tf_op jit(solution)/shard_map/ppermute | solution.py:311
  11.0 14.9 %collective-permute-start.4 = (bf16[64,1024]{1,0:T(8,128)(2,1)}, bf16[64,1024]{1,0:T(8,128)(2,1)S(1)}, u32[]{:S(2)}, u32[]{:S(2)}) collective-permute-start(bf16[64,1024]{1,0:T(8,128)(2,1)} %get-tuple-element.40), channel_id=1, source_target_pairs={{0,26},{2,24},{4,30},{6,28},{8,18},{10,16},{12,22},{14,20},{16,10}... | collective-permute-start | bytes 393224 | tf_op jit(solution)/shard_map/ppermute | solution.py:311
  16.6 13.2 %collective-permute-start.5 = (bf16[64,1024]{1,0:T(8,128)(2,1)}, bf16[64,1024]{1,0:T(8,128)(2,1)S(1)}, u32[]{:S(2)}, u32[]{:S(2)}) collective-permute-start(bf16[64,1024]{1,0:T(8,128)(2,1)} %get-tuple-element.41), channel_id=1, source_target_pairs={{0,10},{2,8},{4,14},{6,12},{8,2},{10,0},{12,6},{14,4},{16,26},{18,... | collective-permute-start | bytes 393224 | tf_op jit(solution)/shard_map/ppermute | solution.py:311
  19.1 13.2 %collective-permute-start.6 = (bf16[64,1024]{1,0:T(8,128)(2,1)}, bf16[64,1024]{1,0:T(8,128)(2,1)S(1)}, u32[]{:S(2)}, u32[]{:S(2)}) collective-permute-start(bf16[64,1024]{1,0:T(8,128)(2,1)} %get-tuple-element.42), channel_id=1, source_target_pairs={{0,24},{2,26},{4,28},{6,30},{8,16},{10,18},{12,20},{14,22},{16,8},... | collective-permute-start | bytes 393224 | tf_op jit(solution)/shard_map/ppermute | solution.py:311
  21.0 12.4 %collective-permute-start.7 = (bf16[64,1024]{1,0:T(8,128)(2,1)}, bf16[64,1024]{1,0:T(8,128)(2,1)S(1)}, u32[]{:S(2)}, u32[]{:S(2)}) collective-permute-start(bf16[64,1024]{1,0:T(8,128)(2,1)} %get-tuple-element.43), channel_id=1, source_target_pairs={{0,8},{2,10},{4,12},{6,14},{8,0},{10,2},{12,4},{14,6},{16,24},{18,... | collective-permute-start | bytes 393224 | tf_op jit(solution)/shard_map/ppermute | solution.py:311
  22.2 16.5 %collective-permute-start.8 = (bf16[64,1024]{1,0:T(8,128)(2,1)}, bf16[64,1024]{1,0:T(8,128)(2,1)S(1)}, u32[]{:S(2)}, u32[]{:S(2)}) collective-permute-start(bf16[64,1024]{1,0:T(8,128)(2,1)} %get-tuple-element.44), channel_id=1, source_target_pairs={{0,22},{2,20},{4,18},{6,16},{8,30},{10,28},{12,26},{14,24},{16,6},... | collective-permute-start | bytes 393224 | tf_op jit(solution)/shard_map/ppermute | solution.py:311
  25.9 12.8 %collective-permute-start.9 = (bf16[64,1024]{1,0:T(8,128)(2,1)}, bf16[64,1024]{1,0:T(8,128)(2,1)S(1)}, u32[]{:S(2)}, u32[]{:S(2)}) collective-permute-start(bf16[64,1024]{1,0:T(8,128)(2,1)} %get-tuple-element.45), channel_id=1, source_target_pairs={{0,6},{2,4},{4,2},{6,0},{8,14},{10,12},{12,10},{14,8},{16,22},{18,... | collective-permute-start | bytes 393224 | tf_op jit(solution)/shard_map/ppermute | solution.py:311
  29.8 10.9 %collective-permute-start.10 = (bf16[64,1024]{1,0:T(8,128)(2,1)}, bf16[64,1024]{1,0:T(8,128)(2,1)S(1)}, u32[]{:S(2)}, u32[]{:S(2)}) collective-permute-start(bf16[64,1024]{1,0:T(8,128)(2,1)} %get-tuple-element.46), channel_id=1, source_target_pairs={{0,20},{2,22},{4,16},{6,18},{8,28},{10,30},{12,24},{14,26},{16,4},... | collective-permute-start | bytes 393224 | tf_op jit(solution)/shard_map/ppermute | solution.py:311
  32.3 9.2 %copy-start.19 = (bf16[64,1024]{1,0:T(8,128)(2,1)S(1)}, bf16[64,1024]{1,0:T(8,128)(2,1)}, u32[]{:S(2)}) copy-start(bf16[64,1024]{1,0:T(8,128)(2,1)} %get-tuple-element.51) | copy-start | bytes 393220
  32.3 12.1 %copy-start.18 = (bf16[64,1024]{1,0:T(8,128)(2,1)S(1)}, bf16[64,1024]{1,0:T(8,128)(2,1)}, u32[]{:S(2)}) copy-start(bf16[64,1024]{1,0:T(8,128)(2,1)} %get-tuple-element.52) | copy-start | bytes 393220
  32.3 12.3 %copy-start.17 = (bf16[64,1024]{1,0:T(8,128)(2,1)S(1)}, bf16[64,1024]{1,0:T(8,128)(2,1)}, u32[]{:S(2)}) copy-start(bf16[64,1024]{1,0:T(8,128)(2,1)} %get-tuple-element.53) | copy-start | bytes 393220
  32.3 13.7 %copy-start = (bf16[1,704,2048]{2,1,0:T(8,128)(2,1)S(1)}, bf16[1,704,2048]{2,1,0:T(8,128)(2,1)}, u32[]{:S(2)}) copy-start(bf16[1,704,2048]{2,1,0:T(8,128)(2,1)} %param.9) | copy-start | bytes 8650756
  32.3 13.7 %copy-start.1 = (bf16[1,704,2048]{2,1,0:T(8,128)(2,1)S(1)}, bf16[1,704,2048]{2,1,0:T(8,128)(2,1)}, u32[]{:S(2)}) copy-start(bf16[1,704,2048]{2,1,0:T(8,128)(2,1)} %param.10) | copy-start | bytes 8650756
  32.3 13.7 %copy-start.2 = (bf16[1,704,2048]{2,1,0:T(8,128)(2,1)S(1)}, bf16[1,704,2048]{2,1,0:T(8,128)(2,1)}, u32[]{:S(2)}) copy-start(bf16[1,704,2048]{2,1,0:T(8,128)(2,1)} %param.11) | copy-start | bytes 8650756
  32.4 9.0 %collective-permute-start.11 = (bf16[64,1024]{1,0:T(8,128)(2,1)}, bf16[64,1024]{1,0:T(8,128)(2,1)S(1)}, u32[]{:S(2)}, u32[]{:S(2)}) collective-permute-start(bf16[64,1024]{1,0:T(8,128)(2,1)} %get-tuple-element.47), channel_id=1, source_target_pairs={{0,4},{2,6},{4,0},{6,2},{8,12},{10,14},{12,8},{14,10},{16,20},{18,... | collective-permute-start | bytes 393224 | tf_op jit(solution)/shard_map/ppermute | solution.py:311
  41.5 11.0 %copy-start.8 = (bf16[768,1024]{1,0:T(8,128)(2,1)}, bf16[768,1024]{1,0:T(8,128)(2,1)S(1)}, u32[]{:S(2)}) copy-start(bf16[768,1024]{1,0:T(8,128)(2,1)S(1)} %collect.2.own_ref.refs_0_) | copy-start | bytes 4718596
  41.5 4.6 %collective-permute-start.12 = (bf16[768,1024]{1,0:T(8,128)(2,1)S(1)}, bf16[768,1024]{1,0:T(8,128)(2,1)S(1)}, u32[]{:S(2)}, u32[]{:S(2)}) collective-permute-start(bf16[768,1024]{1,0:T(8,128)(2,1)S(1)} %collect.2.own_ref.refs_0_), channel_id=1, source_target_pairs={{0,1},{1,0},{2,3},{3,2},{4,5},{5,4},{6,7},{7,6},{8,9},{9,8},{10,11... | collective-permute-start | bytes 4718600 | tf_op jit(solution)/shard_map/ppermute | solution.py:314
  41.6 12.3 %collective-permute-start.14 = (bf16[64,1024]{1,0:T(8,128)(2,1)S(1)}, bf16[64,1024]{1,0:T(8,128)(2,1)S(1)}, u32[]{:S(2)}, u32[]{:S(2)}) collective-permute-start(bf16[64,1024]{1,0:T(8,128)(2,1)S(1)} %copy-done.19), channel_id=1, source_target_pairs={{0,18},{2,16},{4,22},{6,20},{8,26},{10,24},{12,30},{14,28},{16,2},... | collective-permute-start | bytes 393224 | tf_op jit(solution)/shard_map/ppermute | solution.py:311
  44.4 10.7 %collective-permute-start.15 = (bf16[64,1024]{1,0:T(8,128)(2,1)S(1)}, bf16[64,1024]{1,0:T(8,128)(2,1)S(1)}, u32[]{:S(2)}, u32[]{:S(2)}) collective-permute-start(bf16[64,1024]{1,0:T(8,128)(2,1)S(1)} %copy-done.18), channel_id=1, source_target_pairs={{0,16},{2,18},{4,20},{6,22},{8,24},{10,26},{12,28},{14,30},{16,0},... | collective-permute-start | bytes 393224 | tf_op jit(solution)/shard_map/ppermute | solution.py:311
  44.7 10.5 %collective-permute-start.16 = (bf16[64,1024]{1,0:T(8,128)(2,1)S(1)}, bf16[64,1024]{1,0:T(8,128)(2,1)S(1)}, u32[]{:S(2)}, u32[]{:S(2)}) collective-permute-start(bf16[64,1024]{1,0:T(8,128)(2,1)S(1)} %copy-done.17), channel_id=1, source_target_pairs={{0,2},{2,0},{4,6},{6,4},{8,10},{10,8},{12,14},{14,12},{16,18},{18,... | collective-permute-start | bytes 393224 | tf_op jit(solution)/shard_map/ppermute | solution.py:311
  46.1 6.4 %copy-start.10 = (bf16[768,1024]{1,0:T(8,128)(2,1)}, bf16[768,1024]{1,0:T(8,128)(2,1)S(1)}, u32[]{:S(2)}) copy-start(bf16[768,1024]{1,0:T(8,128)(2,1)S(1)} %collective-permute-done.12.other_ref.refs_1_) | copy-start | bytes 4718596
  52.4 1.4 %copy-start.15 = (bf16[704,384]{1,0:T(8,128)(2,1)}, bf16[704,384]{1,0:T(8,128)(2,1)S(1)}, u32[]{:S(2)}) copy-start(bf16[704,384]{1,0:T(8,128)(2,1)S(1)} %get-tuple-element.63.refs_4_) | copy-start | bytes 1622020
  52.4 2.7 %copy-start.14 = (bf16[64,1024]{1,0:T(8,128)(2,1)S(1)}, bf16[64,1024]{1,0:T(8,128)(2,1)}, u32[]{:S(2)}) copy-start(bf16[64,1024]{1,0:T(8,128)(2,1)} %get-tuple-element.54.refs_3_) | copy-start | bytes 393220
  55.2 2.0 %collective-permute-start.17 = (bf16[256,1024]{1,0:T(8,128)(2,1)S(1)}, bf16[256,1024]{1,0:T(8,128)(2,1)S(1)}, u32[]{:S(2)}, u32[]{:S(2)}) collective-permute-start(bf16[256,1024]{1,0:T(8,128)(2,1)S(1)} %collect.3.own_ref.refs_5_), channel_id=1, source_target_pairs={{0,1},{1,0},{2,3},{3,2},{4,5},{5,4},{6,7},{7,6},{8,9},{9,8},{10,11... | collective-permute-start | bytes 1572872 | tf_op jit(solution)/shard_map/ppermute | solution.py:314
  55.3 5.4 %collective-permute-start.13 = (bf16[384,1024]{1,0:T(8,128)(2,1)S(1)}, bf16[384,1024]{1,0:T(8,128)(2,1)S(1)}, u32[]{:S(2)}, u32[]{:S(2)}) collective-permute-start(bf16[384,1024]{1,0:T(8,128)(2,1)S(1)} %get-tuple-element.50), channel_id=1, source_target_pairs={{0,1},{1,0},{2,3},{3,2},{4,5},{5,4},{6,7},{7,6},{8,9},{9,8},{10,11... | collective-permute-start | bytes 2359304 | tf_op jit(solution)/shard_map/ppermute | solution.py:314
  59.3 0.7 copy-start.12
  59.9 0.7 copy-start.3
  60.0 0.7 copy-start.5
  60.0 1.5 %collective-permute-start.18 = (bf16[128,1024]{1,0:T(8,128)(2,1)S(1)}, bf16[128,1024]{1,0:T(8,128)(2,1)S(1)}, u32[]{:S(2)}, u32[]{:S(2)}) collective-permute-start(bf16[128,1024]{1,0:T(8,128)(2,1)S(1)} %get-tuple-element.60), channel_id=1, source_target_pairs={{0,1},{1,0},{2,3},{3,2},{4,5},{5,4},{6,7},{7,6},{8,9},{9,8},{10,11... | collective-permute-start | bytes 786440 | tf_op jit(solution)/shard_map/ppermute | solution.py:314
  60.7 9.8 %copy-start.7 = (s32[256,1]{0,1:T(1,128)S(1)}, s32[256,1]{0,1:T(1,128)}, u32[]{:S(2)}) copy-start(s32[256,1]{0,1:T(1,128)} %param.8) | copy-start | bytes 3076
  62.6 33.6 %all-to-all-start = ((bf16[16,32,1024]{2,1,0:T(8,128)(2,1)}), bf16[16,32,1024]{2,1,0:T(8,128)(2,1)S(1)}, u32[]{:S(2)}, u32[]{:S(2)}) async-start(bf16[16,32,1024]{2,1,0:T(8,128)(2,1)} %bitcast.4), calls=%async_computation | async-start | bytes 2097152 | tf_op jit(solution)/shard_map/all_to_all | solution.py:262
  70.8 0.9 copy-start.4
  71.7 0.9 copy-start.6
  72.6 1.4 %copy-start.9 = (bf16[768,1024]{1,0:T(8,128)(2,1)S(1)}, bf16[768,1024]{1,0:T(8,128)(2,1)}, u32[]{:S(2)}) copy-start(bf16[768,1024]{1,0:T(8,128)(2,1)} %copy-done.8) | copy-start | bytes 4718596
  74.0 1.4 %copy-start.11 = (bf16[768,1024]{1,0:T(8,128)(2,1)S(1)}, bf16[768,1024]{1,0:T(8,128)(2,1)}, u32[]{:S(2)}) copy-start(bf16[768,1024]{1,0:T(8,128)(2,1)} %copy-done.10) | copy-start | bytes 4718596
  75.4 0.9 copy-start.13
  76.4 1.0 %copy-start.16 = (bf16[704,384]{1,0:T(8,128)(2,1)S(1)}, bf16[704,384]{1,0:T(8,128)(2,1)}, u32[]{:S(2)}) copy-start(bf16[704,384]{1,0:T(8,128)(2,1)} %copy-done.15) | copy-start | bytes 1622020

commit v13 on v12

--- a/solution.py
+++ b/solution.py
@@ -327,7 +327,7 @@
     def begin(own):
         rows = own.shape[0] // 2
         return pl.pallas_call(
-            functools.partial(begin_kernel, tile),
+            functools.partial(begin_kernel, units),
             out_shape=[jax.ShapeDtypeStruct((units, rows), F32)] * 3,
             in_specs=[IN_VMEM] * 4,
             out_specs=[IN_VMEM] * 3,
@@ -340,7 +340,7 @@
         other = exchange(own)
         rows = own.shape[0] // 2
         hidden, d_gate, d_up, sent = pl.pallas_call(
-            functools.partial(front_kernel, tile),
+            functools.partial(front_kernel, units),
             out_shape=[jax.ShapeDtypeStruct((units, rows), BF16)] * 3
             + [jax.ShapeDtypeStruct((rows, width), BF16)],
             in_specs=[IN_VMEM] * (5 + len(begun)),

time: 98.5 us -> 98.3 us (level)
  transfers between devices with their start and end apart: 20 -> 20, of which waited for: 11 -> 12; matrix products, arithmetic and copies ran while one was open for 0% -> 0% of each run, Pallas kernels for 25% -> 24%
where the time goes in v13:
time: 98.3 us; the launch traced here: 97.9 us
  starting transfers between devices  34.5 us (35%)
  Pallas kernels  29.3 us (30%)
  waiting for transfers between devices  25.7 us (26%)
  local copies, waits for them, and re-layouts  7.35 us (7%)
  between operations  1.04 us (1%)
    ppermute x15, starting transfers between devices, swap(): lax.ppermute(slabs[k], 'expert', [(e, e ^ k) for e in range(experts)])  25.8 us
    ppermute x15, waiting for transfers between devices, swap(): lax.ppermute(slabs[k], 'expert', [(e, e ^ k) for e in range(experts)])  15 us
    all_to_all x1, waiting for transfers between devices, to_experts(): lax.all_to_all(rows.reshape(experts, rows.shape[0] // experts, rows.shape...  9.93 us
    pallas_call x1, Pallas kernels, grouped(): pl.pallas_call(functools.partial(grads_kernel, sizes), grid=(units // til...  8.91 us
    pallas_call x2, Pallas kernels, front(): pl.pallas_call(functools.partial(front_kernel, units), out_shape=[jax.Sha...  8.05 us
    all_to_all x1, starting transfers between devices, to_experts(): lax.all_to_all(rows.reshape(experts, rows.shape[0] // experts, rows.shape...  7.89 us
    unnamed x40, local copies, waits for them, and re-layouts  7.35 us
    pallas_call x2, Pallas kernels, place(): pl.pallas_call(functools.partial(place_kernel, capacity, partners), out_s...  5.76 us
  transfers between devices with their start and end apart: 20, of which 12 were waited for; matrix products, arithmetic and copies ran while one was open for 0% of the time, Pallas kernels for 24%

profile of v13, /device:TPU:8, one launch (start us, length us, event | category | flops | bytes accessed | tf_op | source)
XLA Modules:
  0.0 97.9 jit_solution(11283420418027726909)
XLA Ops:
  0.6 2.6 %place.2 = (bf16[64,1024]{1,0:T(8,128)(2,1)}, bf16[64,1024]{1,0:T(8,128)(2,1)}, bf16[64,1024]{1,0:T(8,128)(2,1)}, bf16[64,1024]{1,0:T(8,128)(2,1)}, bf16[64,1024]{1,0:T(8,128)(2,1)}) custom-call(s32[1,256]{1,0:T(1,128)} %bitcast.23, bf16[256,1024]{1,0:T(8,128)(2,1)} %x_hbm.3, bf16[256,1024]{1,0:T(8,128)(2,1)} %dy_hbm.3), custom_call_target="tpu_custom_call" | custom-call | tf_op jit(solution)/shard_map/place/pallas_call | solution.py:287
  3.2 3.5 %collective-permute-start = (bf16[64,1024]{1,0:T(8,128)(2,1)}, bf16[64,1024]{1,0:T(8,128)(2,1)S(1)}, u32[]{:S(2)}, u32[]{:S(2)}) collective-permute-start(bf16[64,1024]{1,0:T(8,128)(2,1)} %get-tuple-element.36), channel_id=1, source_target_pairs={{0,30},{2,28},{4,26},{6,24},{8,22},{10,20},{12,18},{14,16},{16,14}... | collective-permute-start | bytes 393224 | tf_op jit(solution)/shard_map/ppermute | solution.py:311
  6.8 2.4 %collective-permute-start.1 = (bf16[64,1024]{1,0:T(8,128)(2,1)}, bf16[64,1024]{1,0:T(8,128)(2,1)S(1)}, u32[]{:S(2)}, u32[]{:S(2)}) collective-permute-start(bf16[64,1024]{1,0:T(8,128)(2,1)} %get-tuple-element.37), channel_id=1, source_target_pairs={{0,14},{2,12},{4,10},{6,8},{8,6},{10,4},{12,2},{14,0},{16,30},{18,... | collective-permute-start | bytes 393224 | tf_op jit(solution)/shard_map/ppermute | solution.py:311
  9.2 0.3 collective-permute-start.2
  9.4 1.5 %collective-permute-start.3 = (bf16[64,1024]{1,0:T(8,128)(2,1)}, bf16[64,1024]{1,0:T(8,128)(2,1)S(1)}, u32[]{:S(2)}, u32[]{:S(2)}) collective-permute-start(bf16[64,1024]{1,0:T(8,128)(2,1)} %get-tuple-element.39), channel_id=1, source_target_pairs={{0,12},{2,14},{4,8},{6,10},{8,4},{10,6},{12,0},{14,2},{16,28},{18,... | collective-permute-start | bytes 393224 | tf_op jit(solution)/shard_map/ppermute | solution.py:311
  11.0 2.5 %collective-permute-start.4 = (bf16[64,1024]{1,0:T(8,128)(2,1)}, bf16[64,1024]{1,0:T(8,128)(2,1)S(1)}, u32[]{:S(2)}, u32[]{:S(2)}) collective-permute-start(bf16[64,1024]{1,0:T(8,128)(2,1)} %get-tuple-element.40), channel_id=1, source_target_pairs={{0,26},{2,24},{4,30},{6,28},{8,18},{10,16},{12,22},{14,20},{16,10}... | collective-permute-start | bytes 393224 | tf_op jit(solution)/shard_map/ppermute | solution.py:311
  13.5 3.1 %place.3 = (bf16[64,1024]{1,0:T(8,128)(2,1)}, bf16[64,1024]{1,0:T(8,128)(2,1)}, bf16[64,1024]{1,0:T(8,128)(2,1)}, bf16[64,1024]{1,0:T(8,128)(2,1)}, bf16[64,1024...) custom-call(s32[1,256]{1,0:T(1,128)} %bitcast.24, ...), custom_call_target="tpu_custom_call" | custom-call | tf_op jit(solution)/shard_map/place/pallas_call | solution.py:287
  16.6 2.5 %collective-permute-start.5 = (bf16[64,1024]{1,0:T(8,128)(2,1)}, bf16[64,1024]{1,0:T(8,128)(2,1)S(1)}, u32[]{:S(2)}, u32[]{:S(2)}) collective-permute-start(bf16[64,1024]{1,0:T(8,128)(2,1)} %get-tuple-element.41), channel_id=1, source_target_pairs={{0,10},{2,8},{4,14},{6,12},{8,2},{10,0},{12,6},{14,4},{16,26},{18,... | collective-permute-start | bytes 393224 | tf_op jit(solution)/shard_map/ppermute | solution.py:311
  19.2 1.8 %collective-permute-done.2.refs_2_ = bf16[64,1024]{1,0:T(8,128)(2,1)S(1)} collective-permute-done((bf16[64,1024]{1,0:T(8,128)(2,1)}, bf16[64,1024]{1,0:T(8,128)(2,1)S(1)}, u32[]{:S(2)}, u32[]{:S(2)}) %collective-permute-start.2) | collective-permute-done | bytes 131104 | tf_op jit(solution)/shard_map/ppermute | solution.py:311
  21.0 0.7 collective-permute-start.7
  21.7 0.5 collective-permute-done.3.refs_3_
  22.2 3.4 %collective-permute-start.8 = (bf16[64,1024]{1,0:T(8,128)(2,1)}, bf16[64,1024]{1,0:T(8,128)(2,1)S(1)}, u32[]{:S(2)}, u32[]{:S(2)}) collective-permute-start(bf16[64,1024]{1,0:T(8,128)(2,1)} %get-tuple-element.44), channel_id=1, source_target_pairs={{0,22},{2,20},{4,18},{6,16},{8,30},{10,28},{12,26},{14,24},{16,6},... | collective-permute-start | bytes 393224 | tf_op jit(solution)/shard_map/ppermute | solution.py:311
  25.6 0.3 collective-permute-done.4.refs_4_
  25.9 3.9 %collective-permute-start.9 = (bf16[64,1024]{1,0:T(8,128)(2,1)}, bf16[64,1024]{1,0:T(8,128)(2,1)S(1)}, u32[]{:S(2)}, u32[]{:S(2)}) collective-permute-start(bf16[64,1024]{1,0:T(8,128)(2,1)} %get-tuple-element.45), channel_id=1, source_target_pairs={{0,6},{2,4},{4,2},{6,0},{8,14},{10,12},{12,10},{14,8},{16,22},{18,... | collective-permute-start | bytes 393224 | tf_op jit(solution)/shard_map/ppermute | solution.py:311
  29.8 2.5 %collective-permute-done.6.refs_6_ = bf16[64,1024]{1,0:T(8,128)(2,1)S(1)} collective-permute-done((bf16[64,1024]{1,0:T(8,128)(2,1)}, bf16[64,1024]{1,0:T(8,128)(2,1)S(1)}, u32[]{:S(2)}, u32[]{:S(2)}) %collective-permute-start.6) | collective-permute-done | bytes 131104 | tf_op jit(solution)/shard_map/ppermute | solution.py:311
  32.4 0.6 collective-permute-start.11
  32.9 0.6 collective-permute-done.7.refs_7_
  33.5 5.3 %collective-permute-done.8.refs_8_ = bf16[64,1024]{1,0:T(8,128)(2,1)S(1)} collective-permute-done((bf16[64,1024]{1,0:T(8,128)(2,1)}, bf16[64,1024]{1,0:T(8,128)(2,1)S(1)}, u32[]{:S(2)}, u32[]{:S(2)}) %collective-permute-start.8) | collective-permute-done | bytes 131104 | tf_op jit(solution)/shard_map/ppermute | solution.py:311
  38.7 2.0 %collective-permute-done.10.refs_10_ = bf16[64,1024]{1,0:T(8,128)(2,1)S(1)} collective-permute-done((bf16[64,1024]{1,0:T(8,128)(2,1)}, bf16[64,1024]{1,0:T(8,128)(2,1)S(1)}, u32[]{:S(2)}, u32[]{:S(2)}) %collective-permute-start.10) | collective-permute-done | bytes 131104 | tf_op jit(solution)/shard_map/ppermute | solution.py:311
  40.7 0.6 collective-permute-done.11.refs_11_
  41.6 2.8 %collective-permute-start.14 = (bf16[64,1024]{1,0:T(8,128)(2,1)S(1)}, bf16[64,1024]{1,0:T(8,128)(2,1)S(1)}, u32[]{:S(2)}, u32[]{:S(2)}) collective-permute-start(bf16[64,1024]{1,0:T(8,128)(2,1)S(1)} %copy-done.19), channel_id=1, source_target_pairs={{0,18},{2,16},{4,22},{6,20},{8,26},{10,24},{12,30},{14,28},{16,2},... | collective-permute-start | bytes 393224 | tf_op jit(solution)/shard_map/ppermute | solution.py:311
  44.4 0.3 collective-permute-start.15
  44.7 1.4 %collective-permute-start.16 = (bf16[64,1024]{1,0:T(8,128)(2,1)S(1)}, bf16[64,1024]{1,0:T(8,128)(2,1)S(1)}, u32[]{:S(2)}, u32[]{:S(2)}) collective-permute-start(bf16[64,1024]{1,0:T(8,128)(2,1)S(1)} %copy-done.17), channel_id=1, source_target_pairs={{0,2},{2,0},{4,6},{6,4},{8,10},{10,8},{12,14},{14,12},{16,18},{18,... | collective-permute-start | bytes 393224 | tf_op jit(solution)/shard_map/ppermute | solution.py:311
  46.1 6.1 %front.2 = (bf16[704,384]{1,0:T(8,128)(2,1)S(1)}, bf16[704,384]{1,0:T(8,128)(2,1)S(1)}, bf16[704,384]{1,0:T(8,128)(2,1)S(1)}, bf16[384,1024]{1,0:T(8,128)(2,1)S(1)}) custom-call(bf16[768,1024]{1,0:T(8,128)(2,1)S(1)} %collect.2.own_ref.refs_0_, bf16[768,1024]{1,0:T(8,128)(2,1)S(1)} %collective-permute-done.12.other_ref.refs_1_, ...), custom_call_target="tpu_custom_call" | custom-call | flops 4429185024 | bytes 17825792 | tf_op jit(solution)/shard_map/front/pallas_call | solution.py:342
  52.2 1.4 %kept.2.kept_ref.refs_4_ = f32[384,1024]{1,0:T(8,128)S(1)} custom-call(bf16[704,384]{1,0:T(8,128)(2,1)S(1)} %get-tuple-element.48.d_gate_ref.refs_2_, bf16[704,384]{1,0:T(8,128)(2,1)S(1)} %get-tuple-element.49.d_up_ref.refs_3_, bf16[704,2048]{1,0:T(8,128)(2,1)S(1)} %bitcast.10, bf16[704,2048]{1,0:T(8,128)(2,1)S(1)} %bitcast.15), custom_call_target="tpu_custom_call" | custom-call | flops 1107296256 | bytes 4456448 | tf_op jit(solution)/shard_map/kept/pallas_call | solution.py:352
  53.7 1.4 %collective-permute-done.15.refs_1_ = bf16[64,1024]{1,0:T(8,128)(2,1)S(1)} collective-permute-done((bf16[64,1024]{1,0:T(8,128)(2,1)S(1)}, bf16[64,1024]{1,0:T(8,128)(2,1)S(1)}, u32[]{:S(2)}, u32[]{:S(2)}) %collective-permute-start.15) | collective-permute-done | bytes 131104 | tf_op jit(solution)/shard_map/ppermute | solution.py:311
  55.2 0.1 collective-permute-start.17
  55.3 0.5 collective-permute-start.13
  55.7 1.3 %begin.1 = (f32[704,128]{1,0:T(8,128)S(1)}, f32[704,128]{1,0:T(8,128)S(1)}, f32[704,128]{1,0:T(8,128)S(1)}) custom-call(bf16[256,1024]{1,0:T(8,128)(2,1)S(1)} %collect.3.own_ref.refs_5_, bf16[704,2048]{1,0:T(8,128)(2,1)S(1)} %bitcast.11, bf16[704,2048]{1,0:T(8,128)(2,1)S(1)} %bitcast.16, bf16[704,2048]{1,0:T(8,128)(2,1)S(1)} %bitcast.20), custom_call_target="tpu_custom_call" | custom-call | flops 738197504 | bytes 6815744 | tf_op jit(solution)/shard_map/begin/pallas_call | solution.py:329
  57.0 0.1 collective-permute-done.17.other_ref.refs_6_
  57.1 1.9 %front.3 = (bf16[704,128]{1,0:T(8,128)(2,1)S(1)}, bf16[704,128]{1,0:T(8,128)(2,1)S(1)}, bf16[704,128]{1,0:T(8,128)(2,1)S(1)}, bf16[128,1024]{1,0:T(8,128)(2,1)S(1)}) custom-call(bf16[256,1024]{1,0:T(8,128)(2,1)S(1)} %collect.3.own_ref.refs_5_, bf16[256,1024]{1,0:T(8,128)(2,1)S(1)} %collective-permute-done.17.other_ref.refs_6_, ...), custom_call_target="tpu_custom_call" | custom-call | flops 1476395008 | bytes 13631488 | tf_op jit(solution)/shard_map/front/pallas_call | solution.py:342
  59.1 0.7 copy-done.12
  59.7 0.1 collective-permute-start.18
  59.9 0.6 kept.3.kept_ref
  60.5 0.1 sum.1.sum_ref
  60.7 0.6 collective-permute-done.18.got_ref
  61.3 1.1 %last_sum.1 = (bf16[512,1024]{1,0:T(8,128)(2,1)}, f32[8,128]{1,0:T(8,128)S(1)}) custom-call(bf16[384,1024]{1,0:T(8,128)(2,1)S(1)} %sum.1.sum_ref, f32[128,1024]{1,0:T(8,128)S(1)} %kept.3.kept_ref, bf16[128,1024]{1,0:T(8,128)(2,1)S(1)} %collective-permute-done.18.got_ref), custom_call_target="tpu_custom_call" | custom-call | tf_op jit(solution)/shard_map/last_sum/pallas_call | solution.py:376
  62.4 7.9 %all-to-all-start = ((bf16[16,32,1024]{2,1,0:T(8,128)(2,1)}), bf16[16,32,1024]{2,1,0:T(8,128)(2,1)S(1)}, u32[]{:S(2)}, u32[]{:S(2)}) async-start(bf16[16,32,1024]{2,1,0:T(8,128)(2,1)} %bitcast.4), calls=%async_computation | async-start | bytes 2097152 | tf_op jit(solution)/shard_map/all_to_all | solution.py:262
  70.3 0.3 placing.1.placing_ref.refs_10_
  70.6 0.9 copy-done.4
  71.5 0.9 copy-done.6
  72.4 1.4 %copy-done.9 = bf16[768,1024]{1,0:T(8,128)(2,1)S(1)} copy-done((bf16[768,1024]{1,0:T(8,128)(2,1)S(1)}, bf16[768,1024]{1,0:T(8,128)(2,1)}, u32[]{:S(2)}) %copy-start.9) | copy-done | bytes 1572888
  73.8 1.4 %copy-done.11 = bf16[768,1024]{1,0:T(8,128)(2,1)S(1)} copy-done((bf16[768,1024]{1,0:T(8,128)(2,1)S(1)}, bf16[768,1024]{1,0:T(8,128)(2,1)}, u32[]{:S(2)}) %copy-start.11) | copy-done | bytes 1572888
  75.2 0.9 copy-done.13
  76.2 1.0 %copy-done.16 = bf16[704,384]{1,0:T(8,128)(2,1)S(1)} copy-done((bf16[704,384]{1,0:T(8,128)(2,1)S(1)}, bf16[704,384]{1,0:T(8,128)(2,1)}, u32[]{:S(2)}) %copy-start.16) | copy-done | bytes 540696
  77.2 8.9 %grads.1 = (bf16[704,2048]{1,0:T(8,128)(2,1)}, bf16[704,2048]{1,0:T(8,128)(2,1)}, bf16[704,2048]{1,0:T(8,128)(2,1)}) custom-call(bf16[768,1024]{1,0:T(8,128)(2,1)S(1)} %copy-done.9, bf16[768,1024]{1,0:T(8,128)(2,1)S(1)} %copy-done.11, bf16[704,384]{1,0:T(8,128)(2,1)S(1)} %get-tuple-element.48.d_gate_ref.refs_2_, ...), custom_call_target="tpu_custom_call" | custom-call | flops 4429185024 | bytes 14942208 | tf_op jit(solution)/shard_map/grads/pallas_call | solution.py:396
  86.1 9.9 %all-to-all-done = bf16[16,32,1024]{2,1,0:T(8,128)(2,1)S(1)} async-done(((bf16[16,32,1024]{2,1,0:T(8,128)(2,1)}), bf16[16,32,1024]{2,1,0:T(8,128)(2,1)S(1)}, u32[]{:S(2)}, u32[]{:S(2)}) %all-to-all-start) | async-done | bytes 1048608 | tf_op jit(solution)/shard_map/all_to_all | solution.py:262
  96.0 1.7 %combine.1 = bf16[256,1024]{1,0:T(8,128)(2,1)} custom-call(bf16[256,512]{1,0:T(8,128)(2,1)S(1)} %placing.1.placing_ref.refs_10_, bf16[512,1024]{1,0:T(8,128)(2,1)S(1)} %bitcast.22), custom_call_target="tpu_custom_call" | custom-call | tf_op jit(solution)/shard_map/combine/pallas_call | solution.py:250
  (46 shorter events, 0.4 us)
Async XLA Ops:
  3.2 13.4 %collective-permute-start = (bf16[64,1024]{1,0:T(8,128)(2,1)}, bf16[64,1024]{1,0:T(8,128)(2,1)S(1)}, u32[]{:S(2)}, u32[]{:S(2)}) collective-permute-start(bf16[64,1024]{1,0:T(8,128)(2,1)} %get-tuple-element.36), channel_id=1, source_target_pairs={{0,30},{2,28},{4,26},{6,24},{8,22},{10,20},{12,18},{14,16},{16,14}... | collective-permute-start | bytes 393224 | tf_op jit(solution)/shard_map/ppermute | solution.py:311
  6.8 12.4 %collective-permute-start.1 = (bf16[64,1024]{1,0:T(8,128)(2,1)}, bf16[64,1024]{1,0:T(8,128)(2,1)S(1)}, u32[]{:S(2)}, u32[]{:S(2)}) collective-permute-start(bf16[64,1024]{1,0:T(8,128)(2,1)} %get-tuple-element.37), channel_id=1, source_target_pairs={{0,14},{2,12},{4,10},{6,8},{8,6},{10,4},{12,2},{14,0},{16,30},{18,... | collective-permute-start | bytes 393224 | tf_op jit(solution)/shard_map/ppermute | solution.py:311
  9.2 11.9 %collective-permute-start.2 = (bf16[64,1024]{1,0:T(8,128)(2,1)}, bf16[64,1024]{1,0:T(8,128)(2,1)S(1)}, u32[]{:S(2)}, u32[]{:S(2)}) collective-permute-start(bf16[64,1024]{1,0:T(8,128)(2,1)} %get-tuple-element.38), channel_id=1, source_target_pairs={{0,28},{2,30},{4,24},{6,26},{8,20},{10,22},{12,16},{14,18},{16,12}... | collective-permute-start | bytes 393224 | tf_op jit(solution)/shard_map/ppermute | solution.py:311
  9.4 12.7 %collective-permute-start.3 = (bf16[64,1024]{1,0:T(8,128)(2,1)}, bf16[64,1024]{1,0:T(8,128)(2,1)S(1)}, u32[]{:S(2)}, u32[]{:S(2)}) collective-permute-start(bf16[64,1024]{1,0:T(8,128)(2,1)} %get-tuple-element.39), channel_id=1, source_target_pairs={{0,12},{2,14},{4,8},{6,10},{8,4},{10,6},{12,0},{14,2},{16,28},{18,... | collective-permute-start | bytes 393224 | tf_op jit(solution)/shard_map/ppermute | solution.py:311
  11.0 14.9 %collective-permute-start.4 = (bf16[64,1024]{1,0:T(8,128)(2,1)}, bf16[64,1024]{1,0:T(8,128)(2,1)S(1)}, u32[]{:S(2)}, u32[]{:S(2)}) collective-permute-start(bf16[64,1024]{1,0:T(8,128)(2,1)} %get-tuple-element.40), channel_id=1, source_target_pairs={{0,26},{2,24},{4,30},{6,28},{8,18},{10,16},{12,22},{14,20},{16,10}... | collective-permute-start | bytes 393224 | tf_op jit(solution)/shard_map/ppermute | solution.py:311
  16.6 13.2 %collective-permute-start.5 = (bf16[64,1024]{1,0:T(8,128)(2,1)}, bf16[64,1024]{1,0:T(8,128)(2,1)S(1)}, u32[]{:S(2)}, u32[]{:S(2)}) collective-permute-start(bf16[64,1024]{1,0:T(8,128)(2,1)} %get-tuple-element.41), channel_id=1, source_target_pairs={{0,10},{2,8},{4,14},{6,12},{8,2},{10,0},{12,6},{14,4},{16,26},{18,... | collective-permute-start | bytes 393224 | tf_op jit(solution)/shard_map/ppermute | solution.py:311
  19.1 13.2 %collective-permute-start.6 = (bf16[64,1024]{1,0:T(8,128)(2,1)}, bf16[64,1024]{1,0:T(8,128)(2,1)S(1)}, u32[]{:S(2)}, u32[]{:S(2)}) collective-permute-start(bf16[64,1024]{1,0:T(8,128)(2,1)} %get-tuple-element.42), channel_id=1, source_target_pairs={{0,24},{2,26},{4,28},{6,30},{8,16},{10,18},{12,20},{14,22},{16,8},... | collective-permute-start | bytes 393224 | tf_op jit(solution)/shard_map/ppermute | solution.py:311
  21.0 12.4 %collective-permute-start.7 = (bf16[64,1024]{1,0:T(8,128)(2,1)}, bf16[64,1024]{1,0:T(8,128)(2,1)S(1)}, u32[]{:S(2)}, u32[]{:S(2)}) collective-permute-start(bf16[64,1024]{1,0:T(8,128)(2,1)} %get-tuple-element.43), channel_id=1, source_target_pairs={{0,8},{2,10},{4,12},{6,14},{8,0},{10,2},{12,4},{14,6},{16,24},{18,... | collective-permute-start | bytes 393224 | tf_op jit(solution)/shard_map/ppermute | solution.py:311
  22.2 16.5 %collective-permute-start.8 = (bf16[64,1024]{1,0:T(8,128)(2,1)}, bf16[64,1024]{1,0:T(8,128)(2,1)S(1)}, u32[]{:S(2)}, u32[]{:S(2)}) collective-permute-start(bf16[64,1024]{1,0:T(8,128)(2,1)} %get-tuple-element.44), channel_id=1, source_target_pairs={{0,22},{2,20},{4,18},{6,16},{8,30},{10,28},{12,26},{14,24},{16,6},... | collective-permute-start | bytes 393224 | tf_op jit(solution)/shard_map/ppermute | solution.py:311
  25.9 12.8 %collective-permute-start.9 = (bf16[64,1024]{1,0:T(8,128)(2,1)}, bf16[64,1024]{1,0:T(8,128)(2,1)S(1)}, u32[]{:S(2)}, u32[]{:S(2)}) collective-permute-start(bf16[64,1024]{1,0:T(8,128)(2,1)} %get-tuple-element.45), channel_id=1, source_target_pairs={{0,6},{2,4},{4,2},{6,0},{8,14},{10,12},{12,10},{14,8},{16,22},{18,... | collective-permute-start | bytes 393224 | tf_op jit(solution)/shard_map/ppermute | solution.py:311
  29.8 10.9 %collective-permute-start.10 = (bf16[64,1024]{1,0:T(8,128)(2,1)}, bf16[64,1024]{1,0:T(8,128)(2,1)S(1)}, u32[]{:S(2)}, u32[]{:S(2)}) collective-permute-start(bf16[64,1024]{1,0:T(8,128)(2,1)} %get-tuple-element.46), channel_id=1, source_target_pairs={{0,20},{2,22},{4,16},{6,18},{8,28},{10,30},{12,24},{14,26},{16,4},... | collective-permute-start | bytes 393224 | tf_op jit(solution)/shard_map/ppermute | solution.py:311
  32.3 9.2 %copy-start.19 = (bf16[64,1024]{1,0:T(8,128)(2,1)S(1)}, bf16[64,1024]{1,0:T(8,128)(2,1)}, u32[]{:S(2)}) copy-start(bf16[64,1024]{1,0:T(8,128)(2,1)} %get-tuple-element.51) | copy-start | bytes 393220
  32.3 12.1 %copy-start.18 = (bf16[64,1024]{1,0:T(8,128)(2,1)S(1)}, bf16[64,1024]{1,0:T(8,128)(2,1)}, u32[]{:S(2)}) copy-start(bf16[64,1024]{1,0:T(8,128)(2,1)} %get-tuple-element.52) | copy-start | bytes 393220
  32.3 12.3 %copy-start.17 = (bf16[64,1024]{1,0:T(8,128)(2,1)S(1)}, bf16[64,1024]{1,0:T(8,128)(2,1)}, u32[]{:S(2)}) copy-start(bf16[64,1024]{1,0:T(8,128)(2,1)} %get-tuple-element.53) | copy-start | bytes 393220
  32.3 13.7 %copy-start = (bf16[1,704,2048]{2,1,0:T(8,128)(2,1)S(1)}, bf16[1,704,2048]{2,1,0:T(8,128)(2,1)}, u32[]{:S(2)}) copy-start(bf16[1,704,2048]{2,1,0:T(8,128)(2,1)} %param.9) | copy-start | bytes 8650756
  32.3 13.7 %copy-start.1 = (bf16[1,704,2048]{2,1,0:T(8,128)(2,1)S(1)}, bf16[1,704,2048]{2,1,0:T(8,128)(2,1)}, u32[]{:S(2)}) copy-start(bf16[1,704,2048]{2,1,0:T(8,128)(2,1)} %param.10) | copy-start | bytes 8650756
  32.3 13.7 %copy-start.2 = (bf16[1,704,2048]{2,1,0:T(8,128)(2,1)S(1)}, bf16[1,704,2048]{2,1,0:T(8,128)(2,1)}, u32[]{:S(2)}) copy-start(bf16[1,704,2048]{2,1,0:T(8,128)(2,1)} %param.11) | copy-start | bytes 8650756
  32.4 9.0 %collective-permute-start.11 = (bf16[64,1024]{1,0:T(8,128)(2,1)}, bf16[64,1024]{1,0:T(8,128)(2,1)S(1)}, u32[]{:S(2)}, u32[]{:S(2)}) collective-permute-start(bf16[64,1024]{1,0:T(8,128)(2,1)} %get-tuple-element.47), channel_id=1, source_target_pairs={{0,4},{2,6},{4,0},{6,2},{8,12},{10,14},{12,8},{14,10},{16,20},{18,... | collective-permute-start | bytes 393224 | tf_op jit(solution)/shard_map/ppermute | solution.py:311
  41.5 10.8 %copy-start.8 = (bf16[768,1024]{1,0:T(8,128)(2,1)}, bf16[768,1024]{1,0:T(8,128)(2,1)S(1)}, u32[]{:S(2)}) copy-start(bf16[768,1024]{1,0:T(8,128)(2,1)S(1)} %collect.2.own_ref.refs_0_) | copy-start | bytes 4718596
  41.5 4.6 %collective-permute-start.12 = (bf16[768,1024]{1,0:T(8,128)(2,1)S(1)}, bf16[768,1024]{1,0:T(8,128)(2,1)S(1)}, u32[]{:S(2)}, u32[]{:S(2)}) collective-permute-start(bf16[768,1024]{1,0:T(8,128)(2,1)S(1)} %collect.2.own_ref.refs_0_), channel_id=1, source_target_pairs={{0,1},{1,0},{2,3},{3,2},{4,5},{5,4},{6,7},{7,6},{8,9},{9,8},{10,11... | collective-permute-start | bytes 4718600 | tf_op jit(solution)/shard_map/ppermute | solution.py:314
  41.6 12.1 %collective-permute-start.14 = (bf16[64,1024]{1,0:T(8,128)(2,1)S(1)}, bf16[64,1024]{1,0:T(8,128)(2,1)S(1)}, u32[]{:S(2)}, u32[]{:S(2)}) collective-permute-start(bf16[64,1024]{1,0:T(8,128)(2,1)S(1)} %copy-done.19), channel_id=1, source_target_pairs={{0,18},{2,16},{4,22},{6,20},{8,26},{10,24},{12,30},{14,28},{16,2},... | collective-permute-start | bytes 393224 | tf_op jit(solution)/shard_map/ppermute | solution.py:311
  44.4 10.7 %collective-permute-start.15 = (bf16[64,1024]{1,0:T(8,128)(2,1)S(1)}, bf16[64,1024]{1,0:T(8,128)(2,1)S(1)}, u32[]{:S(2)}, u32[]{:S(2)}) collective-permute-start(bf16[64,1024]{1,0:T(8,128)(2,1)S(1)} %copy-done.18), channel_id=1, source_target_pairs={{0,16},{2,18},{4,20},{6,22},{8,24},{10,26},{12,28},{14,30},{16,0},... | collective-permute-start | bytes 393224 | tf_op jit(solution)/shard_map/ppermute | solution.py:311
  44.7 10.5 %collective-permute-start.16 = (bf16[64,1024]{1,0:T(8,128)(2,1)S(1)}, bf16[64,1024]{1,0:T(8,128)(2,1)S(1)}, u32[]{:S(2)}, u32[]{:S(2)}) collective-permute-start(bf16[64,1024]{1,0:T(8,128)(2,1)S(1)} %copy-done.17), channel_id=1, source_target_pairs={{0,2},{2,0},{4,6},{6,4},{8,10},{10,8},{12,14},{14,12},{16,18},{18,... | collective-permute-start | bytes 393224 | tf_op jit(solution)/shard_map/ppermute | solution.py:311
  46.1 6.2 %copy-start.10 = (bf16[768,1024]{1,0:T(8,128)(2,1)}, bf16[768,1024]{1,0:T(8,128)(2,1)S(1)}, u32[]{:S(2)}) copy-start(bf16[768,1024]{1,0:T(8,128)(2,1)S(1)} %collective-permute-done.12.other_ref.refs_1_) | copy-start | bytes 4718596
  52.2 1.4 %copy-start.15 = (bf16[704,384]{1,0:T(8,128)(2,1)}, bf16[704,384]{1,0:T(8,128)(2,1)S(1)}, u32[]{:S(2)}) copy-start(bf16[704,384]{1,0:T(8,128)(2,1)S(1)} %get-tuple-element.63.refs_4_) | copy-start | bytes 1622020
  52.2 2.9 %copy-start.14 = (bf16[64,1024]{1,0:T(8,128)(2,1)S(1)}, bf16[64,1024]{1,0:T(8,128)(2,1)}, u32[]{:S(2)}) copy-start(bf16[64,1024]{1,0:T(8,128)(2,1)} %get-tuple-element.54.refs_3_) | copy-start | bytes 393220
  55.2 2.0 %collective-permute-start.17 = (bf16[256,1024]{1,0:T(8,128)(2,1)S(1)}, bf16[256,1024]{1,0:T(8,128)(2,1)S(1)}, u32[]{:S(2)}, u32[]{:S(2)}) collective-permute-start(bf16[256,1024]{1,0:T(8,128)(2,1)S(1)} %collect.3.own_ref.refs_5_), channel_id=1, source_target_pairs={{0,1},{1,0},{2,3},{3,2},{4,5},{5,4},{6,7},{7,6},{8,9},{9,8},{10,11... | collective-permute-start | bytes 1572872 | tf_op jit(solution)/shard_map/ppermute | solution.py:314
  55.3 5.2 %collective-permute-start.13 = (bf16[384,1024]{1,0:T(8,128)(2,1)S(1)}, bf16[384,1024]{1,0:T(8,128)(2,1)S(1)}, u32[]{:S(2)}, u32[]{:S(2)}) collective-permute-start(bf16[384,1024]{1,0:T(8,128)(2,1)S(1)} %get-tuple-element.50), channel_id=1, source_target_pairs={{0,1},{1,0},{2,3},{3,2},{4,5},{5,4},{6,7},{7,6},{8,9},{9,8},{10,11... | collective-permute-start | bytes 2359304 | tf_op jit(solution)/shard_map/ppermute | solution.py:314
  59.1 0.7 copy-start.12
  59.7 0.7 copy-start.3
  59.7 0.8 copy-start.5
  59.7 1.5 %collective-permute-start.18 = (bf16[128,1024]{1,0:T(8,128)(2,1)S(1)}, bf16[128,1024]{1,0:T(8,128)(2,1)S(1)}, u32[]{:S(2)}, u32[]{:S(2)}) collective-permute-start(bf16[128,1024]{1,0:T(8,128)(2,1)S(1)} %get-tuple-element.60), channel_id=1, source_target_pairs={{0,1},{1,0},{2,3},{3,2},{4,5},{5,4},{6,7},{7,6},{8,9},{9,8},{10,11... | collective-permute-start | bytes 786440 | tf_op jit(solution)/shard_map/ppermute | solution.py:314
  60.5 9.8 %copy-start.7 = (s32[256,1]{0,1:T(1,128)S(1)}, s32[256,1]{0,1:T(1,128)}, u32[]{:S(2)}) copy-start(s32[256,1]{0,1:T(1,128)} %param.8) | copy-start | bytes 3076
  62.4 33.6 %all-to-all-start = ((bf16[16,32,1024]{2,1,0:T(8,128)(2,1)}), bf16[16,32,1024]{2,1,0:T(8,128)(2,1)S(1)}, u32[]{:S(2)}, u32[]{:S(2)}) async-start(bf16[16,32,1024]{2,1,0:T(8,128)(2,1)} %bitcast.4), calls=%async_computation | async-start | bytes 2097152 | tf_op jit(solution)/shard_map/all_to_all | solution.py:262
  70.6 0.9 copy-start.4
  71.5 0.9 copy-start.6
  72.4 1.4 %copy-start.9 = (bf16[768,1024]{1,0:T(8,128)(2,1)S(1)}, bf16[768,1024]{1,0:T(8,128)(2,1)}, u32[]{:S(2)}) copy-start(bf16[768,1024]{1,0:T(8,128)(2,1)} %copy-done.8) | copy-start | bytes 4718596
  73.8 1.4 %copy-start.11 = (bf16[768,1024]{1,0:T(8,128)(2,1)S(1)}, bf16[768,1024]{1,0:T(8,128)(2,1)}, u32[]{:S(2)}) copy-start(bf16[768,1024]{1,0:T(8,128)(2,1)} %copy-done.10) | copy-start | bytes 4718596
  75.2 0.9 copy-start.13
  76.2 1.0 %copy-start.16 = (bf16[704,384]{1,0:T(8,128)(2,1)S(1)}, bf16[704,384]{1,0:T(8,128)(2,1)}, u32[]{:S(2)}) copy-start(bf16[704,384]{1,0:T(8,128)(2,1)} %copy-done.15) | copy-start | bytes 1622020
